TPU v7x, 32 devices: a whole 2x2x4 slice. The times are simulated.
32 devices in a mesh: row: 8 (over z, y), proto: 4 (over x, core).
Axes of the slice: x: 2, y: 2, z: 4, core: 2. Of those that a mesh axis runs over, the one named last changes fastest.
Arguments:
- embeddings: bfloat16 [2048, 128], P('row'), may hold values from -6.75 to 6.75
- second_view: bfloat16 [2048, 128], P('row'), may hold values from -6.75 to 6.75
- prototypes: bfloat16 [16384, 128], P('proto'), may hold values from -6.75 to 6.75
- row_scale: float32 [2048], P('row'), may hold values from 1 to 16, as said below
- col_scale: float32 [16384], P('proto'), may hold values from 1 to 16, as said below
Outputs:
- embed_grad: float32 [2048, 128], P(('row', 'proto'))
- proto_grad: float32 [16384, 128], P(('proto', 'row'))
Inputs may be any that keep to these rules, and one draw needn't show every extreme that they name: `row_scale`: positive scalings. `col_scale`: positive scalings.
All inputs are finite; a program needn't handle non-finite values.
Results may differ from a plain program's by a relative error of at most 0.0025.
Values may be sent and summed in bfloat16 or wider, within the bound.
No kernel may reach another device: no remote copies, remote signals or barrier semaphores. Data moves between devices by JAX's collectives and lax.ppermute only.
A program may use at most 64 MiB of HBM per device.

v0:
```python
import jax
import jax.numpy as jnp
from jax import lax
from jax.sharding import PartitionSpec as P

ITERS = 4


def contract_rows(left, right):
    return lax.dot_general(
        left, right, (((0,), (0,)), ((), ())), preferred_element_type=jnp.float32
    )


def contract_width(left, right):
    return lax.dot_general(
        left, right, (((1,), (1,)), ((), ())), preferred_element_type=jnp.float32
    )


def per_device(embeddings, second_view, prototypes, row_scale, col_scale):
    feat_width = embeddings.shape[1]
    proto_count = prototypes.shape[0]
    logit_scale = 1.0 / (0.05 * feat_width)
    view_scale = 1.0 / (0.1 * feat_width)
    plan_mass = 64.0 * proto_count * lax.axis_size("proto")

    def make_plan():
        logits = contract_width(embeddings, prototypes) * logit_scale
        return row_scale[:, None] * col_scale[None, :] * jnp.exp(logits) / plan_mass

    def make_cot():
        return -contract_width(second_view, prototypes) * view_scale

    stored_plan = make_plan()
    cotangent = make_cot()
    weighted = stored_plan * cotangent

    def plan_now():
        return make_plan()

    row_mass, row_weight = lax.psum((stored_plan.sum(1), weighted.sum(1)), "proto")
    row_dual = row_weight / row_mass
    col_mass, col_weight = lax.psum((stored_plan.sum(0), weighted.sum(0)), "row")

    def solve_cols(duals_rows):
        product = lax.psum(jnp.dot(duals_rows, plan_now(), precision=lax.Precision.HIGHEST), "row")
        return (col_weight - product) / col_mass

    col_dual = solve_cols(row_dual)
    for sweep in range(ITERS - 1):
        product = lax.psum(jnp.dot(plan_now(), col_dual, precision=lax.Precision.HIGHEST), "proto")
        row_dual = (row_weight - product) / row_mass
        col_dual = solve_cols(row_dual)
    final_plan, final_cot = (make_plan(), make_cot())
    logit_grad = final_plan * (final_cot - row_dual[:, None] - col_dual[None, :])
    scaled_grad = (logit_scale * logit_grad).astype(jnp.bfloat16)
    scaled_plan = (-view_scale * final_plan).astype(jnp.bfloat16)
    embed_grad = lax.psum_scatter(
        jnp.dot(scaled_grad, prototypes, preferred_element_type=jnp.float32),
        "proto",
        scatter_dimension=0,
        tiled=True,
    )
    stacked = jnp.concatenate((scaled_grad, scaled_plan), 0)
    sources = jnp.concatenate((embeddings, second_view), 0)
    proto_grad = lax.psum_scatter(
        contract_rows(stacked, sources), "row", scatter_dimension=0, tiled=True
    )
    return (embed_grad, proto_grad)


def solution(mesh):
    return jax.shard_map(
        per_device,
        mesh=mesh,
        in_specs=(P("row", None), P("row", None), P("proto", None), P("row"), P("proto")),
        out_specs=(P(("row", "proto"), None), P(("proto", "row"), None)),
        check_vma=False,
    )
```

profile of v0, /device:TPU:0, one launch (start us, length us, event | category | flops | bytes accessed | tf_op | source)
XLA Modules:
  0.0 313.3 jit_solution(4448945470885214365)
XLA Ops:
  7.2 0.0 copy-start
  7.2 0.0 copy-start.2
  7.2 0.0 reduce-scatter.3.cloned.1.call-start
  7.2 1.2 copy-done
  8.4 1.7 fusion.2
  10.1 0.0 copy-done.2
  10.1 0.0 copy-start.1
  10.1 3.3 %multiply_reduce_fusion.1 = (f32[256]{0:T(256)S(1)}, f32[4096]{0:T(1024)S(1)}, f32[256]{0:T(256)S(1)}, f32[4096]{0:T(1024)S(1)}, f32[256,4096]{1,0:T(8,128)}) fusion(f32[256,4096]{1,0:T(8,128)S(1)} %fusion.2, bf16[256,128]{1,0:T(8,128)(2,1)S(1)} %copy-done.2, bf16[4096,128]{1,0:T(8,128)(2,1)S(1)} %copy-done), kind=kOutput, calls=%fused_computation.13 | convolution fusion | flops 276815360 | bytes 9537536 | tf_op jit(solution)/shard_map/dot_general | solution.py:16
  13.5 0.0 copy-done.1
  13.5 8.3 %all-reduce.1 = (f32[256]{0:T(256)S(1)}, f32[256]{0:T(256)S(1)}) all-reduce(f32[256]{0:T(256)S(1)} %get-tuple-element.2, f32[256]{0:T(256)S(1)} %get-tuple-element.4), channel_id=1, replica_groups=mesh['row'=8,'proto'=4] {'proto'}, use_global_device_ids=true, to_apply=%region_1.0 | all-reduce | flops 512 | bytes 4096 | tf_op jit(solution)/shard_map/psum | solution.py:42
  21.8 4.3 %fusion.14 = f32[1,4096]{1,0:T(1,128)S(1)} fusion(f32[256,1]{0,1:T(1,128)S(1)} %bitcast.35, f32[256,4096]{1,0:T(8,128)} %copy-done.1), kind=kOutput, calls=%fused_computation.21 | convolution fusion | flops 13631488 | bytes 4211712 | tf_op jit(solution)/shard_map/dot_general | solution.py:47
  26.1 37.9 %all-reduce = (f32[4096]{0:T(1024)S(1)}, f32[4096]{0:T(1024)S(1)}, f32[4096]{0:T(1024)S(1)}) all-reduce(f32[4096]{0:T(1024)S(1)} %get-tuple-element.5, f32[4096]{0:T(1024)S(1)} %get-tuple-element.3, f32[4096]{0:T(1024)S(1)} %bitcast.27), channel_id=1, replica_groups=mesh['row'=8,'proto'=4] {'row'}, use_global_device_ids=true, to_apply=%region_8.0 | all-reduce | flops 12288 | bytes 98304 | tf_op jit(solution)/shard_map/psum | solution.py:44
  64.0 5.5 %fusion.12 = f32[1,256]{1,0:T(1,128)S(1)} fusion(f32[4096,1]{0,1:T(1,128)S(1)} %bitcast.31, f32[256,4096]{1,0:T(8,128)} %copy-done.1), kind=kOutput, calls=%fused_computation.19 | convolution fusion | flops 13631488 | bytes 4211712 | tf_op jit(solution)/shard_map/dot_general | solution.py:52
  69.5 5.9 %psum.82 = f32[256]{0:T(256)S(1)} all-reduce(f32[256]{0:T(256)S(1)} %bitcast.36), channel_id=1, replica_groups=mesh['row'=8,'proto'=4] {'proto'}, use_global_device_ids=true, to_apply=%region_9.0 | all-reduce | flops 256 | bytes 2048 | tf_op jit(solution)/shard_map/psum | solution.py:52
  75.5 4.3 %fusion.11 = f32[1,4096]{1,0:T(1,128)S(1)} fusion(f32[256,1]{0,1:T(1,128)S(1)} %bitcast.39, f32[256,4096]{1,0:T(8,128)} %copy-done.1), kind=kOutput, calls=%fused_computation.18 | convolution fusion | flops 13631488 | bytes 4211712 | tf_op jit(solution)/shard_map/dot_general | solution.py:47
  79.8 33.1 %psum.83 = f32[4096]{0:T(1024)S(1)} all-reduce(f32[4096]{0:T(1024)S(1)} %bitcast.28), channel_id=1, replica_groups=mesh['row'=8,'proto'=4] {'row'}, use_global_device_ids=true, to_apply=%region_10.0 | all-reduce | flops 4096 | bytes 32768 | tf_op jit(solution)/shard_map/psum | solution.py:47
  113.0 5.5 %fusion.10 = f32[1,256]{1,0:T(1,128)S(1)} fusion(f32[4096,1]{0,1:T(1,128)S(1)} %bitcast.32, f32[256,4096]{1,0:T(8,128)} %copy-done.1), kind=kOutput, calls=%fused_computation.17 | convolution fusion | flops 13631488 | bytes 4211712 | tf_op jit(solution)/shard_map/dot_general | solution.py:52
  118.5 5.8 %psum.84 = f32[256]{0:T(256)S(1)} all-reduce(f32[256]{0:T(256)S(1)} %bitcast.37), channel_id=1, replica_groups=mesh['row'=8,'proto'=4] {'proto'}, use_global_device_ids=true, to_apply=%region_11.0 | all-reduce | flops 256 | bytes 2048 | tf_op jit(solution)/shard_map/psum | solution.py:52
  124.3 4.3 %fusion.9 = f32[1,4096]{1,0:T(1,128)S(1)} fusion(f32[256,1]{0,1:T(1,128)S(1)} %bitcast.40, f32[256,4096]{1,0:T(8,128)} %copy-done.1), kind=kOutput, calls=%fused_computation.16 | convolution fusion | flops 13631488 | bytes 4211712 | tf_op jit(solution)/shard_map/dot_general | solution.py:47
  128.6 33.0 %psum.85 = f32[4096]{0:T(1024)S(1)} all-reduce(f32[4096]{0:T(1024)S(1)} %bitcast.29), channel_id=1, replica_groups=mesh['row'=8,'proto'=4] {'row'}, use_global_device_ids=true, to_apply=%region_12.0 | all-reduce | flops 4096 | bytes 32768 | tf_op jit(solution)/shard_map/psum | solution.py:47
  161.6 5.5 %fusion.8 = f32[1,256]{1,0:T(1,128)S(1)} fusion(f32[4096,1]{0,1:T(1,128)S(1)} %bitcast.33, f32[256,4096]{1,0:T(8,128)} %copy-done.1), kind=kOutput, calls=%fused_computation.15 | convolution fusion | flops 13631488 | bytes 4211712 | tf_op jit(solution)/shard_map/dot_general | solution.py:52
  167.1 5.8 %psum.86 = f32[256]{0:T(256)S(1)} all-reduce(f32[256]{0:T(256)S(1)} %bitcast.38), channel_id=1, replica_groups=mesh['row'=8,'proto'=4] {'proto'}, use_global_device_ids=true, to_apply=%region_13.0 | all-reduce | flops 256 | bytes 2048 | tf_op jit(solution)/shard_map/psum | solution.py:52
  172.9 4.3 %fusion.7 = f32[1,4096]{1,0:T(1,128)S(1)} fusion(f32[256,1]{0,1:T(1,128)S(1)} %bitcast.34, f32[256,4096]{1,0:T(8,128)} %copy-done.1), kind=kOutput, calls=%fused_computation.14 | convolution fusion | flops 13631488 | bytes 4211712 | tf_op jit(solution)/shard_map/dot_general | solution.py:47
  177.3 33.2 %psum.87 = f32[4096]{0:T(1024)S(1)} all-reduce(f32[4096]{0:T(1024)S(1)} %bitcast.30), channel_id=1, replica_groups=mesh['row'=8,'proto'=4] {'row'}, use_global_device_ids=true, to_apply=%region_14.0 | all-reduce | flops 4096 | bytes 32768 | tf_op jit(solution)/shard_map/psum | solution.py:47
  210.5 0.0 copy-start.3
  210.5 6.1 %multiply_convert_fusion = (bf16[256,4096]{1,0:T(8,128)(2,1)}, bf16[256,4096]{1,0:T(8,128)(2,1)S(1)}) fusion(f32[256,4096]{1,0:T(8,128)} %copy-done.1, f32[4096]{0:T(1024)S(1)} %subtract_divide_fusion, f32[256,4096]{1,0:T(8,128)} %get-tuple-element.13, f32[256]{0:T(256)S(1)} %subtract_divide_fusion.4), kind=kLoop, calls=%fused_computation.9 | loop fusion | flops 8388608 | bytes 12600320 | tf_op jit(solution)/shard_map/convert_element_type | solution.py:58
  216.6 1.3 fusion.27
  217.9 0.0 reduce-scatter.3.cloned.1.call-update
  218.0 0.0 reduce-scatter.5.cloned.1.call-start
  218.0 0.0 copy-done.3
  218.0 4.3 %fusion.3 = f32[4096,128]{1,0:T(8,128)} fusion(bf16[256,4096]{1,0:T(8,128)(2,1)} %get-tuple-element.11, bf16[256,4096]{1,0:T(8,128)(2,1)S(1)} %get-tuple-element.12, bf16[256,128]{1,0:T(8,128)(2,1)S(1)} %copy-done.2, bf16[256,128]{1,0:T(8,128)(2,1)S(1)} %copy-done.3), kind=kOutput, calls=%fused_computation.5 | convolution fusion | flops 545521664 | bytes 6422528 | tf_op jit(solution)/shard_map/dot_general | solution.py:10
  222.3 0.0 reduce-scatter.5.cloned.1.call-update
  222.3 11.3 %reduce-scatter.3.cloned.1.call-done = f32[64,128]{1,0:T(8,128)} async-done(((f32[256,128]{1,0:T(8,128)}), f32[64,128]{1,0:T(8,128)}) %reduce-scatter.3.cloned.1.call-update) | async-done | bytes 32784 | tf_op jit(solution)/shard_map/reduce_scatter | solution.py:59
  233.6 72.9 %reduce-scatter.5.cloned.1.call-done = f32[512,128]{1,0:T(8,128)} async-done(((f32[4096,128]{1,0:T(8,128)}), f32[512,128]{1,0:T(8,128)}) %reduce-scatter.5.cloned.1.call-update) | async-done | bytes 262160 | tf_op jit(solution)/shard_map/reduce_scatter | solution.py:67
  (8 shorter events, 0.1 us)
Async XLA Ops:
  7.2 1.2 copy-start
  7.2 2.9 copy-start.2
  7.2 226.4 %reduce-scatter.3.cloned.1.call-start = ((), (), s32[]{:S(2)}) async-start(), calls=%async_computation.2 | async-start | bytes 163840 | tf_op jit(solution)/shard_map/reduce_scatter | solution.py:59
  10.1 3.3 %copy-start.1 = (f32[256,4096]{1,0:T(8,128)}, f32[256,4096]{1,0:T(8,128)S(1)}, u32[]{:S(2)}) copy-start(f32[256,4096]{1,0:T(8,128)S(1)} %fusion.2) | copy-start | bytes 12582916
  210.5 7.6 %copy-start.3 = (bf16[256,128]{1,0:T(8,128)(2,1)S(1)}, bf16[256,128]{1,0:T(8,128)(2,1)}, u32[]{:S(2)}) copy-start(bf16[256,128]{1,0:T(8,128)(2,1)} %param.5) | copy-start | bytes 196612
  218.0 88.5 %reduce-scatter.5.cloned.1.call-start = ((), (), s32[]{:S(2)}) async-start(), calls=%async_computation.3 | async-start | bytes 2359296 | tf_op jit(solution)/shard_map/reduce_scatter | solution.py:67
Sparse Core Ops, SparseCore 0:
  218.1 15.4 reduce-scatter.2
  238.1 68.2 reduce-scatter.4
where the time goes:
time: 314 us; the launch traced here: 313 us
  blocking collectives  163 us (52%)
  waiting for transfers between devices  84.2 us (27%)
  matrix products  44.6 us (14%)
  between operations  14.1 us (4%)
  other arithmetic  6.2 us (2%)
    psum x3, blocking collectives, solve_cols(): lax.psum(jnp.dot(duals_rows, plan_now(), precision=lax.Precision.HIGHEST)...  99.3 us
    reduce_scatter x1, waiting for transfers between devices, per_device(): lax.psum_scatter(contract_rows(stacked, sources), 'row', scatter_dimensio...  72.9 us
    psum x1, blocking collectives, per_device(): lax.psum((stored_plan.sum(0), weighted.sum(0)), 'row')  37.9 us
    psum x3, blocking collectives, per_device(): lax.psum(jnp.dot(plan_now(), col_dual, precision=lax.Precision.HIGHEST),...  17.5 us
    dot_general x4, matrix products, solve_cols(): jnp.dot(duals_rows, plan_now(), precision=lax.Precision.HIGHEST)  17.4 us
    dot_general x3, matrix products, per_device(): jnp.dot(plan_now(), col_dual, precision=lax.Precision.HIGHEST)  16.6 us
    reduce_scatter x1, waiting for transfers between devices, per_device(): lax.psum_scatter(jnp.dot(scaled_grad, prototypes, preferred_element_type=...  11.3 us
    psum x1, blocking collectives, per_device(): lax.psum((stored_plan.sum(1), weighted.sum(1)), 'proto')  8.31 us
  transfers between devices with their start and end apart: 2, of which 2 were waited for; matrix products, arithmetic and copies ran while one was open for 1% of the time, Pallas kernels for 0%

commit v1 on v0

v1 whole, which is shorter than its diff:
```python
import jax
import jax.numpy as jnp
from jax import lax
from jax.sharding import PartitionSpec as P

ITERS = 4


def contract_rows(left, right):
    return lax.dot_general(
        left, right, (((0,), (0,)), ((), ())), preferred_element_type=jnp.float32
    )


def contract_width(left, right):
    return lax.dot_general(
        left, right, (((1,), (1,)), ((), ())), preferred_element_type=jnp.float32
    )


def swap(value, axis, step):
    size = lax.axis_size(axis)
    return lax.ppermute(value, axis, [(i, i ^ step) for i in range(size)])


def sum_over(value, axis):
    size = lax.axis_size(axis)
    parts = [value] + [swap(value, axis, step) for step in range(1, size)]
    return sum(parts[1:], parts[0])


def scatter_sum(value, axis):
    size = lax.axis_size(axis)
    me = lax.axis_index(axis)
    rows = value.shape[0] // size
    block = lambda owner: lax.dynamic_slice_in_dim(value, owner * rows, rows, 0)
    total = block(me)
    for step in range(1, size):
        total = total + swap(block(me ^ step), axis, step)
    return total


def per_device(embeddings, second_view, prototypes, row_scale, col_scale):
    feat_width = embeddings.shape[1]
    proto_count = prototypes.shape[0]
    logit_scale = 1.0 / (0.05 * feat_width)
    view_scale = 1.0 / (0.1 * feat_width)
    plan_mass = 64.0 * proto_count * lax.axis_size("proto")

    logits = contract_width(embeddings, prototypes) * logit_scale
    plan = row_scale[:, None] * col_scale[None, :] * jnp.exp(logits) / plan_mass
    cotangent = -contract_width(second_view, prototypes) * view_scale
    weighted = plan * cotangent

    row_mass, row_weight = sum_over(jnp.stack((plan.sum(1), weighted.sum(1))), "proto")
    row_dual = row_weight / row_mass
    sums = jnp.stack((plan.sum(0), weighted.sum(0), (row_dual[:, None] * plan).sum(0)))
    col_mass, col_weight, product = sum_over(sums, "row")
    col_dual = (col_weight - product) / col_mass
    for sweep in range(ITERS - 1):
        product = sum_over((plan * col_dual[None, :]).sum(1), "proto")
        row_dual = (row_weight - product) / row_mass
        product = sum_over((plan * row_dual[:, None]).sum(0), "row")
        col_dual = (col_weight - product) / col_mass
    logit_grad = plan * (cotangent - row_dual[:, None] - col_dual[None, :])
    scaled_grad = (logit_scale * logit_grad).astype(jnp.bfloat16)
    scaled_plan = (-view_scale * plan).astype(jnp.bfloat16)
    embed_grad = scatter_sum(
        jnp.dot(scaled_grad, prototypes, preferred_element_type=jnp.float32), "proto"
    )
    proto_grad = scatter_sum(
        contract_rows(scaled_grad, embeddings) + contract_rows(scaled_plan, second_view), "row"
    )
    return (embed_grad, proto_grad)


def solution(mesh):
    return jax.shard_map(
        per_device,
        mesh=mesh,
        in_specs=(P("row", None), P("row", None), P("proto", None), P("row"), P("proto")),
        out_specs=(P(("row", "proto"), None), P(("proto", "row"), None)),
        check_vma=False,
    )
```

time: 314 us -> 158 us (0.50)
  the two profiles are of different devices: /device:TPU:0 before, /device:TPU:8 now
where the time goes in v1:
time: 158 us; the launch traced here: 157 us
  waiting for transfers between devices  71.5 us (45%)
  starting transfers between devices  61.9 us (39%)
  other arithmetic  11.9 us (8%)
  matrix products  7.38 us (5%)
  local copies, waits for them, and re-layouts  3.78 us (2%)
    ppermute x50, waiting for transfers between devices, swap(): return lax.ppermute(value, axis, [(i, i ^ step) for i in range(size)])  71.5 us
    ppermute x50, starting transfers between devices, swap(): return lax.ppermute(value, axis, [(i, i ^ step) for i in range(size)])  61.9 us
    dot_general x2, matrix products, contract_width(): lax.dot_general(left, right, (((1,), (1,)), ((), ())), preferred_element_...  5.11 us
    convert_element_type x1, other arithmetic, per_device(): scaled_grad = (logit_scale * logit_grad).astype(jnp.bfloat16)  4.56 us
    add x2, other arithmetic, scatter_sum(): total = total + swap(block(me ^ step), axis, step)  3.56 us
  transfers between devices with their start and end apart: 50, of which 25 were waited for; matrix products, arithmetic and copies ran while one was open for 1% of the time, Pallas kernels for 0%

profile of v1, /device:TPU:8, one launch (start us, length us, event | category | flops | bytes accessed | tf_op | source)
XLA Modules:
  0.0 157.4 jit_solution(12663214126184351374)
XLA Ops:
  0.6 1.2 copy-done
  1.9 1.8 %fusion.2 = f32[256,4096]{1,0:T(8,128)S(1)} fusion(bf16[256,128]{1,0:T(8,128)(2,1)} %param.5, bf16[4096,128]{1,0:T(8,128)(2,1)S(1)} %copy-done, f32[4096]{0:T(1024)} %param.9, f32[256]{0:T(256)} %param.8), kind=kOutput, calls=%fused_computation.4 | convolution fusion | flops 271581184 | bytes 5325824 | tf_op jit(solution)/shard_map/dot_general | solution.py:16
  3.6 3.4 %fusion.4 = (f32[4096]{0:T(1024)S(1)}, f32[256]{0:T(256)S(1)}, f32[4096]{0:T(1024)S(1)}, f32[256]{0:T(256)S(1)}, f32[256,4096]{1,0:T(8,128)}) fusion(f32[256,4096]{1,0:T(8,128)S(1)} %fusion.2, bf16[256,128]{1,0:T(8,128)(2,1)S(1)} %copy-done.3, bf16[4096,128]{1,0:T(8,128)(2,1)S(1)} %copy-done), kind=kOutput, calls=%fused_computation.19 | convolution fusion | flops 276815360 | bytes 9537536 | tf_op jit(solution)/shard_map/dot_general | solution.py:16
  7.1 1.6 collective-permute-start.1
  9.0 1.8 %collective-permute-done.1 = f32[2,256]{1,0:T(2,128)S(1)} collective-permute-done((f32[2,256]{1,0:T(2,128)S(1)}, f32[2,256]{1,0:T(2,128)S(1)}, u32[]{:S(2)}, u32[]{:S(2)}) %collective-permute-start.1) | collective-permute-done | bytes 2080 | tf_op jit(solution)/shard_map/ppermute | solution.py:23
  10.7 0.9 collective-permute-done.2
  12.3 1.6 %collective-permute-start.3 = (f32[3,4096]{1,0:T(4,128)S(1)}, f32[3,4096]{1,0:T(4,128)S(1)}, u32[]{:S(2)}, u32[]{:S(2)}) collective-permute-start(f32[3,4096]{1,0:T(4,128)S(1)} %pad_maximum_fusion), channel_id=1, source_target_pairs={{0,4},{4,0},{8,12},{12,8},{16,20},{20,16},{24,28},{28,24},{1,5},{5... | collective-permute-start | bytes 147464 | tf_op jit(solution)/shard_map/ppermute | solution.py:23
  14.3 1.5 collective-permute-start.5
  15.9 2.6 %collective-permute-start.6 = (f32[3,4096]{1,0:T(4,128)S(1)}, f32[3,4096]{1,0:T(4,128)S(1)}, u32[]{:S(2)}, u32[]{:S(2)}) collective-permute-start(f32[3,4096]{1,0:T(4,128)S(1)} %pad_maximum_fusion), channel_id=1, source_target_pairs={{0,16},{4,20},{8,24},{12,28},{16,0},{20,4},{24,8},{28,12},{1,17},{... | collective-permute-start | bytes 147464 | tf_op jit(solution)/shard_map/ppermute | solution.py:23
  18.5 1.3 collective-permute-start.7
  19.8 1.6 %collective-permute-start.8 = (f32[3,4096]{1,0:T(4,128)S(1)}, f32[3,4096]{1,0:T(4,128)S(1)}, u32[]{:S(2)}, u32[]{:S(2)}) collective-permute-start(f32[3,4096]{1,0:T(4,128)S(1)} %pad_maximum_fusion), channel_id=1, source_target_pairs={{0,24},{4,28},{8,16},{12,20},{16,8},{20,12},{24,0},{28,4},{1,25},{... | collective-permute-start | bytes 147464 | tf_op jit(solution)/shard_map/ppermute | solution.py:23
  21.7 0.7 collective-permute-done.6
  22.4 4.3 %collective-permute-done.7 = f32[3,4096]{1,0:T(4,128)S(1)} collective-permute-done((f32[3,4096]{1,0:T(4,128)S(1)}, f32[3,4096]{1,0:T(4,128)S(1)}, u32[]{:S(2)}, u32[]{:S(2)}) %collective-permute-start.7) | collective-permute-done | bytes 49184 | tf_op jit(solution)/shard_map/ppermute | solution.py:23
  26.8 2.2 %collective-permute-done.8 = f32[3,4096]{1,0:T(4,128)S(1)} collective-permute-done((f32[3,4096]{1,0:T(4,128)S(1)}, f32[3,4096]{1,0:T(4,128)S(1)}, u32[]{:S(2)}, u32[]{:S(2)}) %collective-permute-start.8) | collective-permute-done | bytes 49184 | tf_op jit(solution)/shard_map/ppermute | solution.py:23
  29.0 1.8 %collective-permute-done.9 = f32[3,4096]{1,0:T(4,128)S(1)} collective-permute-done((f32[3,4096]{1,0:T(4,128)S(1)}, f32[3,4096]{1,0:T(4,128)S(1)}, u32[]{:S(2)}, u32[]{:S(2)}) %collective-permute-start.9) | collective-permute-done | bytes 49184 | tf_op jit(solution)/shard_map/ppermute | solution.py:23
  32.1 1.2 collective-permute-start.12
  33.3 1.8 %collective-permute-done.11 = f32[256]{0:T(256)S(1)} collective-permute-done((f32[256]{0:T(256)S(1)}, f32[256]{0:T(256)S(1)}, u32[]{:S(2)}, u32[]{:S(2)}) %collective-permute-start.11) | collective-permute-done | bytes 1056 | tf_op jit(solution)/shard_map/ppermute | solution.py:23
  35.7 0.9 collective-permute-start.13
  36.5 2.7 %collective-permute-start.15 = (f32[4096]{0:T(1024)S(1)}, f32[4096]{0:T(1024)S(1)}, u32[]{:S(2)}, u32[]{:S(2)}) collective-permute-start(f32[4096]{0:T(1024)S(1)} %multiply_reduce_fusion.4), channel_id=1, source_target_pairs={{0,12},{4,8},{8,4},{12,0},{16,28},{20,24},{24,20},{28,16},{1,13},{... | collective-permute-start | bytes 49160 | tf_op jit(solution)/shard_map/ppermute | solution.py:23
  39.2 1.1 collective-permute-start.16
  40.3 2.1 %collective-permute-start.17 = (f32[4096]{0:T(1024)S(1)}, f32[4096]{0:T(1024)S(1)}, u32[]{:S(2)}, u32[]{:S(2)}) collective-permute-start(f32[4096]{0:T(1024)S(1)} %multiply_reduce_fusion.4), channel_id=1, source_target_pairs={{0,20},{4,16},{8,28},{12,24},{16,4},{20,0},{24,12},{28,8},{1,21},{... | collective-permute-start | bytes 49160 | tf_op jit(solution)/shard_map/ppermute | solution.py:23
  42.4 1.4 collective-permute-start.18
  43.8 1.3 collective-permute-start.19
  45.1 0.8 collective-permute-done.17
  46.1 2.3 %collective-permute-done.19 = f32[4096]{0:T(1024)S(1)} collective-permute-done((f32[4096]{0:T(1024)S(1)}, f32[4096]{0:T(1024)S(1)}, u32[]{:S(2)}, u32[]{:S(2)}) %collective-permute-start.19) | collective-permute-done | bytes 16416 | tf_op jit(solution)/shard_map/ppermute | solution.py:23
  49.0 1.5 collective-permute-start.21
  50.8 1.8 %collective-permute-done.21 = f32[256]{0:T(256)S(1)} collective-permute-done((f32[256]{0:T(256)S(1)}, f32[256]{0:T(256)S(1)}, u32[]{:S(2)}, u32[]{:S(2)}) %collective-permute-start.21) | collective-permute-done | bytes 1056 | tf_op jit(solution)/shard_map/ppermute | solution.py:23
  52.6 0.9 collective-permute-done.22
  54.0 1.5 collective-permute-start.23
  55.6 2.7 %collective-permute-start.24 = (f32[4096]{0:T(1024)S(1)}, f32[4096]{0:T(1024)S(1)}, u32[]{:S(2)}, u32[]{:S(2)}) collective-permute-start(f32[4096]{0:T(1024)S(1)} %multiply_reduce_fusion.2), channel_id=1, source_target_pairs={{0,8},{4,12},{8,0},{12,4},{16,24},{20,28},{24,16},{28,20},{1,9},{5... | collective-permute-start | bytes 49160 | tf_op jit(solution)/shard_map/ppermute | solution.py:23
  58.3 2.1 %collective-permute-start.26 = (f32[4096]{0:T(1024)S(1)}, f32[4096]{0:T(1024)S(1)}, u32[]{:S(2)}, u32[]{:S(2)}) collective-permute-start(f32[4096]{0:T(1024)S(1)} %multiply_reduce_fusion.2), channel_id=1, source_target_pairs={{0,16},{4,20},{8,24},{12,28},{16,0},{20,4},{24,8},{28,12},{1,17},{... | collective-permute-start | bytes 49160 | tf_op jit(solution)/shard_map/ppermute | solution.py:23
  60.3 1.7 %collective-permute-start.27 = (f32[4096]{0:T(1024)S(1)}, f32[4096]{0:T(1024)S(1)}, u32[]{:S(2)}, u32[]{:S(2)}) collective-permute-start(f32[4096]{0:T(1024)S(1)} %multiply_reduce_fusion.2), channel_id=1, source_target_pairs={{0,20},{4,16},{8,28},{12,24},{16,4},{20,0},{24,12},{28,8},{1,21},{... | collective-permute-start | bytes 49160 | tf_op jit(solution)/shard_map/ppermute | solution.py:23
  62.7 1.5 collective-permute-start.29
  64.1 1.9 %collective-permute-done.27 = f32[4096]{0:T(1024)S(1)} collective-permute-done((f32[4096]{0:T(1024)S(1)}, f32[4096]{0:T(1024)S(1)}, u32[]{:S(2)}, u32[]{:S(2)}) %collective-permute-start.27) | collective-permute-done | bytes 16416 | tf_op jit(solution)/shard_map/ppermute | solution.py:23
  66.2 1.1 collective-permute-done.29
  68.4 1.2 collective-permute-start.32
  69.7 1.8 %collective-permute-done.31 = f32[256]{0:T(256)S(1)} collective-permute-done((f32[256]{0:T(256)S(1)}, f32[256]{0:T(256)S(1)}, u32[]{:S(2)}, u32[]{:S(2)}) %collective-permute-start.31) | collective-permute-done | bytes 1056 | tf_op jit(solution)/shard_map/ppermute | solution.py:23
  72.0 0.7 collective-permute-start.33
  72.7 4.7 %collective-permute-start.34 = (f32[4096]{0:T(1024)S(1)}, f32[4096]{0:T(1024)S(1)}, u32[]{:S(2)}, u32[]{:S(2)}) collective-permute-start(f32[4096]{0:T(1024)S(1)} %multiply_reduce_fusion), channel_id=1, source_target_pairs={{0,8},{4,12},{8,0},{12,4},{16,24},{20,28},{24,16},{28,20},{1,9},{5... | collective-permute-start | bytes 49160 | tf_op jit(solution)/shard_map/ppermute | solution.py:23
  77.4 0.8 collective-permute-start.35
  78.3 2.9 %collective-permute-start.36 = (f32[4096]{0:T(1024)S(1)}, f32[4096]{0:T(1024)S(1)}, u32[]{:S(2)}, u32[]{:S(2)}) collective-permute-start(f32[4096]{0:T(1024)S(1)} %multiply_reduce_fusion), channel_id=1, source_target_pairs={{0,16},{4,20},{8,24},{12,28},{16,0},{20,4},{24,8},{28,12},{1,17},{... | collective-permute-start | bytes 49160 | tf_op jit(solution)/shard_map/ppermute | solution.py:23
  81.3 1.4 collective-permute-start.38
  82.7 1.4 collective-permute-start.39
  84.1 2.6 %collective-permute-done.37 = f32[4096]{0:T(1024)S(1)} collective-permute-done((f32[4096]{0:T(1024)S(1)}, f32[4096]{0:T(1024)S(1)}, u32[]{:S(2)}, u32[]{:S(2)}) %collective-permute-start.37) | collective-permute-done | bytes 16416 | tf_op jit(solution)/shard_map/ppermute | solution.py:23
  87.4 4.6 %multiply_convert_fusion.1 = bf16[256,4096]{1,0:T(8,128)(2,1)S(1)} fusion(f32[256,4096]{1,0:T(8,128)} %get-tuple-element.23, f32[256,4096]{1,0:T(8,128)} %copy-done.1, f32[4096]{0:T(1024)S(1)} %subtract_divide_fusion, f32[256]{0:T(256)S(1)} %get-tuple-element.7), kind=kLoop, calls=%fused_computation.7 | loop fusion | flops 6291456 | bytes 10503168 | tf_op jit(solution)/shard_map/convert_element_type | solution.py:66
  91.9 0.8 fusion.13
  92.7 1.4 copy-done.2
  94.1 0.8 convolution_add_fusion
  94.9 1.1 constant_dynamic-slice_fusion.6
  96.0 1.6 %collective-permute-start.43 = (f32[512,128]{1,0:T(8,128)S(1)}, f32[512,128]{1,0:T(8,128)S(1)}, u32[]{:S(2)}, u32[]{:S(2)}) collective-permute-start(f32[512,128]{1,0:T(8,128)S(1)} %get-tuple-element.8), channel_id=1, source_target_pairs={{0,4},{4,0},{8,12},{12,8},{16,20},{20,16},{24,28},{28,24},{1,5},{5... | collective-permute-start | bytes 786440 | tf_op jit(solution)/shard_map/ppermute | solution.py:23
  97.6 4.5 %collective-permute-start.44 = (f32[512,128]{1,0:T(8,128)S(1)}, f32[512,128]{1,0:T(8,128)}, u32[]{:S(2)}, u32[]{:S(2)}) collective-permute-start(f32[512,128]{1,0:T(8,128)S(1)} %get-tuple-element.14), channel_id=1, source_target_pairs={{0,8},{4,12},{8,0},{12,4},{16,24},{20,28},{24,16},{28,20},{1,9},{5... | collective-permute-start | bytes 786440 | tf_op jit(solution)/shard_map/ppermute | solution.py:23
  102.2 0.7 fusion.12
  103.0 1.5 collective-permute-start.41
  104.9 2.2 %collective-permute-done.41 = f32[64,128]{1,0:T(8,128)} collective-permute-done((f32[64,128]{1,0:T(8,128)S(1)}, f32[64,128]{1,0:T(8,128)}, u32[]{:S(2)}, u32[]{:S(2)}) %collective-permute-start.41) | collective-permute-done | bytes 32800 | tf_op jit(solution)/shard_map/ppermute | solution.py:23
  107.1 0.8 collective-permute-done.42
  107.9 2.2 %collective-permute-start.47 = (f32[512,128]{1,0:T(8,128)}, f32[512,128]{1,0:T(8,128)}, u32[]{:S(2)}, u32[]{:S(2)}) collective-permute-start(f32[512,128]{1,0:T(8,128)} %get-tuple-element.11), channel_id=1, source_target_pairs={{0,20},{4,16},{8,28},{12,24},{16,4},{20,0},{24,12},{28,8},{1,21},{... | collective-permute-start | bytes 786440 | tf_op jit(solution)/shard_map/ppermute | solution.py:23
  110.7 2.3 %collective-permute-start.49 = (f32[512,128]{1,0:T(8,128)}, f32[512,128]{1,0:T(8,128)}, u32[]{:S(2)}, u32[]{:S(2)}) collective-permute-start(f32[512,128]{1,0:T(8,128)} %get-tuple-element.9), channel_id=1, source_target_pairs={{0,28},{4,24},{8,20},{12,16},{16,12},{20,8},{24,4},{28,0},{1,29},{... | collective-permute-start | bytes 786440 | tf_op jit(solution)/shard_map/ppermute | solution.py:23
  113.0 1.4 add_add_fusion.2
  114.4 1.9 %collective-permute-done.45 = f32[512,128]{1,0:T(8,128)} collective-permute-done((f32[512,128]{1,0:T(8,128)}, f32[512,128]{1,0:T(8,128)}, u32[]{:S(2)}, u32[]{:S(2)}) %collective-permute-start.45) | collective-permute-done | bytes 262176 | tf_op jit(solution)/shard_map/ppermute | solution.py:23
  116.3 20.3 %collective-permute-done.46 = f32[512,128]{1,0:T(8,128)} collective-permute-done((f32[512,128]{1,0:T(8,128)}, f32[512,128]{1,0:T(8,128)}, u32[]{:S(2)}, u32[]{:S(2)}) %collective-permute-start.46) | collective-permute-done | bytes 262176 | tf_op jit(solution)/shard_map/ppermute | solution.py:23
  136.6 5.6 %collective-permute-done.47 = f32[512,128]{1,0:T(8,128)} collective-permute-done((f32[512,128]{1,0:T(8,128)}, f32[512,128]{1,0:T(8,128)}, u32[]{:S(2)}, u32[]{:S(2)}) %collective-permute-start.47) | collective-permute-done | bytes 262176 | tf_op jit(solution)/shard_map/ppermute | solution.py:23
  142.2 7.5 %collective-permute-done.48 = f32[512,128]{1,0:T(8,128)} collective-permute-done((f32[512,128]{1,0:T(8,128)}, f32[512,128]{1,0:T(8,128)}, u32[]{:S(2)}, u32[]{:S(2)}) %collective-permute-start.48) | collective-permute-done | bytes 262176 | tf_op jit(solution)/shard_map/ppermute | solution.py:23
  149.8 5.5 %collective-permute-done.49 = f32[512,128]{1,0:T(8,128)} collective-permute-done((f32[512,128]{1,0:T(8,128)}, f32[512,128]{1,0:T(8,128)}, u32[]{:S(2)}, u32[]{:S(2)}) %collective-permute-start.49) | collective-permute-done | bytes 262176 | tf_op jit(solution)/shard_map/ppermute | solution.py:23
  155.2 2.1 %add_add_fusion = f32[512,128]{1,0:T(8,128)} fusion(f32[512,128]{1,0:T(8,128)} %collective-permute-done.49, f32[512,128]{1,0:T(8,128)} %collective-permute-done.48, f32[512,128]{1,0:T(8,128)} %collective-permute-done.47, f32[512,128]{1,0:T(8,128)} %collective-permute-done.46, f32[512,128]{1,0:T(8,128)} %collective-permute-done.45, ...), kind=kLoop, calls=%fused_computation.21 | loop fusion | flops 458752 | bytes 2359300 | tf_op jit(solution)/shard_map/add | solution.py:39
  (78 shorter events, 9.6 us)
Async XLA Ops:
  0.6 1.2 copy-start
  1.9 1.8 %copy-start.3 = (bf16[256,128]{1,0:T(8,128)(2,1)S(1)}, bf16[256,128]{1,0:T(8,128)(2,1)}, u32[]{:S(2)}) copy-start(bf16[256,128]{1,0:T(8,128)(2,1)} %param.6) | copy-start | bytes 196612
  3.6 67.8 %copy-start.1 = (f32[256,4096]{1,0:T(8,128)}, f32[256,4096]{1,0:T(8,128)S(1)}, u32[]{:S(2)}) copy-start(f32[256,4096]{1,0:T(8,128)S(1)} %fusion.2) | copy-start | bytes 12582916
  7.0 1.9 %collective-permute-start = (f32[2,256]{1,0:T(2,128)S(1)}, f32[2,256]{1,0:T(2,128)S(1)}, u32[]{:S(2)}, u32[]{:S(2)}) collective-permute-start(f32[2,256]{1,0:T(2,128)S(1)} %pad_maximum_fusion.1), channel_id=1, source_target_pairs={{0,1},{1,0},{2,3},{3,2},{4,5},{5,4},{6,7},{7,6},{8,9},{9,8},{10,11... | collective-permute-start | bytes 6152 | tf_op jit(solution)/shard_map/ppermute | solution.py:23
  7.1 3.7 %collective-permute-start.1 = (f32[2,256]{1,0:T(2,128)S(1)}, f32[2,256]{1,0:T(2,128)S(1)}, u32[]{:S(2)}, u32[]{:S(2)}) collective-permute-start(f32[2,256]{1,0:T(2,128)S(1)} %pad_maximum_fusion.1), channel_id=1, source_target_pairs={{0,2},{1,3},{2,0},{3,1},{4,6},{5,7},{6,4},{7,5},{8,10},{9,11},{10,... | collective-permute-start | bytes 6152 | tf_op jit(solution)/shard_map/ppermute | solution.py:23
  8.6 3.0 %collective-permute-start.2 = (f32[2,256]{1,0:T(2,128)S(1)}, f32[2,256]{1,0:T(2,128)S(1)}, u32[]{:S(2)}, u32[]{:S(2)}) collective-permute-start(f32[2,256]{1,0:T(2,128)S(1)} %pad_maximum_fusion.1), channel_id=1, source_target_pairs={{0,3},{1,2},{2,1},{3,0},{4,7},{5,6},{6,5},{7,4},{8,11},{9,10},{10,... | collective-permute-start | bytes 6152 | tf_op jit(solution)/shard_map/ppermute | solution.py:23
  12.3 7.4 %collective-permute-start.3 = (f32[3,4096]{1,0:T(4,128)S(1)}, f32[3,4096]{1,0:T(4,128)S(1)}, u32[]{:S(2)}, u32[]{:S(2)}) collective-permute-start(f32[3,4096]{1,0:T(4,128)S(1)} %pad_maximum_fusion), channel_id=1, source_target_pairs={{0,4},{4,0},{8,12},{12,8},{16,20},{20,16},{24,28},{28,24},{1,5},{5... | collective-permute-start | bytes 147464 | tf_op jit(solution)/shard_map/ppermute | solution.py:23
  13.9 7.4 %collective-permute-start.4 = (f32[3,4096]{1,0:T(4,128)S(1)}, f32[3,4096]{1,0:T(4,128)S(1)}, u32[]{:S(2)}, u32[]{:S(2)}) collective-permute-start(f32[3,4096]{1,0:T(4,128)S(1)} %pad_maximum_fusion), channel_id=1, source_target_pairs={{0,8},{4,12},{8,0},{12,4},{16,24},{20,28},{24,16},{28,20},{1,9},{5... | collective-permute-start | bytes 147464 | tf_op jit(solution)/shard_map/ppermute | solution.py:23
  14.3 7.4 %collective-permute-start.5 = (f32[3,4096]{1,0:T(4,128)S(1)}, f32[3,4096]{1,0:T(4,128)S(1)}, u32[]{:S(2)}, u32[]{:S(2)}) collective-permute-start(f32[3,4096]{1,0:T(4,128)S(1)} %pad_maximum_fusion), channel_id=1, source_target_pairs={{0,12},{4,8},{8,4},{12,0},{16,28},{20,24},{24,20},{28,16},{1,13},{... | collective-permute-start | bytes 147464 | tf_op jit(solution)/shard_map/ppermute | solution.py:23
  15.9 6.5 %collective-permute-start.6 = (f32[3,4096]{1,0:T(4,128)S(1)}, f32[3,4096]{1,0:T(4,128)S(1)}, u32[]{:S(2)}, u32[]{:S(2)}) collective-permute-start(f32[3,4096]{1,0:T(4,128)S(1)} %pad_maximum_fusion), channel_id=1, source_target_pairs={{0,16},{4,20},{8,24},{12,28},{16,0},{20,4},{24,8},{28,12},{1,17},{... | collective-permute-start | bytes 147464 | tf_op jit(solution)/shard_map/ppermute | solution.py:23
  18.5 8.3 %collective-permute-start.7 = (f32[3,4096]{1,0:T(4,128)S(1)}, f32[3,4096]{1,0:T(4,128)S(1)}, u32[]{:S(2)}, u32[]{:S(2)}) collective-permute-start(f32[3,4096]{1,0:T(4,128)S(1)} %pad_maximum_fusion), channel_id=1, source_target_pairs={{0,20},{4,16},{8,28},{12,24},{16,4},{20,0},{24,12},{28,8},{1,21},{... | collective-permute-start | bytes 147464 | tf_op jit(solution)/shard_map/ppermute | solution.py:23
  19.8 9.3 %collective-permute-start.8 = (f32[3,4096]{1,0:T(4,128)S(1)}, f32[3,4096]{1,0:T(4,128)S(1)}, u32[]{:S(2)}, u32[]{:S(2)}) collective-permute-start(f32[3,4096]{1,0:T(4,128)S(1)} %pad_maximum_fusion), channel_id=1, source_target_pairs={{0,24},{4,28},{8,16},{12,20},{16,8},{20,12},{24,0},{28,4},{1,25},{... | collective-permute-start | bytes 147464 | tf_op jit(solution)/shard_map/ppermute | solution.py:23
  21.3 9.5 %collective-permute-start.9 = (f32[3,4096]{1,0:T(4,128)S(1)}, f32[3,4096]{1,0:T(4,128)S(1)}, u32[]{:S(2)}, u32[]{:S(2)}) collective-permute-start(f32[3,4096]{1,0:T(4,128)S(1)} %pad_maximum_fusion), channel_id=1, source_target_pairs={{0,28},{4,24},{8,20},{12,16},{16,12},{20,8},{24,4},{28,0},{1,29},{... | collective-permute-start | bytes 147464 | tf_op jit(solution)/shard_map/ppermute | solution.py:23
  31.4 1.9 %collective-permute-start.10 = (f32[256]{0:T(256)S(1)}, f32[256]{0:T(256)S(1)}, u32[]{:S(2)}, u32[]{:S(2)}) collective-permute-start(f32[256]{0:T(256)S(1)} %multiply_reduce_fusion.5), channel_id=1, source_target_pairs={{0,1},{1,0},{2,3},{3,2},{4,5},{5,4},{6,7},{7,6},{8,9},{9,8},{10,11... | collective-permute-start | bytes 3080 | tf_op jit(solution)/shard_map/ppermute | solution.py:23
  31.4 3.6 %collective-permute-start.11 = (f32[256]{0:T(256)S(1)}, f32[256]{0:T(256)S(1)}, u32[]{:S(2)}, u32[]{:S(2)}) collective-permute-start(f32[256]{0:T(256)S(1)} %multiply_reduce_fusion.5), channel_id=1, source_target_pairs={{0,2},{1,3},{2,0},{3,1},{4,6},{5,7},{6,4},{7,5},{8,10},{9,11},{10,... | collective-permute-start | bytes 3080 | tf_op jit(solution)/shard_map/ppermute | solution.py:23
  32.1 3.0 %collective-permute-start.12 = (f32[256]{0:T(256)S(1)}, f32[256]{0:T(256)S(1)}, u32[]{:S(2)}, u32[]{:S(2)}) collective-permute-start(f32[256]{0:T(256)S(1)} %multiply_reduce_fusion.5), channel_id=1, source_target_pairs={{0,3},{1,2},{2,1},{3,0},{4,7},{5,6},{6,5},{7,4},{8,11},{9,10},{10,... | collective-permute-start | bytes 3080 | tf_op jit(solution)/shard_map/ppermute | solution.py:23
  35.7 6.7 %collective-permute-start.13 = (f32[4096]{0:T(1024)S(1)}, f32[4096]{0:T(1024)S(1)}, u32[]{:S(2)}, u32[]{:S(2)}) collective-permute-start(f32[4096]{0:T(1024)S(1)} %multiply_reduce_fusion.4), channel_id=1, source_target_pairs={{0,4},{4,0},{8,12},{12,8},{16,20},{20,16},{24,28},{28,24},{1,5},{5... | collective-permute-start | bytes 49160 | tf_op jit(solution)/shard_map/ppermute | solution.py:23
  36.5 7.3 %collective-permute-start.14 = (f32[4096]{0:T(1024)S(1)}, f32[4096]{0:T(1024)S(1)}, u32[]{:S(2)}, u32[]{:S(2)}) collective-permute-start(f32[4096]{0:T(1024)S(1)} %multiply_reduce_fusion.4), channel_id=1, source_target_pairs={{0,8},{4,12},{8,0},{12,4},{16,24},{20,28},{24,16},{28,20},{1,9},{5... | collective-permute-start | bytes 49160 | tf_op jit(solution)/shard_map/ppermute | solution.py:23
  36.5 8.5 %collective-permute-start.15 = (f32[4096]{0:T(1024)S(1)}, f32[4096]{0:T(1024)S(1)}, u32[]{:S(2)}, u32[]{:S(2)}) collective-permute-start(f32[4096]{0:T(1024)S(1)} %multiply_reduce_fusion.4), channel_id=1, source_target_pairs={{0,12},{4,8},{8,4},{12,0},{16,28},{20,24},{24,20},{28,16},{1,13},{... | collective-permute-start | bytes 49160 | tf_op jit(solution)/shard_map/ppermute | solution.py:23
  39.2 5.9 %collective-permute-start.16 = (f32[4096]{0:T(1024)S(1)}, f32[4096]{0:T(1024)S(1)}, u32[]{:S(2)}, u32[]{:S(2)}) collective-permute-start(f32[4096]{0:T(1024)S(1)} %multiply_reduce_fusion.4), channel_id=1, source_target_pairs={{0,16},{4,20},{8,24},{12,28},{16,0},{20,4},{24,8},{28,12},{1,17},{... | collective-permute-start | bytes 49160 | tf_op jit(solution)/shard_map/ppermute | solution.py:23
  40.3 5.5 %collective-permute-start.17 = (f32[4096]{0:T(1024)S(1)}, f32[4096]{0:T(1024)S(1)}, u32[]{:S(2)}, u32[]{:S(2)}) collective-permute-start(f32[4096]{0:T(1024)S(1)} %multiply_reduce_fusion.4), channel_id=1, source_target_pairs={{0,20},{4,16},{8,28},{12,24},{16,4},{20,0},{24,12},{28,8},{1,21},{... | collective-permute-start | bytes 49160 | tf_op jit(solution)/shard_map/ppermute | solution.py:23
  42.4 3.7 %collective-permute-start.18 = (f32[4096]{0:T(1024)S(1)}, f32[4096]{0:T(1024)S(1)}, u32[]{:S(2)}, u32[]{:S(2)}) collective-permute-start(f32[4096]{0:T(1024)S(1)} %multiply_reduce_fusion.4), channel_id=1, source_target_pairs={{0,24},{4,28},{8,16},{12,20},{16,8},{20,12},{24,0},{28,4},{1,25},{... | collective-permute-start | bytes 49160 | tf_op jit(solution)/shard_map/ppermute | solution.py:23
  43.8 4.6 %collective-permute-start.19 = (f32[4096]{0:T(1024)S(1)}, f32[4096]{0:T(1024)S(1)}, u32[]{:S(2)}, u32[]{:S(2)}) collective-permute-start(f32[4096]{0:T(1024)S(1)} %multiply_reduce_fusion.4), channel_id=1, source_target_pairs={{0,28},{4,24},{8,20},{12,16},{16,12},{20,8},{24,4},{28,0},{1,29},{... | collective-permute-start | bytes 49160 | tf_op jit(solution)/shard_map/ppermute | solution.py:23
  48.9 1.9 %collective-permute-start.20 = (f32[256]{0:T(256)S(1)}, f32[256]{0:T(256)S(1)}, u32[]{:S(2)}, u32[]{:S(2)}) collective-permute-start(f32[256]{0:T(256)S(1)} %multiply_reduce_fusion.3), channel_id=1, source_target_pairs={{0,1},{1,0},{2,3},{3,2},{4,5},{5,4},{6,7},{7,6},{8,9},{9,8},{10,11... | collective-permute-start | bytes 3080 | tf_op jit(solution)/shard_map/ppermute | solution.py:23
  49.0 3.6 %collective-permute-start.21 = (f32[256]{0:T(256)S(1)}, f32[256]{0:T(256)S(1)}, u32[]{:S(2)}, u32[]{:S(2)}) collective-permute-start(f32[256]{0:T(256)S(1)} %multiply_reduce_fusion.3), channel_id=1, source_target_pairs={{0,2},{1,3},{2,0},{3,1},{4,6},{5,7},{6,4},{7,5},{8,10},{9,11},{10,... | collective-permute-start | bytes 3080 | tf_op jit(solution)/shard_map/ppermute | solution.py:23
  50.5 3.0 %collective-permute-start.22 = (f32[256]{0:T(256)S(1)}, f32[256]{0:T(256)S(1)}, u32[]{:S(2)}, u32[]{:S(2)}) collective-permute-start(f32[256]{0:T(256)S(1)} %multiply_reduce_fusion.3), channel_id=1, source_target_pairs={{0,3},{1,2},{2,1},{3,0},{4,7},{5,6},{6,5},{7,4},{8,11},{9,10},{10,... | collective-permute-start | bytes 3080 | tf_op jit(solution)/shard_map/ppermute | solution.py:23
  54.0 8.0 %collective-permute-start.23 = (f32[4096]{0:T(1024)S(1)}, f32[4096]{0:T(1024)S(1)}, u32[]{:S(2)}, u32[]{:S(2)}) collective-permute-start(f32[4096]{0:T(1024)S(1)} %multiply_reduce_fusion.2), channel_id=1, source_target_pairs={{0,4},{4,0},{8,12},{12,8},{16,20},{20,16},{24,28},{28,24},{1,5},{5... | collective-permute-start | bytes 49160 | tf_op jit(solution)/shard_map/ppermute | solution.py:23
  55.6 7.1 %collective-permute-start.24 = (f32[4096]{0:T(1024)S(1)}, f32[4096]{0:T(1024)S(1)}, u32[]{:S(2)}, u32[]{:S(2)}) collective-permute-start(f32[4096]{0:T(1024)S(1)} %multiply_reduce_fusion.2), channel_id=1, source_target_pairs={{0,8},{4,12},{8,0},{12,4},{16,24},{20,28},{24,16},{28,20},{1,9},{5... | collective-permute-start | bytes 49160 | tf_op jit(solution)/shard_map/ppermute | solution.py:23
  58.3 5.9 %collective-permute-start.25 = (f32[4096]{0:T(1024)S(1)}, f32[4096]{0:T(1024)S(1)}, u32[]{:S(2)}, u32[]{:S(2)}) collective-permute-start(f32[4096]{0:T(1024)S(1)} %multiply_reduce_fusion.2), channel_id=1, source_target_pairs={{0,12},{4,8},{8,4},{12,0},{16,28},{20,24},{24,20},{28,16},{1,13},{... | collective-permute-start | bytes 49160 | tf_op jit(solution)/shard_map/ppermute | solution.py:23
  58.3 5.9 %collective-permute-start.26 = (f32[4096]{0:T(1024)S(1)}, f32[4096]{0:T(1024)S(1)}, u32[]{:S(2)}, u32[]{:S(2)}) collective-permute-start(f32[4096]{0:T(1024)S(1)} %multiply_reduce_fusion.2), channel_id=1, source_target_pairs={{0,16},{4,20},{8,24},{12,28},{16,0},{20,4},{24,8},{28,12},{1,17},{... | collective-permute-start | bytes 49160 | tf_op jit(solution)/shard_map/ppermute | solution.py:23
  60.3 5.7 %collective-permute-start.27 = (f32[4096]{0:T(1024)S(1)}, f32[4096]{0:T(1024)S(1)}, u32[]{:S(2)}, u32[]{:S(2)}) collective-permute-start(f32[4096]{0:T(1024)S(1)} %multiply_reduce_fusion.2), channel_id=1, source_target_pairs={{0,20},{4,16},{8,28},{12,24},{16,4},{20,0},{24,12},{28,8},{1,21},{... | collective-permute-start | bytes 49160 | tf_op jit(solution)/shard_map/ppermute | solution.py:23
  62.1 4.1 %collective-permute-start.28 = (f32[4096]{0:T(1024)S(1)}, f32[4096]{0:T(1024)S(1)}, u32[]{:S(2)}, u32[]{:S(2)}) collective-permute-start(f32[4096]{0:T(1024)S(1)} %multiply_reduce_fusion.2), channel_id=1, source_target_pairs={{0,24},{4,28},{8,16},{12,20},{16,8},{20,12},{24,0},{28,4},{1,25},{... | collective-permute-start | bytes 49160 | tf_op jit(solution)/shard_map/ppermute | solution.py:23
  62.7 4.6 %collective-permute-start.29 = (f32[4096]{0:T(1024)S(1)}, f32[4096]{0:T(1024)S(1)}, u32[]{:S(2)}, u32[]{:S(2)}) collective-permute-start(f32[4096]{0:T(1024)S(1)} %multiply_reduce_fusion.2), channel_id=1, source_target_pairs={{0,28},{4,24},{8,20},{12,16},{16,12},{20,8},{24,4},{28,0},{1,29},{... | collective-permute-start | bytes 49160 | tf_op jit(solution)/shard_map/ppermute | solution.py:23
  67.7 1.9 %collective-permute-start.30 = (f32[256]{0:T(256)S(1)}, f32[256]{0:T(256)S(1)}, u32[]{:S(2)}, u32[]{:S(2)}) collective-permute-start(f32[256]{0:T(256)S(1)} %multiply_reduce_fusion.1), channel_id=1, source_target_pairs={{0,1},{1,0},{2,3},{3,2},{4,5},{5,4},{6,7},{7,6},{8,9},{9,8},{10,11... | collective-permute-start | bytes 3080 | tf_op jit(solution)/shard_map/ppermute | solution.py:23
  67.8 3.6 %collective-permute-start.31 = (f32[256]{0:T(256)S(1)}, f32[256]{0:T(256)S(1)}, u32[]{:S(2)}, u32[]{:S(2)}) collective-permute-start(f32[256]{0:T(256)S(1)} %multiply_reduce_fusion.1), channel_id=1, source_target_pairs={{0,2},{1,3},{2,0},{3,1},{4,6},{5,7},{6,4},{7,5},{8,10},{9,11},{10,... | collective-permute-start | bytes 3080 | tf_op jit(solution)/shard_map/ppermute | solution.py:23
  68.4 3.0 %collective-permute-start.32 = (f32[256]{0:T(256)S(1)}, f32[256]{0:T(256)S(1)}, u32[]{:S(2)}, u32[]{:S(2)}) collective-permute-start(f32[256]{0:T(256)S(1)} %multiply_reduce_fusion.1), channel_id=1, source_target_pairs={{0,3},{1,2},{2,1},{3,0},{4,7},{5,6},{6,5},{7,4},{8,11},{9,10},{10,... | collective-permute-start | bytes 3080 | tf_op jit(solution)/shard_map/ppermute | solution.py:23
  72.0 9.2 %collective-permute-start.33 = (f32[4096]{0:T(1024)S(1)}, f32[4096]{0:T(1024)S(1)}, u32[]{:S(2)}, u32[]{:S(2)}) collective-permute-start(f32[4096]{0:T(1024)S(1)} %multiply_reduce_fusion), channel_id=1, source_target_pairs={{0,4},{4,0},{8,12},{12,8},{16,20},{20,16},{24,28},{28,24},{1,5},{5... | collective-permute-start | bytes 49160 | tf_op jit(solution)/shard_map/ppermute | solution.py:23
  72.7 10.0 %collective-permute-start.34 = (f32[4096]{0:T(1024)S(1)}, f32[4096]{0:T(1024)S(1)}, u32[]{:S(2)}, u32[]{:S(2)}) collective-permute-start(f32[4096]{0:T(1024)S(1)} %multiply_reduce_fusion), channel_id=1, source_target_pairs={{0,8},{4,12},{8,0},{12,4},{16,24},{20,28},{24,16},{28,20},{1,9},{5... | collective-permute-start | bytes 49160 | tf_op jit(solution)/shard_map/ppermute | solution.py:23
  77.4 6.7 %collective-permute-start.35 = (f32[4096]{0:T(1024)S(1)}, f32[4096]{0:T(1024)S(1)}, u32[]{:S(2)}, u32[]{:S(2)}) collective-permute-start(f32[4096]{0:T(1024)S(1)} %multiply_reduce_fusion), channel_id=1, source_target_pairs={{0,12},{4,8},{8,4},{12,0},{16,28},{20,24},{24,20},{28,16},{1,13},{... | collective-permute-start | bytes 49160 | tf_op jit(solution)/shard_map/ppermute | solution.py:23
  78.3 5.9 %collective-permute-start.36 = (f32[4096]{0:T(1024)S(1)}, f32[4096]{0:T(1024)S(1)}, u32[]{:S(2)}, u32[]{:S(2)}) collective-permute-start(f32[4096]{0:T(1024)S(1)} %multiply_reduce_fusion), channel_id=1, source_target_pairs={{0,16},{4,20},{8,24},{12,28},{16,0},{20,4},{24,8},{28,12},{1,17},{... | collective-permute-start | bytes 49160 | tf_op jit(solution)/shard_map/ppermute | solution.py:23
  81.2 5.5 %collective-permute-start.37 = (f32[4096]{0:T(1024)S(1)}, f32[4096]{0:T(1024)S(1)}, u32[]{:S(2)}, u32[]{:S(2)}) collective-permute-start(f32[4096]{0:T(1024)S(1)} %multiply_reduce_fusion), channel_id=1, source_target_pairs={{0,20},{4,16},{8,28},{12,24},{16,4},{20,0},{24,12},{28,8},{1,21},{... | collective-permute-start | bytes 49160 | tf_op jit(solution)/shard_map/ppermute | solution.py:23
  81.3 5.5 %collective-permute-start.38 = (f32[4096]{0:T(1024)S(1)}, f32[4096]{0:T(1024)S(1)}, u32[]{:S(2)}, u32[]{:S(2)}) collective-permute-start(f32[4096]{0:T(1024)S(1)} %multiply_reduce_fusion), channel_id=1, source_target_pairs={{0,24},{4,28},{8,16},{12,20},{16,8},{20,12},{24,0},{28,4},{1,25},{... | collective-permute-start | bytes 49160 | tf_op jit(solution)/shard_map/ppermute | solution.py:23
  82.7 4.6 %collective-permute-start.39 = (f32[4096]{0:T(1024)S(1)}, f32[4096]{0:T(1024)S(1)}, u32[]{:S(2)}, u32[]{:S(2)}) collective-permute-start(f32[4096]{0:T(1024)S(1)} %multiply_reduce_fusion), channel_id=1, source_target_pairs={{0,28},{4,24},{8,20},{12,16},{16,12},{20,8},{24,4},{28,0},{1,29},{... | collective-permute-start | bytes 49160 | tf_op jit(solution)/shard_map/ppermute | solution.py:23
  87.3 4.6 %copy-start.4 = (bf16[256,128]{1,0:T(8,128)(2,1)S(1)}, bf16[256,128]{1,0:T(8,128)(2,1)}, u32[]{:S(2)}) copy-start(bf16[256,128]{1,0:T(8,128)(2,1)} %param.5) | copy-start | bytes 196612
  91.9 2.2 %copy-start.2 = (f32[256,4096]{1,0:T(8,128)S(1)}, f32[256,4096]{1,0:T(8,128)}, u32[]{:S(2)}) copy-start(f32[256,4096]{1,0:T(8,128)} %copy-done.1) | copy-start | bytes 12582916
  96.0 14.1 %collective-permute-start.43 = (f32[512,128]{1,0:T(8,128)S(1)}, f32[512,128]{1,0:T(8,128)S(1)}, u32[]{:S(2)}, u32[]{:S(2)}) collective-permute-start(f32[512,128]{1,0:T(8,128)S(1)} %get-tuple-element.8), channel_id=1, source_target_pairs={{0,4},{4,0},{8,12},{12,8},{16,20},{20,16},{24,28},{28,24},{1,5},{5... | collective-permute-start | bytes 786440 | tf_op jit(solution)/shard_map/ppermute | solution.py:23
  97.6 13.1 %collective-permute-start.44 = (f32[512,128]{1,0:T(8,128)S(1)}, f32[512,128]{1,0:T(8,128)}, u32[]{:S(2)}, u32[]{:S(2)}) collective-permute-start(f32[512,128]{1,0:T(8,128)S(1)} %get-tuple-element.14), channel_id=1, source_target_pairs={{0,8},{4,12},{8,0},{12,4},{16,24},{20,28},{24,16},{28,20},{1,9},{5... | collective-permute-start | bytes 786440 | tf_op jit(solution)/shard_map/ppermute | solution.py:23
  102.9 1.9 %collective-permute-start.40 = (f32[64,128]{1,0:T(8,128)S(1)}, f32[64,128]{1,0:T(8,128)}, u32[]{:S(2)}, u32[]{:S(2)}) collective-permute-start(f32[64,128]{1,0:T(8,128)S(1)} %get-tuple-element.15), channel_id=1, source_target_pairs={{0,1},{1,0},{2,3},{3,2},{4,5},{5,4},{6,7},{7,6},{8,9},{9,8},{10,11... | collective-permute-start | bytes 98312 | tf_op jit(solution)/shard_map/ppermute | solution.py:23
  103.0 4.1 %collective-permute-start.41 = (f32[64,128]{1,0:T(8,128)S(1)}, f32[64,128]{1,0:T(8,128)}, u32[]{:S(2)}, u32[]{:S(2)}) collective-permute-start(f32[64,128]{1,0:T(8,128)S(1)} %get-tuple-element.17), channel_id=1, source_target_pairs={{0,2},{1,3},{2,0},{3,1},{4,6},{5,7},{6,4},{7,5},{8,10},{9,11},{10,... | collective-permute-start | bytes 98312 | tf_op jit(solution)/shard_map/ppermute | solution.py:23
  104.5 3.3 %collective-permute-start.42 = (f32[64,128]{1,0:T(8,128)S(1)}, f32[64,128]{1,0:T(8,128)S(1)}, u32[]{:S(2)}, u32[]{:S(2)}) collective-permute-start(f32[64,128]{1,0:T(8,128)S(1)} %get-tuple-element.16), channel_id=1, source_target_pairs={{0,3},{1,2},{2,1},{3,0},{4,7},{5,6},{6,5},{7,4},{8,11},{9,10},{10,... | collective-permute-start | bytes 98312 | tf_op jit(solution)/shard_map/ppermute | solution.py:23
  104.9 11.4 %collective-permute-start.45 = (f32[512,128]{1,0:T(8,128)}, f32[512,128]{1,0:T(8,128)}, u32[]{:S(2)}, u32[]{:S(2)}) collective-permute-start(f32[512,128]{1,0:T(8,128)} %get-tuple-element.13), channel_id=1, source_target_pairs={{0,12},{4,8},{8,4},{12,0},{16,28},{20,24},{24,20},{28,16},{1,13},{... | collective-permute-start | bytes 786440 | tf_op jit(solution)/shard_map/ppermute | solution.py:23
  107.1 29.5 %collective-permute-start.46 = (f32[512,128]{1,0:T(8,128)}, f32[512,128]{1,0:T(8,128)}, u32[]{:S(2)}, u32[]{:S(2)}) collective-permute-start(f32[512,128]{1,0:T(8,128)} %get-tuple-element.12), channel_id=1, source_target_pairs={{0,16},{4,20},{8,24},{12,28},{16,0},{20,4},{24,8},{28,12},{1,17},{... | collective-permute-start | bytes 786440 | tf_op jit(solution)/shard_map/ppermute | solution.py:23
  107.9 2.8 %copy-start.5 = (f32[64,128]{1,0:T(8,128)}, f32[64,128]{1,0:T(8,128)S(1)}, u32[]{:S(2)}) copy-start(f32[64,128]{1,0:T(8,128)S(1)} %collective-permute-done.42) | copy-start | bytes 98308
  107.9 34.3 %collective-permute-start.47 = (f32[512,128]{1,0:T(8,128)}, f32[512,128]{1,0:T(8,128)}, u32[]{:S(2)}, u32[]{:S(2)}) collective-permute-start(f32[512,128]{1,0:T(8,128)} %get-tuple-element.11), channel_id=1, source_target_pairs={{0,20},{4,16},{8,28},{12,24},{16,4},{20,0},{24,12},{28,8},{1,21},{... | collective-permute-start | bytes 786440 | tf_op jit(solution)/shard_map/ppermute | solution.py:23
  110.1 39.7 %collective-permute-start.48 = (f32[512,128]{1,0:T(8,128)}, f32[512,128]{1,0:T(8,128)}, u32[]{:S(2)}, u32[]{:S(2)}) collective-permute-start(f32[512,128]{1,0:T(8,128)} %get-tuple-element.10), channel_id=1, source_target_pairs={{0,24},{4,28},{8,16},{12,20},{16,8},{20,12},{24,0},{28,4},{1,25},{... | collective-permute-start | bytes 786440 | tf_op jit(solution)/shard_map/ppermute | solution.py:23
  110.7 44.5 %collective-permute-start.49 = (f32[512,128]{1,0:T(8,128)}, f32[512,128]{1,0:T(8,128)}, u32[]{:S(2)}, u32[]{:S(2)}) collective-permute-start(f32[512,128]{1,0:T(8,128)} %get-tuple-element.9), channel_id=1, source_target_pairs={{0,28},{4,24},{8,20},{12,16},{16,12},{20,8},{24,4},{28,0},{1,29},{... | collective-permute-start | bytes 786440 | tf_op jit(solution)/shard_map/ppermute | solution.py:23

commit v2 on v1

--- a/solution.py
+++ b/solution.py
@@ -1,26 +1,433 @@
+import functools
+import math
+
 import jax
 import jax.numpy as jnp
 from jax import lax
+from jax.experimental import pallas as pl
+from jax.experimental.pallas import tpu as pltpu
 from jax.sharding import PartitionSpec as P
 
 ITERS = 4
-
-
-def contract_rows(left, right):
-    return lax.dot_general(
-        left, right, (((0,), (0,)), ((), ())), preferred_element_type=jnp.float32
-    )
-
-
-def contract_width(left, right):
-    return lax.dot_general(
-        left, right, (((1,), (1,)), ((), ())), preferred_element_type=jnp.float32
-    )
+CHUNK = 512
+STEP = 256
+EXT = 16
+PLAN_BYTES = 24 << 20
+LOG2E = 1.4426950408889634
+F32, BF16 = jnp.float32, jnp.bfloat16
+NT = (((1,), (1,)), ((), ()))
+NN = (((1,), (0,)), ((), ()))
+
+
+def mm(left, right, dims=NN):
+    return lax.dot_general(left, right, dims, preferred_element_type=F32)
 
 
 def swap(value, axis, step):
     size = lax.axis_size(axis)
     return lax.ppermute(value, axis, [(i, i ^ step) for i in range(size)])
+
+
+def as_column(row, width):
+    tall = jnp.transpose(jnp.broadcast_to(row, (128, row.shape[1])))
+    return jnp.concatenate([tall] * (width // 128), 1)
+
+
+def rows_of(pieces, height=EXT):
+    index = lax.broadcasted_iota(jnp.int32, (height, pieces[0].shape[1]), 0)
+    total = jnp.zeros(index.shape, F32)
+    for place, piece in enumerate(pieces):
+        total = jnp.where(index == place, piece, total)
+    return total
+
+
+def pieces_of(row):
+    out = []
+    for _ in range(3):
+        out.append(row.astype(BF16).astype(F32))
+        row = row - out[-1]
+    return out, [jnp.ones_like(row)] * 3
+
+
+def prep_kernel(logit_scale, ids, embeddings, second_view, row_scale, send_out):
+    rows, width = embeddings.shape
+
+    @pl.when(ids[1] & 1 == 0)
+    def _():
+        logs, ones = pieces_of(jnp.log(row_scale[...]) / logit_scale)
+        send_out[0:width, :] = jnp.transpose(embeddings[...].astype(F32)).astype(BF16)
+        send_out[width:width + EXT, :] = rows_of(logs + ones).astype(BF16)
+
+    @pl.when(ids[1] & 1 != 0)
+    def _():
+        send_out[0:width, :] = jnp.transpose(second_view[...].astype(F32)).astype(BF16)
+        send_out[width:width + EXT, :] = jnp.zeros((EXT, rows), BF16)
+
+
+def turn_kernel(logit_scale, log_mass, ids, protos, col_scale, protos_out, protos_t, token):
+    count = protos_out.shape[0]
+    width = protos.shape[1]
+    token[...] = jnp.zeros_like(token)
+
+    def step(index, carry):
+        here = pl.ds(pl.multiple_of(index * CHUNK, CHUNK), CHUNK)
+        there = pl.ds(pl.multiple_of((2 * index + (ids[0] & 1)) * CHUNK, CHUNK), CHUNK)
+        block = protos[there, :]
+        logs, ones = pieces_of((jnp.log(col_scale[:, there]) - log_mass) / logit_scale)
+        protos_out[here, 0:width] = block
+        protos_out[here, width:] = jnp.transpose(rows_of(ones + logs, width)).astype(BF16)
+        protos_t[:, here] = jnp.transpose(block.astype(F32)).astype(BF16)
+        return carry
+
+    lax.fori_loop(0, count // CHUNK, step, 0)
+
+
+def stack_kernel(count, *refs):
+    for place in range(count):
+        refs[-1][place] = refs[place][...]
+
+
+def add_kernel(left, right, out):
+    out[...] = left[...] + right[...]
+
+
+def plan_kernel(logit_scale, view_scale, ids, protos, mine_a, theirs_a, mine_b, theirs_b, plan_out, cols_out, sums_out, emb_ext, view_t, row_mass, row_weight):
+    pairs, high, rows = mine_a.shape
+    blocks = 2 * pairs
+    count = protos.shape[0]
+    width = view_t.shape[0]
+    scale = logit_scale * LOG2E
+    emb_ext[high:, :] = jnp.zeros((emb_ext.shape[0] - high, blocks * rows), BF16)
+
+    def fill(embs, views):
+        for block in range(blocks):
+            cols = slice(block * rows, (block + 1) * rows)
+            emb_ext[0:high, cols] = embs[block % 2][block // 2]
+            view_t[:, cols] = views[block % 2][block // 2, 0:width, :]
+
+    for core in range(2):
+        for odd in range(2):
+            a, b = ((mine_a, theirs_a), (mine_b, theirs_b)) if core == 0 else ((theirs_a, mine_a), (theirs_b, mine_b))
+            low, upper = (a, b) if odd == 0 else (b, a)
+            is_this = jnp.logical_and(ids[1] & 1 == core, ids[0] & 1 == odd)
+            pl.when(is_this)(functools.partial(fill, (low[0], upper[0]), (low[1], upper[1])))
+    row_mass[...] = jnp.zeros_like(row_mass)
+    row_weight[...] = jnp.zeros_like(row_weight)
+
+    def folded(block):
+        tiles = [block[:, left:left + 128] for left in range(0, block.shape[1], 128)]
+        across = tiles[0]
+        for tile in tiles[1:]:
+            across = across + tile
+        return across, jnp.sum(block.reshape(block.shape[0] // 8, 8, block.shape[1]), axis=0)
+
+    def step(index, carry):
+        here = pl.ds(pl.multiple_of(index * CHUNK, CHUNK), CHUNK)
+        mass = weight = jnp.zeros((CHUNK, 128), F32)
+        for block in range(blocks):
+            cols = slice(block * rows, (block + 1) * rows)
+            plan = jnp.exp2(scale * mm(protos[here, :], emb_ext[:, cols]))
+            plan_out[here, cols] = plan
+            across, down = folded(plan)
+            mass = mass + across
+            row_mass[:, cols] += down
+            across, down = folded(plan * mm(protos[here, 0:width], view_t[:, cols]))
+            weight = weight + across
+            row_weight[:, cols] += down
+        cols_out[0:1, here] = jnp.sum(jnp.transpose(mass), axis=0, keepdims=True)
+        cols_out[1:2, here] = -view_scale * jnp.sum(jnp.transpose(weight), axis=0, keepdims=True)
+        return carry
+
+    lax.fori_loop(0, count // CHUNK, step, 0)
+    sums_out[0:1, :] = jnp.sum(row_mass[...], axis=0, keepdims=True)
+    sums_out[1:2, :] = -view_scale * jnp.sum(row_weight[...], axis=0, keepdims=True)
+
+
+def added(parts):
+    total = parts[0][...]
+    for other in parts[1:]:
+        total = total + other[...]
+    return total
+
+
+def by_rows(block, spread):
+    tall, wide = block.shape
+    sums = []
+    for top in range(0, tall, 64):
+        group = [jnp.zeros((8, 128), F32) for _ in range(8)]
+        for left in range(0, wide, 128):
+            dual = spread[:, left:left + 128]
+            for place in range(8):
+                here = slice(top + place * 8, top + (place + 1) * 8)
+                group[place] = group[place] + block[here, left:left + 128] * dual
+        sums += group
+    return jnp.sum(jnp.transpose(jnp.concatenate(sums)), axis=0, keepdims=True)
+
+
+def by_cols(block, column):
+    tall, wide = block.shape
+    sums = [jnp.zeros((8, 128), F32) for _ in range(wide // 128)]
+    for top in range(0, tall, 8):
+        dual = column[top:top + 8, :]
+        for place in range(wide // 128):
+            sums[place] = sums[place] + block[top:top + 8, place * 128:(place + 1) * 128] * dual
+    return jnp.concatenate(sums, 1)
+
+
+def chunk(index):
+    return pl.ds(pl.multiple_of(index * STEP, STEP), STEP)
+
+
+def sweep_kernel(opening, shares, plan, cols, *refs):
+    if opening:
+        parts, (_, _, sums_out, part_out, spread, total) = refs[:shares], refs[shares:]
+        sums_out[...] = added(parts)
+        row_dual = sums_out[1:2, :] / sums_out[0:1, :]
+    else:
+        (sums, *parts), (_, _, part_out, spread, total) = refs[:shares + 1], refs[shares + 1:]
+        row_dual = (sums[1:2, :] - added(parts)) / sums[0:1, :]
+    spread[...] = jnp.broadcast_to(row_dual, spread.shape)
+    total[...] = jnp.zeros_like(total)
+    steps = plan.shape[0] // STEP
+
+    def duals(index):
+        here = chunk(index)
+        product = by_rows(plan.at[here, :], spread)
+        return as_column((cols[1:2, here] - product) / cols[0:1, here], 128)
+
+    def step(index, dual):
+        product = by_cols(plan.at[chunk(index - 1), :], dual)
+        dual = duals(index)
+        total[...] += product
+        return dual
+
+    last = lax.fori_loop(1, steps, step, duals(0))
+    total[...] += by_cols(plan.at[chunk(steps - 1), :], last)
+    part_out[...] = jnp.sum(total[...], axis=0, keepdims=True)
+
+
+def embed_before_kernel(logit_scale, protos, emb_ext, after, entry_out, token):
+    del after
+    scale = logit_scale * LOG2E
+    token[...] = jnp.zeros_like(token)
+
+    def step(index, carry):
+        here = chunk(index)
+        entry_out[here, :] = logit_scale * jnp.exp2(scale * mm(protos[here, :], emb_ext[:, 0:entry_out.shape[1]]))
+        return carry
+
+    lax.fori_loop(0, protos.shape[0] // STEP, step, 0)
+
+
+def embed_kernel(view_scale, shares, ids, plan, cols, sums, protos, protos_t, view_t, entries, *refs):
+    parts, (duals_out, rows_out, keep, give, spread, total, whole) = refs[:shares], refs[shares:]
+    width = protos_t.shape[0]
+    rows = entries.shape[1]
+    rows_out[...] = (sums[1:2, :] - added(parts)) / sums[0:1, :]
+    spread[...] = jnp.broadcast_to(rows_out[...], spread.shape)
+    own_dual = rows_out[:, 0:rows]
+    total[...] = jnp.zeros_like(total)
+    steps = plan.shape[0] // STEP
+
+    def duals(index):
+        here = chunk(index)
+        return (cols[1:2, here] - by_rows(plan.at[here, :], spread)) / cols[0:1, here]
+
+    def gradient(index, dual):
+        here = chunk(index)
+        cot = -view_scale * mm(protos[here, 0:width], view_t[:, 0:rows])
+        grad = entries[here, :] * (cot - own_dual - as_column(dual, rows))
+        return mm(protos_t[:, here], grad.astype(BF16))
+
+    def step(index, dual):
+        share = gradient(index - 1, dual)
+        duals_out[:, chunk(index - 1)] = dual
+        dual = duals(index)
+        total[...] += share
+        return dual
+
+    last = lax.fori_loop(1, steps, step, duals(0))
+    duals_out[:, chunk(steps - 1)] = last
+    total[...] += gradient(steps - 1, last)
+    whole[...] = jnp.transpose(total[...])
+    tall = keep.shape[1]
+    for place in range(shares):
+        above, beside = divmod(place, shares // 2)
+        to = ((ids[0] & 1) ^ above) * shares + (ids[1] ^ (2 * beside))
+        keep[place] = whole[pl.ds(pl.multiple_of(to * tall, tall), tall), :]
+        give[place] = whole[pl.ds(pl.multiple_of((to ^ 1) * tall, tall), tall), :]
+
+
+def proto_before_kernel(logit_scale, view_scale, ids, protos, emb_ext, view_t, after, entry_out, second_out, token):
+    del after
+    own, rows = entry_out.shape
+    width = second_out.shape[1]
+    scale = logit_scale * LOG2E
+    token[...] = jnp.zeros_like(token)
+    here = pl.ds(pl.multiple_of((ids[0] >> 1) * own, own), own)
+    total = jnp.zeros((own, width), F32)
+    for start in range(0, rows, 2 * width):
+        cols = slice(start, start + 2 * width)
+        exact = jnp.exp2(scale * mm(protos[here, :], emb_ext[:, cols]))
+        entry_out[:, cols] = logit_scale * exact
+        total = total + mm((-view_scale * exact).astype(BF16), view_t[:, cols], NT)
+    second_out[...] = total
+
+
+def proto_kernel(view_scale, ids, protos, emb_ext, view_t, entries, second, col_dual, row_dual, out):
+    own, width = out.shape
+    here = pl.ds(pl.multiple_of((ids[0] >> 1) * own, own), own)
+    column = as_column(col_dual[:, here], 2 * width)
+    total = second[...]
+    for start in range(0, entries.shape[1], 2 * width):
+        cols = slice(start, start + 2 * width)
+        cot = -view_scale * mm(protos[here, 0:width], view_t[:, cols])
+        grad = entries[:, cols] * (cot - row_dual[:, cols] - column)
+        total = total + mm(grad.astype(BF16), emb_ext[0:width, cols], NT)
+    out[...] = total
+
+
+def call(kernel, out_shape, name, scalars=0, scratch=(), aliases=None, limit=16):
+    def run(*args):
+        whole = pl.BlockSpec(memory_space=pltpu.VMEM)
+        small = pl.BlockSpec(memory_space=pltpu.SMEM)
+        return pl.pallas_call(
+            kernel,
+            out_shape=out_shape,
+            in_specs=[small] * scalars + [whole] * (len(args) - scalars),
+            out_specs=jax.tree.map(lambda _: whole, out_shape),
+            scratch_shapes=[pltpu.VMEM(dims, dtype) for dtype, *dims in scratch],
+            input_output_aliases=aliases or {},
+            compiler_params=pltpu.CompilerParams(vmem_limit_bytes=limit << 20),
+            name=name,
+        )(*args)
+
+    return run
+
+
+def swap_both(value, above, beside):
+    shares = lax.axis_size("proto")
+    pairs = [
+        (row * shares + col, (row ^ above) * shares + (col ^ beside))
+        for row in range(lax.axis_size("row"))
+        for col in range(shares)
+    ]
+    return lax.ppermute(value, ("row", "proto"), pairs)
+
+
+def others():
+    shares = lax.axis_size("proto")
+    return [(above, beside) for above in range(2) for beside in range(0, shares, 2)]
+
+
+def exchange(part):
+    near = call(add_kernel, jax.ShapeDtypeStruct(part.shape, F32), "add", limit=2)(part, swap(part, "proto", 1))
+    return [near if pair == (0, 0) else swap_both(near, *pair) for pair in others()]
+
+
+def kept_plan(embeddings, second_view, prototypes, row_scale, col_scale):
+    rows, width = embeddings.shape
+    blocks, shares = lax.axis_size("row"), lax.axis_size("proto")
+    all_rows = rows * blocks
+    count = prototypes.shape[0] // 2
+    own = 2 * count // blocks
+    ids = jnp.stack((lax.axis_index("row"), lax.axis_index("proto")))
+    scales = (1.0 / (0.05 * width), 1.0 / (0.1 * width))
+    log_mass = math.log(64.0 * prototypes.shape[0] * shares)
+    shape = lambda *dims, dtype=F32: jax.ShapeDtypeStruct(dims, dtype)
+    form = lambda kernel: functools.partial(kernel, *scales)
+    there = lambda value: pltpu.with_memory_space_constraint(value, pltpu.HBM)
+    row_scale = row_scale.reshape(1, rows)
+    col_scale = col_scale.reshape(1, 2 * count)
+    half = shape(width + EXT, rows, dtype=BF16)
+    send = call(functools.partial(prep_kernel, scales[0]), half, "prepare", scalars=1)(
+        ids, there(embeddings), there(second_view), there(row_scale)
+    )
+    protos, protos_t, token = call(
+        functools.partial(turn_kernel, scales[0], log_mass),
+        (shape(count, 2 * width, dtype=BF16), shape(width, count, dtype=BF16), shape(8, 128)),
+        "turn",
+        scalars=1,
+        limit=4,
+    )(ids, there(prototypes), there(col_scale))
+    pairs = blocks // 2
+    stack = call(functools.partial(stack_kernel, pairs), shape(pairs, width + EXT, rows, dtype=BF16), "stack", limit=2)
+    direct = [send] + [swap(send, "row", step) for step in range(2, blocks, 2)]
+    mine_a = stack(*direct)
+    theirs_a = swap(mine_a, "proto", 1)
+    mine_b = stack(*[swap(value, "row", 1) for value in direct], token)
+    theirs_b = swap(mine_b, "proto", 1)
+
+    kept = pltpu.VMEM((count, all_rows), F32)
+    plan, cols, sums, emb_ext, view_t = call(
+        form(plan_kernel),
+        (kept, shape(2, count), shape(2, all_rows), shape(2 * width, all_rows, dtype=BF16), shape(width, all_rows, dtype=BF16)),
+        "plan",
+        scalars=1,
+        scratch=[(F32, 8, all_rows), (F32, 8, all_rows)],
+        limit=12,
+    )(ids, protos, mine_a, theirs_a, mine_b, theirs_b)
+
+    work = [(F32, 8, all_rows), (F32, 8, all_rows)]
+    token = shape(8, 128)
+    parts = exchange(sums)
+    entries, done = call(
+        functools.partial(embed_before_kernel, scales[0]),
+        (shape(count, 2 * rows), token),
+        "embed_before",
+        limit=6,
+    )(protos, emb_ext, parts[0])
+    plan, sums, part = call(
+        functools.partial(sweep_kernel, True, shares),
+        (kept, shape(2, all_rows), shape(1, all_rows)),
+        "sweep",
+        scratch=work,
+        aliases={0: 0},
+        limit=4,
+    )(plan, cols, *parts, done)
+    for sweep in range(ITERS - 2):
+        parts = exchange(part)
+        if sweep == 0:
+            own_entries, second, done = call(
+                form(proto_before_kernel),
+                (shape(own, all_rows), shape(own, width), token),
+                "proto_before",
+                scalars=1,
+                limit=6,
+            )(ids, protos, emb_ext, view_t, parts[0])
+        plan, part = call(
+            functools.partial(sweep_kernel, False, shares),
+            (kept, shape(1, all_rows)),
+            "sweep",
+            scratch=work,
+            aliases={0: 0},
+            limit=4,
+        )(plan, cols, sums, *parts, done)
+    pieces = shape(shares, rows // shares, width)
+    col_dual, row_dual, keep, give = call(
+        functools.partial(embed_kernel, scales[1], shares),
+        (shape(1, count), shape(1, all_rows), pieces, pieces),
+        "embed_grad",
+        scalars=1,
+        scratch=work[:1] + [(F32, width, 2 * rows), (F32, 2 * rows, width)],
+        limit=6,
+    )(ids, plan, cols, sums, protos, protos_t, view_t, entries, *exchange(part))
+    near = call(add_kernel, pieces, "add", limit=2)(keep, swap(give, "proto", 1))
+    embed_grad = near[0]
+    for place, pair in list(enumerate(others()))[1:]:
+        embed_grad = embed_grad + swap_both(near[place], *pair)
+    proto_grad = call(functools.partial(proto_kernel, scales[1]), shape(own, width), "proto_grad", scalars=1, limit=6)(
+        ids, protos, emb_ext, view_t, own_entries, second, col_dual, row_dual
+    )
+    return embed_grad, proto_grad
+
+
+def contract_rows(left, right):
+    return mm(left, right, (((0,), (0,)), ((), ())))
+
+
+def contract_width(left, right):
+    return mm(left, right, NT)
 
 
 def sum_over(value, axis):
@@ -40,7 +447,7 @@
     return total
 
 
-def per_device(embeddings, second_view, prototypes, row_scale, col_scale):
+def split_plan(embeddings, second_view, prototypes, row_scale, col_scale):
     feat_width = embeddings.shape[1]
     proto_count = prototypes.shape[0]
     logit_scale = 1.0 / (0.05 * feat_width)
@@ -74,6 +481,18 @@
     return (embed_grad, proto_grad)
 
 
+def per_device(embeddings, second_view, prototypes, row_scale, col_scale):
+    blocks, shares = lax.axis_size("row"), lax.axis_size("proto")
+    rows, width = embeddings.shape
+    count = prototypes.shape[0]
+    fits = rows * blocks * count * 2 <= PLAN_BYTES
+    even = all(n & (n - 1) == 0 and n > 1 for n in (blocks, shares))
+    even = even and rows % (16 * shares) == 0 and rows % width == 0
+    tiled = rows % 128 == 0 and width % 128 == 0 and count == blocks * CHUNK and blocks % 4 == 0
+    form = kept_plan if fits and even and tiled else split_plan
+    return form(embeddings, second_view, prototypes, row_scale, col_scale)
+
+
 def solution(mesh):
     return jax.shard_map(
         per_device,

time: 158 us -> 81.6 us (0.52)
  the two profiles are of different devices: /device:TPU:8 before, /device:TPU:0 now
where the time goes in v2:
time: 81.6 us; the launch traced here: 81.4 us
  Pallas kernels  32 us (39%)
  starting transfers between devices  29.5 us (36%)
  waiting for transfers between devices  18.4 us (23%)
  between operations  0.84 us (1%)
    pallas_call x17, Pallas kernels, run(): pl.pallas_call(kernel, out_shape=out_shape, in_specs=[small] * scalars +...  32 us
    ppermute x15, starting transfers between devices, swap_both(): return lax.ppermute(value, ('row', 'proto'), pairs)  17.5 us
    ppermute x14, starting transfers between devices, swap(): return lax.ppermute(value, axis, [(i, i ^ step) for i in range(size)])  12 us
    ppermute x14, waiting for transfers between devices, swap(): return lax.ppermute(value, axis, [(i, i ^ step) for i in range(size)])  11.2 us
    ppermute x15, waiting for transfers between devices, swap_both(): return lax.ppermute(value, ('row', 'proto'), pairs)  7.21 us
  transfers between devices with their start and end apart: 29, of which 21 were waited for; matrix products, arithmetic and copies ran while one was open for 0% of the time, Pallas kernels for 11%

profile of v2, /device:TPU:0, one launch (start us, length us, event | category | flops | bytes accessed | tf_op | source)
XLA Modules:
  0.0 81.4 jit_solution(17828070217557972124)
XLA Ops:
  0.6 0.1 pad_add_fusion.ids
  0.7 1.0 %prepare.1.refs_0_ = bf16[144,256]{1,0:T(8,128)(2,1)S(1)} custom-call(s32[2]{0:T(128)S(1)} %pad_add_fusion.ids, bf16[256,128]{1,0:T(8,128)(2,1)} %embeddings.1, bf16[256,128]{1,0:T(8,128)(2,1)} %second_view.1, f32[1,256]{1,0:T(1,128)} %bitcast.19), custom_call_target="tpu_custom_call" | custom-call | tf_op jit(solution)/shard_map/prepare/pallas_call | solution.py:294
  1.7 5.1 %collective-permute-start.2 = (bf16[144,256]{1,0:T(8,128)(2,1)S(1)}, bf16[144,256]{1,0:T(8,128)(2,1)S(1)}, u32[]{:S(2)}, u32[]{:S(2)}) collective-permute-start(bf16[144,256]{1,0:T(8,128)(2,1)S(1)} %prepare.1.refs_0_), channel_id=1, source_target_pairs={{0,24},{4,28},{8,16},{12,20},{16,8},{20,12},{24,0},{28,4},{1,25},{... | collective-permute-start | bytes 221192 | tf_op jit(solution)/shard_map/ppermute | solution.py:28
  6.8 0.0 collective-permute-start.1
  6.8 0.6 collective-permute-start
  7.5 1.7 %collective-permute-start.4 = (bf16[144,256]{1,0:T(8,128)(2,1)S(1)}, bf16[144,256]{1,0:T(8,128)(2,1)S(1)}, u32[]{:S(2)}, u32[]{:S(2)}) collective-permute-start(bf16[144,256]{1,0:T(8,128)(2,1)S(1)} %prepare.1.refs_0_), channel_id=1, source_target_pairs={{0,4},{4,0},{8,12},{12,8},{16,20},{20,16},{24,28},{28,24},{1,5},{5... | collective-permute-start | bytes 221192 | tf_op jit(solution)/shard_map/ppermute | solution.py:28
  9.1 0.4 collective-permute-done.2.refs_3_
  9.6 1.9 %collective-permute-start.7 = (bf16[144,256]{1,0:T(8,128)(2,1)S(1)}, bf16[144,256]{1,0:T(8,128)(2,1)S(1)}, u32[]{:S(2)}, u32[]{:S(2)}) collective-permute-start(bf16[144,256]{1,0:T(8,128)(2,1)S(1)} %collective-permute-done.2.refs_3_), channel_id=1, source_target_pairs={{0,4},{4,0},{8,12},{12,8},{16,20},{20,16},{24,28},{28,24},{1,5},{5... | collective-permute-start | bytes 221192 | tf_op jit(solution)/shard_map/ppermute | solution.py:28
  11.5 1.6 %collective-permute-done.1.refs_2_ = bf16[144,256]{1,0:T(8,128)(2,1)S(1)} collective-permute-done((bf16[144,256]{1,0:T(8,128)(2,1)S(1)}, bf16[144,256]{1,0:T(8,128)(2,1)S(1)}, u32[]{:S(2)}, u32[]{:S(2)}) %collective-permute-start.1) | collective-permute-done | bytes 73760 | tf_op jit(solution)/shard_map/ppermute | solution.py:28
  13.0 1.5 %collective-permute-start.6 = (bf16[144,256]{1,0:T(8,128)(2,1)S(1)}, bf16[144,256]{1,0:T(8,128)(2,1)S(1)}, u32[]{:S(2)}, u32[]{:S(2)}) collective-permute-start(bf16[144,256]{1,0:T(8,128)(2,1)S(1)} %collective-permute-done.1.refs_2_), channel_id=1, source_target_pairs={{0,4},{4,0},{8,12},{12,8},{16,20},{20,16},{24,28},{28,24},{1,5},{5... | collective-permute-start | bytes 221192 | tf_op jit(solution)/shard_map/ppermute | solution.py:28
  14.6 0.0 collective-permute-done.refs_1_
  14.6 0.5 collective-permute-start.5
  15.1 2.0 %turn.1 = (bf16[2048,256]{1,0:T(8,128)(2,1)S(1)}, bf16[128,2048]{1,0:T(8,128)(2,1)S(1)}, f32[8,128]{1,0:T(8,128)S(1)}) custom-call(s32[2]{0:T(128)S(1)} %pad_add_fusion.ids, bf16[4096,128]{1,0:T(8,128)(2,1)} %protos.1, f32[1,4096]{1,0:T(1,128)} %bitcast.18), custom_call_target="tpu_custom_call" | custom-call | tf_op jit(solution)/shard_map/turn/pallas_call | solution.py:294
  17.1 0.1 collective-permute-start.3
  17.1 0.0 collective-permute-done.4.refs_0_
  17.2 0.9 %collective-permute-done.6.refs_2_ = bf16[144,256]{1,0:T(8,128)(2,1)S(1)} collective-permute-done((bf16[144,256]{1,0:T(8,128)(2,1)S(1)}, bf16[144,256]{1,0:T(8,128)(2,1)S(1)}, u32[]{:S(2)}, u32[]{:S(2)}) %collective-permute-start.6) | collective-permute-done | bytes 73760 | tf_op jit(solution)/shard_map/ppermute | solution.py:28
  18.1 0.8 collective-permute-done.5.refs_1_
  18.9 0.1 collective-permute-start.8
  19.0 1.6 %collective-permute-done.8.theirs_b = bf16[4,144,256]{2,1,0:T(8,128)(2,1)S(1)} collective-permute-done((bf16[4,144,256]{2,1,0:T(8,128)(2,1)S(1)}, bf16[4,144,256]{2,1,0:T(8,128)(2,1)S(1)}, u32[]{:S(2)}, u32[]{:S(2)}) %collective-permute-start.8) | collective-permute-done | bytes 294944 | tf_op jit(solution)/shard_map/ppermute | solution.py:28
  20.6 6.3 %plan.1 = (f32[2048,2048]{1,0:T(8,128)S(1)}, f32[2,2048]{1,0:T(2,128)S(1)}, f32[2,2048]{1,0:T(2,128)S(1)}, bf16[256,2048]{1,0:T(8,128)(2,1)S(1)}, bf16[128,2048]{1,0:T(8,128)(2,1)S(1)}) custom-call(s32[2]{0:T(128)S(1)} %pad_add_fusion.ids, bf16[2048,256]{1,0:T(8,128)(2,1)S(1)} %get-tuple-element.26.protos, bf16[4,144,256]{2,1,0:T(8,128)(2,1)S(1)} %stack.14.mine_a, ...), custom_call_target="tpu_custom_call" | custom-call | tf_op jit(solution)/shard_map/plan/pallas_call | solution.py:294
  26.9 0.2 collective-permute-start.9
  27.2 1.0 %collective-permute-done.9.right = f32[2,2048]{1,0:T(2,128)S(1)} collective-permute-done((f32[2,2048]{1,0:T(2,128)S(1)}, f32[2,2048]{1,0:T(2,128)S(1)}, u32[]{:S(2)}, u32[]{:S(2)}) %collective-permute-start.9) | collective-permute-done | bytes 16416 | tf_op jit(solution)/shard_map/ppermute | solution.py:28
  28.2 2.0 %collective-permute-start.12 = (f32[2,2048]{1,0:T(2,128)S(1)}, f32[2,2048]{1,0:T(2,128)S(1)}, u32[]{:S(2)}, u32[]{:S(2)}) collective-permute-start(f32[2,2048]{1,0:T(2,128)S(1)} %add.28.after.refs_0_), channel_id=1, source_target_pairs={{0,6},{1,7},{2,4},{3,5},{4,2},{5,3},{6,0},{7,1},{8,14},{9,15},{10,... | collective-permute-start | bytes 49160 | tf_op jit(solution)/shard_map/ppermute | solution.py:315
  30.2 1.0 %collective-permute-start.11 = (f32[2,2048]{1,0:T(2,128)S(1)}, f32[2,2048]{1,0:T(2,128)S(1)}, u32[]{:S(2)}, u32[]{:S(2)}) collective-permute-start(f32[2,2048]{1,0:T(2,128)S(1)} %add.28.after.refs_0_), channel_id=1, source_target_pairs={{0,4},{1,5},{2,6},{3,7},{4,0},{5,1},{6,2},{7,3},{8,12},{9,13},{10,... | collective-permute-start | bytes 49160 | tf_op jit(solution)/shard_map/ppermute | solution.py:315
  31.2 0.5 collective-permute-start.10
  31.7 1.9 %embed_before.1 = (f32[2048,512]{1,0:T(8,128)S(1)}, f32[8,128]{1,0:T(8,128)S(1)}) custom-call(bf16[2048,256]{1,0:T(8,128)(2,1)S(1)} %get-tuple-element.26.protos, bf16[256,2048]{1,0:T(8,128)(2,1)S(1)} %get-tuple-element.31.emb_ext, f32[2,2048]{1,0:T(2,128)S(1)} %add.28.after.refs_0_), custom_call_target="tpu_custom_call" | custom-call | tf_op jit(solution)/shard_map/embed_before/pallas_call | solution.py:294
  33.7 0.3 collective-permute-done.11.refs_2_
  33.9 1.0 %collective-permute-done.10.refs_1_ = f32[2,2048]{1,0:T(2,128)S(1)} collective-permute-done((f32[2,2048]{1,0:T(2,128)S(1)}, f32[2,2048]{1,0:T(2,128)S(1)}, u32[]{:S(2)}, u32[]{:S(2)}) %collective-permute-start.10) | collective-permute-done | bytes 16416 | tf_op jit(solution)/shard_map/ppermute | solution.py:315
  34.9 3.8 %sweep.3 = (f32[2048,2048]{1,0:T(8,128)S(1)}, f32[2,2048]{1,0:T(2,128)S(1)}, f32[1,2048]{1,0:T(1,128)S(1)}) custom-call(f32[2048,2048]{1,0:T(8,128)S(1)} %get-tuple-element.28.plan, f32[2,2048]{1,0:T(2,128)S(1)} %get-tuple-element.29.cols, f32[2,2048]{1,0:T(2,128)S(1)} %add.28.after.refs_0_, ...), custom_call_target="tpu_custom_call", output_to_operand_aliasing={{0}: (0, {})} | custom-call | tf_op jit(solution)/shard_map/sweep/pallas_call | solution.py:294
  38.7 0.1 collective-permute-start.13
  38.8 1.2 %collective-permute-done.13.right = f32[1,2048]{1,0:T(1,128)S(1)} collective-permute-done((f32[1,2048]{1,0:T(1,128)S(1)}, f32[1,2048]{1,0:T(1,128)S(1)}, u32[]{:S(2)}, u32[]{:S(2)}) %collective-permute-start.13) | collective-permute-done | bytes 8224 | tf_op jit(solution)/shard_map/ppermute | solution.py:28
  40.0 1.0 %collective-permute-start.16 = (f32[1,2048]{1,0:T(1,128)S(1)}, f32[1,2048]{1,0:T(1,128)S(1)}, u32[]{:S(2)}, u32[]{:S(2)}) collective-permute-start(f32[1,2048]{1,0:T(1,128)S(1)} %add.29.after.refs_1_), channel_id=1, source_target_pairs={{0,6},{1,7},{2,4},{3,5},{4,2},{5,3},{6,0},{7,1},{8,14},{9,15},{10,... | collective-permute-start | bytes 24584 | tf_op jit(solution)/shard_map/ppermute | solution.py:315
  41.0 1.0 %collective-permute-start.15 = (f32[1,2048]{1,0:T(1,128)S(1)}, f32[1,2048]{1,0:T(1,128)S(1)}, u32[]{:S(2)}, u32[]{:S(2)}) collective-permute-start(f32[1,2048]{1,0:T(1,128)S(1)} %add.29.after.refs_1_), channel_id=1, source_target_pairs={{0,4},{1,5},{2,6},{3,7},{4,0},{5,1},{6,2},{7,3},{8,12},{9,13},{10,... | collective-permute-start | bytes 24584 | tf_op jit(solution)/shard_map/ppermute | solution.py:315
  42.0 1.5 %collective-permute-start.14 = (f32[1,2048]{1,0:T(1,128)S(1)}, f32[1,2048]{1,0:T(1,128)S(1)}, u32[]{:S(2)}, u32[]{:S(2)}) collective-permute-start(f32[1,2048]{1,0:T(1,128)S(1)} %add.29.after.refs_1_), channel_id=1, source_target_pairs={{0,2},{1,3},{2,0},{3,1},{4,6},{5,7},{6,4},{7,5},{8,10},{9,11},{10,... | collective-permute-start | bytes 24584 | tf_op jit(solution)/shard_map/ppermute | solution.py:315
  43.5 2.0 %proto_before.1 = (f32[512,2048]{1,0:T(8,128)S(1)}, f32[512,128]{1,0:T(8,128)S(1)}, f32[8,128]{1,0:T(8,128)S(1)}) custom-call(s32[2]{0:T(128)S(1)} %pad_add_fusion.ids, bf16[2048,256]{1,0:T(8,128)(2,1)S(1)} %get-tuple-element.26.protos, bf16[256,2048]{1,0:T(8,128)(2,1)S(1)} %get-tuple-element.31.emb_ext, bf16[128,2048]{1,0:T(8,128)(2,1)S(1)} %get-tuple-element.36.view_t, ...), custom_call_target="tpu_custom_call" | custom-call | tf_op jit(solution)/shard_map/proto_before/pallas_call | solution.py:294
  45.5 0.1 collective-permute-done.14.refs_2_
  45.6 3.8 %sweep.4 = (f32[2048,2048]{1,0:T(8,128)S(1)}, f32[1,2048]{1,0:T(1,128)S(1)}) custom-call(f32[2048,2048]{1,0:T(8,128)S(1)} %get-tuple-element.33.plan, f32[2,2048]{1,0:T(2,128)S(1)} %get-tuple-element.29.cols, f32[2,2048]{1,0:T(2,128)S(1)} %get-tuple-element.34.refs_0_.sums, f32[1,2048]{1,0:T(1,128)S(1)} %add.29.after.refs_1_, ...), custom_call_target="tpu_custom_call", output_to_operand_aliasing={{0}: (0, {})} | custom-call | tf_op jit(solution)/shard_map/sweep/pallas_call | solution.py:294
  49.4 0.1 collective-permute-start.17
  49.5 1.2 %collective-permute-done.17.right = f32[1,2048]{1,0:T(1,128)S(1)} collective-permute-done((f32[1,2048]{1,0:T(1,128)S(1)}, f32[1,2048]{1,0:T(1,128)S(1)}, u32[]{:S(2)}, u32[]{:S(2)}) %collective-permute-start.17) | collective-permute-done | bytes 8224 | tf_op jit(solution)/shard_map/ppermute | solution.py:28
  50.7 2.0 %collective-permute-start.20 = (f32[1,2048]{1,0:T(1,128)S(1)}, f32[1,2048]{1,0:T(1,128)S(1)}, u32[]{:S(2)}, u32[]{:S(2)}) collective-permute-start(f32[1,2048]{1,0:T(1,128)S(1)} %add.30.refs_1_), channel_id=1, source_target_pairs={{0,6},{1,7},{2,4},{3,5},{4,2},{5,3},{6,0},{7,1},{8,14},{9,15},{10,... | collective-permute-start | bytes 24584 | tf_op jit(solution)/shard_map/ppermute | solution.py:315
  52.7 1.0 %collective-permute-start.19 = (f32[1,2048]{1,0:T(1,128)S(1)}, f32[1,2048]{1,0:T(1,128)S(1)}, u32[]{:S(2)}, u32[]{:S(2)}) collective-permute-start(f32[1,2048]{1,0:T(1,128)S(1)} %add.30.refs_1_), channel_id=1, source_target_pairs={{0,4},{1,5},{2,6},{3,7},{4,0},{5,1},{6,2},{7,3},{8,12},{9,13},{10,... | collective-permute-start | bytes 24584 | tf_op jit(solution)/shard_map/ppermute | solution.py:315
  53.6 0.5 collective-permute-start.18
  54.2 1.1 %collective-permute-done.20.refs_4_ = f32[1,2048]{1,0:T(1,128)S(1)} collective-permute-done((f32[1,2048]{1,0:T(1,128)S(1)}, f32[1,2048]{1,0:T(1,128)S(1)}, u32[]{:S(2)}, u32[]{:S(2)}) %collective-permute-start.20) | collective-permute-done | bytes 8224 | tf_op jit(solution)/shard_map/ppermute | solution.py:315
  55.3 1.0 %collective-permute-done.19.refs_3_ = f32[1,2048]{1,0:T(1,128)S(1)} collective-permute-done((f32[1,2048]{1,0:T(1,128)S(1)}, f32[1,2048]{1,0:T(1,128)S(1)}, u32[]{:S(2)}, u32[]{:S(2)}) %collective-permute-start.19) | collective-permute-done | bytes 8224 | tf_op jit(solution)/shard_map/ppermute | solution.py:315
  56.3 1.0 %collective-permute-done.18.refs_2_ = f32[1,2048]{1,0:T(1,128)S(1)} collective-permute-done((f32[1,2048]{1,0:T(1,128)S(1)}, f32[1,2048]{1,0:T(1,128)S(1)}, u32[]{:S(2)}, u32[]{:S(2)}) %collective-permute-start.18) | collective-permute-done | bytes 8224 | tf_op jit(solution)/shard_map/ppermute | solution.py:315
  57.3 3.8 %sweep.5 = (f32[2048,2048]{1,0:T(8,128)S(1)}, f32[1,2048]{1,0:T(1,128)S(1)}) custom-call(f32[2048,2048]{1,0:T(8,128)S(1)} %get-tuple-element.38.plan, f32[2,2048]{1,0:T(2,128)S(1)} %get-tuple-element.29.cols, f32[2,2048]{1,0:T(2,128)S(1)} %get-tuple-element.34.refs_0_.sums, f32[1,2048]{1,0:T(1,128)S(1)} %add.30.refs_1_, ...), custom_call_target="tpu_custom_call", output_to_operand_aliasing={{0}: (0, {})} | custom-call | tf_op jit(solution)/shard_map/sweep/pallas_call | solution.py:294
  61.1 0.1 collective-permute-start.21
  61.2 1.2 %collective-permute-done.21.right = f32[1,2048]{1,0:T(1,128)S(1)} collective-permute-done((f32[1,2048]{1,0:T(1,128)S(1)}, f32[1,2048]{1,0:T(1,128)S(1)}, u32[]{:S(2)}, u32[]{:S(2)}) %collective-permute-start.21) | collective-permute-done | bytes 8224 | tf_op jit(solution)/shard_map/ppermute | solution.py:28
  62.4 1.0 %collective-permute-start.24 = (f32[1,2048]{1,0:T(1,128)S(1)}, f32[1,2048]{1,0:T(1,128)S(1)}, u32[]{:S(2)}, u32[]{:S(2)}) collective-permute-start(f32[1,2048]{1,0:T(1,128)S(1)} %add.31.refs_0_), channel_id=1, source_target_pairs={{0,6},{1,7},{2,4},{3,5},{4,2},{5,3},{6,0},{7,1},{8,14},{9,15},{10,... | collective-permute-start | bytes 24584 | tf_op jit(solution)/shard_map/ppermute | solution.py:315
  63.4 1.0 %collective-permute-start.23 = (f32[1,2048]{1,0:T(1,128)S(1)}, f32[1,2048]{1,0:T(1,128)S(1)}, u32[]{:S(2)}, u32[]{:S(2)}) collective-permute-start(f32[1,2048]{1,0:T(1,128)S(1)} %add.31.refs_0_), channel_id=1, source_target_pairs={{0,4},{1,5},{2,6},{3,7},{4,0},{5,1},{6,2},{7,3},{8,12},{9,13},{10,... | collective-permute-start | bytes 24584 | tf_op jit(solution)/shard_map/ppermute | solution.py:315
  64.4 1.5 %collective-permute-start.22 = (f32[1,2048]{1,0:T(1,128)S(1)}, f32[1,2048]{1,0:T(1,128)S(1)}, u32[]{:S(2)}, u32[]{:S(2)}) collective-permute-start(f32[1,2048]{1,0:T(1,128)S(1)} %add.31.refs_0_), channel_id=1, source_target_pairs={{0,2},{1,3},{2,0},{3,1},{4,6},{5,7},{6,4},{7,5},{8,10},{9,11},{10,... | collective-permute-start | bytes 24584 | tf_op jit(solution)/shard_map/ppermute | solution.py:315
  65.8 1.1 %collective-permute-done.24.refs_3_ = f32[1,2048]{1,0:T(1,128)S(1)} collective-permute-done((f32[1,2048]{1,0:T(1,128)S(1)}, f32[1,2048]{1,0:T(1,128)S(1)}, u32[]{:S(2)}, u32[]{:S(2)}) %collective-permute-start.24) | collective-permute-done | bytes 8224 | tf_op jit(solution)/shard_map/ppermute | solution.py:315
  66.9 0.1 collective-permute-done.23.refs_2_
  67.0 1.0 %collective-permute-done.22.refs_1_ = f32[1,2048]{1,0:T(1,128)S(1)} collective-permute-done((f32[1,2048]{1,0:T(1,128)S(1)}, f32[1,2048]{1,0:T(1,128)S(1)}, u32[]{:S(2)}, u32[]{:S(2)}) %collective-permute-start.22) | collective-permute-done | bytes 8224 | tf_op jit(solution)/shard_map/ppermute | solution.py:315
  68.0 4.6 %embed_grad.1 = (f32[1,2048]{1,0:T(1,128)S(1)}, f32[1,2048]{1,0:T(1,128)S(1)}, f32[4,64,128]{2,1,0:T(8,128)S(1)}, f32[4,64,128]{2,1,0:T(8,128)S(1)}) custom-call(s32[2]{0:T(128)S(1)} %pad_add_fusion.ids, f32[2048,2048]{1,0:T(8,128)S(1)} %get-tuple-element.40.plan, f32[2,2048]{1,0:T(2,128)S(1)} %get-tuple-element.29.cols, ...), custom_call_target="tpu_custom_call" | custom-call | tf_op jit(solution)/shard_map/embed_grad/pallas_call | solution.py:294
  72.6 0.1 collective-permute-start.25
  72.7 1.3 %collective-permute-done.25.right = f32[4,64,128]{2,1,0:T(8,128)S(1)} collective-permute-done((f32[4,64,128]{2,1,0:T(8,128)S(1)}, f32[4,64,128]{2,1,0:T(8,128)S(1)}, u32[]{:S(2)}, u32[]{:S(2)}) %collective-permute-start.25) | collective-permute-done | bytes 131104 | tf_op jit(solution)/shard_map/ppermute | solution.py:28
  74.1 1.6 %collective-permute-start.26 = (f32[64,128]{1,0:T(8,128)S(1)}, f32[64,128]{1,0:T(8,128)S(1)}, u32[]{:S(2)}, u32[]{:S(2)}) collective-permute-start(f32[64,128]{1,0:T(8,128)S(1)} %get-tuple-element.50), channel_id=1, source_target_pairs={{0,2},{1,3},{2,0},{3,1},{4,6},{5,7},{6,4},{7,5},{8,10},{9,11},{10,... | collective-permute-start | bytes 98312 | tf_op jit(solution)/shard_map/ppermute | solution.py:315
  75.6 1.0 %collective-permute-start.28 = (f32[64,128]{1,0:T(8,128)S(1)}, f32[64,128]{1,0:T(8,128)S(1)}, u32[]{:S(2)}, u32[]{:S(2)}) collective-permute-start(f32[64,128]{1,0:T(8,128)S(1)} %get-tuple-element.51), channel_id=1, source_target_pairs={{0,6},{1,7},{2,4},{3,5},{4,2},{5,3},{6,0},{7,1},{8,14},{9,15},{10,... | collective-permute-start | bytes 98312 | tf_op jit(solution)/shard_map/ppermute | solution.py:315
  76.7 1.0 %collective-permute-start.27 = (f32[64,128]{1,0:T(8,128)S(1)}, f32[64,128]{1,0:T(8,128)S(1)}, u32[]{:S(2)}, u32[]{:S(2)}) collective-permute-start(f32[64,128]{1,0:T(8,128)S(1)} %get-tuple-element.52), channel_id=1, source_target_pairs={{0,4},{1,5},{2,6},{3,7},{4,0},{5,1},{6,2},{7,3},{8,12},{9,13},{10,... | collective-permute-start | bytes 98312 | tf_op jit(solution)/shard_map/ppermute | solution.py:315
  77.6 2.6 %proto_grad.1 = f32[512,128]{1,0:T(8,128)} custom-call(s32[2]{0:T(128)S(1)} %pad_add_fusion.ids, bf16[2048,256]{1,0:T(8,128)(2,1)S(1)} %get-tuple-element.26.protos, bf16[256,2048]{1,0:T(8,128)(2,1)S(1)} %get-tuple-element.31.emb_ext, bf16[128,2048]{1,0:T(8,128)(2,1)S(1)} %get-tuple-element.36.view_t, f32[512,2048]{1,0:T(8,128)S(1)} %get-tuple-element.46.entries, ...), custom_call_target="tpu_custom_call" | custom-call | tf_op jit(solution)/shard_map/proto_grad/pallas_call | solution.py:294
  80.2 0.3 collective-permute-done.28
  80.5 0.3 collective-permute-done.27
  80.8 0.6 fusion.2
  (14 shorter events, 0.1 us)
Async XLA Ops:
  1.7 7.9 %collective-permute-start.2 = (bf16[144,256]{1,0:T(8,128)(2,1)S(1)}, bf16[144,256]{1,0:T(8,128)(2,1)S(1)}, u32[]{:S(2)}, u32[]{:S(2)}) collective-permute-start(bf16[144,256]{1,0:T(8,128)(2,1)S(1)} %prepare.1.refs_0_), channel_id=1, source_target_pairs={{0,24},{4,28},{8,16},{12,20},{16,8},{20,12},{24,0},{28,4},{1,25},{... | collective-permute-start | bytes 221192 | tf_op jit(solution)/shard_map/ppermute | solution.py:28
  6.8 6.2 %collective-permute-start.1 = (bf16[144,256]{1,0:T(8,128)(2,1)S(1)}, bf16[144,256]{1,0:T(8,128)(2,1)S(1)}, u32[]{:S(2)}, u32[]{:S(2)}) collective-permute-start(bf16[144,256]{1,0:T(8,128)(2,1)S(1)} %prepare.1.refs_0_), channel_id=1, source_target_pairs={{0,16},{4,20},{8,24},{12,28},{16,0},{20,4},{24,8},{28,12},{1,17},{... | collective-permute-start | bytes 221192 | tf_op jit(solution)/shard_map/ppermute | solution.py:28
  6.8 7.7 %collective-permute-start = (bf16[144,256]{1,0:T(8,128)(2,1)S(1)}, bf16[144,256]{1,0:T(8,128)(2,1)S(1)}, u32[]{:S(2)}, u32[]{:S(2)}) collective-permute-start(bf16[144,256]{1,0:T(8,128)(2,1)S(1)} %prepare.1.refs_0_), channel_id=1, source_target_pairs={{0,8},{4,12},{8,0},{12,4},{16,24},{20,28},{24,16},{28,20},{1,9},{5... | collective-permute-start | bytes 221192 | tf_op jit(solution)/shard_map/ppermute | solution.py:28
  7.5 9.7 %collective-permute-start.4 = (bf16[144,256]{1,0:T(8,128)(2,1)S(1)}, bf16[144,256]{1,0:T(8,128)(2,1)S(1)}, u32[]{:S(2)}, u32[]{:S(2)}) collective-permute-start(bf16[144,256]{1,0:T(8,128)(2,1)S(1)} %prepare.1.refs_0_), channel_id=1, source_target_pairs={{0,4},{4,0},{8,12},{12,8},{16,20},{20,16},{24,28},{28,24},{1,5},{5... | collective-permute-start | bytes 221192 | tf_op jit(solution)/shard_map/ppermute | solution.py:28
  9.6 7.6 %collective-permute-start.7 = (bf16[144,256]{1,0:T(8,128)(2,1)S(1)}, bf16[144,256]{1,0:T(8,128)(2,1)S(1)}, u32[]{:S(2)}, u32[]{:S(2)}) collective-permute-start(bf16[144,256]{1,0:T(8,128)(2,1)S(1)} %collective-permute-done.2.refs_3_), channel_id=1, source_target_pairs={{0,4},{4,0},{8,12},{12,8},{16,20},{20,16},{24,28},{28,24},{1,5},{5... | collective-permute-start | bytes 221192 | tf_op jit(solution)/shard_map/ppermute | solution.py:28
  13.0 5.1 %collective-permute-start.6 = (bf16[144,256]{1,0:T(8,128)(2,1)S(1)}, bf16[144,256]{1,0:T(8,128)(2,1)S(1)}, u32[]{:S(2)}, u32[]{:S(2)}) collective-permute-start(bf16[144,256]{1,0:T(8,128)(2,1)S(1)} %collective-permute-done.1.refs_2_), channel_id=1, source_target_pairs={{0,4},{4,0},{8,12},{12,8},{16,20},{20,16},{24,28},{28,24},{1,5},{5... | collective-permute-start | bytes 221192 | tf_op jit(solution)/shard_map/ppermute | solution.py:28
  14.6 4.4 %collective-permute-start.5 = (bf16[144,256]{1,0:T(8,128)(2,1)S(1)}, bf16[144,256]{1,0:T(8,128)(2,1)S(1)}, u32[]{:S(2)}, u32[]{:S(2)}) collective-permute-start(bf16[144,256]{1,0:T(8,128)(2,1)S(1)} %collective-permute-done.refs_1_), channel_id=1, source_target_pairs={{0,4},{4,0},{8,12},{12,8},{16,20},{20,16},{24,28},{28,24},{1,5},{5... | collective-permute-start | bytes 221192 | tf_op jit(solution)/shard_map/ppermute | solution.py:28
  17.1 2.0 %collective-permute-start.3 = (bf16[4,144,256]{2,1,0:T(8,128)(2,1)S(1)}, bf16[4,144,256]{2,1,0:T(8,128)(2,1)S(1)}, u32[]{:S(2)}, u32[]{:S(2)}) collective-permute-start(bf16[4,144,256]{2,1,0:T(8,128)(2,1)S(1)} %stack.14.mine_a), channel_id=1, source_target_pairs={{0,1},{1,0},{2,3},{3,2},{4,5},{5,4},{6,7},{7,6},{8,9},{9,8},{10,11... | collective-permute-start | bytes 884744 | tf_op jit(solution)/shard_map/ppermute | solution.py:28
  18.9 1.6 %collective-permute-start.8 = (bf16[4,144,256]{2,1,0:T(8,128)(2,1)S(1)}, bf16[4,144,256]{2,1,0:T(8,128)(2,1)S(1)}, u32[]{:S(2)}, u32[]{:S(2)}) collective-permute-start(bf16[4,144,256]{2,1,0:T(8,128)(2,1)S(1)} %stack.15.mine_b), channel_id=1, source_target_pairs={{0,1},{1,0},{2,3},{3,2},{4,5},{5,4},{6,7},{7,6},{8,9},{9,8},{10,11... | collective-permute-start | bytes 884744 | tf_op jit(solution)/shard_map/ppermute | solution.py:28
  26.9 1.2 %collective-permute-start.9 = (f32[2,2048]{1,0:T(2,128)S(1)}, f32[2,2048]{1,0:T(2,128)S(1)}, u32[]{:S(2)}, u32[]{:S(2)}) collective-permute-start(f32[2,2048]{1,0:T(2,128)S(1)} %get-tuple-element.30.left), channel_id=1, source_target_pairs={{0,1},{1,0},{2,3},{3,2},{4,5},{5,4},{6,7},{7,6},{8,9},{9,8},{10,11... | collective-permute-start | bytes 49160 | tf_op jit(solution)/shard_map/ppermute | solution.py:28
  28.2 5.4 %collective-permute-start.12 = (f32[2,2048]{1,0:T(2,128)S(1)}, f32[2,2048]{1,0:T(2,128)S(1)}, u32[]{:S(2)}, u32[]{:S(2)}) collective-permute-start(f32[2,2048]{1,0:T(2,128)S(1)} %add.28.after.refs_0_), channel_id=1, source_target_pairs={{0,6},{1,7},{2,4},{3,5},{4,2},{5,3},{6,0},{7,1},{8,14},{9,15},{10,... | collective-permute-start | bytes 49160 | tf_op jit(solution)/shard_map/ppermute | solution.py:315
  30.2 3.7 %collective-permute-start.11 = (f32[2,2048]{1,0:T(2,128)S(1)}, f32[2,2048]{1,0:T(2,128)S(1)}, u32[]{:S(2)}, u32[]{:S(2)}) collective-permute-start(f32[2,2048]{1,0:T(2,128)S(1)} %add.28.after.refs_0_), channel_id=1, source_target_pairs={{0,4},{1,5},{2,6},{3,7},{4,0},{5,1},{6,2},{7,3},{8,12},{9,13},{10,... | collective-permute-start | bytes 49160 | tf_op jit(solution)/shard_map/ppermute | solution.py:315
  31.2 3.7 %collective-permute-start.10 = (f32[2,2048]{1,0:T(2,128)S(1)}, f32[2,2048]{1,0:T(2,128)S(1)}, u32[]{:S(2)}, u32[]{:S(2)}) collective-permute-start(f32[2,2048]{1,0:T(2,128)S(1)} %add.28.after.refs_0_), channel_id=1, source_target_pairs={{0,2},{1,3},{2,0},{3,1},{4,6},{5,7},{6,4},{7,5},{8,10},{9,11},{10,... | collective-permute-start | bytes 49160 | tf_op jit(solution)/shard_map/ppermute | solution.py:315
  38.7 1.2 %collective-permute-start.13 = (f32[1,2048]{1,0:T(1,128)S(1)}, f32[1,2048]{1,0:T(1,128)S(1)}, u32[]{:S(2)}, u32[]{:S(2)}) collective-permute-start(f32[1,2048]{1,0:T(1,128)S(1)} %get-tuple-element.35.left), channel_id=1, source_target_pairs={{0,1},{1,0},{2,3},{3,2},{4,5},{5,4},{6,7},{7,6},{8,9},{9,8},{10,11... | collective-permute-start | bytes 24584 | tf_op jit(solution)/shard_map/ppermute | solution.py:28
  40.0 5.5 %collective-permute-start.16 = (f32[1,2048]{1,0:T(1,128)S(1)}, f32[1,2048]{1,0:T(1,128)S(1)}, u32[]{:S(2)}, u32[]{:S(2)}) collective-permute-start(f32[1,2048]{1,0:T(1,128)S(1)} %add.29.after.refs_1_), channel_id=1, source_target_pairs={{0,6},{1,7},{2,4},{3,5},{4,2},{5,3},{6,0},{7,1},{8,14},{9,15},{10,... | collective-permute-start | bytes 24584 | tf_op jit(solution)/shard_map/ppermute | solution.py:315
  41.0 4.5 %collective-permute-start.15 = (f32[1,2048]{1,0:T(1,128)S(1)}, f32[1,2048]{1,0:T(1,128)S(1)}, u32[]{:S(2)}, u32[]{:S(2)}) collective-permute-start(f32[1,2048]{1,0:T(1,128)S(1)} %add.29.after.refs_1_), channel_id=1, source_target_pairs={{0,4},{1,5},{2,6},{3,7},{4,0},{5,1},{6,2},{7,3},{8,12},{9,13},{10,... | collective-permute-start | bytes 24584 | tf_op jit(solution)/shard_map/ppermute | solution.py:315
  42.0 3.7 %collective-permute-start.14 = (f32[1,2048]{1,0:T(1,128)S(1)}, f32[1,2048]{1,0:T(1,128)S(1)}, u32[]{:S(2)}, u32[]{:S(2)}) collective-permute-start(f32[1,2048]{1,0:T(1,128)S(1)} %add.29.after.refs_1_), channel_id=1, source_target_pairs={{0,2},{1,3},{2,0},{3,1},{4,6},{5,7},{6,4},{7,5},{8,10},{9,11},{10,... | collective-permute-start | bytes 24584 | tf_op jit(solution)/shard_map/ppermute | solution.py:315
  49.4 1.2 %collective-permute-start.17 = (f32[1,2048]{1,0:T(1,128)S(1)}, f32[1,2048]{1,0:T(1,128)S(1)}, u32[]{:S(2)}, u32[]{:S(2)}) collective-permute-start(f32[1,2048]{1,0:T(1,128)S(1)} %get-tuple-element.39.left), channel_id=1, source_target_pairs={{0,1},{1,0},{2,3},{3,2},{4,5},{5,4},{6,7},{7,6},{8,9},{9,8},{10,11... | collective-permute-start | bytes 24584 | tf_op jit(solution)/shard_map/ppermute | solution.py:28
  50.7 4.6 %collective-permute-start.20 = (f32[1,2048]{1,0:T(1,128)S(1)}, f32[1,2048]{1,0:T(1,128)S(1)}, u32[]{:S(2)}, u32[]{:S(2)}) collective-permute-start(f32[1,2048]{1,0:T(1,128)S(1)} %add.30.refs_1_), channel_id=1, source_target_pairs={{0,6},{1,7},{2,4},{3,5},{4,2},{5,3},{6,0},{7,1},{8,14},{9,15},{10,... | collective-permute-start | bytes 24584 | tf_op jit(solution)/shard_map/ppermute | solution.py:315
  52.7 3.7 %collective-permute-start.19 = (f32[1,2048]{1,0:T(1,128)S(1)}, f32[1,2048]{1,0:T(1,128)S(1)}, u32[]{:S(2)}, u32[]{:S(2)}) collective-permute-start(f32[1,2048]{1,0:T(1,128)S(1)} %add.30.refs_1_), channel_id=1, source_target_pairs={{0,4},{1,5},{2,6},{3,7},{4,0},{5,1},{6,2},{7,3},{8,12},{9,13},{10,... | collective-permute-start | bytes 24584 | tf_op jit(solution)/shard_map/ppermute | solution.py:315
  53.6 3.7 %collective-permute-start.18 = (f32[1,2048]{1,0:T(1,128)S(1)}, f32[1,2048]{1,0:T(1,128)S(1)}, u32[]{:S(2)}, u32[]{:S(2)}) collective-permute-start(f32[1,2048]{1,0:T(1,128)S(1)} %add.30.refs_1_), channel_id=1, source_target_pairs={{0,2},{1,3},{2,0},{3,1},{4,6},{5,7},{6,4},{7,5},{8,10},{9,11},{10,... | collective-permute-start | bytes 24584 | tf_op jit(solution)/shard_map/ppermute | solution.py:315
  61.1 1.2 %collective-permute-start.21 = (f32[1,2048]{1,0:T(1,128)S(1)}, f32[1,2048]{1,0:T(1,128)S(1)}, u32[]{:S(2)}, u32[]{:S(2)}) collective-permute-start(f32[1,2048]{1,0:T(1,128)S(1)} %get-tuple-element.43.left), channel_id=1, source_target_pairs={{0,1},{1,0},{2,3},{3,2},{4,5},{5,4},{6,7},{7,6},{8,9},{9,8},{10,11... | collective-permute-start | bytes 24584 | tf_op jit(solution)/shard_map/ppermute | solution.py:28
  62.4 4.5 %collective-permute-start.24 = (f32[1,2048]{1,0:T(1,128)S(1)}, f32[1,2048]{1,0:T(1,128)S(1)}, u32[]{:S(2)}, u32[]{:S(2)}) collective-permute-start(f32[1,2048]{1,0:T(1,128)S(1)} %add.31.refs_0_), channel_id=1, source_target_pairs={{0,6},{1,7},{2,4},{3,5},{4,2},{5,3},{6,0},{7,1},{8,14},{9,15},{10,... | collective-permute-start | bytes 24584 | tf_op jit(solution)/shard_map/ppermute | solution.py:315
  63.4 3.7 %collective-permute-start.23 = (f32[1,2048]{1,0:T(1,128)S(1)}, f32[1,2048]{1,0:T(1,128)S(1)}, u32[]{:S(2)}, u32[]{:S(2)}) collective-permute-start(f32[1,2048]{1,0:T(1,128)S(1)} %add.31.refs_0_), channel_id=1, source_target_pairs={{0,4},{1,5},{2,6},{3,7},{4,0},{5,1},{6,2},{7,3},{8,12},{9,13},{10,... | collective-permute-start | bytes 24584 | tf_op jit(solution)/shard_map/ppermute | solution.py:315
  64.4 3.7 %collective-permute-start.22 = (f32[1,2048]{1,0:T(1,128)S(1)}, f32[1,2048]{1,0:T(1,128)S(1)}, u32[]{:S(2)}, u32[]{:S(2)}) collective-permute-start(f32[1,2048]{1,0:T(1,128)S(1)} %add.31.refs_0_), channel_id=1, source_target_pairs={{0,2},{1,3},{2,0},{3,1},{4,6},{5,7},{6,4},{7,5},{8,10},{9,11},{10,... | collective-permute-start | bytes 24584 | tf_op jit(solution)/shard_map/ppermute | solution.py:315
  72.6 1.4 %collective-permute-start.25 = (f32[4,64,128]{2,1,0:T(8,128)S(1)}, f32[4,64,128]{2,1,0:T(8,128)S(1)}, u32[]{:S(2)}, u32[]{:S(2)}) collective-permute-start(f32[4,64,128]{2,1,0:T(8,128)S(1)} %get-tuple-element.45), channel_id=1, source_target_pairs={{0,1},{1,0},{2,3},{3,2},{4,5},{5,4},{6,7},{7,6},{8,9},{9,8},{10,11... | collective-permute-start | bytes 393224 | tf_op jit(solution)/shard_map/ppermute | solution.py:28
  74.1 6.2 %collective-permute-start.26 = (f32[64,128]{1,0:T(8,128)S(1)}, f32[64,128]{1,0:T(8,128)S(1)}, u32[]{:S(2)}, u32[]{:S(2)}) collective-permute-start(f32[64,128]{1,0:T(8,128)S(1)} %get-tuple-element.50), channel_id=1, source_target_pairs={{0,2},{1,3},{2,0},{3,1},{4,6},{5,7},{6,4},{7,5},{8,10},{9,11},{10,... | collective-permute-start | bytes 98312 | tf_op jit(solution)/shard_map/ppermute | solution.py:315
  75.6 4.8 %collective-permute-start.28 = (f32[64,128]{1,0:T(8,128)S(1)}, f32[64,128]{1,0:T(8,128)S(1)}, u32[]{:S(2)}, u32[]{:S(2)}) collective-permute-start(f32[64,128]{1,0:T(8,128)S(1)} %get-tuple-element.51), channel_id=1, source_target_pairs={{0,6},{1,7},{2,4},{3,5},{4,2},{5,3},{6,0},{7,1},{8,14},{9,15},{10,... | collective-permute-start | bytes 98312 | tf_op jit(solution)/shard_map/ppermute | solution.py:315
  76.7 4.1 %collective-permute-start.27 = (f32[64,128]{1,0:T(8,128)S(1)}, f32[64,128]{1,0:T(8,128)S(1)}, u32[]{:S(2)}, u32[]{:S(2)}) collective-permute-start(f32[64,128]{1,0:T(8,128)S(1)} %get-tuple-element.52), channel_id=1, source_target_pairs={{0,4},{1,5},{2,6},{3,7},{4,0},{5,1},{6,2},{7,3},{8,12},{9,13},{10,... | collective-permute-start | bytes 98312 | tf_op jit(solution)/shard_map/ppermute | solution.py:315

commit v3 on v2

--- a/solution.py
+++ b/solution.py
@@ -64,7 +64,7 @@
         send_out[width:width + EXT, :] = jnp.zeros((EXT, rows), BF16)
 
 
-def turn_kernel(logit_scale, log_mass, ids, protos, col_scale, protos_out, protos_t, token):
+def extend_kernel(logit_scale, log_mass, ids, protos, col_scale, protos_out, token):
     count = protos_out.shape[0]
     width = protos.shape[1]
     token[...] = jnp.zeros_like(token)
@@ -76,7 +76,6 @@
         logs, ones = pieces_of((jnp.log(col_scale[:, there]) - log_mass) / logit_scale)
         protos_out[here, 0:width] = block
         protos_out[here, width:] = jnp.transpose(rows_of(ones + logs, width)).astype(BF16)
-        protos_t[:, here] = jnp.transpose(block.astype(F32)).astype(BF16)
         return carry
 
     lax.fori_loop(0, count // CHUNK, step, 0)
@@ -91,26 +90,25 @@
     out[...] = left[...] + right[...]
 
 
-def plan_kernel(logit_scale, view_scale, ids, protos, mine_a, theirs_a, mine_b, theirs_b, plan_out, cols_out, sums_out, emb_ext, view_t, row_mass, row_weight):
-    pairs, high, rows = mine_a.shape
-    blocks = 2 * pairs
+def plan_kernel(logit_scale, view_scale, second, ids, protos, mine, theirs, *refs):
+    if second:
+        _, cols_in, sums_in, *refs = refs
+    plan_out, cols_out, sums_out, emb_ext, view_t, row_mass, row_weight = refs
+    blocks, high, rows = mine.shape
     count = protos.shape[0]
     width = view_t.shape[0]
     scale = logit_scale * LOG2E
+    first_col = blocks * rows if second else 0
     emb_ext[high:, :] = jnp.zeros((emb_ext.shape[0] - high, blocks * rows), BF16)
 
-    def fill(embs, views):
+    def fill(emb, view):
         for block in range(blocks):
             cols = slice(block * rows, (block + 1) * rows)
-            emb_ext[0:high, cols] = embs[block % 2][block // 2]
-            view_t[:, cols] = views[block % 2][block // 2, 0:width, :]
-
-    for core in range(2):
-        for odd in range(2):
-            a, b = ((mine_a, theirs_a), (mine_b, theirs_b)) if core == 0 else ((theirs_a, mine_a), (theirs_b, mine_b))
-            low, upper = (a, b) if odd == 0 else (b, a)
-            is_this = jnp.logical_and(ids[1] & 1 == core, ids[0] & 1 == odd)
-            pl.when(is_this)(functools.partial(fill, (low[0], upper[0]), (low[1], upper[1])))
+            emb_ext[0:high, cols] = emb[block]
+            view_t[:, cols] = view[block, 0:width, :]
+
+    pl.when(ids[1] & 1 == 0)(lambda: fill(mine, theirs))
+    pl.when(ids[1] & 1 != 0)(lambda: fill(theirs, mine))
     row_mass[...] = jnp.zeros_like(row_mass)
     row_weight[...] = jnp.zeros_like(row_weight)
 
@@ -127,20 +125,31 @@
         for block in range(blocks):
             cols = slice(block * rows, (block + 1) * rows)
             plan = jnp.exp2(scale * mm(protos[here, :], emb_ext[:, cols]))
-            plan_out[here, cols] = plan
+            plan_out[here, first_col + block * rows:first_col + (block + 1) * rows] = plan
             across, down = folded(plan)
             mass = mass + across
             row_mass[:, cols] += down
             across, down = folded(plan * mm(protos[here, 0:width], view_t[:, cols]))
             weight = weight + across
             row_weight[:, cols] += down
-        cols_out[0:1, here] = jnp.sum(jnp.transpose(mass), axis=0, keepdims=True)
-        cols_out[1:2, here] = -view_scale * jnp.sum(jnp.transpose(weight), axis=0, keepdims=True)
+        mass = jnp.sum(jnp.transpose(mass), axis=0, keepdims=True)
+        weight = -view_scale * jnp.sum(jnp.transpose(weight), axis=0, keepdims=True)
+        cols_out[0:1, here] = mass + cols_in[0:1, here] if second else mass
+        cols_out[1:2, here] = weight + cols_in[1:2, here] if second else weight
         return carry
 
     lax.fori_loop(0, count // CHUNK, step, 0)
-    sums_out[0:1, :] = jnp.sum(row_mass[...], axis=0, keepdims=True)
-    sums_out[1:2, :] = -view_scale * jnp.sum(row_weight[...], axis=0, keepdims=True)
+    if second:
+        sums_out[:, 0:first_col] = sums_in[...]
+    sums_out[0:1, first_col:] = jnp.sum(row_mass[...], axis=0, keepdims=True)
+    sums_out[1:2, first_col:] = -view_scale * jnp.sum(row_weight[...], axis=0, keepdims=True)
+
+
+def received_kernel(plain, turned, *refs):
+    out = refs[-1]
+    half = out.shape[1] // 2
+    other = added(refs[plain:plain + turned])
+    out[...] = added(refs[:plain]) + jnp.concatenate((other[:, half:], other[:, :half]), 1)
 
 
 def added(parts):
@@ -178,13 +187,13 @@
     return pl.ds(pl.multiple_of(index * STEP, STEP), STEP)
 
 
-def sweep_kernel(opening, shares, plan, cols, *refs):
+def sweep_kernel(opening, terms, plan, cols, *refs):
     if opening:
-        parts, (_, _, sums_out, part_out, spread, total) = refs[:shares], refs[shares:]
+        parts, (_, sums_out, part_out, spread, total) = refs[:terms], refs[terms:]
         sums_out[...] = added(parts)
         row_dual = sums_out[1:2, :] / sums_out[0:1, :]
     else:
-        (sums, *parts), (_, _, part_out, spread, total) = refs[:shares + 1], refs[shares + 1:]
+        (sums, *parts), (_, part_out, spread, total) = refs[:terms + 1], refs[terms + 1:]
         row_dual = (sums[1:2, :] - added(parts)) / sums[0:1, :]
     spread[...] = jnp.broadcast_to(row_dual, spread.shape)
     total[...] = jnp.zeros_like(total)
@@ -206,26 +215,32 @@
     part_out[...] = jnp.sum(total[...], axis=0, keepdims=True)
 
 
-def embed_before_kernel(logit_scale, protos, emb_ext, after, entry_out, token):
+def embed_before_kernel(logit_scale, protos, emb_a, emb_b, after, entry_out, protos_t, token):
     del after
     scale = logit_scale * LOG2E
+    rows = entry_out.shape[1] // 2
     token[...] = jnp.zeros_like(token)
 
     def step(index, carry):
         here = chunk(index)
-        entry_out[here, :] = logit_scale * jnp.exp2(scale * mm(protos[here, :], emb_ext[:, 0:entry_out.shape[1]]))
+        for half, emb in enumerate((emb_a, emb_b)):
+            entry = jnp.exp2(scale * mm(protos[here, :], emb[:, 0:rows]))
+            entry_out[here, half * rows:(half + 1) * rows] = logit_scale * entry
+        protos_t[:, here] = jnp.transpose(protos[here, 0:protos_t.shape[0]].astype(F32)).astype(BF16)
         return carry
 
     lax.fori_loop(0, protos.shape[0] // STEP, step, 0)
 
 
-def embed_kernel(view_scale, shares, ids, plan, cols, sums, protos, protos_t, view_t, entries, *refs):
-    parts, (duals_out, rows_out, keep, give, spread, total, whole) = refs[:shares], refs[shares:]
+def embed_kernel(view_scale, shares, terms, ids, plan, cols, sums, protos, protos_t, view_a, view_b, entries, *refs):
+    parts, (duals_out, rows_out, keep, give, spread, total, whole) = refs[:terms], refs[terms:]
     width = protos_t.shape[0]
     rows = entries.shape[1]
     rows_out[...] = (sums[1:2, :] - added(parts)) / sums[0:1, :]
     spread[...] = jnp.broadcast_to(rows_out[...], spread.shape)
-    own_dual = rows_out[:, 0:rows]
+    half = rows // 2
+    split = rows_out.shape[1] // 2
+    own_dual = jnp.concatenate((rows_out[:, 0:half], rows_out[:, split:split + half]), 1)
     total[...] = jnp.zeros_like(total)
     steps = plan.shape[0] // STEP
 
@@ -235,7 +250,8 @@
 
     def gradient(index, dual):
         here = chunk(index)
-        cot = -view_scale * mm(protos[here, 0:width], view_t[:, 0:rows])
+        block = protos[here, 0:width]
+        cot = -view_scale * jnp.concatenate([mm(block, view[:, 0:half]) for view in (view_a, view_b)], 1)
         grad = entries[here, :] * (cot - own_dual - as_column(dual, rows))
         return mm(protos_t[:, here], grad.astype(BF16))
 
@@ -253,12 +269,12 @@
     tall = keep.shape[1]
     for place in range(shares):
         above, beside = divmod(place, shares // 2)
-        to = ((ids[0] & 1) ^ above) * shares + (ids[1] ^ (2 * beside))
+        to = above * shares + (ids[1] ^ (2 * beside))
         keep[place] = whole[pl.ds(pl.multiple_of(to * tall, tall), tall), :]
         give[place] = whole[pl.ds(pl.multiple_of((to ^ 1) * tall, tall), tall), :]
 
 
-def proto_before_kernel(logit_scale, view_scale, ids, protos, emb_ext, view_t, after, entry_out, second_out, token):
+def proto_before_kernel(logit_scale, view_scale, ids, protos, emb_a, emb_b, view_a, view_b, after, entry_out, second_out, token):
     del after
     own, rows = entry_out.shape
     width = second_out.shape[1]
@@ -266,24 +282,28 @@
     token[...] = jnp.zeros_like(token)
     here = pl.ds(pl.multiple_of((ids[0] >> 1) * own, own), own)
     total = jnp.zeros((own, width), F32)
-    for start in range(0, rows, 2 * width):
-        cols = slice(start, start + 2 * width)
-        exact = jnp.exp2(scale * mm(protos[here, :], emb_ext[:, cols]))
-        entry_out[:, cols] = logit_scale * exact
-        total = total + mm((-view_scale * exact).astype(BF16), view_t[:, cols], NT)
+    for first_col, emb, view in ((0, emb_a, view_a), (rows // 2, emb_b, view_b)):
+        for start in range(0, rows // 2, 2 * width):
+            cols = slice(start, start + 2 * width)
+            exact = jnp.exp2(scale * mm(protos[here, :], emb[:, cols]))
+            entry_out[:, first_col + start:first_col + start + 2 * width] = logit_scale * exact
+            total = total + mm((-view_scale * exact).astype(BF16), view[:, cols], NT)
     second_out[...] = total
 
 
-def proto_kernel(view_scale, ids, protos, emb_ext, view_t, entries, second, col_dual, row_dual, out):
+def proto_kernel(view_scale, ids, protos, emb_a, emb_b, view_a, view_b, entries, second, col_dual, row_dual, out):
     own, width = out.shape
     here = pl.ds(pl.multiple_of((ids[0] >> 1) * own, own), own)
     column = as_column(col_dual[:, here], 2 * width)
     total = second[...]
-    for start in range(0, entries.shape[1], 2 * width):
-        cols = slice(start, start + 2 * width)
-        cot = -view_scale * mm(protos[here, 0:width], view_t[:, cols])
-        grad = entries[:, cols] * (cot - row_dual[:, cols] - column)
-        total = total + mm(grad.astype(BF16), emb_ext[0:width, cols], NT)
+    split = entries.shape[1] // 2
+    for first_col, emb, view in ((0, emb_a, view_a), (split, emb_b, view_b)):
+        for start in range(0, split, 2 * width):
+            cols = slice(start, start + 2 * width)
+            both = slice(first_col + start, first_col + start + 2 * width)
+            cot = -view_scale * mm(protos[here, 0:width], view[:, cols])
+            grad = entries[:, both] * (cot - row_dual[:, both] - column)
+            total = total + mm(grad.astype(BF16), emb[0:width, cols], NT)
     out[...] = total
 
 
@@ -305,12 +325,13 @@
     return run
 
 
-def swap_both(value, above, beside):
+def swap_both(value, above, beside, cores=(0, 1)):
     shares = lax.axis_size("proto")
     pairs = [
         (row * shares + col, (row ^ above) * shares + (col ^ beside))
         for row in range(lax.axis_size("row"))
         for col in range(shares)
+        if col % 2 in cores
     ]
     return lax.ppermute(value, ("row", "proto"), pairs)
 
@@ -320,9 +341,16 @@
     return [(above, beside) for above in range(2) for beside in range(0, shares, 2)]
 
 
-def exchange(part):
-    near = call(add_kernel, jax.ShapeDtypeStruct(part.shape, F32), "add", limit=2)(part, swap(part, "proto", 1))
-    return [near if pair == (0, 0) else swap_both(near, *pair) for pair in others()]
+def exchange(part, work=None):
+    shape = jax.ShapeDtypeStruct(part.shape, F32)
+    near = call(add_kernel, shape, "add", limit=2)(part, swap(part, "proto", 1))
+    plain = [pair for pair in others() if pair[0] == 0 and pair != (0, 0)]
+    turned = [pair for pair in others() if pair[0] == 1]
+    got = [swap_both(near, *pair, cores=(0,)) for pair in plain] + [swap_both(near, *pair, cores=(1,)) for pair in turned]
+    made = work(near) if work else ()
+    kernel = functools.partial(received_kernel, len(plain), len(turned))
+    got = call(kernel, shape, "received", limit=2)(*got, *made[-1:])
+    return [near, got, swap(got, "proto", 1)], made[:-1]
 
 
 def kept_plan(embeddings, second_view, prototypes, row_scale, col_scale):
@@ -343,81 +371,95 @@
     send = call(functools.partial(prep_kernel, scales[0]), half, "prepare", scalars=1)(
         ids, there(embeddings), there(second_view), there(row_scale)
     )
-    protos, protos_t, token = call(
-        functools.partial(turn_kernel, scales[0], log_mass),
-        (shape(count, 2 * width, dtype=BF16), shape(width, count, dtype=BF16), shape(8, 128)),
-        "turn",
+    protos, token = call(
+        functools.partial(extend_kernel, scales[0], log_mass),
+        (shape(count, 2 * width, dtype=BF16), shape(8, 128)),
+        "extend",
         scalars=1,
         limit=4,
     )(ids, there(prototypes), there(col_scale))
     pairs = blocks // 2
     stack = call(functools.partial(stack_kernel, pairs), shape(pairs, width + EXT, rows, dtype=BF16), "stack", limit=2)
     direct = [send] + [swap(send, "row", step) for step in range(2, blocks, 2)]
-    mine_a = stack(*direct)
+    mine_a = stack(*direct, token)
     theirs_a = swap(mine_a, "proto", 1)
-    mine_b = stack(*[swap(value, "row", 1) for value in direct], token)
+    mine_b = stack(*[swap(value, "row", 1) for value in direct])
     theirs_b = swap(mine_b, "proto", 1)
 
     kept = pltpu.VMEM((count, all_rows), F32)
-    plan, cols, sums, emb_ext, view_t = call(
-        form(plan_kernel),
-        (kept, shape(2, count), shape(2, all_rows), shape(2 * width, all_rows, dtype=BF16), shape(width, all_rows, dtype=BF16)),
-        "plan",
+    some = all_rows // 2
+    turned = (shape(2 * width, some, dtype=BF16), shape(width, some, dtype=BF16))
+    work = [(F32, 8, some), (F32, 8, some)]
+    plan, cols, sums, emb_a, view_a = call(
+        functools.partial(plan_kernel, *scales, False),
+        (kept, shape(2, count), shape(2, some)) + turned,
+        "plan_ours",
         scalars=1,
-        scratch=[(F32, 8, all_rows), (F32, 8, all_rows)],
+        scratch=work,
         limit=12,
-    )(ids, protos, mine_a, theirs_a, mine_b, theirs_b)
-
-    work = [(F32, 8, all_rows), (F32, 8, all_rows)]
+    )(ids, protos, mine_a, theirs_a)
+    plan, cols, sums, emb_b, view_b = call(
+        functools.partial(plan_kernel, *scales, True),
+        (kept, shape(2, count), shape(2, all_rows)) + turned,
+        "plan_theirs",
+        scalars=1,
+        scratch=work,
+        aliases={4: 0},
+        limit=12,
+    )(ids, protos, mine_b, theirs_b, plan, cols, sums)
+
     token = shape(8, 128)
-    parts = exchange(sums)
-    entries, done = call(
+    embed_before = call(
         functools.partial(embed_before_kernel, scales[0]),
-        (shape(count, 2 * rows), token),
+        (shape(count, 2 * rows), shape(width, count, dtype=BF16), token),
         "embed_before",
         limit=6,
-    )(protos, emb_ext, parts[0])
+    )
+    proto_before = call(
+        form(proto_before_kernel),
+        (shape(own, all_rows), shape(own, width), token),
+        "proto_before",
+        scalars=1,
+        limit=6,
+    )
+    work = [(F32, 8, all_rows), (F32, 8, all_rows)]
+    parts, (entries, protos_t) = exchange(sums, lambda near: embed_before(protos, emb_a, emb_b, near))
     plan, sums, part = call(
-        functools.partial(sweep_kernel, True, shares),
+        functools.partial(sweep_kernel, True, len(parts)),
         (kept, shape(2, all_rows), shape(1, all_rows)),
         "sweep",
         scratch=work,
         aliases={0: 0},
         limit=4,
-    )(plan, cols, *parts, done)
+    )(plan, cols, *parts)
+    parts, (own_entries, second) = exchange(
+        part, lambda near: proto_before(ids, protos, emb_a, emb_b, view_a, view_b, near)
+    )
     for sweep in range(ITERS - 2):
-        parts = exchange(part)
-        if sweep == 0:
-            own_entries, second, done = call(
-                form(proto_before_kernel),
-                (shape(own, all_rows), shape(own, width), token),
-                "proto_before",
-                scalars=1,
-                limit=6,
-            )(ids, protos, emb_ext, view_t, parts[0])
         plan, part = call(
-            functools.partial(sweep_kernel, False, shares),
+            functools.partial(sweep_kernel, False, len(parts)),
             (kept, shape(1, all_rows)),
             "sweep",
             scratch=work,
             aliases={0: 0},
             limit=4,
-        )(plan, cols, sums, *parts, done)
+        )(plan, cols, sums, *parts)
+        parts, _ = exchange(part)
     pieces = shape(shares, rows // shares, width)
     col_dual, row_dual, keep, give = call(
-        functools.partial(embed_kernel, scales[1], shares),
+        functools.partial(embed_kernel, scales[1], shares, len(parts)),
         (shape(1, count), shape(1, all_rows), pieces, pieces),
         "embed_grad",
         scalars=1,
         scratch=work[:1] + [(F32, width, 2 * rows), (F32, 2 * rows, width)],
         limit=6,
-    )(ids, plan, cols, sums, protos, protos_t, view_t, entries, *exchange(part))
+    )(ids, plan, cols, sums, protos, protos_t, view_a, view_b, entries, *parts)
     near = call(add_kernel, pieces, "add", limit=2)(keep, swap(give, "proto", 1))
     embed_grad = near[0]
     for place, pair in list(enumerate(others()))[1:]:
         embed_grad = embed_grad + swap_both(near[place], *pair)
     proto_grad = call(functools.partial(proto_kernel, scales[1]), shape(own, width), "proto_grad", scalars=1, limit=6)(
-        ids, protos, emb_ext, view_t, own_entries, second, col_dual, row_dual
+        ids, protos, emb_a, emb_b, view_a, view_b, own_entries, second, col_dual, row_dual
     )
     return embed_grad, proto_grad
 

time: 81.6 us -> 94.5 us (1.16)
  starting transfers between devices: 29.5 us -> 40.1 us
  Pallas kernels: 32 us -> 33.9 us
    ppermute x14 -> x18, starting transfers between devices: 12 us -> 19.6 us  [swap(): return lax.ppermute(value, axis, [(i, i ^ step) for i in range(size)])]
    ppermute x15, starting transfers between devices: 17.5 us -> 20.5 us  [swap_both(): return lax.ppermute(value, ('row', 'proto'), pairs)]
    pallas_call x17 -> x22, Pallas kernels: 32 us -> 33.9 us  [run(): pl.pallas_call(kernel, out_shape=out_shape, in_specs=[small] * scalars +...]
    ppermute x14 -> x18, waiting for transfers between devices: 11.2 us -> 11.5 us  [swap(): return lax.ppermute(value, axis, [(i, i ^ step) for i in range(size)])]
  transfers between devices with their start and end apart: 29 -> 33, of which waited for: 21 -> 19; matrix products, arithmetic and copies ran while one was open for 0% -> 0% of each run, Pallas kernels for 11% -> 13%
where the time goes in v3:
time: 94.5 us; the launch traced here: 94.1 us
  starting transfers between devices  40.1 us (42%)
  Pallas kernels  33.9 us (36%)
  waiting for transfers between devices  18.5 us (20%)
  between operations  0.96 us (1%)
    pallas_call x22, Pallas kernels, run(): pl.pallas_call(kernel, out_shape=out_shape, in_specs=[small] * scalars +...  33.9 us
    ppermute x15, starting transfers between devices, swap_both(): return lax.ppermute(value, ('row', 'proto'), pairs)  20.5 us
    ppermute x18, starting transfers between devices, swap(): return lax.ppermute(value, axis, [(i, i ^ step) for i in range(size)])  19.6 us
    ppermute x18, waiting for transfers between devices, swap(): return lax.ppermute(value, axis, [(i, i ^ step) for i in range(size)])  11.5 us
    ppermute x15, waiting for transfers between devices, swap_both(): return lax.ppermute(value, ('row', 'proto'), pairs)  7.03 us
  transfers between devices with their start and end apart: 33, of which 19 were waited for; matrix products, arithmetic and copies ran while one was open for 0% of the time, Pallas kernels for 13%

profile of v3, /device:TPU:0, one launch (start us, length us, event | category | flops | bytes accessed | tf_op | source)
XLA Modules:
  0.0 94.1 jit_solution(9530223940656125934)
XLA Ops:
  0.6 0.1 pad_add_fusion.ids
  0.7 1.0 %prepare.1.refs_0_ = bf16[144,256]{1,0:T(8,128)(2,1)S(1)} custom-call(s32[2]{0:T(128)S(1)} %pad_add_fusion.ids, bf16[256,128]{1,0:T(8,128)(2,1)} %embeddings.1, bf16[256,128]{1,0:T(8,128)(2,1)} %second_view.1, f32[1,256]{1,0:T(1,128)} %bitcast.19), custom_call_target="tpu_custom_call" | custom-call | tf_op jit(solution)/shard_map/prepare/pallas_call | solution.py:314
  1.7 5.1 %collective-permute-start.5 = (bf16[144,256]{1,0:T(8,128)(2,1)S(1)}, bf16[144,256]{1,0:T(8,128)(2,1)S(1)}, u32[]{:S(2)}, u32[]{:S(2)}) collective-permute-start(bf16[144,256]{1,0:T(8,128)(2,1)S(1)} %prepare.1.refs_0_), channel_id=1, source_target_pairs={{0,24},{4,28},{8,16},{12,20},{16,8},{20,12},{24,0},{28,4},{1,25},{... | collective-permute-start | bytes 221192 | tf_op jit(solution)/shard_map/ppermute | solution.py:28
  6.8 0.6 collective-permute-start.1
  7.5 1.7 %collective-permute-start = (bf16[144,256]{1,0:T(8,128)(2,1)S(1)}, bf16[144,256]{1,0:T(8,128)(2,1)S(1)}, u32[]{:S(2)}, u32[]{:S(2)}) collective-permute-start(bf16[144,256]{1,0:T(8,128)(2,1)S(1)} %prepare.1.refs_0_), channel_id=1, source_target_pairs={{0,4},{4,0},{8,12},{12,8},{16,20},{20,16},{24,28},{28,24},{1,5},{5... | collective-permute-start | bytes 221192 | tf_op jit(solution)/shard_map/ppermute | solution.py:28
  9.1 0.4 collective-permute-done.5.refs_3_
  9.6 1.9 %collective-permute-start.6 = (bf16[144,256]{1,0:T(8,128)(2,1)S(1)}, bf16[144,256]{1,0:T(8,128)(2,1)S(1)}, u32[]{:S(2)}, u32[]{:S(2)}) collective-permute-start(bf16[144,256]{1,0:T(8,128)(2,1)S(1)} %collective-permute-done.5.refs_3_), channel_id=1, source_target_pairs={{0,4},{4,0},{8,12},{12,8},{16,20},{20,16},{24,28},{28,24},{1,5},{5... | collective-permute-start | bytes 221192 | tf_op jit(solution)/shard_map/ppermute | solution.py:28
  11.5 1.6 %collective-permute-done.3.refs_2_ = bf16[144,256]{1,0:T(8,128)(2,1)S(1)} collective-permute-done((bf16[144,256]{1,0:T(8,128)(2,1)S(1)}, bf16[144,256]{1,0:T(8,128)(2,1)S(1)}, u32[]{:S(2)}, u32[]{:S(2)}) %collective-permute-start.3) | collective-permute-done | bytes 73760 | tf_op jit(solution)/shard_map/ppermute | solution.py:28
  13.0 1.5 %collective-permute-start.4 = (bf16[144,256]{1,0:T(8,128)(2,1)S(1)}, bf16[144,256]{1,0:T(8,128)(2,1)S(1)}, u32[]{:S(2)}, u32[]{:S(2)}) collective-permute-start(bf16[144,256]{1,0:T(8,128)(2,1)S(1)} %collective-permute-done.3.refs_2_), channel_id=1, source_target_pairs={{0,4},{4,0},{8,12},{12,8},{16,20},{20,16},{24,28},{28,24},{1,5},{5... | collective-permute-start | bytes 221192 | tf_op jit(solution)/shard_map/ppermute | solution.py:28
  14.6 0.5 collective-permute-start.2
  15.1 1.9 %extend.1 = (bf16[2048,256]{1,0:T(8,128)(2,1)S(1)}, f32[8,128]{1,0:T(8,128)S(1)}) custom-call(s32[2]{0:T(128)S(1)} %pad_add_fusion.ids, bf16[4096,128]{1,0:T(8,128)(2,1)} %protos.1, f32[1,4096]{1,0:T(1,128)} %bitcast.18), custom_call_target="tpu_custom_call" | custom-call | tf_op jit(solution)/shard_map/extend/pallas_call | solution.py:314
  17.1 0.1 collective-permute-start.8
  17.2 1.0 %collective-permute-done.4.refs_2_ = bf16[144,256]{1,0:T(8,128)(2,1)S(1)} collective-permute-done((bf16[144,256]{1,0:T(8,128)(2,1)S(1)}, bf16[144,256]{1,0:T(8,128)(2,1)S(1)}, u32[]{:S(2)}, u32[]{:S(2)}) %collective-permute-start.4) | collective-permute-done | bytes 73760 | tf_op jit(solution)/shard_map/ppermute | solution.py:28
  18.1 0.8 collective-permute-done.2.refs_1_
  18.9 0.1 collective-permute-start.7
  19.0 4.0 %plan_ours.1 = (f32[2048,2048]{1,0:T(8,128)S(1)}, f32[2,2048]{1,0:T(2,128)S(1)}, f32[2,1024]{1,0:T(2,128)S(1)}, bf16[256,1024]{1,0:T(8,128)(2,1)S(1)}, bf16[128,1024]{1,0:T(8,128)(2,1)S(1)}) custom-call(s32[2]{0:T(128)S(1)} %pad_add_fusion.ids, bf16[2048,256]{1,0:T(8,128)(2,1)S(1)} %get-tuple-element.31.protos, bf16[4,144,256]{2,1,0:T(8,128)(2,1)S(1)} %stack.15.mine, ...), custom_call_target="tpu_custom_call" | custom-call | tf_op jit(solution)/shard_map/plan_ours/pallas_call | solution.py:314
  23.1 4.0 %plan_theirs.1 = (f32[2048,2048]{1,0:T(8,128)S(1)}, f32[2,2048]{1,0:T(2,128)S(1)}, f32[2,2048]{1,0:T(2,128)S(1)}, bf16[256,1024]{1,0:T(8,128)(2,1)S(1)}, bf16[128,1024]{1,0:T(8,128)(2,1)S(1)}) custom-call(s32[2]{0:T(128)S(1)} %pad_add_fusion.ids, bf16[2048,256]{1,0:T(8,128)(2,1)S(1)} %get-tuple-element.31.protos, ...), custom_call_target="tpu_custom_call", output_to_operand_aliasing={{0}: (4, {})} | custom-call | tf_op jit(solution)/shard_map/plan_theirs/pallas_call | solution.py:314
  27.1 0.6 collective-permute-start.9
  27.6 0.8 collective-permute-done.9.right
  28.5 0.7 collective-permute-start.12
  29.2 0.7 collective-permute-start.11
  29.8 3.4 %collective-permute-start.10 = (f32[2,2048]{1,0:T(2,128)S(1)}, f32[2,2048]{1,0:T(2,128)S(1)}, u32[]{:S(2)}, u32[]{:S(2)}) collective-permute-start(f32[2,2048]{1,0:T(2,128)S(1)} %add.28.after.refs_0_), channel_id=1, source_target_pairs={{0,2},{2,0},{4,6},{6,4},{8,10},{10,8},{12,14},{14,12},{16,18},{18,... | collective-permute-start | bytes 49160 | tf_op jit(solution)/shard_map/ppermute | solution.py:336
  33.2 1.9 %embed_before.1 = (f32[2048,512]{1,0:T(8,128)S(1)}, bf16[128,2048]{1,0:T(8,128)(2,1)S(1)}, f32[8,128]{1,0:T(8,128)S(1)}) custom-call(bf16[2048,256]{1,0:T(8,128)(2,1)S(1)} %get-tuple-element.31.protos, bf16[256,1024]{1,0:T(8,128)(2,1)S(1)} %get-tuple-element.39.emb_a, bf16[256,1024]{1,0:T(8,128)(2,1)S(1)} %get-tuple-element.40.emb_b, ...), custom_call_target="tpu_custom_call" | custom-call | tf_op jit(solution)/shard_map/embed_before/pallas_call | solution.py:314
  35.2 0.3 collective-permute-done.10.refs_0_
  35.5 2.3 %collective-permute-start.13 = (f32[2,2048]{1,0:T(2,128)S(1)}, f32[2,2048]{1,0:T(2,128)S(1)}, u32[]{:S(2)}, u32[]{:S(2)}) collective-permute-start(f32[2,2048]{1,0:T(2,128)S(1)} %received.4.refs_1_), channel_id=1, source_target_pairs={{0,1},{1,0},{2,3},{3,2},{4,5},{5,4},{6,7},{7,6},{8,9},{9,8},{10,11... | collective-permute-start | bytes 49160 | tf_op jit(solution)/shard_map/ppermute | solution.py:28
  37.8 0.8 collective-permute-done.13.refs_2_
  38.6 3.8 %sweep.3 = (f32[2048,2048]{1,0:T(8,128)S(1)}, f32[2,2048]{1,0:T(2,128)S(1)}, f32[1,2048]{1,0:T(1,128)S(1)}) custom-call(f32[2048,2048]{1,0:T(8,128)S(1)} %get-tuple-element.36.plan, f32[2,2048]{1,0:T(2,128)S(1)} %get-tuple-element.37.cols, f32[2,2048]{1,0:T(2,128)S(1)} %add.28.after.refs_0_, ...), custom_call_target="tpu_custom_call", output_to_operand_aliasing={{0}: (0, {})} | custom-call | tf_op jit(solution)/shard_map/sweep/pallas_call | solution.py:314
  42.5 0.4 collective-permute-start.14
  42.9 0.8 collective-permute-done.14.right
  43.7 0.6 collective-permute-start.17
  44.4 0.7 collective-permute-start.16
  45.0 2.4 %collective-permute-start.15 = (f32[1,2048]{1,0:T(1,128)S(1)}, f32[1,2048]{1,0:T(1,128)S(1)}, u32[]{:S(2)}, u32[]{:S(2)}) collective-permute-start(f32[1,2048]{1,0:T(1,128)S(1)} %add.29.after.refs_1_), channel_id=1, source_target_pairs={{0,2},{2,0},{4,6},{6,4},{8,10},{10,8},{12,14},{14,12},{16,18},{18,... | collective-permute-start | bytes 24584 | tf_op jit(solution)/shard_map/ppermute | solution.py:336
  47.5 2.0 %proto_before.1 = (f32[512,2048]{1,0:T(8,128)S(1)}, f32[512,128]{1,0:T(8,128)S(1)}, f32[8,128]{1,0:T(8,128)S(1)}) custom-call(s32[2]{0:T(128)S(1)} %pad_add_fusion.ids, bf16[2048,256]{1,0:T(8,128)(2,1)S(1)} %get-tuple-element.31.protos, bf16[256,1024]{1,0:T(8,128)(2,1)S(1)} %get-tuple-element.39.emb_a, bf16[256,1024]{1,0:T(8,128)(2,1)S(1)} %get-tuple-element.40.emb_b, ...), custom_call_target="tpu_custom_call" | custom-call | tf_op jit(solution)/shard_map/proto_before/pallas_call | solution.py:314
  49.6 1.0 %collective-permute-done.15.refs_0_ = f32[1,2048]{1,0:T(1,128)S(1)} collective-permute-done((f32[1,2048]{1,0:T(1,128)S(1)}, f32[1,2048]{1,0:T(1,128)S(1)}, u32[]{:S(2)}, u32[]{:S(2)}) %collective-permute-start.15) | collective-permute-done | bytes 8224 | tf_op jit(solution)/shard_map/ppermute | solution.py:336
  50.6 1.6 %collective-permute-start.18 = (f32[1,2048]{1,0:T(1,128)S(1)}, f32[1,2048]{1,0:T(1,128)S(1)}, u32[]{:S(2)}, u32[]{:S(2)}) collective-permute-start(f32[1,2048]{1,0:T(1,128)S(1)} %received.5.refs_2_), channel_id=1, source_target_pairs={{0,1},{1,0},{2,3},{3,2},{4,5},{5,4},{6,7},{7,6},{8,9},{9,8},{10,11... | collective-permute-start | bytes 24584 | tf_op jit(solution)/shard_map/ppermute | solution.py:28
  52.2 0.8 collective-permute-done.18.refs_3_
  53.0 3.8 %sweep.4 = (f32[2048,2048]{1,0:T(8,128)S(1)}, f32[1,2048]{1,0:T(1,128)S(1)}) custom-call(f32[2048,2048]{1,0:T(8,128)S(1)} %get-tuple-element.42.plan, f32[2,2048]{1,0:T(2,128)S(1)} %get-tuple-element.37.cols, f32[2,2048]{1,0:T(2,128)S(1)} %get-tuple-element.43.refs_0_.sums, f32[1,2048]{1,0:T(1,128)S(1)} %add.29.after.refs_1_, ...), custom_call_target="tpu_custom_call", output_to_operand_aliasing={{0}: (0, {})} | custom-call | tf_op jit(solution)/shard_map/sweep/pallas_call | solution.py:314
  56.8 0.4 collective-permute-start.19
  57.2 0.8 collective-permute-done.19.right
  58.1 0.6 collective-permute-start.22
  58.7 0.7 collective-permute-start.21
  59.4 3.4 %collective-permute-start.20 = (f32[1,2048]{1,0:T(1,128)S(1)}, f32[1,2048]{1,0:T(1,128)S(1)}, u32[]{:S(2)}, u32[]{:S(2)}) collective-permute-start(f32[1,2048]{1,0:T(1,128)S(1)} %add.30.refs_1_), channel_id=1, source_target_pairs={{0,2},{2,0},{4,6},{6,4},{8,10},{10,8},{12,14},{14,12},{16,18},{18,... | collective-permute-start | bytes 24584 | tf_op jit(solution)/shard_map/ppermute | solution.py:336
  62.8 2.1 %collective-permute-done.20.refs_0_ = f32[1,2048]{1,0:T(1,128)S(1)} collective-permute-done((f32[1,2048]{1,0:T(1,128)S(1)}, f32[1,2048]{1,0:T(1,128)S(1)}, u32[]{:S(2)}, u32[]{:S(2)}) %collective-permute-start.20) | collective-permute-done | bytes 8224 | tf_op jit(solution)/shard_map/ppermute | solution.py:336
  65.0 1.5 %collective-permute-start.23 = (f32[1,2048]{1,0:T(1,128)S(1)}, f32[1,2048]{1,0:T(1,128)S(1)}, u32[]{:S(2)}, u32[]{:S(2)}) collective-permute-start(f32[1,2048]{1,0:T(1,128)S(1)} %received.6.refs_2_), channel_id=1, source_target_pairs={{0,1},{1,0},{2,3},{3,2},{4,5},{5,4},{6,7},{7,6},{8,9},{9,8},{10,11... | collective-permute-start | bytes 24584 | tf_op jit(solution)/shard_map/ppermute | solution.py:28
  66.5 0.8 collective-permute-done.23.refs_3_
  67.3 3.8 %sweep.5 = (f32[2048,2048]{1,0:T(8,128)S(1)}, f32[1,2048]{1,0:T(1,128)S(1)}) custom-call(f32[2048,2048]{1,0:T(8,128)S(1)} %get-tuple-element.48.plan, f32[2,2048]{1,0:T(2,128)S(1)} %get-tuple-element.37.cols, f32[2,2048]{1,0:T(2,128)S(1)} %get-tuple-element.43.refs_0_.sums, f32[1,2048]{1,0:T(1,128)S(1)} %add.30.refs_1_, ...), custom_call_target="tpu_custom_call", output_to_operand_aliasing={{0}: (0, {})} | custom-call | tf_op jit(solution)/shard_map/sweep/pallas_call | solution.py:314
  71.2 0.4 collective-permute-start.24
  71.6 0.8 collective-permute-done.24.right
  72.4 0.6 collective-permute-start.27
  73.1 0.7 collective-permute-start.26
  73.7 2.4 %collective-permute-start.25 = (f32[1,2048]{1,0:T(1,128)S(1)}, f32[1,2048]{1,0:T(1,128)S(1)}, u32[]{:S(2)}, u32[]{:S(2)}) collective-permute-start(f32[1,2048]{1,0:T(1,128)S(1)} %add.31.refs_0_), channel_id=1, source_target_pairs={{0,2},{2,0},{4,6},{6,4},{8,10},{10,8},{12,14},{14,12},{16,18},{18,... | collective-permute-start | bytes 24584 | tf_op jit(solution)/shard_map/ppermute | solution.py:336
  76.2 3.1 %collective-permute-done.25.refs_0_ = f32[1,2048]{1,0:T(1,128)S(1)} collective-permute-done((f32[1,2048]{1,0:T(1,128)S(1)}, f32[1,2048]{1,0:T(1,128)S(1)}, u32[]{:S(2)}, u32[]{:S(2)}) %collective-permute-start.25) | collective-permute-done | bytes 8224 | tf_op jit(solution)/shard_map/ppermute | solution.py:336
  79.3 0.5 collective-permute-start.28
  79.8 0.8 collective-permute-done.28.refs_2_
  80.6 4.6 %embed_grad.1 = (f32[1,2048]{1,0:T(1,128)S(1)}, f32[1,2048]{1,0:T(1,128)S(1)}, f32[4,64,128]{2,1,0:T(8,128)S(1)}, f32[4,64,128]{2,1,0:T(8,128)S(1)}) custom-call(s32[2]{0:T(128)S(1)} %pad_add_fusion.ids, f32[2048,2048]{1,0:T(8,128)S(1)} %get-tuple-element.50.plan, f32[2,2048]{1,0:T(2,128)S(1)} %get-tuple-element.37.cols, ...), custom_call_target="tpu_custom_call" | custom-call | tf_op jit(solution)/shard_map/embed_grad/pallas_call | solution.py:314
  85.3 0.4 collective-permute-start.29
  85.7 1.0 %collective-permute-done.29.right = f32[4,64,128]{2,1,0:T(8,128)S(1)} collective-permute-done((f32[4,64,128]{2,1,0:T(8,128)S(1)}, f32[4,64,128]{2,1,0:T(8,128)S(1)}, u32[]{:S(2)}, u32[]{:S(2)}) %collective-permute-start.29) | collective-permute-done | bytes 131104 | tf_op jit(solution)/shard_map/ppermute | solution.py:28
  86.7 1.6 %collective-permute-start.30 = (f32[64,128]{1,0:T(8,128)S(1)}, f32[64,128]{1,0:T(8,128)S(1)}, u32[]{:S(2)}, u32[]{:S(2)}) collective-permute-start(f32[64,128]{1,0:T(8,128)S(1)} %get-tuple-element.60), channel_id=1, source_target_pairs={{0,2},{1,3},{2,0},{3,1},{4,6},{5,7},{6,4},{7,5},{8,10},{9,11},{10,... | collective-permute-start | bytes 98312 | tf_op jit(solution)/shard_map/ppermute | solution.py:336
  88.3 1.0 %collective-permute-start.32 = (f32[64,128]{1,0:T(8,128)S(1)}, f32[64,128]{1,0:T(8,128)S(1)}, u32[]{:S(2)}, u32[]{:S(2)}) collective-permute-start(f32[64,128]{1,0:T(8,128)S(1)} %get-tuple-element.61), channel_id=1, source_target_pairs={{0,6},{1,7},{2,4},{3,5},{4,2},{5,3},{6,0},{7,1},{8,14},{9,15},{10,... | collective-permute-start | bytes 98312 | tf_op jit(solution)/shard_map/ppermute | solution.py:336
  89.3 1.0 %collective-permute-start.31 = (f32[64,128]{1,0:T(8,128)S(1)}, f32[64,128]{1,0:T(8,128)S(1)}, u32[]{:S(2)}, u32[]{:S(2)}) collective-permute-start(f32[64,128]{1,0:T(8,128)S(1)} %get-tuple-element.62), channel_id=1, source_target_pairs={{0,4},{1,5},{2,6},{3,7},{4,0},{5,1},{6,2},{7,3},{8,12},{9,13},{10,... | collective-permute-start | bytes 98312 | tf_op jit(solution)/shard_map/ppermute | solution.py:336
  90.3 2.6 %proto_grad.1 = f32[512,128]{1,0:T(8,128)} custom-call(s32[2]{0:T(128)S(1)} %pad_add_fusion.ids, bf16[2048,256]{1,0:T(8,128)(2,1)S(1)} %get-tuple-element.31.protos, bf16[256,1024]{1,0:T(8,128)(2,1)S(1)} %get-tuple-element.39.emb_a, bf16[256,1024]{1,0:T(8,128)(2,1)S(1)} %get-tuple-element.40.emb_b, bf16[128,1024]{1,0:T(8,128)(2,1)S(1)} %get-tuple-element.45.view_a, ...), custom_call_target="tpu_custom_call" | custom-call | tf_op jit(solution)/shard_map/proto_grad/pallas_call | solution.py:314
  92.9 0.2 collective-permute-done.32
  93.1 0.3 collective-permute-done.31
  93.5 0.6 fusion.2
  (27 shorter events, 0.2 us)
Async XLA Ops:
  1.7 7.9 %collective-permute-start.5 = (bf16[144,256]{1,0:T(8,128)(2,1)S(1)}, bf16[144,256]{1,0:T(8,128)(2,1)S(1)}, u32[]{:S(2)}, u32[]{:S(2)}) collective-permute-start(bf16[144,256]{1,0:T(8,128)(2,1)S(1)} %prepare.1.refs_0_), channel_id=1, source_target_pairs={{0,24},{4,28},{8,16},{12,20},{16,8},{20,12},{24,0},{28,4},{1,25},{... | collective-permute-start | bytes 221192 | tf_op jit(solution)/shard_map/ppermute | solution.py:28
  6.8 6.2 %collective-permute-start.3 = (bf16[144,256]{1,0:T(8,128)(2,1)S(1)}, bf16[144,256]{1,0:T(8,128)(2,1)S(1)}, u32[]{:S(2)}, u32[]{:S(2)}) collective-permute-start(bf16[144,256]{1,0:T(8,128)(2,1)S(1)} %prepare.1.refs_0_), channel_id=1, source_target_pairs={{0,16},{4,20},{8,24},{12,28},{16,0},{20,4},{24,8},{28,12},{1,17},{... | collective-permute-start | bytes 221192 | tf_op jit(solution)/shard_map/ppermute | solution.py:28
  6.8 7.7 %collective-permute-start.1 = (bf16[144,256]{1,0:T(8,128)(2,1)S(1)}, bf16[144,256]{1,0:T(8,128)(2,1)S(1)}, u32[]{:S(2)}, u32[]{:S(2)}) collective-permute-start(bf16[144,256]{1,0:T(8,128)(2,1)S(1)} %prepare.1.refs_0_), channel_id=1, source_target_pairs={{0,8},{4,12},{8,0},{12,4},{16,24},{20,28},{24,16},{28,20},{1,9},{5... | collective-permute-start | bytes 221192 | tf_op jit(solution)/shard_map/ppermute | solution.py:28
  7.5 9.7 %collective-permute-start = (bf16[144,256]{1,0:T(8,128)(2,1)S(1)}, bf16[144,256]{1,0:T(8,128)(2,1)S(1)}, u32[]{:S(2)}, u32[]{:S(2)}) collective-permute-start(bf16[144,256]{1,0:T(8,128)(2,1)S(1)} %prepare.1.refs_0_), channel_id=1, source_target_pairs={{0,4},{4,0},{8,12},{12,8},{16,20},{20,16},{24,28},{28,24},{1,5},{5... | collective-permute-start | bytes 221192 | tf_op jit(solution)/shard_map/ppermute | solution.py:28
  9.6 7.6 %collective-permute-start.6 = (bf16[144,256]{1,0:T(8,128)(2,1)S(1)}, bf16[144,256]{1,0:T(8,128)(2,1)S(1)}, u32[]{:S(2)}, u32[]{:S(2)}) collective-permute-start(bf16[144,256]{1,0:T(8,128)(2,1)S(1)} %collective-permute-done.5.refs_3_), channel_id=1, source_target_pairs={{0,4},{4,0},{8,12},{12,8},{16,20},{20,16},{24,28},{28,24},{1,5},{5... | collective-permute-start | bytes 221192 | tf_op jit(solution)/shard_map/ppermute | solution.py:28
  13.0 5.1 %collective-permute-start.4 = (bf16[144,256]{1,0:T(8,128)(2,1)S(1)}, bf16[144,256]{1,0:T(8,128)(2,1)S(1)}, u32[]{:S(2)}, u32[]{:S(2)}) collective-permute-start(bf16[144,256]{1,0:T(8,128)(2,1)S(1)} %collective-permute-done.3.refs_2_), channel_id=1, source_target_pairs={{0,4},{4,0},{8,12},{12,8},{16,20},{20,16},{24,28},{28,24},{1,5},{5... | collective-permute-start | bytes 221192 | tf_op jit(solution)/shard_map/ppermute | solution.py:28
  14.6 4.4 %collective-permute-start.2 = (bf16[144,256]{1,0:T(8,128)(2,1)S(1)}, bf16[144,256]{1,0:T(8,128)(2,1)S(1)}, u32[]{:S(2)}, u32[]{:S(2)}) collective-permute-start(bf16[144,256]{1,0:T(8,128)(2,1)S(1)} %collective-permute-done.1.refs_1_), channel_id=1, source_target_pairs={{0,4},{4,0},{8,12},{12,8},{16,20},{20,16},{24,28},{28,24},{1,5},{5... | collective-permute-start | bytes 221192 | tf_op jit(solution)/shard_map/ppermute | solution.py:28
  17.1 2.0 %collective-permute-start.8 = (bf16[4,144,256]{2,1,0:T(8,128)(2,1)S(1)}, bf16[4,144,256]{2,1,0:T(8,128)(2,1)S(1)}, u32[]{:S(2)}, u32[]{:S(2)}) collective-permute-start(bf16[4,144,256]{2,1,0:T(8,128)(2,1)S(1)} %stack.15.mine), channel_id=1, source_target_pairs={{0,1},{1,0},{2,3},{3,2},{4,5},{5,4},{6,7},{7,6},{8,9},{9,8},{10,11... | collective-permute-start | bytes 884744 | tf_op jit(solution)/shard_map/ppermute | solution.py:28
  18.9 4.1 %collective-permute-start.7 = (bf16[4,144,256]{2,1,0:T(8,128)(2,1)S(1)}, bf16[4,144,256]{2,1,0:T(8,128)(2,1)S(1)}, u32[]{:S(2)}, u32[]{:S(2)}) collective-permute-start(bf16[4,144,256]{2,1,0:T(8,128)(2,1)S(1)} %stack.14.mine), channel_id=1, source_target_pairs={{0,1},{1,0},{2,3},{3,2},{4,5},{5,4},{6,7},{7,6},{8,9},{9,8},{10,11... | collective-permute-start | bytes 884744 | tf_op jit(solution)/shard_map/ppermute | solution.py:28
  27.1 1.4 %collective-permute-start.9 = (f32[2,2048]{1,0:T(2,128)S(1)}, f32[2,2048]{1,0:T(2,128)S(1)}, u32[]{:S(2)}, u32[]{:S(2)}) collective-permute-start(f32[2,2048]{1,0:T(2,128)S(1)} %get-tuple-element.38.left), channel_id=1, source_target_pairs={{0,1},{1,0},{2,3},{3,2},{4,5},{5,4},{6,7},{7,6},{8,9},{9,8},{10,11... | collective-permute-start | bytes 49160 | tf_op jit(solution)/shard_map/ppermute | solution.py:28
  28.5 6.7 %collective-permute-start.12 = (f32[2,2048]{1,0:T(2,128)S(1)}, f32[2,2048]{1,0:T(2,128)S(1)}, u32[]{:S(2)}, u32[]{:S(2)}) collective-permute-start(f32[2,2048]{1,0:T(2,128)S(1)} %add.28.after.refs_0_), channel_id=1, source_target_pairs={{1,7},{3,5},{5,3},{7,1},{9,15},{11,13},{13,11},{15,9},{17,23},{19,... | collective-permute-start | bytes 49160 | tf_op jit(solution)/shard_map/ppermute | solution.py:336
  29.2 6.0 %collective-permute-start.11 = (f32[2,2048]{1,0:T(2,128)S(1)}, f32[2,2048]{1,0:T(2,128)S(1)}, u32[]{:S(2)}, u32[]{:S(2)}) collective-permute-start(f32[2,2048]{1,0:T(2,128)S(1)} %add.28.after.refs_0_), channel_id=1, source_target_pairs={{1,5},{3,7},{5,1},{7,3},{9,13},{11,15},{13,9},{15,11},{17,21},{19,... | collective-permute-start | bytes 49160 | tf_op jit(solution)/shard_map/ppermute | solution.py:336
  29.8 5.6 %collective-permute-start.10 = (f32[2,2048]{1,0:T(2,128)S(1)}, f32[2,2048]{1,0:T(2,128)S(1)}, u32[]{:S(2)}, u32[]{:S(2)}) collective-permute-start(f32[2,2048]{1,0:T(2,128)S(1)} %add.28.after.refs_0_), channel_id=1, source_target_pairs={{0,2},{2,0},{4,6},{6,4},{8,10},{10,8},{12,14},{14,12},{16,18},{18,... | collective-permute-start | bytes 49160 | tf_op jit(solution)/shard_map/ppermute | solution.py:336
  35.5 3.2 %collective-permute-start.13 = (f32[2,2048]{1,0:T(2,128)S(1)}, f32[2,2048]{1,0:T(2,128)S(1)}, u32[]{:S(2)}, u32[]{:S(2)}) collective-permute-start(f32[2,2048]{1,0:T(2,128)S(1)} %received.4.refs_1_), channel_id=1, source_target_pairs={{0,1},{1,0},{2,3},{3,2},{4,5},{5,4},{6,7},{7,6},{8,9},{9,8},{10,11... | collective-permute-start | bytes 49160 | tf_op jit(solution)/shard_map/ppermute | solution.py:28
  42.5 1.2 %collective-permute-start.14 = (f32[1,2048]{1,0:T(1,128)S(1)}, f32[1,2048]{1,0:T(1,128)S(1)}, u32[]{:S(2)}, u32[]{:S(2)}) collective-permute-start(f32[1,2048]{1,0:T(1,128)S(1)} %get-tuple-element.44.left), channel_id=1, source_target_pairs={{0,1},{1,0},{2,3},{3,2},{4,5},{5,4},{6,7},{7,6},{8,9},{9,8},{10,11... | collective-permute-start | bytes 24584 | tf_op jit(solution)/shard_map/ppermute | solution.py:28
  43.7 5.8 %collective-permute-start.17 = (f32[1,2048]{1,0:T(1,128)S(1)}, f32[1,2048]{1,0:T(1,128)S(1)}, u32[]{:S(2)}, u32[]{:S(2)}) collective-permute-start(f32[1,2048]{1,0:T(1,128)S(1)} %add.29.after.refs_1_), channel_id=1, source_target_pairs={{1,7},{3,5},{5,3},{7,1},{9,15},{11,13},{13,11},{15,9},{17,23},{19,... | collective-permute-start | bytes 24584 | tf_op jit(solution)/shard_map/ppermute | solution.py:336
  44.4 5.2 %collective-permute-start.16 = (f32[1,2048]{1,0:T(1,128)S(1)}, f32[1,2048]{1,0:T(1,128)S(1)}, u32[]{:S(2)}, u32[]{:S(2)}) collective-permute-start(f32[1,2048]{1,0:T(1,128)S(1)} %add.29.after.refs_1_), channel_id=1, source_target_pairs={{1,5},{3,7},{5,1},{7,3},{9,13},{11,15},{13,9},{15,11},{17,21},{19,... | collective-permute-start | bytes 24584 | tf_op jit(solution)/shard_map/ppermute | solution.py:336
  45.0 5.5 %collective-permute-start.15 = (f32[1,2048]{1,0:T(1,128)S(1)}, f32[1,2048]{1,0:T(1,128)S(1)}, u32[]{:S(2)}, u32[]{:S(2)}) collective-permute-start(f32[1,2048]{1,0:T(1,128)S(1)} %add.29.after.refs_1_), channel_id=1, source_target_pairs={{0,2},{2,0},{4,6},{6,4},{8,10},{10,8},{12,14},{14,12},{16,18},{18,... | collective-permute-start | bytes 24584 | tf_op jit(solution)/shard_map/ppermute | solution.py:336
  50.6 2.4 %collective-permute-start.18 = (f32[1,2048]{1,0:T(1,128)S(1)}, f32[1,2048]{1,0:T(1,128)S(1)}, u32[]{:S(2)}, u32[]{:S(2)}) collective-permute-start(f32[1,2048]{1,0:T(1,128)S(1)} %received.5.refs_2_), channel_id=1, source_target_pairs={{0,1},{1,0},{2,3},{3,2},{4,5},{5,4},{6,7},{7,6},{8,9},{9,8},{10,11... | collective-permute-start | bytes 24584 | tf_op jit(solution)/shard_map/ppermute | solution.py:28
  56.8 1.2 %collective-permute-start.19 = (f32[1,2048]{1,0:T(1,128)S(1)}, f32[1,2048]{1,0:T(1,128)S(1)}, u32[]{:S(2)}, u32[]{:S(2)}) collective-permute-start(f32[1,2048]{1,0:T(1,128)S(1)} %get-tuple-element.49.left), channel_id=1, source_target_pairs={{0,1},{1,0},{2,3},{3,2},{4,5},{5,4},{6,7},{7,6},{8,9},{9,8},{10,11... | collective-permute-start | bytes 24584 | tf_op jit(solution)/shard_map/ppermute | solution.py:28
  58.1 4.7 %collective-permute-start.22 = (f32[1,2048]{1,0:T(1,128)S(1)}, f32[1,2048]{1,0:T(1,128)S(1)}, u32[]{:S(2)}, u32[]{:S(2)}) collective-permute-start(f32[1,2048]{1,0:T(1,128)S(1)} %add.30.refs_1_), channel_id=1, source_target_pairs={{1,7},{3,5},{5,3},{7,1},{9,15},{11,13},{13,11},{15,9},{17,23},{19,... | collective-permute-start | bytes 24584 | tf_op jit(solution)/shard_map/ppermute | solution.py:336
  58.7 4.1 %collective-permute-start.21 = (f32[1,2048]{1,0:T(1,128)S(1)}, f32[1,2048]{1,0:T(1,128)S(1)}, u32[]{:S(2)}, u32[]{:S(2)}) collective-permute-start(f32[1,2048]{1,0:T(1,128)S(1)} %add.30.refs_1_), channel_id=1, source_target_pairs={{1,5},{3,7},{5,1},{7,3},{9,13},{11,15},{13,9},{15,11},{17,21},{19,... | collective-permute-start | bytes 24584 | tf_op jit(solution)/shard_map/ppermute | solution.py:336
  59.4 5.5 %collective-permute-start.20 = (f32[1,2048]{1,0:T(1,128)S(1)}, f32[1,2048]{1,0:T(1,128)S(1)}, u32[]{:S(2)}, u32[]{:S(2)}) collective-permute-start(f32[1,2048]{1,0:T(1,128)S(1)} %add.30.refs_1_), channel_id=1, source_target_pairs={{0,2},{2,0},{4,6},{6,4},{8,10},{10,8},{12,14},{14,12},{16,18},{18,... | collective-permute-start | bytes 24584 | tf_op jit(solution)/shard_map/ppermute | solution.py:336
  65.0 2.4 %collective-permute-start.23 = (f32[1,2048]{1,0:T(1,128)S(1)}, f32[1,2048]{1,0:T(1,128)S(1)}, u32[]{:S(2)}, u32[]{:S(2)}) collective-permute-start(f32[1,2048]{1,0:T(1,128)S(1)} %received.6.refs_2_), channel_id=1, source_target_pairs={{0,1},{1,0},{2,3},{3,2},{4,5},{5,4},{6,7},{7,6},{8,9},{9,8},{10,11... | collective-permute-start | bytes 24584 | tf_op jit(solution)/shard_map/ppermute | solution.py:28
  71.2 1.2 %collective-permute-start.24 = (f32[1,2048]{1,0:T(1,128)S(1)}, f32[1,2048]{1,0:T(1,128)S(1)}, u32[]{:S(2)}, u32[]{:S(2)}) collective-permute-start(f32[1,2048]{1,0:T(1,128)S(1)} %get-tuple-element.53.left), channel_id=1, source_target_pairs={{0,1},{1,0},{2,3},{3,2},{4,5},{5,4},{6,7},{7,6},{8,9},{9,8},{10,11... | collective-permute-start | bytes 24584 | tf_op jit(solution)/shard_map/ppermute | solution.py:28
  72.4 3.8 %collective-permute-start.27 = (f32[1,2048]{1,0:T(1,128)S(1)}, f32[1,2048]{1,0:T(1,128)S(1)}, u32[]{:S(2)}, u32[]{:S(2)}) collective-permute-start(f32[1,2048]{1,0:T(1,128)S(1)} %add.31.refs_0_), channel_id=1, source_target_pairs={{1,7},{3,5},{5,3},{7,1},{9,15},{11,13},{13,11},{15,9},{17,23},{19,... | collective-permute-start | bytes 24584 | tf_op jit(solution)/shard_map/ppermute | solution.py:336
  73.1 3.1 %collective-permute-start.26 = (f32[1,2048]{1,0:T(1,128)S(1)}, f32[1,2048]{1,0:T(1,128)S(1)}, u32[]{:S(2)}, u32[]{:S(2)}) collective-permute-start(f32[1,2048]{1,0:T(1,128)S(1)} %add.31.refs_0_), channel_id=1, source_target_pairs={{1,5},{3,7},{5,1},{7,3},{9,13},{11,15},{13,9},{15,11},{17,21},{19,... | collective-permute-start | bytes 24584 | tf_op jit(solution)/shard_map/ppermute | solution.py:336
  73.7 5.5 %collective-permute-start.25 = (f32[1,2048]{1,0:T(1,128)S(1)}, f32[1,2048]{1,0:T(1,128)S(1)}, u32[]{:S(2)}, u32[]{:S(2)}) collective-permute-start(f32[1,2048]{1,0:T(1,128)S(1)} %add.31.refs_0_), channel_id=1, source_target_pairs={{0,2},{2,0},{4,6},{6,4},{8,10},{10,8},{12,14},{14,12},{16,18},{18,... | collective-permute-start | bytes 24584 | tf_op jit(solution)/shard_map/ppermute | solution.py:336
  79.3 1.3 %collective-permute-start.28 = (f32[1,2048]{1,0:T(1,128)S(1)}, f32[1,2048]{1,0:T(1,128)S(1)}, u32[]{:S(2)}, u32[]{:S(2)}) collective-permute-start(f32[1,2048]{1,0:T(1,128)S(1)} %received.7.refs_1_), channel_id=1, source_target_pairs={{0,1},{1,0},{2,3},{3,2},{4,5},{5,4},{6,7},{7,6},{8,9},{9,8},{10,11... | collective-permute-start | bytes 24584 | tf_op jit(solution)/shard_map/ppermute | solution.py:28
  85.3 1.4 %collective-permute-start.29 = (f32[4,64,128]{2,1,0:T(8,128)S(1)}, f32[4,64,128]{2,1,0:T(8,128)S(1)}, u32[]{:S(2)}, u32[]{:S(2)}) collective-permute-start(f32[4,64,128]{2,1,0:T(8,128)S(1)} %get-tuple-element.55), channel_id=1, source_target_pairs={{0,1},{1,0},{2,3},{3,2},{4,5},{5,4},{6,7},{7,6},{8,9},{9,8},{10,11... | collective-permute-start | bytes 393224 | tf_op jit(solution)/shard_map/ppermute | solution.py:28
  86.7 6.2 %collective-permute-start.30 = (f32[64,128]{1,0:T(8,128)S(1)}, f32[64,128]{1,0:T(8,128)S(1)}, u32[]{:S(2)}, u32[]{:S(2)}) collective-permute-start(f32[64,128]{1,0:T(8,128)S(1)} %get-tuple-element.60), channel_id=1, source_target_pairs={{0,2},{1,3},{2,0},{3,1},{4,6},{5,7},{6,4},{7,5},{8,10},{9,11},{10,... | collective-permute-start | bytes 98312 | tf_op jit(solution)/shard_map/ppermute | solution.py:336
  88.3 4.8 %collective-permute-start.32 = (f32[64,128]{1,0:T(8,128)S(1)}, f32[64,128]{1,0:T(8,128)S(1)}, u32[]{:S(2)}, u32[]{:S(2)}) collective-permute-start(f32[64,128]{1,0:T(8,128)S(1)} %get-tuple-element.61), channel_id=1, source_target_pairs={{0,6},{1,7},{2,4},{3,5},{4,2},{5,3},{6,0},{7,1},{8,14},{9,15},{10,... | collective-permute-start | bytes 98312 | tf_op jit(solution)/shard_map/ppermute | solution.py:336
  89.3 4.1 %collective-permute-start.31 = (f32[64,128]{1,0:T(8,128)S(1)}, f32[64,128]{1,0:T(8,128)S(1)}, u32[]{:S(2)}, u32[]{:S(2)}) collective-permute-start(f32[64,128]{1,0:T(8,128)S(1)} %get-tuple-element.62), channel_id=1, source_target_pairs={{0,4},{1,5},{2,6},{3,7},{4,0},{5,1},{6,2},{7,3},{8,12},{9,13},{10,... | collective-permute-start | bytes 98312 | tf_op jit(solution)/shard_map/ppermute | solution.py:336

commit v4 on v2

--- a/solution.py
+++ b/solution.py
@@ -64,7 +64,7 @@
         send_out[width:width + EXT, :] = jnp.zeros((EXT, rows), BF16)
 
 
-def turn_kernel(logit_scale, log_mass, ids, protos, col_scale, protos_out, protos_t, token):
+def extend_kernel(logit_scale, log_mass, ids, protos, col_scale, protos_out, token):
     count = protos_out.shape[0]
     width = protos.shape[1]
     token[...] = jnp.zeros_like(token)
@@ -76,7 +76,6 @@
         logs, ones = pieces_of((jnp.log(col_scale[:, there]) - log_mass) / logit_scale)
         protos_out[here, 0:width] = block
         protos_out[here, width:] = jnp.transpose(rows_of(ones + logs, width)).astype(BF16)
-        protos_t[:, here] = jnp.transpose(block.astype(F32)).astype(BF16)
         return carry
 
     lax.fori_loop(0, count // CHUNK, step, 0)
@@ -143,11 +142,16 @@
     sums_out[1:2, :] = -view_scale * jnp.sum(row_weight[...], axis=0, keepdims=True)
 
 
-def added(parts):
-    total = parts[0][...]
-    for other in parts[1:]:
+def received_kernel(terms, *refs):
+    total = refs[0][...]
+    for other in refs[1:terms]:
         total = total + other[...]
-    return total
+    refs[-1][...] = total
+
+
+def picked(ids, ours, theirs):
+    odd = jnp.full(ours.shape, ids[1] & 1, jnp.int32) == 1
+    return jnp.where(odd, ours[...], theirs[...])
 
 
 def by_rows(block, spread):
@@ -178,14 +182,14 @@
     return pl.ds(pl.multiple_of(index * STEP, STEP), STEP)
 
 
-def sweep_kernel(opening, shares, plan, cols, *refs):
+def sweep_kernel(opening, ids, plan, cols, *refs):
     if opening:
-        parts, (_, _, sums_out, part_out, spread, total) = refs[:shares], refs[shares:]
-        sums_out[...] = added(parts)
+        ours, theirs, _, sums_out, part_out, spread, total = refs
+        sums_out[...] = picked(ids, ours, theirs)
         row_dual = sums_out[1:2, :] / sums_out[0:1, :]
     else:
-        (sums, *parts), (_, _, part_out, spread, total) = refs[:shares + 1], refs[shares + 1:]
-        row_dual = (sums[1:2, :] - added(parts)) / sums[0:1, :]
+        sums, ours, theirs, _, part_out, spread, total = refs
+        row_dual = (sums[1:2, :] - picked(ids, ours, theirs)) / sums[0:1, :]
     spread[...] = jnp.broadcast_to(row_dual, spread.shape)
     total[...] = jnp.zeros_like(total)
     steps = plan.shape[0] // STEP
@@ -206,7 +210,7 @@
     part_out[...] = jnp.sum(total[...], axis=0, keepdims=True)
 
 
-def embed_before_kernel(logit_scale, protos, emb_ext, after, entry_out, token):
+def embed_before_kernel(logit_scale, protos, emb_ext, after, entry_out, protos_t, token):
     del after
     scale = logit_scale * LOG2E
     token[...] = jnp.zeros_like(token)
@@ -214,16 +218,17 @@
     def step(index, carry):
         here = chunk(index)
         entry_out[here, :] = logit_scale * jnp.exp2(scale * mm(protos[here, :], emb_ext[:, 0:entry_out.shape[1]]))
+        protos_t[:, here] = jnp.transpose(protos[here, 0:protos_t.shape[0]].astype(F32)).astype(BF16)
         return carry
 
     lax.fori_loop(0, protos.shape[0] // STEP, step, 0)
 
 
-def embed_kernel(view_scale, shares, ids, plan, cols, sums, protos, protos_t, view_t, entries, *refs):
-    parts, (duals_out, rows_out, keep, give, spread, total, whole) = refs[:shares], refs[shares:]
+def embed_kernel(view_scale, ids, plan, cols, sums, protos, protos_t, view_t, entries, ours, theirs, duals_out, rows_out, keep, give, spread, total, whole):
+    shares = keep.shape[0]
     width = protos_t.shape[0]
     rows = entries.shape[1]
-    rows_out[...] = (sums[1:2, :] - added(parts)) / sums[0:1, :]
+    rows_out[...] = (sums[1:2, :] - picked(ids, ours, theirs)) / sums[0:1, :]
     spread[...] = jnp.broadcast_to(rows_out[...], spread.shape)
     own_dual = rows_out[:, 0:rows]
     total[...] = jnp.zeros_like(total)
@@ -305,13 +310,13 @@
     return run
 
 
-def swap_both(value, above, beside):
+def swap_both(value, above, beside, cores=(0, 1)):
     shares = lax.axis_size("proto")
-    pairs = [
-        (row * shares + col, (row ^ above) * shares + (col ^ beside))
-        for row in range(lax.axis_size("row"))
-        for col in range(shares)
-    ]
+    pairs = []
+    for row in range(lax.axis_size("row")):
+        for col in range(shares):
+            partner = (row ^ above, col ^ beside) if col % 2 in cores else (row, col)
+            pairs.append((row * shares + col, partner[0] * shares + partner[1]))
     return lax.ppermute(value, ("row", "proto"), pairs)
 
 
@@ -320,9 +325,14 @@
     return [(above, beside) for above in range(2) for beside in range(0, shares, 2)]
 
 
-def exchange(part):
-    near = call(add_kernel, jax.ShapeDtypeStruct(part.shape, F32), "add", limit=2)(part, swap(part, "proto", 1))
-    return [near if pair == (0, 0) else swap_both(near, *pair) for pair in others()]
+def exchange(part, work=None):
+    shape = jax.ShapeDtypeStruct(part.shape, F32)
+    near = call(add_kernel, shape, "add", limit=2)(part, swap(part, "proto", 1))
+    got = [swap_both(near, *pair, cores=(1,)) for pair in others() if pair != (0, 0)]
+    made = work(near) if work else ()
+    kernel = functools.partial(received_kernel, len(got) + 1)
+    total = call(kernel, shape, "received", limit=2)(near, *got, *made[-1:])
+    return [total, swap(total, "proto", 1)], made[:-1]
 
 
 def kept_plan(embeddings, second_view, prototypes, row_scale, col_scale):
@@ -343,10 +353,10 @@
     send = call(functools.partial(prep_kernel, scales[0]), half, "prepare", scalars=1)(
         ids, there(embeddings), there(second_view), there(row_scale)
     )
-    protos, protos_t, token = call(
-        functools.partial(turn_kernel, scales[0], log_mass),
-        (shape(count, 2 * width, dtype=BF16), shape(width, count, dtype=BF16), shape(8, 128)),
-        "turn",
+    protos, token = call(
+        functools.partial(extend_kernel, scales[0], log_mass),
+        (shape(count, 2 * width, dtype=BF16), shape(8, 128)),
+        "extend",
         scalars=1,
         limit=4,
     )(ids, there(prototypes), there(col_scale))
@@ -370,48 +380,50 @@
 
     work = [(F32, 8, all_rows), (F32, 8, all_rows)]
     token = shape(8, 128)
-    parts = exchange(sums)
-    entries, done = call(
+    embed_before = call(
         functools.partial(embed_before_kernel, scales[0]),
-        (shape(count, 2 * rows), token),
+        (shape(count, 2 * rows), shape(width, count, dtype=BF16), token),
         "embed_before",
         limit=6,
-    )(protos, emb_ext, parts[0])
+    )
+    proto_before = call(
+        form(proto_before_kernel),
+        (shape(own, all_rows), shape(own, width), token),
+        "proto_before",
+        scalars=1,
+        limit=6,
+    )
+    parts, (entries, protos_t) = exchange(sums, lambda near: embed_before(protos, emb_ext, near))
     plan, sums, part = call(
-        functools.partial(sweep_kernel, True, shares),
+        functools.partial(sweep_kernel, True),
         (kept, shape(2, all_rows), shape(1, all_rows)),
         "sweep",
+        scalars=1,
         scratch=work,
-        aliases={0: 0},
+        aliases={1: 0},
         limit=4,
-    )(plan, cols, *parts, done)
+    )(ids, plan, cols, *parts)
+    parts, (own_entries, second) = exchange(part, lambda near: proto_before(ids, protos, emb_ext, view_t, near))
     for sweep in range(ITERS - 2):
-        parts = exchange(part)
-        if sweep == 0:
-            own_entries, second, done = call(
-                form(proto_before_kernel),
-                (shape(own, all_rows), shape(own, width), token),
-                "proto_before",
-                scalars=1,
-                limit=6,
-            )(ids, protos, emb_ext, view_t, parts[0])
         plan, part = call(
-            functools.partial(sweep_kernel, False, shares),
+            functools.partial(sweep_kernel, False),
             (kept, shape(1, all_rows)),
             "sweep",
+            scalars=1,
             scratch=work,
-            aliases={0: 0},
+            aliases={1: 0},
             limit=4,
-        )(plan, cols, sums, *parts, done)
+        )(ids, plan, cols, sums, *parts)
+        parts, _ = exchange(part)
     pieces = shape(shares, rows // shares, width)
     col_dual, row_dual, keep, give = call(
-        functools.partial(embed_kernel, scales[1], shares),
+        functools.partial(embed_kernel, scales[1]),
         (shape(1, count), shape(1, all_rows), pieces, pieces),
         "embed_grad",
         scalars=1,
         scratch=work[:1] + [(F32, width, 2 * rows), (F32, 2 * rows, width)],
         limit=6,
-    )(ids, plan, cols, sums, protos, protos_t, view_t, entries, *exchange(part))
+    )(ids, plan, cols, sums, protos, protos_t, view_t, entries, *parts)
     near = call(add_kernel, pieces, "add", limit=2)(keep, swap(give, "proto", 1))
     embed_grad = near[0]
     for place, pair in list(enumerate(others()))[1:]:

time: 81.6 us -> 105 us (1.29)
  starting transfers between devices: 29.5 us -> 55.4 us
  waiting for transfers between devices: 18.4 us -> 13.6 us
  Pallas kernels: 32 us -> 33.6 us
    ppermute x14 -> x18, starting transfers between devices: 12 us -> 43.9 us  [swap(): return lax.ppermute(value, axis, [(i, i ^ step) for i in range(size)])]
    ppermute x15, waiting for transfers between devices: 7.21 us -> 0.37 us  [swap_both(): return lax.ppermute(value, ('row', 'proto'), pairs)]
    ppermute x15, starting transfers between devices: 17.5 us -> 11.5 us  [swap_both(): return lax.ppermute(value, ('row', 'proto'), pairs)]
    ppermute x14 -> x18, waiting for transfers between devices: 11.2 us -> 13.2 us  [swap(): return lax.ppermute(value, axis, [(i, i ^ step) for i in range(size)])]
    pallas_call x17 -> x21, Pallas kernels: 32 us -> 33.6 us  [run(): pl.pallas_call(kernel, out_shape=out_shape, in_specs=[small] * scalars +...]
  transfers between devices with their start and end apart: 29 -> 33, of which waited for: 21 -> 15; matrix products, arithmetic and copies ran while one was open for 0% -> 0% of each run, Pallas kernels for 11% -> 8%
where the time goes in v4:
time: 105 us; the launch traced here: 104 us
  starting transfers between devices  55.4 us (53%)
  Pallas kernels  33.6 us (32%)
  waiting for transfers between devices  13.6 us (13%)
    ppermute x18, starting transfers between devices, swap(): return lax.ppermute(value, axis, [(i, i ^ step) for i in range(size)])  43.9 us
    pallas_call x21, Pallas kernels, run(): pl.pallas_call(kernel, out_shape=out_shape, in_specs=[small] * scalars +...  33.6 us
    ppermute x18, waiting for transfers between devices, swap(): return lax.ppermute(value, axis, [(i, i ^ step) for i in range(size)])  13.2 us
    ppermute x15, starting transfers between devices, swap_both(): return lax.ppermute(value, ('row', 'proto'), pairs)  11.5 us
  transfers between devices with their start and end apart: 33, of which 15 were waited for; matrix products, arithmetic and copies ran while one was open for 0% of the time, Pallas kernels for 8%

profile of v4, /device:TPU:0, one launch (start us, length us, event | category | flops | bytes accessed | tf_op | source)
XLA Modules:
  0.0 104.3 jit_solution(16804864854592084730)
XLA Ops:
  0.6 0.1 pad_add_fusion.ids
  0.7 1.0 prepare.1.refs_0_
  1.7 5.1 %collective-permute-start.2 = (bf16[144,256]{1,0:T(8,128)(2,1)S(1)}, bf16[144,256]{1,0:T(8,128)(2,1)S(1)}, u32[]{:S(2)}, u32[]{:S(2)}) collective-permute-start(bf16[144,256]{1,0:T(8,128)(2,1)S(1)} %prepare.1.refs_0_), channel_id=1, source_target_pairs={{0,24},{4,28},{8,16},{12,20},{16,8},{20,12},{24,0},{28,4},{1,25},{... | collective-permute-start | bytes 221192 | tf_op jit(solution)/shard_map/ppermute | solution.py:28
  6.8 0.0 collective-permute-start.1
  6.8 0.6 collective-permute-start
  7.5 1.7 %collective-permute-start.4 = (bf16[144,256]{1,0:T(8,128)(2,1)S(1)}, bf16[144,256]{1,0:T(8,128)(2,1)S(1)}, u32[]{:S(2)}, u32[]{:S(2)}) collective-permute-start(bf16[144,256]{1,0:T(8,128)(2,1)S(1)} %prepare.1.refs_0_), channel_id=1, source_target_pairs={{0,4},{4,0},{8,12},{12,8},{16,20},{20,16},{24,28},{28,24},{1,5},{5... | collective-permute-start | bytes 221192 | tf_op jit(solution)/shard_map/ppermute | solution.py:28
  9.1 0.4 collective-permute-done.2.refs_3_
  9.6 1.9 %collective-permute-start.7 = (bf16[144,256]{1,0:T(8,128)(2,1)S(1)}, bf16[144,256]{1,0:T(8,128)(2,1)S(1)}, u32[]{:S(2)}, u32[]{:S(2)}) collective-permute-start(bf16[144,256]{1,0:T(8,128)(2,1)S(1)} %collective-permute-done.2.refs_3_), channel_id=1, source_target_pairs={{0,4},{4,0},{8,12},{12,8},{16,20},{20,16},{24,28},{28,24},{1,5},{5... | collective-permute-start | bytes 221192 | tf_op jit(solution)/shard_map/ppermute | solution.py:28
  11.5 1.6 %collective-permute-done.1.refs_2_ = bf16[144,256]{1,0:T(8,128)(2,1)S(1)} collective-permute-done((bf16[144,256]{1,0:T(8,128)(2,1)S(1)}, bf16[144,256]{1,0:T(8,128)(2,1)S(1)}, u32[]{:S(2)}, u32[]{:S(2)}) %collective-permute-start.1) | collective-permute-done | bytes 73760 | tf_op jit(solution)/shard_map/ppermute | solution.py:28
  13.0 1.5 %collective-permute-start.6 = (bf16[144,256]{1,0:T(8,128)(2,1)S(1)}, bf16[144,256]{1,0:T(8,128)(2,1)S(1)}, u32[]{:S(2)}, u32[]{:S(2)}) collective-permute-start(bf16[144,256]{1,0:T(8,128)(2,1)S(1)} %collective-permute-done.1.refs_2_), channel_id=1, source_target_pairs={{0,4},{4,0},{8,12},{12,8},{16,20},{20,16},{24,28},{28,24},{1,5},{5... | collective-permute-start | bytes 221192 | tf_op jit(solution)/shard_map/ppermute | solution.py:28
  14.6 0.0 collective-permute-done.refs_1_
  14.6 0.5 collective-permute-start.5
  15.1 1.9 %extend.1 = (bf16[2048,256]{1,0:T(8,128)(2,1)S(1)}, f32[8,128]{1,0:T(8,128)S(1)}) custom-call(s32[2]{0:T(128)S(1)} %pad_add_fusion.ids, bf16[4096,128]{1,0:T(8,128)(2,1)} %protos.1, f32[1,4096]{1,0:T(1,128)} %bitcast.18), custom_call_target="tpu_custom_call" | custom-call | tf_op jit(solution)/shard_map/extend/pallas_call | solution.py:299
  17.1 0.1 collective-permute-start.3
  17.1 0.0 collective-permute-done.7.refs_3_
  17.2 1.0 collective-permute-done.6.refs_2_
  18.1 0.8 collective-permute-done.5.refs_1_
  18.9 0.1 collective-permute-start.8
  19.0 0.0 collective-permute-done.3.theirs_a
  19.0 1.6 %collective-permute-done.8.theirs_b = bf16[4,144,256]{2,1,0:T(8,128)(2,1)S(1)} collective-permute-done((bf16[4,144,256]{2,1,0:T(8,128)(2,1)S(1)}, bf16[4,144,256]{2,1,0:T(8,128)(2,1)S(1)}, u32[]{:S(2)}, u32[]{:S(2)}) %collective-permute-start.8) | collective-permute-done | bytes 294944 | tf_op jit(solution)/shard_map/ppermute | solution.py:28
  20.6 6.4 %plan.1 = (f32[2048,2048]{1,0:T(8,128)S(1)}, f32[2,2048]{1,0:T(2,128)S(1)}, f32[2,2048]{1,0:T(2,128)S(1)}, bf16[256,2048]{1,0:T(8,128)(2,1)S(1)}, bf16[128,2048]{1,0:T(8,128)(2,1)S(1)}) custom-call(s32[2]{0:T(128)S(1)} %pad_add_fusion.ids, bf16[2048,256]{1,0:T(8,128)(2,1)S(1)} %get-tuple-element.26.protos, bf16[4,144,256]{2,1,0:T(8,128)(2,1)S(1)} %stack.14.mine_a, ...), custom_call_target="tpu_custom_call" | custom-call | tf_op jit(solution)/shard_map/plan/pallas_call | solution.py:299
  26.9 0.2 collective-permute-start.9
  27.2 1.0 %collective-permute-done.9.right = f32[2,2048]{1,0:T(2,128)S(1)} collective-permute-done((f32[2,2048]{1,0:T(2,128)S(1)}, f32[2,2048]{1,0:T(2,128)S(1)}, u32[]{:S(2)}, u32[]{:S(2)}) %collective-permute-start.9) | collective-permute-done | bytes 16416 | tf_op jit(solution)/shard_map/ppermute | solution.py:28
  28.2 0.7 collective-permute-start.12
  28.9 0.7 collective-permute-start.11
  29.5 0.7 collective-permute-start.10
  30.2 1.9 %embed_before.1 = (f32[2048,512]{1,0:T(8,128)S(1)}, bf16[128,2048]{1,0:T(8,128)(2,1)S(1)}, f32[8,128]{1,0:T(8,128)S(1)}) custom-call(bf16[2048,256]{1,0:T(8,128)(2,1)S(1)} %get-tuple-element.26.protos, bf16[256,2048]{1,0:T(8,128)(2,1)S(1)} %get-tuple-element.31.emb_ext, f32[2,2048]{1,0:T(2,128)S(1)} %add.28.after.refs_0_), custom_call_target="tpu_custom_call" | custom-call | tf_op jit(solution)/shard_map/embed_before/pallas_call | solution.py:299
  32.1 0.0 collective-permute-done.11.refs_2_
  32.2 6.9 %collective-permute-start.13 = (f32[2,2048]{1,0:T(2,128)S(1)}, f32[2,2048]{1,0:T(2,128)S(1)}, u32[]{:S(2)}, u32[]{:S(2)}) collective-permute-start(f32[2,2048]{1,0:T(2,128)S(1)} %received.4.refs_0_), channel_id=1, source_target_pairs={{0,1},{1,0},{2,3},{3,2},{4,5},{5,4},{6,7},{7,6},{8,9},{9,8},{10,11... | collective-permute-start | bytes 49160 | tf_op jit(solution)/shard_map/ppermute | solution.py:28
  39.1 0.8 collective-permute-done.13.refs_1_
  39.9 4.4 %sweep.3 = (f32[2048,2048]{1,0:T(8,128)S(1)}, f32[2,2048]{1,0:T(2,128)S(1)}, f32[1,2048]{1,0:T(1,128)S(1)}) custom-call(s32[2]{0:T(128)S(1)} %pad_add_fusion.ids, f32[2048,2048]{1,0:T(8,128)S(1)} %get-tuple-element.28.plan, f32[2,2048]{1,0:T(2,128)S(1)} %get-tuple-element.29.cols, f32[2,2048]{1,0:T(2,128)S(1)} %received.4.refs_0_, ...), custom_call_target="tpu_custom_call", output_to_operand_aliasing={{0}: (1, {})} | custom-call | tf_op jit(solution)/shard_map/sweep/pallas_call | solution.py:299
  44.3 0.4 collective-permute-start.14
  44.7 0.8 collective-permute-done.14.right
  45.5 0.6 collective-permute-start.17
  46.2 0.7 collective-permute-start.16
  46.9 0.7 collective-permute-start.15
  47.5 2.0 %proto_before.1 = (f32[512,2048]{1,0:T(8,128)S(1)}, f32[512,128]{1,0:T(8,128)S(1)}, f32[8,128]{1,0:T(8,128)S(1)}) custom-call(s32[2]{0:T(128)S(1)} %pad_add_fusion.ids, bf16[2048,256]{1,0:T(8,128)(2,1)S(1)} %get-tuple-element.26.protos, bf16[256,2048]{1,0:T(8,128)(2,1)S(1)} %get-tuple-element.31.emb_ext, bf16[128,2048]{1,0:T(8,128)(2,1)S(1)} %get-tuple-element.36.view_t, ...), custom_call_target="tpu_custom_call" | custom-call | tf_op jit(solution)/shard_map/proto_before/pallas_call | solution.py:299
  49.6 6.8 %collective-permute-start.18 = (f32[1,2048]{1,0:T(1,128)S(1)}, f32[1,2048]{1,0:T(1,128)S(1)}, u32[]{:S(2)}, u32[]{:S(2)}) collective-permute-start(f32[1,2048]{1,0:T(1,128)S(1)} %received.5.refs_1_), channel_id=1, source_target_pairs={{0,1},{1,0},{2,3},{3,2},{4,5},{5,4},{6,7},{7,6},{8,9},{9,8},{10,11... | collective-permute-start | bytes 24584 | tf_op jit(solution)/shard_map/ppermute | solution.py:28
  56.4 0.8 collective-permute-done.18.refs_2_
  57.2 4.4 %sweep.4 = (f32[2048,2048]{1,0:T(8,128)S(1)}, f32[1,2048]{1,0:T(1,128)S(1)}) custom-call(s32[2]{0:T(128)S(1)} %pad_add_fusion.ids, f32[2048,2048]{1,0:T(8,128)S(1)} %get-tuple-element.33.plan, f32[2,2048]{1,0:T(2,128)S(1)} %get-tuple-element.29.cols, f32[2,2048]{1,0:T(2,128)S(1)} %get-tuple-element.34.refs_0_.sums, ...), custom_call_target="tpu_custom_call", output_to_operand_aliasing={{0}: (1, {})} | custom-call | tf_op jit(solution)/shard_map/sweep/pallas_call | solution.py:299
  61.6 0.4 collective-permute-start.19
  62.0 0.8 collective-permute-done.19.right
  62.8 0.6 collective-permute-start.22
  63.5 0.7 collective-permute-start.21
  64.2 0.7 collective-permute-start.20
  64.9 8.6 %collective-permute-start.23 = (f32[1,2048]{1,0:T(1,128)S(1)}, f32[1,2048]{1,0:T(1,128)S(1)}, u32[]{:S(2)}, u32[]{:S(2)}) collective-permute-start(f32[1,2048]{1,0:T(1,128)S(1)} %received.6.refs_1_), channel_id=1, source_target_pairs={{0,1},{1,0},{2,3},{3,2},{4,5},{5,4},{6,7},{7,6},{8,9},{9,8},{10,11... | collective-permute-start | bytes 24584 | tf_op jit(solution)/shard_map/ppermute | solution.py:28
  73.5 0.8 collective-permute-done.23.refs_2_
  74.4 4.4 %sweep.5 = (f32[2048,2048]{1,0:T(8,128)S(1)}, f32[1,2048]{1,0:T(1,128)S(1)}) custom-call(s32[2]{0:T(128)S(1)} %pad_add_fusion.ids, f32[2048,2048]{1,0:T(8,128)S(1)} %get-tuple-element.38.plan, f32[2,2048]{1,0:T(2,128)S(1)} %get-tuple-element.29.cols, f32[2,2048]{1,0:T(2,128)S(1)} %get-tuple-element.34.refs_0_.sums, ...), custom_call_target="tpu_custom_call", output_to_operand_aliasing={{0}: (1, {})} | custom-call | tf_op jit(solution)/shard_map/sweep/pallas_call | solution.py:299
  78.7 0.4 collective-permute-start.24
  79.1 0.8 collective-permute-done.24.right
  80.0 0.6 collective-permute-start.27
  80.6 0.7 collective-permute-start.26
  81.3 0.7 collective-permute-start.25
  82.0 8.2 %collective-permute-start.28 = (f32[1,2048]{1,0:T(1,128)S(1)}, f32[1,2048]{1,0:T(1,128)S(1)}, u32[]{:S(2)}, u32[]{:S(2)}) collective-permute-start(f32[1,2048]{1,0:T(1,128)S(1)} %received.7.ours), channel_id=1, source_target_pairs={{0,1},{1,0},{2,3},{3,2},{4,5},{5,4},{6,7},{7,6},{8,9},{9,8},{10,11... | collective-permute-start | bytes 24584 | tf_op jit(solution)/shard_map/ppermute | solution.py:28
  90.2 0.8 collective-permute-done.28.theirs
  91.1 4.6 %embed_grad.1 = (f32[1,2048]{1,0:T(1,128)S(1)}, f32[1,2048]{1,0:T(1,128)S(1)}, f32[4,64,128]{2,1,0:T(8,128)S(1)}, f32[4,64,128]{2,1,0:T(8,128)S(1)}) custom-call(s32[2]{0:T(128)S(1)} %pad_add_fusion.ids, f32[2048,2048]{1,0:T(8,128)S(1)} %get-tuple-element.40.plan, f32[2,2048]{1,0:T(2,128)S(1)} %get-tuple-element.29.cols, ...), custom_call_target="tpu_custom_call" | custom-call | tf_op jit(solution)/shard_map/embed_grad/pallas_call | solution.py:299
  95.7 0.4 collective-permute-start.29
  96.1 1.0 collective-permute-done.29.right
  97.1 1.3 %collective-permute-start.30 = (f32[64,128]{1,0:T(8,128)S(1)}, f32[64,128]{1,0:T(8,128)S(1)}, u32[]{:S(2)}, u32[]{:S(2)}) collective-permute-start(f32[64,128]{1,0:T(8,128)S(1)} %get-tuple-element.50), channel_id=1, source_target_pairs={{0,2},{1,3},{2,0},{3,1},{4,6},{5,7},{6,4},{7,5},{8,10},{9,11},{10,... | collective-permute-start | bytes 98312 | tf_op jit(solution)/shard_map/ppermute | solution.py:320
  98.4 1.3 %collective-permute-start.32 = (f32[64,128]{1,0:T(8,128)S(1)}, f32[64,128]{1,0:T(8,128)S(1)}, u32[]{:S(2)}, u32[]{:S(2)}) collective-permute-start(f32[64,128]{1,0:T(8,128)S(1)} %get-tuple-element.51), channel_id=1, source_target_pairs={{0,6},{1,7},{2,4},{3,5},{4,2},{5,3},{6,0},{7,1},{8,14},{9,15},{10,... | collective-permute-start | bytes 98312 | tf_op jit(solution)/shard_map/ppermute | solution.py:320
  99.7 1.0 collective-permute-start.31
  100.7 2.6 %proto_grad.1 = f32[512,128]{1,0:T(8,128)} custom-call(s32[2]{0:T(128)S(1)} %pad_add_fusion.ids, bf16[2048,256]{1,0:T(8,128)(2,1)S(1)} %get-tuple-element.26.protos, bf16[256,2048]{1,0:T(8,128)(2,1)S(1)} %get-tuple-element.31.emb_ext, bf16[128,2048]{1,0:T(8,128)(2,1)S(1)} %get-tuple-element.36.view_t, f32[512,2048]{1,0:T(8,128)S(1)} %get-tuple-element.46.entries, ...), custom_call_target="tpu_custom_call" | custom-call | tf_op jit(solution)/shard_map/proto_grad/pallas_call | solution.py:299
  103.3 0.3 collective-permute-done.31
  103.6 0.6 fusion.2
  (26 shorter events, 0.1 us)
Async XLA Ops:
  1.7 7.9 %collective-permute-start.2 = (bf16[144,256]{1,0:T(8,128)(2,1)S(1)}, bf16[144,256]{1,0:T(8,128)(2,1)S(1)}, u32[]{:S(2)}, u32[]{:S(2)}) collective-permute-start(bf16[144,256]{1,0:T(8,128)(2,1)S(1)} %prepare.1.refs_0_), channel_id=1, source_target_pairs={{0,24},{4,28},{8,16},{12,20},{16,8},{20,12},{24,0},{28,4},{1,25},{... | collective-permute-start | bytes 221192 | tf_op jit(solution)/shard_map/ppermute | solution.py:28
  6.8 6.2 %collective-permute-start.1 = (bf16[144,256]{1,0:T(8,128)(2,1)S(1)}, bf16[144,256]{1,0:T(8,128)(2,1)S(1)}, u32[]{:S(2)}, u32[]{:S(2)}) collective-permute-start(bf16[144,256]{1,0:T(8,128)(2,1)S(1)} %prepare.1.refs_0_), channel_id=1, source_target_pairs={{0,16},{4,20},{8,24},{12,28},{16,0},{20,4},{24,8},{28,12},{1,17},{... | collective-permute-start | bytes 221192 | tf_op jit(solution)/shard_map/ppermute | solution.py:28
  6.8 7.7 %collective-permute-start = (bf16[144,256]{1,0:T(8,128)(2,1)S(1)}, bf16[144,256]{1,0:T(8,128)(2,1)S(1)}, u32[]{:S(2)}, u32[]{:S(2)}) collective-permute-start(bf16[144,256]{1,0:T(8,128)(2,1)S(1)} %prepare.1.refs_0_), channel_id=1, source_target_pairs={{0,8},{4,12},{8,0},{12,4},{16,24},{20,28},{24,16},{28,20},{1,9},{5... | collective-permute-start | bytes 221192 | tf_op jit(solution)/shard_map/ppermute | solution.py:28
  7.5 9.7 %collective-permute-start.4 = (bf16[144,256]{1,0:T(8,128)(2,1)S(1)}, bf16[144,256]{1,0:T(8,128)(2,1)S(1)}, u32[]{:S(2)}, u32[]{:S(2)}) collective-permute-start(bf16[144,256]{1,0:T(8,128)(2,1)S(1)} %prepare.1.refs_0_), channel_id=1, source_target_pairs={{0,4},{4,0},{8,12},{12,8},{16,20},{20,16},{24,28},{28,24},{1,5},{5... | collective-permute-start | bytes 221192 | tf_op jit(solution)/shard_map/ppermute | solution.py:28
  9.6 7.6 %collective-permute-start.7 = (bf16[144,256]{1,0:T(8,128)(2,1)S(1)}, bf16[144,256]{1,0:T(8,128)(2,1)S(1)}, u32[]{:S(2)}, u32[]{:S(2)}) collective-permute-start(bf16[144,256]{1,0:T(8,128)(2,1)S(1)} %collective-permute-done.2.refs_3_), channel_id=1, source_target_pairs={{0,4},{4,0},{8,12},{12,8},{16,20},{20,16},{24,28},{28,24},{1,5},{5... | collective-permute-start | bytes 221192 | tf_op jit(solution)/shard_map/ppermute | solution.py:28
  13.0 5.1 %collective-permute-start.6 = (bf16[144,256]{1,0:T(8,128)(2,1)S(1)}, bf16[144,256]{1,0:T(8,128)(2,1)S(1)}, u32[]{:S(2)}, u32[]{:S(2)}) collective-permute-start(bf16[144,256]{1,0:T(8,128)(2,1)S(1)} %collective-permute-done.1.refs_2_), channel_id=1, source_target_pairs={{0,4},{4,0},{8,12},{12,8},{16,20},{20,16},{24,28},{28,24},{1,5},{5... | collective-permute-start | bytes 221192 | tf_op jit(solution)/shard_map/ppermute | solution.py:28
  14.6 4.4 %collective-permute-start.5 = (bf16[144,256]{1,0:T(8,128)(2,1)S(1)}, bf16[144,256]{1,0:T(8,128)(2,1)S(1)}, u32[]{:S(2)}, u32[]{:S(2)}) collective-permute-start(bf16[144,256]{1,0:T(8,128)(2,1)S(1)} %collective-permute-done.refs_1_), channel_id=1, source_target_pairs={{0,4},{4,0},{8,12},{12,8},{16,20},{20,16},{24,28},{28,24},{1,5},{5... | collective-permute-start | bytes 221192 | tf_op jit(solution)/shard_map/ppermute | solution.py:28
  17.1 2.0 %collective-permute-start.3 = (bf16[4,144,256]{2,1,0:T(8,128)(2,1)S(1)}, bf16[4,144,256]{2,1,0:T(8,128)(2,1)S(1)}, u32[]{:S(2)}, u32[]{:S(2)}) collective-permute-start(bf16[4,144,256]{2,1,0:T(8,128)(2,1)S(1)} %stack.14.mine_a), channel_id=1, source_target_pairs={{0,1},{1,0},{2,3},{3,2},{4,5},{5,4},{6,7},{7,6},{8,9},{9,8},{10,11... | collective-permute-start | bytes 884744 | tf_op jit(solution)/shard_map/ppermute | solution.py:28
  18.9 1.6 %collective-permute-start.8 = (bf16[4,144,256]{2,1,0:T(8,128)(2,1)S(1)}, bf16[4,144,256]{2,1,0:T(8,128)(2,1)S(1)}, u32[]{:S(2)}, u32[]{:S(2)}) collective-permute-start(bf16[4,144,256]{2,1,0:T(8,128)(2,1)S(1)} %stack.15.mine_b), channel_id=1, source_target_pairs={{0,1},{1,0},{2,3},{3,2},{4,5},{5,4},{6,7},{7,6},{8,9},{9,8},{10,11... | collective-permute-start | bytes 884744 | tf_op jit(solution)/shard_map/ppermute | solution.py:28
  26.9 1.2 %collective-permute-start.9 = (f32[2,2048]{1,0:T(2,128)S(1)}, f32[2,2048]{1,0:T(2,128)S(1)}, u32[]{:S(2)}, u32[]{:S(2)}) collective-permute-start(f32[2,2048]{1,0:T(2,128)S(1)} %get-tuple-element.30.left), channel_id=1, source_target_pairs={{0,1},{1,0},{2,3},{3,2},{4,5},{5,4},{6,7},{7,6},{8,9},{9,8},{10,11... | collective-permute-start | bytes 49160 | tf_op jit(solution)/shard_map/ppermute | solution.py:28
  28.2 3.9 %collective-permute-start.12 = (f32[2,2048]{1,0:T(2,128)S(1)}, f32[2,2048]{1,0:T(2,128)S(1)}, u32[]{:S(2)}, u32[]{:S(2)}) collective-permute-start(f32[2,2048]{1,0:T(2,128)S(1)} %add.28.after.refs_0_), channel_id=1, source_target_pairs={{0,0},{1,7},{2,2},{3,5},{4,4},{5,3},{6,6},{7,1},{8,8},{9,15},{10,1... | collective-permute-start | bytes 49160 | tf_op jit(solution)/shard_map/ppermute | solution.py:320
  28.9 3.3 %collective-permute-start.11 = (f32[2,2048]{1,0:T(2,128)S(1)}, f32[2,2048]{1,0:T(2,128)S(1)}, u32[]{:S(2)}, u32[]{:S(2)}) collective-permute-start(f32[2,2048]{1,0:T(2,128)S(1)} %add.28.after.refs_0_), channel_id=1, source_target_pairs={{0,0},{1,5},{2,2},{3,7},{4,4},{5,1},{6,6},{7,3},{8,8},{9,13},{10,1... | collective-permute-start | bytes 49160 | tf_op jit(solution)/shard_map/ppermute | solution.py:320
  29.5 2.6 %collective-permute-start.10 = (f32[2,2048]{1,0:T(2,128)S(1)}, f32[2,2048]{1,0:T(2,128)S(1)}, u32[]{:S(2)}, u32[]{:S(2)}) collective-permute-start(f32[2,2048]{1,0:T(2,128)S(1)} %add.28.after.refs_0_), channel_id=1, source_target_pairs={{0,0},{1,3},{2,2},{3,1},{4,4},{5,7},{6,6},{7,5},{8,8},{9,11},{10,1... | collective-permute-start | bytes 49160 | tf_op jit(solution)/shard_map/ppermute | solution.py:320
  32.2 7.7 %collective-permute-start.13 = (f32[2,2048]{1,0:T(2,128)S(1)}, f32[2,2048]{1,0:T(2,128)S(1)}, u32[]{:S(2)}, u32[]{:S(2)}) collective-permute-start(f32[2,2048]{1,0:T(2,128)S(1)} %received.4.refs_0_), channel_id=1, source_target_pairs={{0,1},{1,0},{2,3},{3,2},{4,5},{5,4},{6,7},{7,6},{8,9},{9,8},{10,11... | collective-permute-start | bytes 49160 | tf_op jit(solution)/shard_map/ppermute | solution.py:28
  44.3 1.2 %collective-permute-start.14 = (f32[1,2048]{1,0:T(1,128)S(1)}, f32[1,2048]{1,0:T(1,128)S(1)}, u32[]{:S(2)}, u32[]{:S(2)}) collective-permute-start(f32[1,2048]{1,0:T(1,128)S(1)} %get-tuple-element.35.left), channel_id=1, source_target_pairs={{0,1},{1,0},{2,3},{3,2},{4,5},{5,4},{6,7},{7,6},{8,9},{9,8},{10,11... | collective-permute-start | bytes 24584 | tf_op jit(solution)/shard_map/ppermute | solution.py:28
  45.5 4.0 %collective-permute-start.17 = (f32[1,2048]{1,0:T(1,128)S(1)}, f32[1,2048]{1,0:T(1,128)S(1)}, u32[]{:S(2)}, u32[]{:S(2)}) collective-permute-start(f32[1,2048]{1,0:T(1,128)S(1)} %add.29.after.refs_0_), channel_id=1, source_target_pairs={{0,0},{1,7},{2,2},{3,5},{4,4},{5,3},{6,6},{7,1},{8,8},{9,15},{10,1... | collective-permute-start | bytes 24584 | tf_op jit(solution)/shard_map/ppermute | solution.py:320
  46.2 3.4 %collective-permute-start.16 = (f32[1,2048]{1,0:T(1,128)S(1)}, f32[1,2048]{1,0:T(1,128)S(1)}, u32[]{:S(2)}, u32[]{:S(2)}) collective-permute-start(f32[1,2048]{1,0:T(1,128)S(1)} %add.29.after.refs_0_), channel_id=1, source_target_pairs={{0,0},{1,5},{2,2},{3,7},{4,4},{5,1},{6,6},{7,3},{8,8},{9,13},{10,1... | collective-permute-start | bytes 24584 | tf_op jit(solution)/shard_map/ppermute | solution.py:320
  46.9 2.7 %collective-permute-start.15 = (f32[1,2048]{1,0:T(1,128)S(1)}, f32[1,2048]{1,0:T(1,128)S(1)}, u32[]{:S(2)}, u32[]{:S(2)}) collective-permute-start(f32[1,2048]{1,0:T(1,128)S(1)} %add.29.after.refs_0_), channel_id=1, source_target_pairs={{0,0},{1,3},{2,2},{3,1},{4,4},{5,7},{6,6},{7,5},{8,8},{9,11},{10,1... | collective-permute-start | bytes 24584 | tf_op jit(solution)/shard_map/ppermute | solution.py:320
  49.6 7.6 %collective-permute-start.18 = (f32[1,2048]{1,0:T(1,128)S(1)}, f32[1,2048]{1,0:T(1,128)S(1)}, u32[]{:S(2)}, u32[]{:S(2)}) collective-permute-start(f32[1,2048]{1,0:T(1,128)S(1)} %received.5.refs_1_), channel_id=1, source_target_pairs={{0,1},{1,0},{2,3},{3,2},{4,5},{5,4},{6,7},{7,6},{8,9},{9,8},{10,11... | collective-permute-start | bytes 24584 | tf_op jit(solution)/shard_map/ppermute | solution.py:28
  61.6 1.2 %collective-permute-start.19 = (f32[1,2048]{1,0:T(1,128)S(1)}, f32[1,2048]{1,0:T(1,128)S(1)}, u32[]{:S(2)}, u32[]{:S(2)}) collective-permute-start(f32[1,2048]{1,0:T(1,128)S(1)} %get-tuple-element.39.left), channel_id=1, source_target_pairs={{0,1},{1,0},{2,3},{3,2},{4,5},{5,4},{6,7},{7,6},{8,9},{9,8},{10,11... | collective-permute-start | bytes 24584 | tf_op jit(solution)/shard_map/ppermute | solution.py:28
  62.8 2.0 %collective-permute-start.22 = (f32[1,2048]{1,0:T(1,128)S(1)}, f32[1,2048]{1,0:T(1,128)S(1)}, u32[]{:S(2)}, u32[]{:S(2)}) collective-permute-start(f32[1,2048]{1,0:T(1,128)S(1)} %add.30.refs_0_), channel_id=1, source_target_pairs={{0,0},{1,7},{2,2},{3,5},{4,4},{5,3},{6,6},{7,1},{8,8},{9,15},{10,1... | collective-permute-start | bytes 24584 | tf_op jit(solution)/shard_map/ppermute | solution.py:320
  63.5 1.4 %collective-permute-start.21 = (f32[1,2048]{1,0:T(1,128)S(1)}, f32[1,2048]{1,0:T(1,128)S(1)}, u32[]{:S(2)}, u32[]{:S(2)}) collective-permute-start(f32[1,2048]{1,0:T(1,128)S(1)} %add.30.refs_0_), channel_id=1, source_target_pairs={{0,0},{1,5},{2,2},{3,7},{4,4},{5,1},{6,6},{7,3},{8,8},{9,13},{10,1... | collective-permute-start | bytes 24584 | tf_op jit(solution)/shard_map/ppermute | solution.py:320
  64.2 0.7 collective-permute-start.20
  64.9 9.5 %collective-permute-start.23 = (f32[1,2048]{1,0:T(1,128)S(1)}, f32[1,2048]{1,0:T(1,128)S(1)}, u32[]{:S(2)}, u32[]{:S(2)}) collective-permute-start(f32[1,2048]{1,0:T(1,128)S(1)} %received.6.refs_1_), channel_id=1, source_target_pairs={{0,1},{1,0},{2,3},{3,2},{4,5},{5,4},{6,7},{7,6},{8,9},{9,8},{10,11... | collective-permute-start | bytes 24584 | tf_op jit(solution)/shard_map/ppermute | solution.py:28
  78.7 1.2 %collective-permute-start.24 = (f32[1,2048]{1,0:T(1,128)S(1)}, f32[1,2048]{1,0:T(1,128)S(1)}, u32[]{:S(2)}, u32[]{:S(2)}) collective-permute-start(f32[1,2048]{1,0:T(1,128)S(1)} %get-tuple-element.43.left), channel_id=1, source_target_pairs={{0,1},{1,0},{2,3},{3,2},{4,5},{5,4},{6,7},{7,6},{8,9},{9,8},{10,11... | collective-permute-start | bytes 24584 | tf_op jit(solution)/shard_map/ppermute | solution.py:28
  80.0 2.0 %collective-permute-start.27 = (f32[1,2048]{1,0:T(1,128)S(1)}, f32[1,2048]{1,0:T(1,128)S(1)}, u32[]{:S(2)}, u32[]{:S(2)}) collective-permute-start(f32[1,2048]{1,0:T(1,128)S(1)} %add.31.refs_0_), channel_id=1, source_target_pairs={{0,0},{1,7},{2,2},{3,5},{4,4},{5,3},{6,6},{7,1},{8,8},{9,15},{10,1... | collective-permute-start | bytes 24584 | tf_op jit(solution)/shard_map/ppermute | solution.py:320
  80.6 1.4 %collective-permute-start.26 = (f32[1,2048]{1,0:T(1,128)S(1)}, f32[1,2048]{1,0:T(1,128)S(1)}, u32[]{:S(2)}, u32[]{:S(2)}) collective-permute-start(f32[1,2048]{1,0:T(1,128)S(1)} %add.31.refs_0_), channel_id=1, source_target_pairs={{0,0},{1,5},{2,2},{3,7},{4,4},{5,1},{6,6},{7,3},{8,8},{9,13},{10,1... | collective-permute-start | bytes 24584 | tf_op jit(solution)/shard_map/ppermute | solution.py:320
  81.3 0.7 collective-permute-start.25
  82.0 9.1 %collective-permute-start.28 = (f32[1,2048]{1,0:T(1,128)S(1)}, f32[1,2048]{1,0:T(1,128)S(1)}, u32[]{:S(2)}, u32[]{:S(2)}) collective-permute-start(f32[1,2048]{1,0:T(1,128)S(1)} %received.7.ours), channel_id=1, source_target_pairs={{0,1},{1,0},{2,3},{3,2},{4,5},{5,4},{6,7},{7,6},{8,9},{9,8},{10,11... | collective-permute-start | bytes 24584 | tf_op jit(solution)/shard_map/ppermute | solution.py:28
  95.7 1.4 %collective-permute-start.29 = (f32[4,64,128]{2,1,0:T(8,128)S(1)}, f32[4,64,128]{2,1,0:T(8,128)S(1)}, u32[]{:S(2)}, u32[]{:S(2)}) collective-permute-start(f32[4,64,128]{2,1,0:T(8,128)S(1)} %get-tuple-element.45), channel_id=1, source_target_pairs={{0,1},{1,0},{2,3},{3,2},{4,5},{5,4},{6,7},{7,6},{8,9},{9,8},{10,11... | collective-permute-start | bytes 393224 | tf_op jit(solution)/shard_map/ppermute | solution.py:28
  97.1 6.2 %collective-permute-start.30 = (f32[64,128]{1,0:T(8,128)S(1)}, f32[64,128]{1,0:T(8,128)S(1)}, u32[]{:S(2)}, u32[]{:S(2)}) collective-permute-start(f32[64,128]{1,0:T(8,128)S(1)} %get-tuple-element.50), channel_id=1, source_target_pairs={{0,2},{1,3},{2,0},{3,1},{4,6},{5,7},{6,4},{7,5},{8,10},{9,11},{10,... | collective-permute-start | bytes 98312 | tf_op jit(solution)/shard_map/ppermute | solution.py:320
  98.4 4.9 %collective-permute-start.32 = (f32[64,128]{1,0:T(8,128)S(1)}, f32[64,128]{1,0:T(8,128)S(1)}, u32[]{:S(2)}, u32[]{:S(2)}) collective-permute-start(f32[64,128]{1,0:T(8,128)S(1)} %get-tuple-element.51), channel_id=1, source_target_pairs={{0,6},{1,7},{2,4},{3,5},{4,2},{5,3},{6,0},{7,1},{8,14},{9,15},{10,... | collective-permute-start | bytes 98312 | tf_op jit(solution)/shard_map/ppermute | solution.py:320
  99.7 3.9 %collective-permute-start.31 = (f32[64,128]{1,0:T(8,128)S(1)}, f32[64,128]{1,0:T(8,128)S(1)}, u32[]{:S(2)}, u32[]{:S(2)}) collective-permute-start(f32[64,128]{1,0:T(8,128)S(1)} %get-tuple-element.52), channel_id=1, source_target_pairs={{0,4},{1,5},{2,6},{3,7},{4,0},{5,1},{6,2},{7,3},{8,12},{9,13},{10,... | collective-permute-start | bytes 98312 | tf_op jit(solution)/shard_map/ppermute | solution.py:320

commit v5 on v2

--- a/solution.py
+++ b/solution.py
@@ -28,9 +28,12 @@
     return lax.ppermute(value, axis, [(i, i ^ step) for i in range(size)])
 
 
-def as_column(row, width):
-    tall = jnp.transpose(jnp.broadcast_to(row, (128, row.shape[1])))
-    return jnp.concatenate([tall] * (width // 128), 1)
+def lane_sums(block):
+    return jnp.broadcast_to(jnp.sum(block, axis=1, keepdims=True), (block.shape[0], 128))
+
+
+def widened(column, width):
+    return jnp.concatenate([column] * (width // 128), 1)
 
 
 def rows_of(pieces, height=EXT):
@@ -134,8 +137,9 @@
             across, down = folded(plan * mm(protos[here, 0:width], view_t[:, cols]))
             weight = weight + across
             row_weight[:, cols] += down
-        cols_out[0:1, here] = jnp.sum(jnp.transpose(mass), axis=0, keepdims=True)
-        cols_out[1:2, here] = -view_scale * jnp.sum(jnp.transpose(weight), axis=0, keepdims=True)
+        inverse = 1.0 / lane_sums(mass)
+        cols_out[0, here, :] = inverse
+        cols_out[1, here, :] = -view_scale * lane_sums(weight) * inverse
         return carry
 
     lax.fori_loop(0, count // CHUNK, step, 0)
@@ -150,18 +154,18 @@
     return total
 
 
-def by_rows(block, spread):
+def by_rows(block, cols, here, spread):
     tall, wide = block.shape
-    sums = []
+    duals = []
     for top in range(0, tall, 64):
         group = [jnp.zeros((8, 128), F32) for _ in range(8)]
         for left in range(0, wide, 128):
             dual = spread[:, left:left + 128]
             for place in range(8):
-                here = slice(top + place * 8, top + (place + 1) * 8)
-                group[place] = group[place] + block[here, left:left + 128] * dual
-        sums += group
-    return jnp.sum(jnp.transpose(jnp.concatenate(sums)), axis=0, keepdims=True)
+                rows = slice(top + place * 8, top + (place + 1) * 8)
+                group[place] = group[place] + block[rows, left:left + 128] * dual
+        duals.append(lane_sums(jnp.concatenate(group)))
+    return cols[1, here, :] - cols[0, here, :] * jnp.concatenate(duals)
 
 
 def by_cols(block, column):
@@ -192,8 +196,7 @@
 
     def duals(index):
         here = chunk(index)
-        product = by_rows(plan.at[here, :], spread)
-        return as_column((cols[1:2, here] - product) / cols[0:1, here], 128)
+        return by_rows(plan.at[here, :], cols, here, spread)
 
     def step(index, dual):
         product = by_cols(plan.at[chunk(index - 1), :], dual)
@@ -231,23 +234,23 @@
 
     def duals(index):
         here = chunk(index)
-        return (cols[1:2, here] - by_rows(plan.at[here, :], spread)) / cols[0:1, here]
+        return by_rows(plan.at[here, :], cols, here, spread)
 
     def gradient(index, dual):
         here = chunk(index)
         cot = -view_scale * mm(protos[here, 0:width], view_t[:, 0:rows])
-        grad = entries[here, :] * (cot - own_dual - as_column(dual, rows))
+        grad = entries[here, :] * (cot - own_dual - widened(dual, rows))
         return mm(protos_t[:, here], grad.astype(BF16))
 
     def step(index, dual):
         share = gradient(index - 1, dual)
-        duals_out[:, chunk(index - 1)] = dual
+        duals_out[chunk(index - 1), :] = dual
         dual = duals(index)
         total[...] += share
         return dual
 
     last = lax.fori_loop(1, steps, step, duals(0))
-    duals_out[:, chunk(steps - 1)] = last
+    duals_out[chunk(steps - 1), :] = last
     total[...] += gradient(steps - 1, last)
     whole[...] = jnp.transpose(total[...])
     tall = keep.shape[1]
@@ -277,7 +280,7 @@
 def proto_kernel(view_scale, ids, protos, emb_ext, view_t, entries, second, col_dual, row_dual, out):
     own, width = out.shape
     here = pl.ds(pl.multiple_of((ids[0] >> 1) * own, own), own)
-    column = as_column(col_dual[:, here], 2 * width)
+    column = widened(col_dual[here, :], 2 * width)
     total = second[...]
     for start in range(0, entries.shape[1], 2 * width):
         cols = slice(start, start + 2 * width)
@@ -361,7 +364,7 @@
     kept = pltpu.VMEM((count, all_rows), F32)
     plan, cols, sums, emb_ext, view_t = call(
         form(plan_kernel),
-        (kept, shape(2, count), shape(2, all_rows), shape(2 * width, all_rows, dtype=BF16), shape(width, all_rows, dtype=BF16)),
+        (kept, shape(2, count, 128), shape(2, all_rows), shape(2 * width, all_rows, dtype=BF16), shape(width, all_rows, dtype=BF16)),
         "plan",
         scalars=1,
         scratch=[(F32, 8, all_rows), (F32, 8, all_rows)],
@@ -406,7 +409,7 @@
     pieces = shape(shares, rows // shares, width)
     col_dual, row_dual, keep, give = call(
         functools.partial(embed_kernel, scales[1], shares),
-        (shape(1, count), shape(1, all_rows), pieces, pieces),
+        (shape(count, 128), shape(1, all_rows), pieces, pieces),
         "embed_grad",
         scalars=1,
         scratch=work[:1] + [(F32, width, 2 * rows), (F32, 2 * rows, width)],

time: 81.6 us -> 79.4 us (0.973)
  Pallas kernels: 32 us -> 29.9 us
    pallas_call x17, Pallas kernels: 32 us -> 29.9 us  [run(): pl.pallas_call(kernel, out_shape=out_shape, in_specs=[small] * scalars +...]
where the time goes in v5:
time: 79.4 us; the launch traced here: 79.2 us
  Pallas kernels  29.9 us (38%)
  starting transfers between devices  29.5 us (37%)
  waiting for transfers between devices  18.3 us (23%)
  between operations  0.83 us (1%)
    pallas_call x17, Pallas kernels, run(): pl.pallas_call(kernel, out_shape=out_shape, in_specs=[small] * scalars +...  29.9 us
    ppermute x15, starting transfers between devices, swap_both(): return lax.ppermute(value, ('row', 'proto'), pairs)  17.5 us
    ppermute x14, starting transfers between devices, swap(): return lax.ppermute(value, axis, [(i, i ^ step) for i in range(size)])  12 us
    ppermute x14, waiting for transfers between devices, swap(): return lax.ppermute(value, axis, [(i, i ^ step) for i in range(size)])  11.2 us
    ppermute x15, waiting for transfers between devices, swap_both(): return lax.ppermute(value, ('row', 'proto'), pairs)  7.13 us
  transfers between devices with their start and end apart: 29, of which 21 were waited for; matrix products, arithmetic and copies ran while one was open for 0% of the time, Pallas kernels for 11%

profile of v5, /device:TPU:0, one launch (start us, length us, event | category | flops | bytes accessed | tf_op | source)
XLA Modules:
  0.0 79.2 jit_solution(18201980697089872480)
XLA Ops:
  0.6 0.1 pad_add_fusion.ids
  0.7 1.0 %prepare.1.refs_0_ = bf16[144,256]{1,0:T(8,128)(2,1)S(1)} custom-call(s32[2]{0:T(128)S(1)} %pad_add_fusion.ids, bf16[256,128]{1,0:T(8,128)(2,1)} %embeddings.1, bf16[256,128]{1,0:T(8,128)(2,1)} %second_view.1, f32[1,256]{1,0:T(1,128)} %bitcast.19), custom_call_target="tpu_custom_call" | custom-call | tf_op jit(solution)/shard_map/prepare/pallas_call | solution.py:297
  1.7 5.1 %collective-permute-start.2 = (bf16[144,256]{1,0:T(8,128)(2,1)S(1)}, bf16[144,256]{1,0:T(8,128)(2,1)S(1)}, u32[]{:S(2)}, u32[]{:S(2)}) collective-permute-start(bf16[144,256]{1,0:T(8,128)(2,1)S(1)} %prepare.1.refs_0_), channel_id=1, source_target_pairs={{0,24},{4,28},{8,16},{12,20},{16,8},{20,12},{24,0},{28,4},{1,25},{... | collective-permute-start | bytes 221192 | tf_op jit(solution)/shard_map/ppermute | solution.py:28
  6.8 0.0 collective-permute-start.1
  6.8 0.6 collective-permute-start
  7.5 1.7 %collective-permute-start.4 = (bf16[144,256]{1,0:T(8,128)(2,1)S(1)}, bf16[144,256]{1,0:T(8,128)(2,1)S(1)}, u32[]{:S(2)}, u32[]{:S(2)}) collective-permute-start(bf16[144,256]{1,0:T(8,128)(2,1)S(1)} %prepare.1.refs_0_), channel_id=1, source_target_pairs={{0,4},{4,0},{8,12},{12,8},{16,20},{20,16},{24,28},{28,24},{1,5},{5... | collective-permute-start | bytes 221192 | tf_op jit(solution)/shard_map/ppermute | solution.py:28
  9.1 0.4 collective-permute-done.2.refs_3_
  9.6 1.9 %collective-permute-start.7 = (bf16[144,256]{1,0:T(8,128)(2,1)S(1)}, bf16[144,256]{1,0:T(8,128)(2,1)S(1)}, u32[]{:S(2)}, u32[]{:S(2)}) collective-permute-start(bf16[144,256]{1,0:T(8,128)(2,1)S(1)} %collective-permute-done.2.refs_3_), channel_id=1, source_target_pairs={{0,4},{4,0},{8,12},{12,8},{16,20},{20,16},{24,28},{28,24},{1,5},{5... | collective-permute-start | bytes 221192 | tf_op jit(solution)/shard_map/ppermute | solution.py:28
  11.5 1.6 %collective-permute-done.1.refs_2_ = bf16[144,256]{1,0:T(8,128)(2,1)S(1)} collective-permute-done((bf16[144,256]{1,0:T(8,128)(2,1)S(1)}, bf16[144,256]{1,0:T(8,128)(2,1)S(1)}, u32[]{:S(2)}, u32[]{:S(2)}) %collective-permute-start.1) | collective-permute-done | bytes 73760 | tf_op jit(solution)/shard_map/ppermute | solution.py:28
  13.0 1.5 %collective-permute-start.6 = (bf16[144,256]{1,0:T(8,128)(2,1)S(1)}, bf16[144,256]{1,0:T(8,128)(2,1)S(1)}, u32[]{:S(2)}, u32[]{:S(2)}) collective-permute-start(bf16[144,256]{1,0:T(8,128)(2,1)S(1)} %collective-permute-done.1.refs_2_), channel_id=1, source_target_pairs={{0,4},{4,0},{8,12},{12,8},{16,20},{20,16},{24,28},{28,24},{1,5},{5... | collective-permute-start | bytes 221192 | tf_op jit(solution)/shard_map/ppermute | solution.py:28
  14.6 0.0 collective-permute-done.refs_1_
  14.6 0.5 collective-permute-start.5
  15.1 2.0 %turn.1 = (bf16[2048,256]{1,0:T(8,128)(2,1)S(1)}, bf16[128,2048]{1,0:T(8,128)(2,1)S(1)}, f32[8,128]{1,0:T(8,128)S(1)}) custom-call(s32[2]{0:T(128)S(1)} %pad_add_fusion.ids, bf16[4096,128]{1,0:T(8,128)(2,1)} %protos.1, f32[1,4096]{1,0:T(1,128)} %bitcast.18), custom_call_target="tpu_custom_call" | custom-call | tf_op jit(solution)/shard_map/turn/pallas_call | solution.py:297
  17.1 0.1 collective-permute-start.3
  17.2 0.0 collective-permute-done.7.refs_3_
  17.2 0.9 %collective-permute-done.6.refs_2_ = bf16[144,256]{1,0:T(8,128)(2,1)S(1)} collective-permute-done((bf16[144,256]{1,0:T(8,128)(2,1)S(1)}, bf16[144,256]{1,0:T(8,128)(2,1)S(1)}, u32[]{:S(2)}, u32[]{:S(2)}) %collective-permute-start.6) | collective-permute-done | bytes 73760 | tf_op jit(solution)/shard_map/ppermute | solution.py:28
  18.1 0.8 %collective-permute-done.5.refs_1_ = bf16[144,256]{1,0:T(8,128)(2,1)S(1)} collective-permute-done((bf16[144,256]{1,0:T(8,128)(2,1)S(1)}, bf16[144,256]{1,0:T(8,128)(2,1)S(1)}, u32[]{:S(2)}, u32[]{:S(2)}) %collective-permute-start.5) | collective-permute-done | bytes 73760 | tf_op jit(solution)/shard_map/ppermute | solution.py:28
  18.9 0.1 collective-permute-start.8
  19.0 1.6 %collective-permute-done.8.theirs_b = bf16[4,144,256]{2,1,0:T(8,128)(2,1)S(1)} collective-permute-done((bf16[4,144,256]{2,1,0:T(8,128)(2,1)S(1)}, bf16[4,144,256]{2,1,0:T(8,128)(2,1)S(1)}, u32[]{:S(2)}, u32[]{:S(2)}) %collective-permute-start.8) | collective-permute-done | bytes 294944 | tf_op jit(solution)/shard_map/ppermute | solution.py:28
  20.6 6.4 %plan.1 = (f32[2048,2048]{1,0:T(8,128)S(1)}, f32[2,2048,128]{2,1,0:T(8,128)S(1)}, f32[2,2048]{1,0:T(2,128)S(1)}, bf16[256,2048]{1,0:T(8,128)(2,1)S(1)}, bf16[128,2048]{1,0:T(8,128)(2,1)S(1)}) custom-call(s32[2]{0:T(128)S(1)} %pad_add_fusion.ids, bf16[2048,256]{1,0:T(8,128)(2,1)S(1)} %get-tuple-element.26.protos, bf16[4,144,256]{2,1,0:T(8,128)(2,1)S(1)} %stack.14.mine_a, ...), custom_call_target="tpu_custom_call" | custom-call | tf_op jit(solution)/shard_map/plan/pallas_call | solution.py:297
  27.0 0.2 collective-permute-start.9
  27.2 1.0 %collective-permute-done.9.right = f32[2,2048]{1,0:T(2,128)S(1)} collective-permute-done((f32[2,2048]{1,0:T(2,128)S(1)}, f32[2,2048]{1,0:T(2,128)S(1)}, u32[]{:S(2)}, u32[]{:S(2)}) %collective-permute-start.9) | collective-permute-done | bytes 16416 | tf_op jit(solution)/shard_map/ppermute | solution.py:28
  28.2 2.0 %collective-permute-start.12 = (f32[2,2048]{1,0:T(2,128)S(1)}, f32[2,2048]{1,0:T(2,128)S(1)}, u32[]{:S(2)}, u32[]{:S(2)}) collective-permute-start(f32[2,2048]{1,0:T(2,128)S(1)} %add.28.after.refs_0_), channel_id=1, source_target_pairs={{0,6},{1,7},{2,4},{3,5},{4,2},{5,3},{6,0},{7,1},{8,14},{9,15},{10,... | collective-permute-start | bytes 49160 | tf_op jit(solution)/shard_map/ppermute | solution.py:318
  30.2 1.0 %collective-permute-start.11 = (f32[2,2048]{1,0:T(2,128)S(1)}, f32[2,2048]{1,0:T(2,128)S(1)}, u32[]{:S(2)}, u32[]{:S(2)}) collective-permute-start(f32[2,2048]{1,0:T(2,128)S(1)} %add.28.after.refs_0_), channel_id=1, source_target_pairs={{0,4},{1,5},{2,6},{3,7},{4,0},{5,1},{6,2},{7,3},{8,12},{9,13},{10,... | collective-permute-start | bytes 49160 | tf_op jit(solution)/shard_map/ppermute | solution.py:318
  31.2 0.5 collective-permute-start.10
  31.7 1.9 %embed_before.1 = (f32[2048,512]{1,0:T(8,128)S(1)}, f32[8,128]{1,0:T(8,128)S(1)}) custom-call(bf16[2048,256]{1,0:T(8,128)(2,1)S(1)} %get-tuple-element.26.protos, bf16[256,2048]{1,0:T(8,128)(2,1)S(1)} %get-tuple-element.31.emb_ext, f32[2,2048]{1,0:T(2,128)S(1)} %add.28.after.refs_0_), custom_call_target="tpu_custom_call" | custom-call | tf_op jit(solution)/shard_map/embed_before/pallas_call | solution.py:297
  33.7 0.3 collective-permute-done.11.refs_2_
  33.9 1.0 %collective-permute-done.10.refs_1_ = f32[2,2048]{1,0:T(2,128)S(1)} collective-permute-done((f32[2,2048]{1,0:T(2,128)S(1)}, f32[2,2048]{1,0:T(2,128)S(1)}, u32[]{:S(2)}, u32[]{:S(2)}) %collective-permute-start.10) | collective-permute-done | bytes 16416 | tf_op jit(solution)/shard_map/ppermute | solution.py:318
  34.9 3.0 %sweep.3 = (f32[2048,2048]{1,0:T(8,128)S(1)}, f32[2,2048]{1,0:T(2,128)S(1)}, f32[1,2048]{1,0:T(1,128)S(1)}) custom-call(f32[2048,2048]{1,0:T(8,128)S(1)} %get-tuple-element.28.plan, f32[2,2048,128]{2,1,0:T(8,128)S(1)} %get-tuple-element.29.cols, f32[2,2048]{1,0:T(2,128)S(1)} %add.28.after.refs_0_, ...), custom_call_target="tpu_custom_call", output_to_operand_aliasing={{0}: (0, {})} | custom-call | tf_op jit(solution)/shard_map/sweep/pallas_call | solution.py:297
  37.9 0.1 collective-permute-start.13
  38.0 1.2 %collective-permute-done.13.right = f32[1,2048]{1,0:T(1,128)S(1)} collective-permute-done((f32[1,2048]{1,0:T(1,128)S(1)}, f32[1,2048]{1,0:T(1,128)S(1)}, u32[]{:S(2)}, u32[]{:S(2)}) %collective-permute-start.13) | collective-permute-done | bytes 8224 | tf_op jit(solution)/shard_map/ppermute | solution.py:28
  39.2 1.0 %collective-permute-start.16 = (f32[1,2048]{1,0:T(1,128)S(1)}, f32[1,2048]{1,0:T(1,128)S(1)}, u32[]{:S(2)}, u32[]{:S(2)}) collective-permute-start(f32[1,2048]{1,0:T(1,128)S(1)} %add.29.after.refs_1_), channel_id=1, source_target_pairs={{0,6},{1,7},{2,4},{3,5},{4,2},{5,3},{6,0},{7,1},{8,14},{9,15},{10,... | collective-permute-start | bytes 24584 | tf_op jit(solution)/shard_map/ppermute | solution.py:318
  40.2 1.0 %collective-permute-start.15 = (f32[1,2048]{1,0:T(1,128)S(1)}, f32[1,2048]{1,0:T(1,128)S(1)}, u32[]{:S(2)}, u32[]{:S(2)}) collective-permute-start(f32[1,2048]{1,0:T(1,128)S(1)} %add.29.after.refs_1_), channel_id=1, source_target_pairs={{0,4},{1,5},{2,6},{3,7},{4,0},{5,1},{6,2},{7,3},{8,12},{9,13},{10,... | collective-permute-start | bytes 24584 | tf_op jit(solution)/shard_map/ppermute | solution.py:318
  41.2 1.5 %collective-permute-start.14 = (f32[1,2048]{1,0:T(1,128)S(1)}, f32[1,2048]{1,0:T(1,128)S(1)}, u32[]{:S(2)}, u32[]{:S(2)}) collective-permute-start(f32[1,2048]{1,0:T(1,128)S(1)} %add.29.after.refs_1_), channel_id=1, source_target_pairs={{0,2},{1,3},{2,0},{3,1},{4,6},{5,7},{6,4},{7,5},{8,10},{9,11},{10,... | collective-permute-start | bytes 24584 | tf_op jit(solution)/shard_map/ppermute | solution.py:318
  42.7 2.0 %proto_before.1 = (f32[512,2048]{1,0:T(8,128)S(1)}, f32[512,128]{1,0:T(8,128)S(1)}, f32[8,128]{1,0:T(8,128)S(1)}) custom-call(s32[2]{0:T(128)S(1)} %pad_add_fusion.ids, bf16[2048,256]{1,0:T(8,128)(2,1)S(1)} %get-tuple-element.26.protos, bf16[256,2048]{1,0:T(8,128)(2,1)S(1)} %get-tuple-element.31.emb_ext, bf16[128,2048]{1,0:T(8,128)(2,1)S(1)} %get-tuple-element.36.view_t, ...), custom_call_target="tpu_custom_call" | custom-call | tf_op jit(solution)/shard_map/proto_before/pallas_call | solution.py:297
  44.7 0.1 collective-permute-done.14.refs_2_
  44.8 3.0 %sweep.4 = (f32[2048,2048]{1,0:T(8,128)S(1)}, f32[1,2048]{1,0:T(1,128)S(1)}) custom-call(f32[2048,2048]{1,0:T(8,128)S(1)} %get-tuple-element.33.plan, f32[2,2048,128]{2,1,0:T(8,128)S(1)} %get-tuple-element.29.cols, f32[2,2048]{1,0:T(2,128)S(1)} %get-tuple-element.34.refs_0_.sums, f32[1,2048]{1,0:T(1,128)S(1)} %add.29.after.refs_1_, ...), custom_call_target="tpu_custom_call", output_to_operand_aliasing={{0}: (0, {})} | custom-call | tf_op jit(solution)/shard_map/sweep/pallas_call | solution.py:297
  47.8 0.1 collective-permute-start.17
  47.9 1.2 %collective-permute-done.17.right = f32[1,2048]{1,0:T(1,128)S(1)} collective-permute-done((f32[1,2048]{1,0:T(1,128)S(1)}, f32[1,2048]{1,0:T(1,128)S(1)}, u32[]{:S(2)}, u32[]{:S(2)}) %collective-permute-start.17) | collective-permute-done | bytes 8224 | tf_op jit(solution)/shard_map/ppermute | solution.py:28
  49.1 2.0 %collective-permute-start.20 = (f32[1,2048]{1,0:T(1,128)S(1)}, f32[1,2048]{1,0:T(1,128)S(1)}, u32[]{:S(2)}, u32[]{:S(2)}) collective-permute-start(f32[1,2048]{1,0:T(1,128)S(1)} %add.30.refs_1_), channel_id=1, source_target_pairs={{0,6},{1,7},{2,4},{3,5},{4,2},{5,3},{6,0},{7,1},{8,14},{9,15},{10,... | collective-permute-start | bytes 24584 | tf_op jit(solution)/shard_map/ppermute | solution.py:318
  51.1 1.0 %collective-permute-start.19 = (f32[1,2048]{1,0:T(1,128)S(1)}, f32[1,2048]{1,0:T(1,128)S(1)}, u32[]{:S(2)}, u32[]{:S(2)}) collective-permute-start(f32[1,2048]{1,0:T(1,128)S(1)} %add.30.refs_1_), channel_id=1, source_target_pairs={{0,4},{1,5},{2,6},{3,7},{4,0},{5,1},{6,2},{7,3},{8,12},{9,13},{10,... | collective-permute-start | bytes 24584 | tf_op jit(solution)/shard_map/ppermute | solution.py:318
  52.0 0.5 collective-permute-start.18
  52.6 1.1 %collective-permute-done.20.refs_4_ = f32[1,2048]{1,0:T(1,128)S(1)} collective-permute-done((f32[1,2048]{1,0:T(1,128)S(1)}, f32[1,2048]{1,0:T(1,128)S(1)}, u32[]{:S(2)}, u32[]{:S(2)}) %collective-permute-start.20) | collective-permute-done | bytes 8224 | tf_op jit(solution)/shard_map/ppermute | solution.py:318
  53.7 1.0 %collective-permute-done.19.refs_3_ = f32[1,2048]{1,0:T(1,128)S(1)} collective-permute-done((f32[1,2048]{1,0:T(1,128)S(1)}, f32[1,2048]{1,0:T(1,128)S(1)}, u32[]{:S(2)}, u32[]{:S(2)}) %collective-permute-start.19) | collective-permute-done | bytes 8224 | tf_op jit(solution)/shard_map/ppermute | solution.py:318
  54.7 1.0 %collective-permute-done.18.refs_2_ = f32[1,2048]{1,0:T(1,128)S(1)} collective-permute-done((f32[1,2048]{1,0:T(1,128)S(1)}, f32[1,2048]{1,0:T(1,128)S(1)}, u32[]{:S(2)}, u32[]{:S(2)}) %collective-permute-start.18) | collective-permute-done | bytes 8224 | tf_op jit(solution)/shard_map/ppermute | solution.py:318
  55.7 3.0 %sweep.5 = (f32[2048,2048]{1,0:T(8,128)S(1)}, f32[1,2048]{1,0:T(1,128)S(1)}) custom-call(f32[2048,2048]{1,0:T(8,128)S(1)} %get-tuple-element.38.plan, f32[2,2048,128]{2,1,0:T(8,128)S(1)} %get-tuple-element.29.cols, f32[2,2048]{1,0:T(2,128)S(1)} %get-tuple-element.34.refs_0_.sums, f32[1,2048]{1,0:T(1,128)S(1)} %add.30.refs_1_, ...), custom_call_target="tpu_custom_call", output_to_operand_aliasing={{0}: (0, {})} | custom-call | tf_op jit(solution)/shard_map/sweep/pallas_call | solution.py:297
  58.7 0.1 collective-permute-start.21
  58.8 1.2 %collective-permute-done.21.right = f32[1,2048]{1,0:T(1,128)S(1)} collective-permute-done((f32[1,2048]{1,0:T(1,128)S(1)}, f32[1,2048]{1,0:T(1,128)S(1)}, u32[]{:S(2)}, u32[]{:S(2)}) %collective-permute-start.21) | collective-permute-done | bytes 8224 | tf_op jit(solution)/shard_map/ppermute | solution.py:28
  59.9 1.0 %collective-permute-start.24 = (f32[1,2048]{1,0:T(1,128)S(1)}, f32[1,2048]{1,0:T(1,128)S(1)}, u32[]{:S(2)}, u32[]{:S(2)}) collective-permute-start(f32[1,2048]{1,0:T(1,128)S(1)} %add.31.refs_0_), channel_id=1, source_target_pairs={{0,6},{1,7},{2,4},{3,5},{4,2},{5,3},{6,0},{7,1},{8,14},{9,15},{10,... | collective-permute-start | bytes 24584 | tf_op jit(solution)/shard_map/ppermute | solution.py:318
  61.0 1.0 %collective-permute-start.23 = (f32[1,2048]{1,0:T(1,128)S(1)}, f32[1,2048]{1,0:T(1,128)S(1)}, u32[]{:S(2)}, u32[]{:S(2)}) collective-permute-start(f32[1,2048]{1,0:T(1,128)S(1)} %add.31.refs_0_), channel_id=1, source_target_pairs={{0,4},{1,5},{2,6},{3,7},{4,0},{5,1},{6,2},{7,3},{8,12},{9,13},{10,... | collective-permute-start | bytes 24584 | tf_op jit(solution)/shard_map/ppermute | solution.py:318
  61.9 1.5 %collective-permute-start.22 = (f32[1,2048]{1,0:T(1,128)S(1)}, f32[1,2048]{1,0:T(1,128)S(1)}, u32[]{:S(2)}, u32[]{:S(2)}) collective-permute-start(f32[1,2048]{1,0:T(1,128)S(1)} %add.31.refs_0_), channel_id=1, source_target_pairs={{0,2},{1,3},{2,0},{3,1},{4,6},{5,7},{6,4},{7,5},{8,10},{9,11},{10,... | collective-permute-start | bytes 24584 | tf_op jit(solution)/shard_map/ppermute | solution.py:318
  63.4 1.1 %collective-permute-done.24.refs_3_ = f32[1,2048]{1,0:T(1,128)S(1)} collective-permute-done((f32[1,2048]{1,0:T(1,128)S(1)}, f32[1,2048]{1,0:T(1,128)S(1)}, u32[]{:S(2)}, u32[]{:S(2)}) %collective-permute-start.24) | collective-permute-done | bytes 8224 | tf_op jit(solution)/shard_map/ppermute | solution.py:318
  64.5 0.1 collective-permute-done.23.refs_2_
  64.6 1.0 %collective-permute-done.22.refs_1_ = f32[1,2048]{1,0:T(1,128)S(1)} collective-permute-done((f32[1,2048]{1,0:T(1,128)S(1)}, f32[1,2048]{1,0:T(1,128)S(1)}, u32[]{:S(2)}, u32[]{:S(2)}) %collective-permute-start.22) | collective-permute-done | bytes 8224 | tf_op jit(solution)/shard_map/ppermute | solution.py:318
  65.6 4.9 %embed_grad.1 = (f32[2048,128]{1,0:T(8,128)S(1)}, f32[1,2048]{1,0:T(1,128)S(1)}, f32[4,64,128]{2,1,0:T(8,128)S(1)}, f32[4,64,128]{2,1,0:T(8,128)S(1)}) custom-call(s32[2]{0:T(128)S(1)} %pad_add_fusion.ids, f32[2048,2048]{1,0:T(8,128)S(1)} %get-tuple-element.40.plan, f32[2,2048,128]{2,1,0:T(8,128)S(1)} %get-tuple-element.29.cols, ...), custom_call_target="tpu_custom_call" | custom-call | tf_op jit(solution)/shard_map/embed_grad/pallas_call | solution.py:297
  70.5 0.1 collective-permute-start.25
  70.5 1.3 %collective-permute-done.25.right = f32[4,64,128]{2,1,0:T(8,128)S(1)} collective-permute-done((f32[4,64,128]{2,1,0:T(8,128)S(1)}, f32[4,64,128]{2,1,0:T(8,128)S(1)}, u32[]{:S(2)}, u32[]{:S(2)}) %collective-permute-start.25) | collective-permute-done | bytes 131104 | tf_op jit(solution)/shard_map/ppermute | solution.py:28
  71.9 1.6 %collective-permute-start.26 = (f32[64,128]{1,0:T(8,128)S(1)}, f32[64,128]{1,0:T(8,128)S(1)}, u32[]{:S(2)}, u32[]{:S(2)}) collective-permute-start(f32[64,128]{1,0:T(8,128)S(1)} %get-tuple-element.50), channel_id=1, source_target_pairs={{0,2},{1,3},{2,0},{3,1},{4,6},{5,7},{6,4},{7,5},{8,10},{9,11},{10,... | collective-permute-start | bytes 98312 | tf_op jit(solution)/shard_map/ppermute | solution.py:318
  73.5 1.0 %collective-permute-start.28 = (f32[64,128]{1,0:T(8,128)S(1)}, f32[64,128]{1,0:T(8,128)S(1)}, u32[]{:S(2)}, u32[]{:S(2)}) collective-permute-start(f32[64,128]{1,0:T(8,128)S(1)} %get-tuple-element.51), channel_id=1, source_target_pairs={{0,6},{1,7},{2,4},{3,5},{4,2},{5,3},{6,0},{7,1},{8,14},{9,15},{10,... | collective-permute-start | bytes 98312 | tf_op jit(solution)/shard_map/ppermute | solution.py:318
  74.5 1.0 %collective-permute-start.27 = (f32[64,128]{1,0:T(8,128)S(1)}, f32[64,128]{1,0:T(8,128)S(1)}, u32[]{:S(2)}, u32[]{:S(2)}) collective-permute-start(f32[64,128]{1,0:T(8,128)S(1)} %get-tuple-element.52), channel_id=1, source_target_pairs={{0,4},{1,5},{2,6},{3,7},{4,0},{5,1},{6,2},{7,3},{8,12},{9,13},{10,... | collective-permute-start | bytes 98312 | tf_op jit(solution)/shard_map/ppermute | solution.py:318
  75.5 2.7 %proto_grad.1 = f32[512,128]{1,0:T(8,128)} custom-call(s32[2]{0:T(128)S(1)} %pad_add_fusion.ids, bf16[2048,256]{1,0:T(8,128)(2,1)S(1)} %get-tuple-element.26.protos, bf16[256,2048]{1,0:T(8,128)(2,1)S(1)} %get-tuple-element.31.emb_ext, bf16[128,2048]{1,0:T(8,128)(2,1)S(1)} %get-tuple-element.36.view_t, f32[512,2048]{1,0:T(8,128)S(1)} %get-tuple-element.46.entries, ...), custom_call_target="tpu_custom_call" | custom-call | tf_op jit(solution)/shard_map/proto_grad/pallas_call | solution.py:297
  78.1 0.2 collective-permute-done.28
  78.3 0.3 collective-permute-done.27
  78.6 0.6 fusion.2
  (14 shorter events, 0.1 us)
Async XLA Ops:
  1.7 7.9 %collective-permute-start.2 = (bf16[144,256]{1,0:T(8,128)(2,1)S(1)}, bf16[144,256]{1,0:T(8,128)(2,1)S(1)}, u32[]{:S(2)}, u32[]{:S(2)}) collective-permute-start(bf16[144,256]{1,0:T(8,128)(2,1)S(1)} %prepare.1.refs_0_), channel_id=1, source_target_pairs={{0,24},{4,28},{8,16},{12,20},{16,8},{20,12},{24,0},{28,4},{1,25},{... | collective-permute-start | bytes 221192 | tf_op jit(solution)/shard_map/ppermute | solution.py:28
  6.8 6.2 %collective-permute-start.1 = (bf16[144,256]{1,0:T(8,128)(2,1)S(1)}, bf16[144,256]{1,0:T(8,128)(2,1)S(1)}, u32[]{:S(2)}, u32[]{:S(2)}) collective-permute-start(bf16[144,256]{1,0:T(8,128)(2,1)S(1)} %prepare.1.refs_0_), channel_id=1, source_target_pairs={{0,16},{4,20},{8,24},{12,28},{16,0},{20,4},{24,8},{28,12},{1,17},{... | collective-permute-start | bytes 221192 | tf_op jit(solution)/shard_map/ppermute | solution.py:28
  6.8 7.7 %collective-permute-start = (bf16[144,256]{1,0:T(8,128)(2,1)S(1)}, bf16[144,256]{1,0:T(8,128)(2,1)S(1)}, u32[]{:S(2)}, u32[]{:S(2)}) collective-permute-start(bf16[144,256]{1,0:T(8,128)(2,1)S(1)} %prepare.1.refs_0_), channel_id=1, source_target_pairs={{0,8},{4,12},{8,0},{12,4},{16,24},{20,28},{24,16},{28,20},{1,9},{5... | collective-permute-start | bytes 221192 | tf_op jit(solution)/shard_map/ppermute | solution.py:28
  7.5 9.7 %collective-permute-start.4 = (bf16[144,256]{1,0:T(8,128)(2,1)S(1)}, bf16[144,256]{1,0:T(8,128)(2,1)S(1)}, u32[]{:S(2)}, u32[]{:S(2)}) collective-permute-start(bf16[144,256]{1,0:T(8,128)(2,1)S(1)} %prepare.1.refs_0_), channel_id=1, source_target_pairs={{0,4},{4,0},{8,12},{12,8},{16,20},{20,16},{24,28},{28,24},{1,5},{5... | collective-permute-start | bytes 221192 | tf_op jit(solution)/shard_map/ppermute | solution.py:28
  9.6 7.6 %collective-permute-start.7 = (bf16[144,256]{1,0:T(8,128)(2,1)S(1)}, bf16[144,256]{1,0:T(8,128)(2,1)S(1)}, u32[]{:S(2)}, u32[]{:S(2)}) collective-permute-start(bf16[144,256]{1,0:T(8,128)(2,1)S(1)} %collective-permute-done.2.refs_3_), channel_id=1, source_target_pairs={{0,4},{4,0},{8,12},{12,8},{16,20},{20,16},{24,28},{28,24},{1,5},{5... | collective-permute-start | bytes 221192 | tf_op jit(solution)/shard_map/ppermute | solution.py:28
  13.0 5.1 %collective-permute-start.6 = (bf16[144,256]{1,0:T(8,128)(2,1)S(1)}, bf16[144,256]{1,0:T(8,128)(2,1)S(1)}, u32[]{:S(2)}, u32[]{:S(2)}) collective-permute-start(bf16[144,256]{1,0:T(8,128)(2,1)S(1)} %collective-permute-done.1.refs_2_), channel_id=1, source_target_pairs={{0,4},{4,0},{8,12},{12,8},{16,20},{20,16},{24,28},{28,24},{1,5},{5... | collective-permute-start | bytes 221192 | tf_op jit(solution)/shard_map/ppermute | solution.py:28
  14.6 4.4 %collective-permute-start.5 = (bf16[144,256]{1,0:T(8,128)(2,1)S(1)}, bf16[144,256]{1,0:T(8,128)(2,1)S(1)}, u32[]{:S(2)}, u32[]{:S(2)}) collective-permute-start(bf16[144,256]{1,0:T(8,128)(2,1)S(1)} %collective-permute-done.refs_1_), channel_id=1, source_target_pairs={{0,4},{4,0},{8,12},{12,8},{16,20},{20,16},{24,28},{28,24},{1,5},{5... | collective-permute-start | bytes 221192 | tf_op jit(solution)/shard_map/ppermute | solution.py:28
  17.1 2.0 %collective-permute-start.3 = (bf16[4,144,256]{2,1,0:T(8,128)(2,1)S(1)}, bf16[4,144,256]{2,1,0:T(8,128)(2,1)S(1)}, u32[]{:S(2)}, u32[]{:S(2)}) collective-permute-start(bf16[4,144,256]{2,1,0:T(8,128)(2,1)S(1)} %stack.14.mine_a), channel_id=1, source_target_pairs={{0,1},{1,0},{2,3},{3,2},{4,5},{5,4},{6,7},{7,6},{8,9},{9,8},{10,11... | collective-permute-start | bytes 884744 | tf_op jit(solution)/shard_map/ppermute | solution.py:28
  18.9 1.6 %collective-permute-start.8 = (bf16[4,144,256]{2,1,0:T(8,128)(2,1)S(1)}, bf16[4,144,256]{2,1,0:T(8,128)(2,1)S(1)}, u32[]{:S(2)}, u32[]{:S(2)}) collective-permute-start(bf16[4,144,256]{2,1,0:T(8,128)(2,1)S(1)} %stack.15.mine_b), channel_id=1, source_target_pairs={{0,1},{1,0},{2,3},{3,2},{4,5},{5,4},{6,7},{7,6},{8,9},{9,8},{10,11... | collective-permute-start | bytes 884744 | tf_op jit(solution)/shard_map/ppermute | solution.py:28
  27.0 1.2 %collective-permute-start.9 = (f32[2,2048]{1,0:T(2,128)S(1)}, f32[2,2048]{1,0:T(2,128)S(1)}, u32[]{:S(2)}, u32[]{:S(2)}) collective-permute-start(f32[2,2048]{1,0:T(2,128)S(1)} %get-tuple-element.30.left), channel_id=1, source_target_pairs={{0,1},{1,0},{2,3},{3,2},{4,5},{5,4},{6,7},{7,6},{8,9},{9,8},{10,11... | collective-permute-start | bytes 49160 | tf_op jit(solution)/shard_map/ppermute | solution.py:28
  28.2 5.4 %collective-permute-start.12 = (f32[2,2048]{1,0:T(2,128)S(1)}, f32[2,2048]{1,0:T(2,128)S(1)}, u32[]{:S(2)}, u32[]{:S(2)}) collective-permute-start(f32[2,2048]{1,0:T(2,128)S(1)} %add.28.after.refs_0_), channel_id=1, source_target_pairs={{0,6},{1,7},{2,4},{3,5},{4,2},{5,3},{6,0},{7,1},{8,14},{9,15},{10,... | collective-permute-start | bytes 49160 | tf_op jit(solution)/shard_map/ppermute | solution.py:318
  30.2 3.7 %collective-permute-start.11 = (f32[2,2048]{1,0:T(2,128)S(1)}, f32[2,2048]{1,0:T(2,128)S(1)}, u32[]{:S(2)}, u32[]{:S(2)}) collective-permute-start(f32[2,2048]{1,0:T(2,128)S(1)} %add.28.after.refs_0_), channel_id=1, source_target_pairs={{0,4},{1,5},{2,6},{3,7},{4,0},{5,1},{6,2},{7,3},{8,12},{9,13},{10,... | collective-permute-start | bytes 49160 | tf_op jit(solution)/shard_map/ppermute | solution.py:318
  31.2 3.7 %collective-permute-start.10 = (f32[2,2048]{1,0:T(2,128)S(1)}, f32[2,2048]{1,0:T(2,128)S(1)}, u32[]{:S(2)}, u32[]{:S(2)}) collective-permute-start(f32[2,2048]{1,0:T(2,128)S(1)} %add.28.after.refs_0_), channel_id=1, source_target_pairs={{0,2},{1,3},{2,0},{3,1},{4,6},{5,7},{6,4},{7,5},{8,10},{9,11},{10,... | collective-permute-start | bytes 49160 | tf_op jit(solution)/shard_map/ppermute | solution.py:318
  37.9 1.2 %collective-permute-start.13 = (f32[1,2048]{1,0:T(1,128)S(1)}, f32[1,2048]{1,0:T(1,128)S(1)}, u32[]{:S(2)}, u32[]{:S(2)}) collective-permute-start(f32[1,2048]{1,0:T(1,128)S(1)} %get-tuple-element.35.left), channel_id=1, source_target_pairs={{0,1},{1,0},{2,3},{3,2},{4,5},{5,4},{6,7},{7,6},{8,9},{9,8},{10,11... | collective-permute-start | bytes 24584 | tf_op jit(solution)/shard_map/ppermute | solution.py:28
  39.2 5.5 %collective-permute-start.16 = (f32[1,2048]{1,0:T(1,128)S(1)}, f32[1,2048]{1,0:T(1,128)S(1)}, u32[]{:S(2)}, u32[]{:S(2)}) collective-permute-start(f32[1,2048]{1,0:T(1,128)S(1)} %add.29.after.refs_1_), channel_id=1, source_target_pairs={{0,6},{1,7},{2,4},{3,5},{4,2},{5,3},{6,0},{7,1},{8,14},{9,15},{10,... | collective-permute-start | bytes 24584 | tf_op jit(solution)/shard_map/ppermute | solution.py:318
  40.2 4.5 %collective-permute-start.15 = (f32[1,2048]{1,0:T(1,128)S(1)}, f32[1,2048]{1,0:T(1,128)S(1)}, u32[]{:S(2)}, u32[]{:S(2)}) collective-permute-start(f32[1,2048]{1,0:T(1,128)S(1)} %add.29.after.refs_1_), channel_id=1, source_target_pairs={{0,4},{1,5},{2,6},{3,7},{4,0},{5,1},{6,2},{7,3},{8,12},{9,13},{10,... | collective-permute-start | bytes 24584 | tf_op jit(solution)/shard_map/ppermute | solution.py:318
  41.2 3.7 %collective-permute-start.14 = (f32[1,2048]{1,0:T(1,128)S(1)}, f32[1,2048]{1,0:T(1,128)S(1)}, u32[]{:S(2)}, u32[]{:S(2)}) collective-permute-start(f32[1,2048]{1,0:T(1,128)S(1)} %add.29.after.refs_1_), channel_id=1, source_target_pairs={{0,2},{1,3},{2,0},{3,1},{4,6},{5,7},{6,4},{7,5},{8,10},{9,11},{10,... | collective-permute-start | bytes 24584 | tf_op jit(solution)/shard_map/ppermute | solution.py:318
  47.8 1.2 %collective-permute-start.17 = (f32[1,2048]{1,0:T(1,128)S(1)}, f32[1,2048]{1,0:T(1,128)S(1)}, u32[]{:S(2)}, u32[]{:S(2)}) collective-permute-start(f32[1,2048]{1,0:T(1,128)S(1)} %get-tuple-element.39.left), channel_id=1, source_target_pairs={{0,1},{1,0},{2,3},{3,2},{4,5},{5,4},{6,7},{7,6},{8,9},{9,8},{10,11... | collective-permute-start | bytes 24584 | tf_op jit(solution)/shard_map/ppermute | solution.py:28
  49.1 4.6 %collective-permute-start.20 = (f32[1,2048]{1,0:T(1,128)S(1)}, f32[1,2048]{1,0:T(1,128)S(1)}, u32[]{:S(2)}, u32[]{:S(2)}) collective-permute-start(f32[1,2048]{1,0:T(1,128)S(1)} %add.30.refs_1_), channel_id=1, source_target_pairs={{0,6},{1,7},{2,4},{3,5},{4,2},{5,3},{6,0},{7,1},{8,14},{9,15},{10,... | collective-permute-start | bytes 24584 | tf_op jit(solution)/shard_map/ppermute | solution.py:318
  51.1 3.7 %collective-permute-start.19 = (f32[1,2048]{1,0:T(1,128)S(1)}, f32[1,2048]{1,0:T(1,128)S(1)}, u32[]{:S(2)}, u32[]{:S(2)}) collective-permute-start(f32[1,2048]{1,0:T(1,128)S(1)} %add.30.refs_1_), channel_id=1, source_target_pairs={{0,4},{1,5},{2,6},{3,7},{4,0},{5,1},{6,2},{7,3},{8,12},{9,13},{10,... | collective-permute-start | bytes 24584 | tf_op jit(solution)/shard_map/ppermute | solution.py:318
  52.0 3.7 %collective-permute-start.18 = (f32[1,2048]{1,0:T(1,128)S(1)}, f32[1,2048]{1,0:T(1,128)S(1)}, u32[]{:S(2)}, u32[]{:S(2)}) collective-permute-start(f32[1,2048]{1,0:T(1,128)S(1)} %add.30.refs_1_), channel_id=1, source_target_pairs={{0,2},{1,3},{2,0},{3,1},{4,6},{5,7},{6,4},{7,5},{8,10},{9,11},{10,... | collective-permute-start | bytes 24584 | tf_op jit(solution)/shard_map/ppermute | solution.py:318
  58.7 1.2 %collective-permute-start.21 = (f32[1,2048]{1,0:T(1,128)S(1)}, f32[1,2048]{1,0:T(1,128)S(1)}, u32[]{:S(2)}, u32[]{:S(2)}) collective-permute-start(f32[1,2048]{1,0:T(1,128)S(1)} %get-tuple-element.43.left), channel_id=1, source_target_pairs={{0,1},{1,0},{2,3},{3,2},{4,5},{5,4},{6,7},{7,6},{8,9},{9,8},{10,11... | collective-permute-start | bytes 24584 | tf_op jit(solution)/shard_map/ppermute | solution.py:28
  59.9 4.5 %collective-permute-start.24 = (f32[1,2048]{1,0:T(1,128)S(1)}, f32[1,2048]{1,0:T(1,128)S(1)}, u32[]{:S(2)}, u32[]{:S(2)}) collective-permute-start(f32[1,2048]{1,0:T(1,128)S(1)} %add.31.refs_0_), channel_id=1, source_target_pairs={{0,6},{1,7},{2,4},{3,5},{4,2},{5,3},{6,0},{7,1},{8,14},{9,15},{10,... | collective-permute-start | bytes 24584 | tf_op jit(solution)/shard_map/ppermute | solution.py:318
  61.0 3.7 %collective-permute-start.23 = (f32[1,2048]{1,0:T(1,128)S(1)}, f32[1,2048]{1,0:T(1,128)S(1)}, u32[]{:S(2)}, u32[]{:S(2)}) collective-permute-start(f32[1,2048]{1,0:T(1,128)S(1)} %add.31.refs_0_), channel_id=1, source_target_pairs={{0,4},{1,5},{2,6},{3,7},{4,0},{5,1},{6,2},{7,3},{8,12},{9,13},{10,... | collective-permute-start | bytes 24584 | tf_op jit(solution)/shard_map/ppermute | solution.py:318
  61.9 3.7 %collective-permute-start.22 = (f32[1,2048]{1,0:T(1,128)S(1)}, f32[1,2048]{1,0:T(1,128)S(1)}, u32[]{:S(2)}, u32[]{:S(2)}) collective-permute-start(f32[1,2048]{1,0:T(1,128)S(1)} %add.31.refs_0_), channel_id=1, source_target_pairs={{0,2},{1,3},{2,0},{3,1},{4,6},{5,7},{6,4},{7,5},{8,10},{9,11},{10,... | collective-permute-start | bytes 24584 | tf_op jit(solution)/shard_map/ppermute | solution.py:318
  70.5 1.4 %collective-permute-start.25 = (f32[4,64,128]{2,1,0:T(8,128)S(1)}, f32[4,64,128]{2,1,0:T(8,128)S(1)}, u32[]{:S(2)}, u32[]{:S(2)}) collective-permute-start(f32[4,64,128]{2,1,0:T(8,128)S(1)} %get-tuple-element.45), channel_id=1, source_target_pairs={{0,1},{1,0},{2,3},{3,2},{4,5},{5,4},{6,7},{7,6},{8,9},{9,8},{10,11... | collective-permute-start | bytes 393224 | tf_op jit(solution)/shard_map/ppermute | solution.py:28
  71.9 6.2 %collective-permute-start.26 = (f32[64,128]{1,0:T(8,128)S(1)}, f32[64,128]{1,0:T(8,128)S(1)}, u32[]{:S(2)}, u32[]{:S(2)}) collective-permute-start(f32[64,128]{1,0:T(8,128)S(1)} %get-tuple-element.50), channel_id=1, source_target_pairs={{0,2},{1,3},{2,0},{3,1},{4,6},{5,7},{6,4},{7,5},{8,10},{9,11},{10,... | collective-permute-start | bytes 98312 | tf_op jit(solution)/shard_map/ppermute | solution.py:318
  73.5 4.8 %collective-permute-start.28 = (f32[64,128]{1,0:T(8,128)S(1)}, f32[64,128]{1,0:T(8,128)S(1)}, u32[]{:S(2)}, u32[]{:S(2)}) collective-permute-start(f32[64,128]{1,0:T(8,128)S(1)} %get-tuple-element.51), channel_id=1, source_target_pairs={{0,6},{1,7},{2,4},{3,5},{4,2},{5,3},{6,0},{7,1},{8,14},{9,15},{10,... | collective-permute-start | bytes 98312 | tf_op jit(solution)/shard_map/ppermute | solution.py:318
  74.5 4.1 %collective-permute-start.27 = (f32[64,128]{1,0:T(8,128)S(1)}, f32[64,128]{1,0:T(8,128)S(1)}, u32[]{:S(2)}, u32[]{:S(2)}) collective-permute-start(f32[64,128]{1,0:T(8,128)S(1)} %get-tuple-element.52), channel_id=1, source_target_pairs={{0,4},{1,5},{2,6},{3,7},{4,0},{5,1},{6,2},{7,3},{8,12},{9,13},{10,... | collective-permute-start | bytes 98312 | tf_op jit(solution)/shard_map/ppermute | solution.py:318

commit v6 on v5

--- a/solution.py
+++ b/solution.py
@@ -90,8 +90,8 @@
         refs[-1][place] = refs[place][...]
 
 
-def add_kernel(left, right, out):
-    out[...] = left[...] + right[...]
+def add_kernel(left, right, *refs):
+    refs[-1][...] = left[...] + right[...]
 
 
 def plan_kernel(logit_scale, view_scale, ids, protos, mine_a, theirs_a, mine_b, theirs_b, plan_out, cols_out, sums_out, emb_ext, view_t, row_mass, row_weight):
@@ -222,37 +222,42 @@
     lax.fori_loop(0, protos.shape[0] // STEP, step, 0)
 
 
-def embed_kernel(view_scale, shares, ids, plan, cols, sums, protos, protos_t, view_t, entries, *refs):
-    parts, (duals_out, rows_out, keep, give, spread, total, whole) = refs[:shares], refs[shares:]
+def cotangent_kernel(view_scale, block, ids, protos, view_t, after, cot_out, token):
+    del after
+    width = view_t.shape[0]
+    tall, wide = cot_out.shape
+    token[...] = jnp.zeros_like(token)
+    first = pl.multiple_of(block(ids) * tall, tall)
+
+    def step(index, carry):
+        here = chunk(index)
+        from_row = pl.ds(pl.multiple_of(first + index * STEP, STEP), STEP)
+        cot_out[here, :] = -view_scale * mm(protos[from_row, 0:width], view_t[:, 0:wide])
+        return carry
+
+    lax.fori_loop(0, tall // STEP, step, 0)
+
+
+def embed_kernel(shares, ids, plan, cols, sums, protos_t, entries, cots, *refs):
+    parts, (_, duals_out, rows_out, keep, give, spread, whole) = refs[:shares], refs[shares:]
     width = protos_t.shape[0]
     rows = entries.shape[1]
     rows_out[...] = (sums[1:2, :] - added(parts)) / sums[0:1, :]
     spread[...] = jnp.broadcast_to(rows_out[...], spread.shape)
     own_dual = rows_out[:, 0:rows]
-    total[...] = jnp.zeros_like(total)
-    steps = plan.shape[0] // STEP
-
-    def duals(index):
+
+    def duals(index, carry):
         here = chunk(index)
-        return by_rows(plan.at[here, :], cols, here, spread)
-
-    def gradient(index, dual):
-        here = chunk(index)
-        cot = -view_scale * mm(protos[here, 0:width], view_t[:, 0:rows])
-        grad = entries[here, :] * (cot - own_dual - widened(dual, rows))
-        return mm(protos_t[:, here], grad.astype(BF16))
-
-    def step(index, dual):
-        share = gradient(index - 1, dual)
-        duals_out[chunk(index - 1), :] = dual
-        dual = duals(index)
-        total[...] += share
-        return dual
-
-    last = lax.fori_loop(1, steps, step, duals(0))
-    duals_out[chunk(steps - 1), :] = last
-    total[...] += gradient(steps - 1, last)
-    whole[...] = jnp.transpose(total[...])
+        duals_out[here, :] = by_rows(plan.at[here, :], cols, here, spread)
+        return carry
+
+    lax.fori_loop(0, plan.shape[0] // STEP, duals, 0)
+    total = jnp.zeros((width, rows), F32)
+    for start in range(0, plan.shape[0], CHUNK):
+        here = slice(start, start + CHUNK)
+        grad = entries[here, :] * (cots[here, :] - own_dual - widened(duals_out[here, :], rows))
+        total = total + mm(protos_t[:, here], grad.astype(BF16))
+    whole[...] = jnp.transpose(total)
     tall = keep.shape[1]
     for place in range(shares):
         above, beside = divmod(place, shares // 2)
@@ -277,17 +282,19 @@
     second_out[...] = total
 
 
-def proto_kernel(view_scale, ids, protos, emb_ext, view_t, entries, second, col_dual, row_dual, out):
-    own, width = out.shape
+def proto_kernel(half, ids, emb_ext, entries, cots, so_far, col_dual, row_dual, *outs):
+    own, width = outs[0].shape
     here = pl.ds(pl.multiple_of((ids[0] >> 1) * own, own), own)
     column = widened(col_dual[here, :], 2 * width)
-    total = second[...]
-    for start in range(0, entries.shape[1], 2 * width):
+    total = so_far[...]
+    some = entries.shape[1] // 2
+    for start in range(half * some, (half + 1) * some, 2 * width):
         cols = slice(start, start + 2 * width)
-        cot = -view_scale * mm(protos[here, 0:width], view_t[:, cols])
-        grad = entries[:, cols] * (cot - row_dual[:, cols] - column)
+        grad = entries[:, cols] * (cots[:, cols] - row_dual[:, cols] - column)
         total = total + mm(grad.astype(BF16), emb_ext[0:width, cols], NT)
-    out[...] = total
+    outs[0][...] = total
+    for token in outs[1:]:
+        token[...] = jnp.zeros_like(token)
 
 
 def call(kernel, out_shape, name, scalars=0, scratch=(), aliases=None, limit=16):
@@ -388,8 +395,13 @@
         aliases={0: 0},
         limit=4,
     )(plan, cols, *parts, done)
+    cotangent = lambda dims, block: call(
+        functools.partial(cotangent_kernel, scales[1], block), (shape(*dims), token), "cotangent", scalars=1, limit=4
+    )
     for sweep in range(ITERS - 2):
         parts = exchange(part)
+        if sweep == ITERS - 3:
+            cots, done = cotangent((count, 2 * rows), lambda ids: 0)(ids, protos, view_t, parts[0])
         if sweep == 0:
             own_entries, second, done = call(
                 form(proto_before_kernel),
@@ -406,22 +418,24 @@
             aliases={0: 0},
             limit=4,
         )(plan, cols, sums, *parts, done)
+    parts = exchange(part)
+    own_cots, done = cotangent((own, all_rows), lambda ids: ids[0] >> 1)(ids, protos, view_t, parts[0])
     pieces = shape(shares, rows // shares, width)
     col_dual, row_dual, keep, give = call(
-        functools.partial(embed_kernel, scales[1], shares),
+        functools.partial(embed_kernel, shares),
         (shape(count, 128), shape(1, all_rows), pieces, pieces),
         "embed_grad",
         scalars=1,
-        scratch=work[:1] + [(F32, width, 2 * rows), (F32, 2 * rows, width)],
-        limit=6,
-    )(ids, plan, cols, sums, protos, protos_t, view_t, entries, *exchange(part))
-    near = call(add_kernel, pieces, "add", limit=2)(keep, swap(give, "proto", 1))
+        scratch=work[:1] + [(F32, 2 * rows, width)],
+        limit=8,
+    )(ids, plan, cols, sums, protos_t, entries, cots, *parts, done)
+    half = lambda number, outs: call(functools.partial(proto_kernel, number), outs, "proto_grad", scalars=1, limit=6)
+    second, done = half(0, (shape(own, width), token))(ids, emb_ext, own_entries, own_cots, second, col_dual, row_dual)
+    near = call(add_kernel, pieces, "add", limit=2)(keep, swap(give, "proto", 1), done)
     embed_grad = near[0]
     for place, pair in list(enumerate(others()))[1:]:
         embed_grad = embed_grad + swap_both(near[place], *pair)
-    proto_grad = call(functools.partial(proto_kernel, scales[1]), shape(own, width), "proto_grad", scalars=1, limit=6)(
-        ids, protos, emb_ext, view_t, own_entries, second, col_dual, row_dual
-    )
+    proto_grad = half(1, (shape(own, width),))(ids, emb_ext, own_entries, own_cots, second, col_dual, row_dual)[0]
     return embed_grad, proto_grad
 
 

time: 79.4 us -> 77.7 us (0.979)
  waiting for transfers between devices: 18.3 us -> 14.5 us
  Pallas kernels: 29.9 us -> 31.9 us
    ppermute x15, waiting for transfers between devices: 7.13 us -> 4.35 us  [swap_both(): return lax.ppermute(value, ('row', 'proto'), pairs)]
    pallas_call x17 -> x20, Pallas kernels: 29.9 us -> 31.9 us  [run(): pl.pallas_call(kernel, out_shape=out_shape, in_specs=[small] * scalars +...]
    ppermute x14, waiting for transfers between devices: 11.2 us -> 10.2 us  [swap(): return lax.ppermute(value, axis, [(i, i ^ step) for i in range(size)])]
  transfers between devices with their start and end apart: 29 -> 29, of which waited for: 21 -> 17; matrix products, arithmetic and copies ran while one was open for 0% -> 0% of each run, Pallas kernels for 11% -> 16%
where the time goes in v6:
time: 77.7 us; the launch traced here: 77.5 us
  Pallas kernels  31.9 us (41%)
  starting transfers between devices  29.5 us (38%)
  waiting for transfers between devices  14.5 us (19%)
  between operations  0.88 us (1%)
    pallas_call x20, Pallas kernels, run(): pl.pallas_call(kernel, out_shape=out_shape, in_specs=[small] * scalars +...  31.9 us
    ppermute x15, starting transfers between devices, swap_both(): return lax.ppermute(value, ('row', 'proto'), pairs)  17.5 us
    ppermute x14, starting transfers between devices, swap(): return lax.ppermute(value, axis, [(i, i ^ step) for i in range(size)])  12 us
    ppermute x14, waiting for transfers between devices, swap(): return lax.ppermute(value, axis, [(i, i ^ step) for i in range(size)])  10.2 us
    ppermute x15, waiting for transfers between devices, swap_both(): return lax.ppermute(value, ('row', 'proto'), pairs)  4.35 us
  transfers between devices with their start and end apart: 29, of which 17 were waited for; matrix products, arithmetic and copies ran while one was open for 0% of the time, Pallas kernels for 16%

profile of v6, /device:TPU:0, one launch (start us, length us, event | category | flops | bytes accessed | tf_op | source)
XLA Modules:
  0.0 77.5 jit_solution(14171931933155228651)
XLA Ops:
  0.6 0.1 pad_add_fusion.ids
  0.7 1.0 %prepare.1.refs_0_ = bf16[144,256]{1,0:T(8,128)(2,1)S(1)} custom-call(s32[2]{0:T(128)S(1)} %pad_add_fusion.ids, bf16[256,128]{1,0:T(8,128)(2,1)} %embeddings.1, bf16[256,128]{1,0:T(8,128)(2,1)} %second_view.1, f32[1,256]{1,0:T(1,128)} %bitcast.19), custom_call_target="tpu_custom_call" | custom-call | tf_op jit(solution)/shard_map/prepare/pallas_call | solution.py:304
  1.7 5.1 %collective-permute-start.2 = (bf16[144,256]{1,0:T(8,128)(2,1)S(1)}, bf16[144,256]{1,0:T(8,128)(2,1)S(1)}, u32[]{:S(2)}, u32[]{:S(2)}) collective-permute-start(bf16[144,256]{1,0:T(8,128)(2,1)S(1)} %prepare.1.refs_0_), channel_id=1, source_target_pairs={{0,24},{4,28},{8,16},{12,20},{16,8},{20,12},{24,0},{28,4},{1,25},{... | collective-permute-start | bytes 221192 | tf_op jit(solution)/shard_map/ppermute | solution.py:28
  6.8 0.0 collective-permute-start.1
  6.8 0.6 collective-permute-start
  7.5 1.7 %collective-permute-start.4 = (bf16[144,256]{1,0:T(8,128)(2,1)S(1)}, bf16[144,256]{1,0:T(8,128)(2,1)S(1)}, u32[]{:S(2)}, u32[]{:S(2)}) collective-permute-start(bf16[144,256]{1,0:T(8,128)(2,1)S(1)} %prepare.1.refs_0_), channel_id=1, source_target_pairs={{0,4},{4,0},{8,12},{12,8},{16,20},{20,16},{24,28},{28,24},{1,5},{5... | collective-permute-start | bytes 221192 | tf_op jit(solution)/shard_map/ppermute | solution.py:28
  9.1 0.4 collective-permute-done.2.refs_3_
  9.6 1.9 %collective-permute-start.7 = (bf16[144,256]{1,0:T(8,128)(2,1)S(1)}, bf16[144,256]{1,0:T(8,128)(2,1)S(1)}, u32[]{:S(2)}, u32[]{:S(2)}) collective-permute-start(bf16[144,256]{1,0:T(8,128)(2,1)S(1)} %collective-permute-done.2.refs_3_), channel_id=1, source_target_pairs={{0,4},{4,0},{8,12},{12,8},{16,20},{20,16},{24,28},{28,24},{1,5},{5... | collective-permute-start | bytes 221192 | tf_op jit(solution)/shard_map/ppermute | solution.py:28
  11.5 1.6 %collective-permute-done.1.refs_2_ = bf16[144,256]{1,0:T(8,128)(2,1)S(1)} collective-permute-done((bf16[144,256]{1,0:T(8,128)(2,1)S(1)}, bf16[144,256]{1,0:T(8,128)(2,1)S(1)}, u32[]{:S(2)}, u32[]{:S(2)}) %collective-permute-start.1) | collective-permute-done | bytes 73760 | tf_op jit(solution)/shard_map/ppermute | solution.py:28
  13.0 1.5 %collective-permute-start.6 = (bf16[144,256]{1,0:T(8,128)(2,1)S(1)}, bf16[144,256]{1,0:T(8,128)(2,1)S(1)}, u32[]{:S(2)}, u32[]{:S(2)}) collective-permute-start(bf16[144,256]{1,0:T(8,128)(2,1)S(1)} %collective-permute-done.1.refs_2_), channel_id=1, source_target_pairs={{0,4},{4,0},{8,12},{12,8},{16,20},{20,16},{24,28},{28,24},{1,5},{5... | collective-permute-start | bytes 221192 | tf_op jit(solution)/shard_map/ppermute | solution.py:28
  14.6 0.0 collective-permute-done.refs_1_
  14.6 0.5 collective-permute-start.5
  15.1 2.0 %turn.1 = (bf16[2048,256]{1,0:T(8,128)(2,1)S(1)}, bf16[128,2048]{1,0:T(8,128)(2,1)S(1)}, f32[8,128]{1,0:T(8,128)S(1)}) custom-call(s32[2]{0:T(128)S(1)} %pad_add_fusion.ids, bf16[4096,128]{1,0:T(8,128)(2,1)} %protos.1, f32[1,4096]{1,0:T(1,128)} %bitcast.18), custom_call_target="tpu_custom_call" | custom-call | tf_op jit(solution)/shard_map/turn/pallas_call | solution.py:304
  17.1 0.1 collective-permute-start.3
  17.2 0.0 collective-permute-done.7.refs_3_
  17.2 0.9 %collective-permute-done.6.refs_2_ = bf16[144,256]{1,0:T(8,128)(2,1)S(1)} collective-permute-done((bf16[144,256]{1,0:T(8,128)(2,1)S(1)}, bf16[144,256]{1,0:T(8,128)(2,1)S(1)}, u32[]{:S(2)}, u32[]{:S(2)}) %collective-permute-start.6) | collective-permute-done | bytes 73760 | tf_op jit(solution)/shard_map/ppermute | solution.py:28
  18.1 0.8 %collective-permute-done.5.refs_1_ = bf16[144,256]{1,0:T(8,128)(2,1)S(1)} collective-permute-done((bf16[144,256]{1,0:T(8,128)(2,1)S(1)}, bf16[144,256]{1,0:T(8,128)(2,1)S(1)}, u32[]{:S(2)}, u32[]{:S(2)}) %collective-permute-start.5) | collective-permute-done | bytes 73760 | tf_op jit(solution)/shard_map/ppermute | solution.py:28
  18.9 0.1 collective-permute-start.8
  19.0 0.0 collective-permute-done.3.theirs_a
  19.0 1.6 %collective-permute-done.8.theirs_b = bf16[4,144,256]{2,1,0:T(8,128)(2,1)S(1)} collective-permute-done((bf16[4,144,256]{2,1,0:T(8,128)(2,1)S(1)}, bf16[4,144,256]{2,1,0:T(8,128)(2,1)S(1)}, u32[]{:S(2)}, u32[]{:S(2)}) %collective-permute-start.8) | collective-permute-done | bytes 294944 | tf_op jit(solution)/shard_map/ppermute | solution.py:28
  20.6 6.3 %plan.1 = (f32[2048,2048]{1,0:T(8,128)S(1)}, f32[2,2048,128]{2,1,0:T(8,128)S(1)}, f32[2,2048]{1,0:T(2,128)S(1)}, bf16[256,2048]{1,0:T(8,128)(2,1)S(1)}, bf16[128,2048]{1,0:T(8,128)(2,1)S(1)}) custom-call(s32[2]{0:T(128)S(1)} %pad_add_fusion.ids, bf16[2048,256]{1,0:T(8,128)(2,1)S(1)} %get-tuple-element.32.protos, bf16[4,144,256]{2,1,0:T(8,128)(2,1)S(1)} %stack.14.mine_a, ...), custom_call_target="tpu_custom_call" | custom-call | tf_op jit(solution)/shard_map/plan/pallas_call | solution.py:304
  26.9 0.2 collective-permute-start.9
  27.1 1.1 %collective-permute-done.9.right = f32[2,2048]{1,0:T(2,128)S(1)} collective-permute-done((f32[2,2048]{1,0:T(2,128)S(1)}, f32[2,2048]{1,0:T(2,128)S(1)}, u32[]{:S(2)}, u32[]{:S(2)}) %collective-permute-start.9) | collective-permute-done | bytes 16416 | tf_op jit(solution)/shard_map/ppermute | solution.py:28
  28.2 2.0 %collective-permute-start.12 = (f32[2,2048]{1,0:T(2,128)S(1)}, f32[2,2048]{1,0:T(2,128)S(1)}, u32[]{:S(2)}, u32[]{:S(2)}) collective-permute-start(f32[2,2048]{1,0:T(2,128)S(1)} %add.28.after.refs_0_), channel_id=1, source_target_pairs={{0,6},{1,7},{2,4},{3,5},{4,2},{5,3},{6,0},{7,1},{8,14},{9,15},{10,... | collective-permute-start | bytes 49160 | tf_op jit(solution)/shard_map/ppermute | solution.py:325
  30.1 1.0 %collective-permute-start.11 = (f32[2,2048]{1,0:T(2,128)S(1)}, f32[2,2048]{1,0:T(2,128)S(1)}, u32[]{:S(2)}, u32[]{:S(2)}) collective-permute-start(f32[2,2048]{1,0:T(2,128)S(1)} %add.28.after.refs_0_), channel_id=1, source_target_pairs={{0,4},{1,5},{2,6},{3,7},{4,0},{5,1},{6,2},{7,3},{8,12},{9,13},{10,... | collective-permute-start | bytes 49160 | tf_op jit(solution)/shard_map/ppermute | solution.py:325
  31.1 0.5 collective-permute-start.10
  31.7 1.9 %embed_before.1 = (f32[2048,512]{1,0:T(8,128)S(1)}, f32[8,128]{1,0:T(8,128)S(1)}) custom-call(bf16[2048,256]{1,0:T(8,128)(2,1)S(1)} %get-tuple-element.32.protos, bf16[256,2048]{1,0:T(8,128)(2,1)S(1)} %get-tuple-element.37.emb_ext, f32[2,2048]{1,0:T(2,128)S(1)} %add.28.after.refs_0_), custom_call_target="tpu_custom_call" | custom-call | tf_op jit(solution)/shard_map/embed_before/pallas_call | solution.py:304
  33.6 0.3 collective-permute-done.11.refs_2_
  33.9 1.0 %collective-permute-done.10.refs_1_ = f32[2,2048]{1,0:T(2,128)S(1)} collective-permute-done((f32[2,2048]{1,0:T(2,128)S(1)}, f32[2,2048]{1,0:T(2,128)S(1)}, u32[]{:S(2)}, u32[]{:S(2)}) %collective-permute-start.10) | collective-permute-done | bytes 16416 | tf_op jit(solution)/shard_map/ppermute | solution.py:325
  34.9 2.9 %sweep.3 = (f32[2048,2048]{1,0:T(8,128)S(1)}, f32[2,2048]{1,0:T(2,128)S(1)}, f32[1,2048]{1,0:T(1,128)S(1)}) custom-call(f32[2048,2048]{1,0:T(8,128)S(1)} %get-tuple-element.34.plan, f32[2,2048,128]{2,1,0:T(8,128)S(1)} %get-tuple-element.35.cols, f32[2,2048]{1,0:T(2,128)S(1)} %add.28.after.refs_0_, ...), custom_call_target="tpu_custom_call", output_to_operand_aliasing={{0}: (0, {})} | custom-call | tf_op jit(solution)/shard_map/sweep/pallas_call | solution.py:304
  37.8 0.1 collective-permute-start.13
  37.9 1.2 %collective-permute-done.13.right = f32[1,2048]{1,0:T(1,128)S(1)} collective-permute-done((f32[1,2048]{1,0:T(1,128)S(1)}, f32[1,2048]{1,0:T(1,128)S(1)}, u32[]{:S(2)}, u32[]{:S(2)}) %collective-permute-start.13) | collective-permute-done | bytes 8224 | tf_op jit(solution)/shard_map/ppermute | solution.py:28
  39.0 1.0 %collective-permute-start.16 = (f32[1,2048]{1,0:T(1,128)S(1)}, f32[1,2048]{1,0:T(1,128)S(1)}, u32[]{:S(2)}, u32[]{:S(2)}) collective-permute-start(f32[1,2048]{1,0:T(1,128)S(1)} %add.29.after.refs_1_), channel_id=1, source_target_pairs={{0,6},{1,7},{2,4},{3,5},{4,2},{5,3},{6,0},{7,1},{8,14},{9,15},{10,... | collective-permute-start | bytes 24584 | tf_op jit(solution)/shard_map/ppermute | solution.py:325
  40.0 1.0 %collective-permute-start.15 = (f32[1,2048]{1,0:T(1,128)S(1)}, f32[1,2048]{1,0:T(1,128)S(1)}, u32[]{:S(2)}, u32[]{:S(2)}) collective-permute-start(f32[1,2048]{1,0:T(1,128)S(1)} %add.29.after.refs_1_), channel_id=1, source_target_pairs={{0,4},{1,5},{2,6},{3,7},{4,0},{5,1},{6,2},{7,3},{8,12},{9,13},{10,... | collective-permute-start | bytes 24584 | tf_op jit(solution)/shard_map/ppermute | solution.py:325
  41.0 1.5 %collective-permute-start.14 = (f32[1,2048]{1,0:T(1,128)S(1)}, f32[1,2048]{1,0:T(1,128)S(1)}, u32[]{:S(2)}, u32[]{:S(2)}) collective-permute-start(f32[1,2048]{1,0:T(1,128)S(1)} %add.29.after.refs_1_), channel_id=1, source_target_pairs={{0,2},{1,3},{2,0},{3,1},{4,6},{5,7},{6,4},{7,5},{8,10},{9,11},{10,... | collective-permute-start | bytes 24584 | tf_op jit(solution)/shard_map/ppermute | solution.py:325
  42.5 2.0 %proto_before.1 = (f32[512,2048]{1,0:T(8,128)S(1)}, f32[512,128]{1,0:T(8,128)S(1)}, f32[8,128]{1,0:T(8,128)S(1)}) custom-call(s32[2]{0:T(128)S(1)} %pad_add_fusion.ids, bf16[2048,256]{1,0:T(8,128)(2,1)S(1)} %get-tuple-element.32.protos, bf16[256,2048]{1,0:T(8,128)(2,1)S(1)} %get-tuple-element.37.emb_ext, bf16[128,2048]{1,0:T(8,128)(2,1)S(1)} %get-tuple-element.42.view_t, ...), custom_call_target="tpu_custom_call" | custom-call | tf_op jit(solution)/shard_map/proto_before/pallas_call | solution.py:304
  44.6 0.1 collective-permute-done.14.refs_2_
  44.7 2.9 %sweep.4 = (f32[2048,2048]{1,0:T(8,128)S(1)}, f32[1,2048]{1,0:T(1,128)S(1)}) custom-call(f32[2048,2048]{1,0:T(8,128)S(1)} %get-tuple-element.39.plan, f32[2,2048,128]{2,1,0:T(8,128)S(1)} %get-tuple-element.35.cols, f32[2,2048]{1,0:T(2,128)S(1)} %get-tuple-element.40.refs_0_.sums, f32[1,2048]{1,0:T(1,128)S(1)} %add.29.after.refs_1_, ...), custom_call_target="tpu_custom_call", output_to_operand_aliasing={{0}: (0, {})} | custom-call | tf_op jit(solution)/shard_map/sweep/pallas_call | solution.py:304
  47.6 0.1 collective-permute-start.17
  47.7 1.2 %collective-permute-done.17.right = f32[1,2048]{1,0:T(1,128)S(1)} collective-permute-done((f32[1,2048]{1,0:T(1,128)S(1)}, f32[1,2048]{1,0:T(1,128)S(1)}, u32[]{:S(2)}, u32[]{:S(2)}) %collective-permute-start.17) | collective-permute-done | bytes 8224 | tf_op jit(solution)/shard_map/ppermute | solution.py:28
  48.8 2.0 %collective-permute-start.20 = (f32[1,2048]{1,0:T(1,128)S(1)}, f32[1,2048]{1,0:T(1,128)S(1)}, u32[]{:S(2)}, u32[]{:S(2)}) collective-permute-start(f32[1,2048]{1,0:T(1,128)S(1)} %add.30.after.refs_1_), channel_id=1, source_target_pairs={{0,6},{1,7},{2,4},{3,5},{4,2},{5,3},{6,0},{7,1},{8,14},{9,15},{10,... | collective-permute-start | bytes 24584 | tf_op jit(solution)/shard_map/ppermute | solution.py:325
  50.8 1.0 %collective-permute-start.19 = (f32[1,2048]{1,0:T(1,128)S(1)}, f32[1,2048]{1,0:T(1,128)S(1)}, u32[]{:S(2)}, u32[]{:S(2)}) collective-permute-start(f32[1,2048]{1,0:T(1,128)S(1)} %add.30.after.refs_1_), channel_id=1, source_target_pairs={{0,4},{1,5},{2,6},{3,7},{4,0},{5,1},{6,2},{7,3},{8,12},{9,13},{10,... | collective-permute-start | bytes 24584 | tf_op jit(solution)/shard_map/ppermute | solution.py:325
  51.8 0.5 collective-permute-start.18
  52.3 2.3 %cotangent.2 = (f32[2048,512]{1,0:T(8,128)S(1)}, f32[8,128]{1,0:T(8,128)S(1)}) custom-call(s32[2]{0:T(128)S(1)} %pad_add_fusion.ids, bf16[2048,256]{1,0:T(8,128)(2,1)S(1)} %get-tuple-element.32.protos, bf16[128,2048]{1,0:T(8,128)(2,1)S(1)} %get-tuple-element.42.view_t, f32[1,2048]{1,0:T(1,128)S(1)} %add.30.after.refs_1_), custom_call_target="tpu_custom_call" | custom-call | tf_op jit(solution)/shard_map/cotangent/pallas_call | solution.py:304
  54.6 0.8 %collective-permute-done.18.refs_2_ = f32[1,2048]{1,0:T(1,128)S(1)} collective-permute-done((f32[1,2048]{1,0:T(1,128)S(1)}, f32[1,2048]{1,0:T(1,128)S(1)}, u32[]{:S(2)}, u32[]{:S(2)}) %collective-permute-start.18) | collective-permute-done | bytes 8224 | tf_op jit(solution)/shard_map/ppermute | solution.py:325
  55.4 2.9 %sweep.5 = (f32[2048,2048]{1,0:T(8,128)S(1)}, f32[1,2048]{1,0:T(1,128)S(1)}) custom-call(f32[2048,2048]{1,0:T(8,128)S(1)} %get-tuple-element.44.plan, f32[2,2048,128]{2,1,0:T(8,128)S(1)} %get-tuple-element.35.cols, f32[2,2048]{1,0:T(2,128)S(1)} %get-tuple-element.40.refs_0_.sums, f32[1,2048]{1,0:T(1,128)S(1)} %add.30.after.refs_1_, ...), custom_call_target="tpu_custom_call", output_to_operand_aliasing={{0}: (0, {})} | custom-call | tf_op jit(solution)/shard_map/sweep/pallas_call | solution.py:304
  58.4 0.1 collective-permute-start.21
  58.4 1.2 %collective-permute-done.21.right = f32[1,2048]{1,0:T(1,128)S(1)} collective-permute-done((f32[1,2048]{1,0:T(1,128)S(1)}, f32[1,2048]{1,0:T(1,128)S(1)}, u32[]{:S(2)}, u32[]{:S(2)}) %collective-permute-start.21) | collective-permute-done | bytes 8224 | tf_op jit(solution)/shard_map/ppermute | solution.py:28
  59.6 1.2 %collective-permute-start.24 = (f32[1,2048]{1,0:T(1,128)S(1)}, f32[1,2048]{1,0:T(1,128)S(1)}, u32[]{:S(2)}, u32[]{:S(2)}) collective-permute-start(f32[1,2048]{1,0:T(1,128)S(1)} %add.31.after.refs_0_), channel_id=1, source_target_pairs={{0,6},{1,7},{2,4},{3,5},{4,2},{5,3},{6,0},{7,1},{8,14},{9,15},{10,... | collective-permute-start | bytes 24584 | tf_op jit(solution)/shard_map/ppermute | solution.py:325
  60.8 1.0 %collective-permute-start.23 = (f32[1,2048]{1,0:T(1,128)S(1)}, f32[1,2048]{1,0:T(1,128)S(1)}, u32[]{:S(2)}, u32[]{:S(2)}) collective-permute-start(f32[1,2048]{1,0:T(1,128)S(1)} %add.31.after.refs_0_), channel_id=1, source_target_pairs={{0,4},{1,5},{2,6},{3,7},{4,0},{5,1},{6,2},{7,3},{8,12},{9,13},{10,... | collective-permute-start | bytes 24584 | tf_op jit(solution)/shard_map/ppermute | solution.py:325
  61.8 1.3 %collective-permute-start.22 = (f32[1,2048]{1,0:T(1,128)S(1)}, f32[1,2048]{1,0:T(1,128)S(1)}, u32[]{:S(2)}, u32[]{:S(2)}) collective-permute-start(f32[1,2048]{1,0:T(1,128)S(1)} %add.31.after.refs_0_), channel_id=1, source_target_pairs={{0,2},{1,3},{2,0},{3,1},{4,6},{5,7},{6,4},{7,5},{8,10},{9,11},{10,... | collective-permute-start | bytes 24584 | tf_op jit(solution)/shard_map/ppermute | solution.py:325
  63.1 1.4 %cotangent.3 = (f32[512,2048]{1,0:T(8,128)S(1)}, f32[8,128]{1,0:T(8,128)S(1)}) custom-call(s32[2]{0:T(128)S(1)} %pad_add_fusion.ids, bf16[2048,256]{1,0:T(8,128)(2,1)S(1)} %get-tuple-element.32.protos, bf16[128,2048]{1,0:T(8,128)(2,1)S(1)} %get-tuple-element.42.view_t, f32[1,2048]{1,0:T(1,128)S(1)} %add.31.after.refs_0_), custom_call_target="tpu_custom_call" | custom-call | tf_op jit(solution)/shard_map/cotangent/pallas_call | solution.py:304
  64.5 0.9 %collective-permute-done.22.refs_1_ = f32[1,2048]{1,0:T(1,128)S(1)} collective-permute-done((f32[1,2048]{1,0:T(1,128)S(1)}, f32[1,2048]{1,0:T(1,128)S(1)}, u32[]{:S(2)}, u32[]{:S(2)}) %collective-permute-start.22) | collective-permute-done | bytes 8224 | tf_op jit(solution)/shard_map/ppermute | solution.py:325
  65.4 3.4 %embed_grad.1 = (f32[2048,128]{1,0:T(8,128)S(1)}, f32[1,2048]{1,0:T(1,128)S(1)}, f32[4,64,128]{2,1,0:T(8,128)S(1)}, f32[4,64,128]{2,1,0:T(8,128)S(1)}) custom-call(s32[2]{0:T(128)S(1)} %pad_add_fusion.ids, f32[2048,2048]{1,0:T(8,128)S(1)} %get-tuple-element.47.plan, f32[2,2048,128]{2,1,0:T(8,128)S(1)} %get-tuple-element.35.cols, ...), custom_call_target="tpu_custom_call" | custom-call | tf_op jit(solution)/shard_map/embed_grad/pallas_call | solution.py:304
  68.8 0.1 collective-permute-start.25
  68.9 1.0 %proto_grad.2 = (f32[512,128]{1,0:T(8,128)S(1)}, f32[8,128]{1,0:T(8,128)S(1)}) custom-call(s32[2]{0:T(128)S(1)} %pad_add_fusion.ids, bf16[256,2048]{1,0:T(8,128)(2,1)S(1)} %get-tuple-element.37.emb_ext, f32[512,2048]{1,0:T(8,128)S(1)} %get-tuple-element.55.entries, f32[512,2048]{1,0:T(8,128)S(1)} %get-tuple-element.56.cots, ...), custom_call_target="tpu_custom_call" | custom-call | tf_op jit(solution)/shard_map/proto_grad/pallas_call | solution.py:304
  69.9 0.3 collective-permute-done.25.right
  70.3 1.4 %collective-permute-start.26 = (f32[64,128]{1,0:T(8,128)S(1)}, f32[64,128]{1,0:T(8,128)S(1)}, u32[]{:S(2)}, u32[]{:S(2)}) collective-permute-start(f32[64,128]{1,0:T(8,128)S(1)} %get-tuple-element.62), channel_id=1, source_target_pairs={{0,2},{1,3},{2,0},{3,1},{4,6},{5,7},{6,4},{7,5},{8,10},{9,11},{10,... | collective-permute-start | bytes 98312 | tf_op jit(solution)/shard_map/ppermute | solution.py:325
  71.7 1.2 %collective-permute-start.28 = (f32[64,128]{1,0:T(8,128)S(1)}, f32[64,128]{1,0:T(8,128)S(1)}, u32[]{:S(2)}, u32[]{:S(2)}) collective-permute-start(f32[64,128]{1,0:T(8,128)S(1)} %get-tuple-element.63), channel_id=1, source_target_pairs={{0,6},{1,7},{2,4},{3,5},{4,2},{5,3},{6,0},{7,1},{8,14},{9,15},{10,... | collective-permute-start | bytes 98312 | tf_op jit(solution)/shard_map/ppermute | solution.py:325
  72.8 1.0 %collective-permute-start.27 = (f32[64,128]{1,0:T(8,128)S(1)}, f32[64,128]{1,0:T(8,128)S(1)}, u32[]{:S(2)}, u32[]{:S(2)}) collective-permute-start(f32[64,128]{1,0:T(8,128)S(1)} %get-tuple-element.64), channel_id=1, source_target_pairs={{0,4},{1,5},{2,6},{3,7},{4,0},{5,1},{6,2},{7,3},{8,12},{9,13},{10,... | collective-permute-start | bytes 98312 | tf_op jit(solution)/shard_map/ppermute | solution.py:325
  73.8 1.7 %proto_grad.3 = f32[512,128]{1,0:T(8,128)} custom-call(s32[2]{0:T(128)S(1)} %pad_add_fusion.ids, bf16[256,2048]{1,0:T(8,128)(2,1)S(1)} %get-tuple-element.37.emb_ext, f32[512,2048]{1,0:T(8,128)S(1)} %get-tuple-element.55.entries, f32[512,2048]{1,0:T(8,128)S(1)} %get-tuple-element.56.cots, f32[512,128]{1,0:T(8,128)S(1)} %get-tuple-element.61.so_far, ...), custom_call_target="tpu_custom_call" | custom-call | tf_op jit(solution)/shard_map/proto_grad/pallas_call | solution.py:304
  75.6 0.9 %collective-permute-done.28 = f32[64,128]{1,0:T(8,128)S(1)} collective-permute-done((f32[64,128]{1,0:T(8,128)S(1)}, f32[64,128]{1,0:T(8,128)S(1)}, u32[]{:S(2)}, u32[]{:S(2)}) %collective-permute-start.28) | collective-permute-done | bytes 32800 | tf_op jit(solution)/shard_map/ppermute | solution.py:325
  76.5 0.3 collective-permute-done.27
  76.8 0.6 fusion.2
  (17 shorter events, 0.1 us)
Async XLA Ops:
  1.7 7.9 %collective-permute-start.2 = (bf16[144,256]{1,0:T(8,128)(2,1)S(1)}, bf16[144,256]{1,0:T(8,128)(2,1)S(1)}, u32[]{:S(2)}, u32[]{:S(2)}) collective-permute-start(bf16[144,256]{1,0:T(8,128)(2,1)S(1)} %prepare.1.refs_0_), channel_id=1, source_target_pairs={{0,24},{4,28},{8,16},{12,20},{16,8},{20,12},{24,0},{28,4},{1,25},{... | collective-permute-start | bytes 221192 | tf_op jit(solution)/shard_map/ppermute | solution.py:28
  6.8 6.2 %collective-permute-start.1 = (bf16[144,256]{1,0:T(8,128)(2,1)S(1)}, bf16[144,256]{1,0:T(8,128)(2,1)S(1)}, u32[]{:S(2)}, u32[]{:S(2)}) collective-permute-start(bf16[144,256]{1,0:T(8,128)(2,1)S(1)} %prepare.1.refs_0_), channel_id=1, source_target_pairs={{0,16},{4,20},{8,24},{12,28},{16,0},{20,4},{24,8},{28,12},{1,17},{... | collective-permute-start | bytes 221192 | tf_op jit(solution)/shard_map/ppermute | solution.py:28
  6.8 7.7 %collective-permute-start = (bf16[144,256]{1,0:T(8,128)(2,1)S(1)}, bf16[144,256]{1,0:T(8,128)(2,1)S(1)}, u32[]{:S(2)}, u32[]{:S(2)}) collective-permute-start(bf16[144,256]{1,0:T(8,128)(2,1)S(1)} %prepare.1.refs_0_), channel_id=1, source_target_pairs={{0,8},{4,12},{8,0},{12,4},{16,24},{20,28},{24,16},{28,20},{1,9},{5... | collective-permute-start | bytes 221192 | tf_op jit(solution)/shard_map/ppermute | solution.py:28
  7.5 9.7 %collective-permute-start.4 = (bf16[144,256]{1,0:T(8,128)(2,1)S(1)}, bf16[144,256]{1,0:T(8,128)(2,1)S(1)}, u32[]{:S(2)}, u32[]{:S(2)}) collective-permute-start(bf16[144,256]{1,0:T(8,128)(2,1)S(1)} %prepare.1.refs_0_), channel_id=1, source_target_pairs={{0,4},{4,0},{8,12},{12,8},{16,20},{20,16},{24,28},{28,24},{1,5},{5... | collective-permute-start | bytes 221192 | tf_op jit(solution)/shard_map/ppermute | solution.py:28
  9.6 7.6 %collective-permute-start.7 = (bf16[144,256]{1,0:T(8,128)(2,1)S(1)}, bf16[144,256]{1,0:T(8,128)(2,1)S(1)}, u32[]{:S(2)}, u32[]{:S(2)}) collective-permute-start(bf16[144,256]{1,0:T(8,128)(2,1)S(1)} %collective-permute-done.2.refs_3_), channel_id=1, source_target_pairs={{0,4},{4,0},{8,12},{12,8},{16,20},{20,16},{24,28},{28,24},{1,5},{5... | collective-permute-start | bytes 221192 | tf_op jit(solution)/shard_map/ppermute | solution.py:28
  13.0 5.1 %collective-permute-start.6 = (bf16[144,256]{1,0:T(8,128)(2,1)S(1)}, bf16[144,256]{1,0:T(8,128)(2,1)S(1)}, u32[]{:S(2)}, u32[]{:S(2)}) collective-permute-start(bf16[144,256]{1,0:T(8,128)(2,1)S(1)} %collective-permute-done.1.refs_2_), channel_id=1, source_target_pairs={{0,4},{4,0},{8,12},{12,8},{16,20},{20,16},{24,28},{28,24},{1,5},{5... | collective-permute-start | bytes 221192 | tf_op jit(solution)/shard_map/ppermute | solution.py:28
  14.6 4.4 %collective-permute-start.5 = (bf16[144,256]{1,0:T(8,128)(2,1)S(1)}, bf16[144,256]{1,0:T(8,128)(2,1)S(1)}, u32[]{:S(2)}, u32[]{:S(2)}) collective-permute-start(bf16[144,256]{1,0:T(8,128)(2,1)S(1)} %collective-permute-done.refs_1_), channel_id=1, source_target_pairs={{0,4},{4,0},{8,12},{12,8},{16,20},{20,16},{24,28},{28,24},{1,5},{5... | collective-permute-start | bytes 221192 | tf_op jit(solution)/shard_map/ppermute | solution.py:28
  17.1 2.0 %collective-permute-start.3 = (bf16[4,144,256]{2,1,0:T(8,128)(2,1)S(1)}, bf16[4,144,256]{2,1,0:T(8,128)(2,1)S(1)}, u32[]{:S(2)}, u32[]{:S(2)}) collective-permute-start(bf16[4,144,256]{2,1,0:T(8,128)(2,1)S(1)} %stack.14.mine_a), channel_id=1, source_target_pairs={{0,1},{1,0},{2,3},{3,2},{4,5},{5,4},{6,7},{7,6},{8,9},{9,8},{10,11... | collective-permute-start | bytes 884744 | tf_op jit(solution)/shard_map/ppermute | solution.py:28
  18.9 1.6 %collective-permute-start.8 = (bf16[4,144,256]{2,1,0:T(8,128)(2,1)S(1)}, bf16[4,144,256]{2,1,0:T(8,128)(2,1)S(1)}, u32[]{:S(2)}, u32[]{:S(2)}) collective-permute-start(bf16[4,144,256]{2,1,0:T(8,128)(2,1)S(1)} %stack.15.mine_b), channel_id=1, source_target_pairs={{0,1},{1,0},{2,3},{3,2},{4,5},{5,4},{6,7},{7,6},{8,9},{9,8},{10,11... | collective-permute-start | bytes 884744 | tf_op jit(solution)/shard_map/ppermute | solution.py:28
  26.9 1.2 %collective-permute-start.9 = (f32[2,2048]{1,0:T(2,128)S(1)}, f32[2,2048]{1,0:T(2,128)S(1)}, u32[]{:S(2)}, u32[]{:S(2)}) collective-permute-start(f32[2,2048]{1,0:T(2,128)S(1)} %get-tuple-element.36.left), channel_id=1, source_target_pairs={{0,1},{1,0},{2,3},{3,2},{4,5},{5,4},{6,7},{7,6},{8,9},{9,8},{10,11... | collective-permute-start | bytes 49160 | tf_op jit(solution)/shard_map/ppermute | solution.py:28
  28.2 5.4 %collective-permute-start.12 = (f32[2,2048]{1,0:T(2,128)S(1)}, f32[2,2048]{1,0:T(2,128)S(1)}, u32[]{:S(2)}, u32[]{:S(2)}) collective-permute-start(f32[2,2048]{1,0:T(2,128)S(1)} %add.28.after.refs_0_), channel_id=1, source_target_pairs={{0,6},{1,7},{2,4},{3,5},{4,2},{5,3},{6,0},{7,1},{8,14},{9,15},{10,... | collective-permute-start | bytes 49160 | tf_op jit(solution)/shard_map/ppermute | solution.py:325
  30.1 3.7 %collective-permute-start.11 = (f32[2,2048]{1,0:T(2,128)S(1)}, f32[2,2048]{1,0:T(2,128)S(1)}, u32[]{:S(2)}, u32[]{:S(2)}) collective-permute-start(f32[2,2048]{1,0:T(2,128)S(1)} %add.28.after.refs_0_), channel_id=1, source_target_pairs={{0,4},{1,5},{2,6},{3,7},{4,0},{5,1},{6,2},{7,3},{8,12},{9,13},{10,... | collective-permute-start | bytes 49160 | tf_op jit(solution)/shard_map/ppermute | solution.py:325
  31.1 3.7 %collective-permute-start.10 = (f32[2,2048]{1,0:T(2,128)S(1)}, f32[2,2048]{1,0:T(2,128)S(1)}, u32[]{:S(2)}, u32[]{:S(2)}) collective-permute-start(f32[2,2048]{1,0:T(2,128)S(1)} %add.28.after.refs_0_), channel_id=1, source_target_pairs={{0,2},{1,3},{2,0},{3,1},{4,6},{5,7},{6,4},{7,5},{8,10},{9,11},{10,... | collective-permute-start | bytes 49160 | tf_op jit(solution)/shard_map/ppermute | solution.py:325
  37.8 1.2 %collective-permute-start.13 = (f32[1,2048]{1,0:T(1,128)S(1)}, f32[1,2048]{1,0:T(1,128)S(1)}, u32[]{:S(2)}, u32[]{:S(2)}) collective-permute-start(f32[1,2048]{1,0:T(1,128)S(1)} %get-tuple-element.41.left), channel_id=1, source_target_pairs={{0,1},{1,0},{2,3},{3,2},{4,5},{5,4},{6,7},{7,6},{8,9},{9,8},{10,11... | collective-permute-start | bytes 24584 | tf_op jit(solution)/shard_map/ppermute | solution.py:28
  39.0 5.5 %collective-permute-start.16 = (f32[1,2048]{1,0:T(1,128)S(1)}, f32[1,2048]{1,0:T(1,128)S(1)}, u32[]{:S(2)}, u32[]{:S(2)}) collective-permute-start(f32[1,2048]{1,0:T(1,128)S(1)} %add.29.after.refs_1_), channel_id=1, source_target_pairs={{0,6},{1,7},{2,4},{3,5},{4,2},{5,3},{6,0},{7,1},{8,14},{9,15},{10,... | collective-permute-start | bytes 24584 | tf_op jit(solution)/shard_map/ppermute | solution.py:325
  40.0 4.5 %collective-permute-start.15 = (f32[1,2048]{1,0:T(1,128)S(1)}, f32[1,2048]{1,0:T(1,128)S(1)}, u32[]{:S(2)}, u32[]{:S(2)}) collective-permute-start(f32[1,2048]{1,0:T(1,128)S(1)} %add.29.after.refs_1_), channel_id=1, source_target_pairs={{0,4},{1,5},{2,6},{3,7},{4,0},{5,1},{6,2},{7,3},{8,12},{9,13},{10,... | collective-permute-start | bytes 24584 | tf_op jit(solution)/shard_map/ppermute | solution.py:325
  41.0 3.7 %collective-permute-start.14 = (f32[1,2048]{1,0:T(1,128)S(1)}, f32[1,2048]{1,0:T(1,128)S(1)}, u32[]{:S(2)}, u32[]{:S(2)}) collective-permute-start(f32[1,2048]{1,0:T(1,128)S(1)} %add.29.after.refs_1_), channel_id=1, source_target_pairs={{0,2},{1,3},{2,0},{3,1},{4,6},{5,7},{6,4},{7,5},{8,10},{9,11},{10,... | collective-permute-start | bytes 24584 | tf_op jit(solution)/shard_map/ppermute | solution.py:325
  47.6 1.2 %collective-permute-start.17 = (f32[1,2048]{1,0:T(1,128)S(1)}, f32[1,2048]{1,0:T(1,128)S(1)}, u32[]{:S(2)}, u32[]{:S(2)}) collective-permute-start(f32[1,2048]{1,0:T(1,128)S(1)} %get-tuple-element.45.left), channel_id=1, source_target_pairs={{0,1},{1,0},{2,3},{3,2},{4,5},{5,4},{6,7},{7,6},{8,9},{9,8},{10,11... | collective-permute-start | bytes 24584 | tf_op jit(solution)/shard_map/ppermute | solution.py:28
  48.8 5.8 %collective-permute-start.20 = (f32[1,2048]{1,0:T(1,128)S(1)}, f32[1,2048]{1,0:T(1,128)S(1)}, u32[]{:S(2)}, u32[]{:S(2)}) collective-permute-start(f32[1,2048]{1,0:T(1,128)S(1)} %add.30.after.refs_1_), channel_id=1, source_target_pairs={{0,6},{1,7},{2,4},{3,5},{4,2},{5,3},{6,0},{7,1},{8,14},{9,15},{10,... | collective-permute-start | bytes 24584 | tf_op jit(solution)/shard_map/ppermute | solution.py:325
  50.8 3.8 %collective-permute-start.19 = (f32[1,2048]{1,0:T(1,128)S(1)}, f32[1,2048]{1,0:T(1,128)S(1)}, u32[]{:S(2)}, u32[]{:S(2)}) collective-permute-start(f32[1,2048]{1,0:T(1,128)S(1)} %add.30.after.refs_1_), channel_id=1, source_target_pairs={{0,4},{1,5},{2,6},{3,7},{4,0},{5,1},{6,2},{7,3},{8,12},{9,13},{10,... | collective-permute-start | bytes 24584 | tf_op jit(solution)/shard_map/ppermute | solution.py:325
  51.8 3.7 %collective-permute-start.18 = (f32[1,2048]{1,0:T(1,128)S(1)}, f32[1,2048]{1,0:T(1,128)S(1)}, u32[]{:S(2)}, u32[]{:S(2)}) collective-permute-start(f32[1,2048]{1,0:T(1,128)S(1)} %add.30.after.refs_1_), channel_id=1, source_target_pairs={{0,2},{1,3},{2,0},{3,1},{4,6},{5,7},{6,4},{7,5},{8,10},{9,11},{10,... | collective-permute-start | bytes 24584 | tf_op jit(solution)/shard_map/ppermute | solution.py:325
  58.4 1.2 %collective-permute-start.21 = (f32[1,2048]{1,0:T(1,128)S(1)}, f32[1,2048]{1,0:T(1,128)S(1)}, u32[]{:S(2)}, u32[]{:S(2)}) collective-permute-start(f32[1,2048]{1,0:T(1,128)S(1)} %get-tuple-element.51.left), channel_id=1, source_target_pairs={{0,1},{1,0},{2,3},{3,2},{4,5},{5,4},{6,7},{7,6},{8,9},{9,8},{10,11... | collective-permute-start | bytes 24584 | tf_op jit(solution)/shard_map/ppermute | solution.py:28
  59.6 4.9 %collective-permute-start.24 = (f32[1,2048]{1,0:T(1,128)S(1)}, f32[1,2048]{1,0:T(1,128)S(1)}, u32[]{:S(2)}, u32[]{:S(2)}) collective-permute-start(f32[1,2048]{1,0:T(1,128)S(1)} %add.31.after.refs_0_), channel_id=1, source_target_pairs={{0,6},{1,7},{2,4},{3,5},{4,2},{5,3},{6,0},{7,1},{8,14},{9,15},{10,... | collective-permute-start | bytes 24584 | tf_op jit(solution)/shard_map/ppermute | solution.py:325
  60.8 3.7 %collective-permute-start.23 = (f32[1,2048]{1,0:T(1,128)S(1)}, f32[1,2048]{1,0:T(1,128)S(1)}, u32[]{:S(2)}, u32[]{:S(2)}) collective-permute-start(f32[1,2048]{1,0:T(1,128)S(1)} %add.31.after.refs_0_), channel_id=1, source_target_pairs={{0,4},{1,5},{2,6},{3,7},{4,0},{5,1},{6,2},{7,3},{8,12},{9,13},{10,... | collective-permute-start | bytes 24584 | tf_op jit(solution)/shard_map/ppermute | solution.py:325
  61.8 3.7 %collective-permute-start.22 = (f32[1,2048]{1,0:T(1,128)S(1)}, f32[1,2048]{1,0:T(1,128)S(1)}, u32[]{:S(2)}, u32[]{:S(2)}) collective-permute-start(f32[1,2048]{1,0:T(1,128)S(1)} %add.31.after.refs_0_), channel_id=1, source_target_pairs={{0,2},{1,3},{2,0},{3,1},{4,6},{5,7},{6,4},{7,5},{8,10},{9,11},{10,... | collective-permute-start | bytes 24584 | tf_op jit(solution)/shard_map/ppermute | solution.py:325
  68.8 1.4 %collective-permute-start.25 = (f32[4,64,128]{2,1,0:T(8,128)S(1)}, f32[4,64,128]{2,1,0:T(8,128)S(1)}, u32[]{:S(2)}, u32[]{:S(2)}) collective-permute-start(f32[4,64,128]{2,1,0:T(8,128)S(1)} %get-tuple-element.54), channel_id=1, source_target_pairs={{0,1},{1,0},{2,3},{3,2},{4,5},{5,4},{6,7},{7,6},{8,9},{9,8},{10,11... | collective-permute-start | bytes 393224 | tf_op jit(solution)/shard_map/ppermute | solution.py:28
  70.3 5.3 %collective-permute-start.26 = (f32[64,128]{1,0:T(8,128)S(1)}, f32[64,128]{1,0:T(8,128)S(1)}, u32[]{:S(2)}, u32[]{:S(2)}) collective-permute-start(f32[64,128]{1,0:T(8,128)S(1)} %get-tuple-element.62), channel_id=1, source_target_pairs={{0,2},{1,3},{2,0},{3,1},{4,6},{5,7},{6,4},{7,5},{8,10},{9,11},{10,... | collective-permute-start | bytes 98312 | tf_op jit(solution)/shard_map/ppermute | solution.py:325
  71.7 4.8 %collective-permute-start.28 = (f32[64,128]{1,0:T(8,128)S(1)}, f32[64,128]{1,0:T(8,128)S(1)}, u32[]{:S(2)}, u32[]{:S(2)}) collective-permute-start(f32[64,128]{1,0:T(8,128)S(1)} %get-tuple-element.63), channel_id=1, source_target_pairs={{0,6},{1,7},{2,4},{3,5},{4,2},{5,3},{6,0},{7,1},{8,14},{9,15},{10,... | collective-permute-start | bytes 98312 | tf_op jit(solution)/shard_map/ppermute | solution.py:325
  72.8 4.0 %collective-permute-start.27 = (f32[64,128]{1,0:T(8,128)S(1)}, f32[64,128]{1,0:T(8,128)S(1)}, u32[]{:S(2)}, u32[]{:S(2)}) collective-permute-start(f32[64,128]{1,0:T(8,128)S(1)} %get-tuple-element.64), channel_id=1, source_target_pairs={{0,4},{1,5},{2,6},{3,7},{4,0},{5,1},{6,2},{7,3},{8,12},{9,13},{10,... | collective-permute-start | bytes 98312 | tf_op jit(solution)/shard_map/ppermute | solution.py:325

commit v7 on v6

--- a/solution.py
+++ b/solution.py
@@ -142,7 +142,7 @@
         cols_out[1, here, :] = -view_scale * lane_sums(weight) * inverse
         return carry
 
-    lax.fori_loop(0, count // CHUNK, step, 0)
+    lax.fori_loop(0, count // CHUNK, step, 0, unroll=True)
     sums_out[0:1, :] = jnp.sum(row_mass[...], axis=0, keepdims=True)
     sums_out[1:2, :] = -view_scale * jnp.sum(row_weight[...], axis=0, keepdims=True)
 
@@ -204,7 +204,7 @@
         total[...] += product
         return dual
 
-    last = lax.fori_loop(1, steps, step, duals(0))
+    last = lax.fori_loop(1, steps, step, duals(0), unroll=2)
     total[...] += by_cols(plan.at[chunk(steps - 1), :], last)
     part_out[...] = jnp.sum(total[...], axis=0, keepdims=True)
 
@@ -251,7 +251,7 @@
         duals_out[here, :] = by_rows(plan.at[here, :], cols, here, spread)
         return carry
 
-    lax.fori_loop(0, plan.shape[0] // STEP, duals, 0)
+    lax.fori_loop(0, plan.shape[0] // STEP, duals, 0, unroll=2)
     total = jnp.zeros((width, rows), F32)
     for start in range(0, plan.shape[0], CHUNK):
         here = slice(start, start + CHUNK)

time: 77.7 us -> 75.5 us (0.972)
  Pallas kernels: 31.9 us -> 29.8 us
    pallas_call x20, Pallas kernels: 31.9 us -> 29.8 us  [run(): pl.pallas_call(kernel, out_shape=out_shape, in_specs=[small] * scalars +...]
where the time goes in v7:
time: 75.5 us; the launch traced here: 75.3 us
  Pallas kernels  29.8 us (39%)
  starting transfers between devices  29.5 us (39%)
  waiting for transfers between devices  14.5 us (19%)
  between operations  0.88 us (1%)
    pallas_call x20, Pallas kernels, run(): pl.pallas_call(kernel, out_shape=out_shape, in_specs=[small] * scalars +...  29.8 us
    ppermute x15, starting transfers between devices, swap_both(): return lax.ppermute(value, ('row', 'proto'), pairs)  17.5 us
    ppermute x14, starting transfers between devices, swap(): return lax.ppermute(value, axis, [(i, i ^ step) for i in range(size)])  12 us
    ppermute x14, waiting for transfers between devices, swap(): return lax.ppermute(value, axis, [(i, i ^ step) for i in range(size)])  10.2 us
    ppermute x15, waiting for transfers between devices, swap_both(): return lax.ppermute(value, ('row', 'proto'), pairs)  4.35 us
  transfers between devices with their start and end apart: 29, of which 17 were waited for; matrix products, arithmetic and copies ran while one was open for 0% of the time, Pallas kernels for 16%

profile of v7, /device:TPU:0, one launch (start us, length us, event | category | flops | bytes accessed | tf_op | source)
XLA Modules:
  0.0 75.3 jit_solution(9522877760699644417)
XLA Ops:
  0.6 0.1 pad_add_fusion.ids
  0.7 1.0 %prepare.1.refs_0_ = bf16[144,256]{1,0:T(8,128)(2,1)S(1)} custom-call(s32[2]{0:T(128)S(1)} %pad_add_fusion.ids, bf16[256,128]{1,0:T(8,128)(2,1)} %embeddings.1, bf16[256,128]{1,0:T(8,128)(2,1)} %second_view.1, f32[1,256]{1,0:T(1,128)} %bitcast.19), custom_call_target="tpu_custom_call" | custom-call | tf_op jit(solution)/shard_map/prepare/pallas_call | solution.py:304
  1.7 5.1 %collective-permute-start.2 = (bf16[144,256]{1,0:T(8,128)(2,1)S(1)}, bf16[144,256]{1,0:T(8,128)(2,1)S(1)}, u32[]{:S(2)}, u32[]{:S(2)}) collective-permute-start(bf16[144,256]{1,0:T(8,128)(2,1)S(1)} %prepare.1.refs_0_), channel_id=1, source_target_pairs={{0,24},{4,28},{8,16},{12,20},{16,8},{20,12},{24,0},{28,4},{1,25},{... | collective-permute-start | bytes 221192 | tf_op jit(solution)/shard_map/ppermute | solution.py:28
  6.8 0.6 collective-permute-start
  7.5 1.7 %collective-permute-start.4 = (bf16[144,256]{1,0:T(8,128)(2,1)S(1)}, bf16[144,256]{1,0:T(8,128)(2,1)S(1)}, u32[]{:S(2)}, u32[]{:S(2)}) collective-permute-start(bf16[144,256]{1,0:T(8,128)(2,1)S(1)} %prepare.1.refs_0_), channel_id=1, source_target_pairs={{0,4},{4,0},{8,12},{12,8},{16,20},{20,16},{24,28},{28,24},{1,5},{5... | collective-permute-start | bytes 221192 | tf_op jit(solution)/shard_map/ppermute | solution.py:28
  9.1 0.4 collective-permute-done.2.refs_3_
  9.6 1.9 %collective-permute-start.7 = (bf16[144,256]{1,0:T(8,128)(2,1)S(1)}, bf16[144,256]{1,0:T(8,128)(2,1)S(1)}, u32[]{:S(2)}, u32[]{:S(2)}) collective-permute-start(bf16[144,256]{1,0:T(8,128)(2,1)S(1)} %collective-permute-done.2.refs_3_), channel_id=1, source_target_pairs={{0,4},{4,0},{8,12},{12,8},{16,20},{20,16},{24,28},{28,24},{1,5},{5... | collective-permute-start | bytes 221192 | tf_op jit(solution)/shard_map/ppermute | solution.py:28
  11.5 1.6 %collective-permute-done.1.refs_2_ = bf16[144,256]{1,0:T(8,128)(2,1)S(1)} collective-permute-done((bf16[144,256]{1,0:T(8,128)(2,1)S(1)}, bf16[144,256]{1,0:T(8,128)(2,1)S(1)}, u32[]{:S(2)}, u32[]{:S(2)}) %collective-permute-start.1) | collective-permute-done | bytes 73760 | tf_op jit(solution)/shard_map/ppermute | solution.py:28
  13.0 1.5 %collective-permute-start.6 = (bf16[144,256]{1,0:T(8,128)(2,1)S(1)}, bf16[144,256]{1,0:T(8,128)(2,1)S(1)}, u32[]{:S(2)}, u32[]{:S(2)}) collective-permute-start(bf16[144,256]{1,0:T(8,128)(2,1)S(1)} %collective-permute-done.1.refs_2_), channel_id=1, source_target_pairs={{0,4},{4,0},{8,12},{12,8},{16,20},{20,16},{24,28},{28,24},{1,5},{5... | collective-permute-start | bytes 221192 | tf_op jit(solution)/shard_map/ppermute | solution.py:28
  14.6 0.5 collective-permute-start.5
  15.1 2.0 %turn.1 = (bf16[2048,256]{1,0:T(8,128)(2,1)S(1)}, bf16[128,2048]{1,0:T(8,128)(2,1)S(1)}, f32[8,128]{1,0:T(8,128)S(1)}) custom-call(s32[2]{0:T(128)S(1)} %pad_add_fusion.ids, bf16[4096,128]{1,0:T(8,128)(2,1)} %protos.1, f32[1,4096]{1,0:T(1,128)} %bitcast.18), custom_call_target="tpu_custom_call" | custom-call | tf_op jit(solution)/shard_map/turn/pallas_call | solution.py:304
  17.1 0.1 collective-permute-start.3
  17.1 0.0 collective-permute-done.4.refs_0_
  17.2 0.9 %collective-permute-done.6.refs_2_ = bf16[144,256]{1,0:T(8,128)(2,1)S(1)} collective-permute-done((bf16[144,256]{1,0:T(8,128)(2,1)S(1)}, bf16[144,256]{1,0:T(8,128)(2,1)S(1)}, u32[]{:S(2)}, u32[]{:S(2)}) %collective-permute-start.6) | collective-permute-done | bytes 73760 | tf_op jit(solution)/shard_map/ppermute | solution.py:28
  18.1 0.8 %collective-permute-done.5.refs_1_ = bf16[144,256]{1,0:T(8,128)(2,1)S(1)} collective-permute-done((bf16[144,256]{1,0:T(8,128)(2,1)S(1)}, bf16[144,256]{1,0:T(8,128)(2,1)S(1)}, u32[]{:S(2)}, u32[]{:S(2)}) %collective-permute-start.5) | collective-permute-done | bytes 73760 | tf_op jit(solution)/shard_map/ppermute | solution.py:28
  18.9 0.1 collective-permute-start.8
  19.0 1.6 %collective-permute-done.8.theirs_b = bf16[4,144,256]{2,1,0:T(8,128)(2,1)S(1)} collective-permute-done((bf16[4,144,256]{2,1,0:T(8,128)(2,1)S(1)}, bf16[4,144,256]{2,1,0:T(8,128)(2,1)S(1)}, u32[]{:S(2)}, u32[]{:S(2)}) %collective-permute-start.8) | collective-permute-done | bytes 294944 | tf_op jit(solution)/shard_map/ppermute | solution.py:28
  20.6 5.5 %plan.1 = (f32[2048,2048]{1,0:T(8,128)S(1)}, f32[2,2048,128]{2,1,0:T(8,128)S(1)}, f32[2,2048]{1,0:T(2,128)S(1)}, bf16[256,2048]{1,0:T(8,128)(2,1)S(1)}, bf16[128,2048]{1,0:T(8,128)(2,1)S(1)}) custom-call(s32[2]{0:T(128)S(1)} %pad_add_fusion.ids, bf16[2048,256]{1,0:T(8,128)(2,1)S(1)} %get-tuple-element.32.protos, bf16[4,144,256]{2,1,0:T(8,128)(2,1)S(1)} %stack.14.mine_a, ...), custom_call_target="tpu_custom_call" | custom-call | tf_op jit(solution)/shard_map/plan/pallas_call | solution.py:304
  26.1 0.2 collective-permute-start.9
  26.3 1.0 %collective-permute-done.9.right = f32[2,2048]{1,0:T(2,128)S(1)} collective-permute-done((f32[2,2048]{1,0:T(2,128)S(1)}, f32[2,2048]{1,0:T(2,128)S(1)}, u32[]{:S(2)}, u32[]{:S(2)}) %collective-permute-start.9) | collective-permute-done | bytes 16416 | tf_op jit(solution)/shard_map/ppermute | solution.py:28
  27.4 2.0 %collective-permute-start.12 = (f32[2,2048]{1,0:T(2,128)S(1)}, f32[2,2048]{1,0:T(2,128)S(1)}, u32[]{:S(2)}, u32[]{:S(2)}) collective-permute-start(f32[2,2048]{1,0:T(2,128)S(1)} %add.28.after.refs_0_), channel_id=1, source_target_pairs={{0,6},{1,7},{2,4},{3,5},{4,2},{5,3},{6,0},{7,1},{8,14},{9,15},{10,... | collective-permute-start | bytes 49160 | tf_op jit(solution)/shard_map/ppermute | solution.py:325
  29.4 1.0 %collective-permute-start.11 = (f32[2,2048]{1,0:T(2,128)S(1)}, f32[2,2048]{1,0:T(2,128)S(1)}, u32[]{:S(2)}, u32[]{:S(2)}) collective-permute-start(f32[2,2048]{1,0:T(2,128)S(1)} %add.28.after.refs_0_), channel_id=1, source_target_pairs={{0,4},{1,5},{2,6},{3,7},{4,0},{5,1},{6,2},{7,3},{8,12},{9,13},{10,... | collective-permute-start | bytes 49160 | tf_op jit(solution)/shard_map/ppermute | solution.py:325
  30.3 0.5 collective-permute-start.10
  30.9 1.9 %embed_before.1 = (f32[2048,512]{1,0:T(8,128)S(1)}, f32[8,128]{1,0:T(8,128)S(1)}) custom-call(bf16[2048,256]{1,0:T(8,128)(2,1)S(1)} %get-tuple-element.32.protos, bf16[256,2048]{1,0:T(8,128)(2,1)S(1)} %get-tuple-element.37.emb_ext, f32[2,2048]{1,0:T(2,128)S(1)} %add.28.after.refs_0_), custom_call_target="tpu_custom_call" | custom-call | tf_op jit(solution)/shard_map/embed_before/pallas_call | solution.py:304
  32.8 0.0 collective-permute-done.12.refs_3_
  32.8 0.3 collective-permute-done.11.refs_2_
  33.1 1.0 %collective-permute-done.10.refs_1_ = f32[2,2048]{1,0:T(2,128)S(1)} collective-permute-done((f32[2,2048]{1,0:T(2,128)S(1)}, f32[2,2048]{1,0:T(2,128)S(1)}, u32[]{:S(2)}, u32[]{:S(2)}) %collective-permute-start.10) | collective-permute-done | bytes 16416 | tf_op jit(solution)/shard_map/ppermute | solution.py:325
  34.1 2.6 %sweep.3 = (f32[2048,2048]{1,0:T(8,128)S(1)}, f32[2,2048]{1,0:T(2,128)S(1)}, f32[1,2048]{1,0:T(1,128)S(1)}) custom-call(f32[2048,2048]{1,0:T(8,128)S(1)} %get-tuple-element.34.plan, f32[2,2048,128]{2,1,0:T(8,128)S(1)} %get-tuple-element.35.cols, f32[2,2048]{1,0:T(2,128)S(1)} %add.28.after.refs_0_, ...), custom_call_target="tpu_custom_call", output_to_operand_aliasing={{0}: (0, {})} | custom-call | tf_op jit(solution)/shard_map/sweep/pallas_call | solution.py:304
  36.7 0.1 collective-permute-start.13
  36.7 1.2 %collective-permute-done.13.right = f32[1,2048]{1,0:T(1,128)S(1)} collective-permute-done((f32[1,2048]{1,0:T(1,128)S(1)}, f32[1,2048]{1,0:T(1,128)S(1)}, u32[]{:S(2)}, u32[]{:S(2)}) %collective-permute-start.13) | collective-permute-done | bytes 8224 | tf_op jit(solution)/shard_map/ppermute | solution.py:28
  37.9 1.0 %collective-permute-start.16 = (f32[1,2048]{1,0:T(1,128)S(1)}, f32[1,2048]{1,0:T(1,128)S(1)}, u32[]{:S(2)}, u32[]{:S(2)}) collective-permute-start(f32[1,2048]{1,0:T(1,128)S(1)} %add.29.after.refs_1_), channel_id=1, source_target_pairs={{0,6},{1,7},{2,4},{3,5},{4,2},{5,3},{6,0},{7,1},{8,14},{9,15},{10,... | collective-permute-start | bytes 24584 | tf_op jit(solution)/shard_map/ppermute | solution.py:325
  38.9 1.0 %collective-permute-start.15 = (f32[1,2048]{1,0:T(1,128)S(1)}, f32[1,2048]{1,0:T(1,128)S(1)}, u32[]{:S(2)}, u32[]{:S(2)}) collective-permute-start(f32[1,2048]{1,0:T(1,128)S(1)} %add.29.after.refs_1_), channel_id=1, source_target_pairs={{0,4},{1,5},{2,6},{3,7},{4,0},{5,1},{6,2},{7,3},{8,12},{9,13},{10,... | collective-permute-start | bytes 24584 | tf_op jit(solution)/shard_map/ppermute | solution.py:325
  39.9 1.5 %collective-permute-start.14 = (f32[1,2048]{1,0:T(1,128)S(1)}, f32[1,2048]{1,0:T(1,128)S(1)}, u32[]{:S(2)}, u32[]{:S(2)}) collective-permute-start(f32[1,2048]{1,0:T(1,128)S(1)} %add.29.after.refs_1_), channel_id=1, source_target_pairs={{0,2},{1,3},{2,0},{3,1},{4,6},{5,7},{6,4},{7,5},{8,10},{9,11},{10,... | collective-permute-start | bytes 24584 | tf_op jit(solution)/shard_map/ppermute | solution.py:325
  41.4 2.0 %proto_before.1 = (f32[512,2048]{1,0:T(8,128)S(1)}, f32[512,128]{1,0:T(8,128)S(1)}, f32[8,128]{1,0:T(8,128)S(1)}) custom-call(s32[2]{0:T(128)S(1)} %pad_add_fusion.ids, bf16[2048,256]{1,0:T(8,128)(2,1)S(1)} %get-tuple-element.32.protos, bf16[256,2048]{1,0:T(8,128)(2,1)S(1)} %get-tuple-element.37.emb_ext, bf16[128,2048]{1,0:T(8,128)(2,1)S(1)} %get-tuple-element.42.view_t, ...), custom_call_target="tpu_custom_call" | custom-call | tf_op jit(solution)/shard_map/proto_before/pallas_call | solution.py:304
  43.4 0.0 collective-permute-done.16.refs_4_
  43.5 0.1 collective-permute-done.14.refs_2_
  43.5 2.6 %sweep.4 = (f32[2048,2048]{1,0:T(8,128)S(1)}, f32[1,2048]{1,0:T(1,128)S(1)}) custom-call(f32[2048,2048]{1,0:T(8,128)S(1)} %get-tuple-element.39.plan, f32[2,2048,128]{2,1,0:T(8,128)S(1)} %get-tuple-element.35.cols, f32[2,2048]{1,0:T(2,128)S(1)} %get-tuple-element.40.refs_0_.sums, f32[1,2048]{1,0:T(1,128)S(1)} %add.29.after.refs_1_, ...), custom_call_target="tpu_custom_call", output_to_operand_aliasing={{0}: (0, {})} | custom-call | tf_op jit(solution)/shard_map/sweep/pallas_call | solution.py:304
  46.1 0.1 collective-permute-start.17
  46.2 1.2 %collective-permute-done.17.right = f32[1,2048]{1,0:T(1,128)S(1)} collective-permute-done((f32[1,2048]{1,0:T(1,128)S(1)}, f32[1,2048]{1,0:T(1,128)S(1)}, u32[]{:S(2)}, u32[]{:S(2)}) %collective-permute-start.17) | collective-permute-done | bytes 8224 | tf_op jit(solution)/shard_map/ppermute | solution.py:28
  47.4 2.0 %collective-permute-start.20 = (f32[1,2048]{1,0:T(1,128)S(1)}, f32[1,2048]{1,0:T(1,128)S(1)}, u32[]{:S(2)}, u32[]{:S(2)}) collective-permute-start(f32[1,2048]{1,0:T(1,128)S(1)} %add.30.after.refs_1_), channel_id=1, source_target_pairs={{0,6},{1,7},{2,4},{3,5},{4,2},{5,3},{6,0},{7,1},{8,14},{9,15},{10,... | collective-permute-start | bytes 24584 | tf_op jit(solution)/shard_map/ppermute | solution.py:325
  49.3 1.0 %collective-permute-start.19 = (f32[1,2048]{1,0:T(1,128)S(1)}, f32[1,2048]{1,0:T(1,128)S(1)}, u32[]{:S(2)}, u32[]{:S(2)}) collective-permute-start(f32[1,2048]{1,0:T(1,128)S(1)} %add.30.after.refs_1_), channel_id=1, source_target_pairs={{0,4},{1,5},{2,6},{3,7},{4,0},{5,1},{6,2},{7,3},{8,12},{9,13},{10,... | collective-permute-start | bytes 24584 | tf_op jit(solution)/shard_map/ppermute | solution.py:325
  50.3 0.5 collective-permute-start.18
  50.8 2.3 %cotangent.2 = (f32[2048,512]{1,0:T(8,128)S(1)}, f32[8,128]{1,0:T(8,128)S(1)}) custom-call(s32[2]{0:T(128)S(1)} %pad_add_fusion.ids, bf16[2048,256]{1,0:T(8,128)(2,1)S(1)} %get-tuple-element.32.protos, bf16[128,2048]{1,0:T(8,128)(2,1)S(1)} %get-tuple-element.42.view_t, f32[1,2048]{1,0:T(1,128)S(1)} %add.30.after.refs_1_), custom_call_target="tpu_custom_call" | custom-call | tf_op jit(solution)/shard_map/cotangent/pallas_call | solution.py:304
  53.1 0.0 collective-permute-done.19.refs_3_
  53.1 0.8 %collective-permute-done.18.refs_2_ = f32[1,2048]{1,0:T(1,128)S(1)} collective-permute-done((f32[1,2048]{1,0:T(1,128)S(1)}, f32[1,2048]{1,0:T(1,128)S(1)}, u32[]{:S(2)}, u32[]{:S(2)}) %collective-permute-start.18) | collective-permute-done | bytes 8224 | tf_op jit(solution)/shard_map/ppermute | solution.py:325
  54.0 2.6 %sweep.5 = (f32[2048,2048]{1,0:T(8,128)S(1)}, f32[1,2048]{1,0:T(1,128)S(1)}) custom-call(f32[2048,2048]{1,0:T(8,128)S(1)} %get-tuple-element.44.plan, f32[2,2048,128]{2,1,0:T(8,128)S(1)} %get-tuple-element.35.cols, f32[2,2048]{1,0:T(2,128)S(1)} %get-tuple-element.40.refs_0_.sums, f32[1,2048]{1,0:T(1,128)S(1)} %add.30.after.refs_1_, ...), custom_call_target="tpu_custom_call", output_to_operand_aliasing={{0}: (0, {})} | custom-call | tf_op jit(solution)/shard_map/sweep/pallas_call | solution.py:304
  56.5 0.1 collective-permute-start.21
  56.6 1.2 %collective-permute-done.21.right = f32[1,2048]{1,0:T(1,128)S(1)} collective-permute-done((f32[1,2048]{1,0:T(1,128)S(1)}, f32[1,2048]{1,0:T(1,128)S(1)}, u32[]{:S(2)}, u32[]{:S(2)}) %collective-permute-start.21) | collective-permute-done | bytes 8224 | tf_op jit(solution)/shard_map/ppermute | solution.py:28
  57.8 1.2 %collective-permute-start.24 = (f32[1,2048]{1,0:T(1,128)S(1)}, f32[1,2048]{1,0:T(1,128)S(1)}, u32[]{:S(2)}, u32[]{:S(2)}) collective-permute-start(f32[1,2048]{1,0:T(1,128)S(1)} %add.31.after.refs_0_), channel_id=1, source_target_pairs={{0,6},{1,7},{2,4},{3,5},{4,2},{5,3},{6,0},{7,1},{8,14},{9,15},{10,... | collective-permute-start | bytes 24584 | tf_op jit(solution)/shard_map/ppermute | solution.py:325
  58.9 1.0 %collective-permute-start.23 = (f32[1,2048]{1,0:T(1,128)S(1)}, f32[1,2048]{1,0:T(1,128)S(1)}, u32[]{:S(2)}, u32[]{:S(2)}) collective-permute-start(f32[1,2048]{1,0:T(1,128)S(1)} %add.31.after.refs_0_), channel_id=1, source_target_pairs={{0,4},{1,5},{2,6},{3,7},{4,0},{5,1},{6,2},{7,3},{8,12},{9,13},{10,... | collective-permute-start | bytes 24584 | tf_op jit(solution)/shard_map/ppermute | solution.py:325
  59.9 1.3 %collective-permute-start.22 = (f32[1,2048]{1,0:T(1,128)S(1)}, f32[1,2048]{1,0:T(1,128)S(1)}, u32[]{:S(2)}, u32[]{:S(2)}) collective-permute-start(f32[1,2048]{1,0:T(1,128)S(1)} %add.31.after.refs_0_), channel_id=1, source_target_pairs={{0,2},{1,3},{2,0},{3,1},{4,6},{5,7},{6,4},{7,5},{8,10},{9,11},{10,... | collective-permute-start | bytes 24584 | tf_op jit(solution)/shard_map/ppermute | solution.py:325
  61.3 1.4 %cotangent.3 = (f32[512,2048]{1,0:T(8,128)S(1)}, f32[8,128]{1,0:T(8,128)S(1)}) custom-call(s32[2]{0:T(128)S(1)} %pad_add_fusion.ids, bf16[2048,256]{1,0:T(8,128)(2,1)S(1)} %get-tuple-element.32.protos, bf16[128,2048]{1,0:T(8,128)(2,1)S(1)} %get-tuple-element.42.view_t, f32[1,2048]{1,0:T(1,128)S(1)} %add.31.after.refs_0_), custom_call_target="tpu_custom_call" | custom-call | tf_op jit(solution)/shard_map/cotangent/pallas_call | solution.py:304
  62.7 0.9 %collective-permute-done.22.refs_1_ = f32[1,2048]{1,0:T(1,128)S(1)} collective-permute-done((f32[1,2048]{1,0:T(1,128)S(1)}, f32[1,2048]{1,0:T(1,128)S(1)}, u32[]{:S(2)}, u32[]{:S(2)}) %collective-permute-start.22) | collective-permute-done | bytes 8224 | tf_op jit(solution)/shard_map/ppermute | solution.py:325
  63.6 3.1 %embed_grad.1 = (f32[2048,128]{1,0:T(8,128)S(1)}, f32[1,2048]{1,0:T(1,128)S(1)}, f32[4,64,128]{2,1,0:T(8,128)S(1)}, f32[4,64,128]{2,1,0:T(8,128)S(1)}) custom-call(s32[2]{0:T(128)S(1)} %pad_add_fusion.ids, f32[2048,2048]{1,0:T(8,128)S(1)} %get-tuple-element.47.plan, f32[2,2048,128]{2,1,0:T(8,128)S(1)} %get-tuple-element.35.cols, ...), custom_call_target="tpu_custom_call" | custom-call | tf_op jit(solution)/shard_map/embed_grad/pallas_call | solution.py:304
  66.7 0.1 collective-permute-start.25
  66.8 1.0 %proto_grad.2 = (f32[512,128]{1,0:T(8,128)S(1)}, f32[8,128]{1,0:T(8,128)S(1)}) custom-call(s32[2]{0:T(128)S(1)} %pad_add_fusion.ids, bf16[256,2048]{1,0:T(8,128)(2,1)S(1)} %get-tuple-element.37.emb_ext, f32[512,2048]{1,0:T(8,128)S(1)} %get-tuple-element.55.entries, f32[512,2048]{1,0:T(8,128)S(1)} %get-tuple-element.56.cots, ...), custom_call_target="tpu_custom_call" | custom-call | tf_op jit(solution)/shard_map/proto_grad/pallas_call | solution.py:304
  67.8 0.3 collective-permute-done.25.right
  68.1 1.4 %collective-permute-start.26 = (f32[64,128]{1,0:T(8,128)S(1)}, f32[64,128]{1,0:T(8,128)S(1)}, u32[]{:S(2)}, u32[]{:S(2)}) collective-permute-start(f32[64,128]{1,0:T(8,128)S(1)} %get-tuple-element.62), channel_id=1, source_target_pairs={{0,2},{1,3},{2,0},{3,1},{4,6},{5,7},{6,4},{7,5},{8,10},{9,11},{10,... | collective-permute-start | bytes 98312 | tf_op jit(solution)/shard_map/ppermute | solution.py:325
  69.5 1.2 %collective-permute-start.28 = (f32[64,128]{1,0:T(8,128)S(1)}, f32[64,128]{1,0:T(8,128)S(1)}, u32[]{:S(2)}, u32[]{:S(2)}) collective-permute-start(f32[64,128]{1,0:T(8,128)S(1)} %get-tuple-element.63), channel_id=1, source_target_pairs={{0,6},{1,7},{2,4},{3,5},{4,2},{5,3},{6,0},{7,1},{8,14},{9,15},{10,... | collective-permute-start | bytes 98312 | tf_op jit(solution)/shard_map/ppermute | solution.py:325
  70.7 1.0 %collective-permute-start.27 = (f32[64,128]{1,0:T(8,128)S(1)}, f32[64,128]{1,0:T(8,128)S(1)}, u32[]{:S(2)}, u32[]{:S(2)}) collective-permute-start(f32[64,128]{1,0:T(8,128)S(1)} %get-tuple-element.64), channel_id=1, source_target_pairs={{0,4},{1,5},{2,6},{3,7},{4,0},{5,1},{6,2},{7,3},{8,12},{9,13},{10,... | collective-permute-start | bytes 98312 | tf_op jit(solution)/shard_map/ppermute | solution.py:325
  71.7 1.7 %proto_grad.3 = f32[512,128]{1,0:T(8,128)} custom-call(s32[2]{0:T(128)S(1)} %pad_add_fusion.ids, bf16[256,2048]{1,0:T(8,128)(2,1)S(1)} %get-tuple-element.37.emb_ext, f32[512,2048]{1,0:T(8,128)S(1)} %get-tuple-element.55.entries, f32[512,2048]{1,0:T(8,128)S(1)} %get-tuple-element.56.cots, f32[512,128]{1,0:T(8,128)S(1)} %get-tuple-element.61.so_far, ...), custom_call_target="tpu_custom_call" | custom-call | tf_op jit(solution)/shard_map/proto_grad/pallas_call | solution.py:304
  73.4 0.9 %collective-permute-done.28 = f32[64,128]{1,0:T(8,128)S(1)} collective-permute-done((f32[64,128]{1,0:T(8,128)S(1)}, f32[64,128]{1,0:T(8,128)S(1)}, u32[]{:S(2)}, u32[]{:S(2)}) %collective-permute-start.28) | collective-permute-done | bytes 32800 | tf_op jit(solution)/shard_map/ppermute | solution.py:325
  74.4 0.3 collective-permute-done.27
  74.7 0.6 fusion.2
  (17 shorter events, 0.1 us)
Async XLA Ops:
  1.7 7.9 %collective-permute-start.2 = (bf16[144,256]{1,0:T(8,128)(2,1)S(1)}, bf16[144,256]{1,0:T(8,128)(2,1)S(1)}, u32[]{:S(2)}, u32[]{:S(2)}) collective-permute-start(bf16[144,256]{1,0:T(8,128)(2,1)S(1)} %prepare.1.refs_0_), channel_id=1, source_target_pairs={{0,24},{4,28},{8,16},{12,20},{16,8},{20,12},{24,0},{28,4},{1,25},{... | collective-permute-start | bytes 221192 | tf_op jit(solution)/shard_map/ppermute | solution.py:28
  6.8 6.2 %collective-permute-start.1 = (bf16[144,256]{1,0:T(8,128)(2,1)S(1)}, bf16[144,256]{1,0:T(8,128)(2,1)S(1)}, u32[]{:S(2)}, u32[]{:S(2)}) collective-permute-start(bf16[144,256]{1,0:T(8,128)(2,1)S(1)} %prepare.1.refs_0_), channel_id=1, source_target_pairs={{0,16},{4,20},{8,24},{12,28},{16,0},{20,4},{24,8},{28,12},{1,17},{... | collective-permute-start | bytes 221192 | tf_op jit(solution)/shard_map/ppermute | solution.py:28
  6.8 7.7 %collective-permute-start = (bf16[144,256]{1,0:T(8,128)(2,1)S(1)}, bf16[144,256]{1,0:T(8,128)(2,1)S(1)}, u32[]{:S(2)}, u32[]{:S(2)}) collective-permute-start(bf16[144,256]{1,0:T(8,128)(2,1)S(1)} %prepare.1.refs_0_), channel_id=1, source_target_pairs={{0,8},{4,12},{8,0},{12,4},{16,24},{20,28},{24,16},{28,20},{1,9},{5... | collective-permute-start | bytes 221192 | tf_op jit(solution)/shard_map/ppermute | solution.py:28
  7.5 9.7 %collective-permute-start.4 = (bf16[144,256]{1,0:T(8,128)(2,1)S(1)}, bf16[144,256]{1,0:T(8,128)(2,1)S(1)}, u32[]{:S(2)}, u32[]{:S(2)}) collective-permute-start(bf16[144,256]{1,0:T(8,128)(2,1)S(1)} %prepare.1.refs_0_), channel_id=1, source_target_pairs={{0,4},{4,0},{8,12},{12,8},{16,20},{20,16},{24,28},{28,24},{1,5},{5... | collective-permute-start | bytes 221192 | tf_op jit(solution)/shard_map/ppermute | solution.py:28
  9.6 7.6 %collective-permute-start.7 = (bf16[144,256]{1,0:T(8,128)(2,1)S(1)}, bf16[144,256]{1,0:T(8,128)(2,1)S(1)}, u32[]{:S(2)}, u32[]{:S(2)}) collective-permute-start(bf16[144,256]{1,0:T(8,128)(2,1)S(1)} %collective-permute-done.2.refs_3_), channel_id=1, source_target_pairs={{0,4},{4,0},{8,12},{12,8},{16,20},{20,16},{24,28},{28,24},{1,5},{5... | collective-permute-start | bytes 221192 | tf_op jit(solution)/shard_map/ppermute | solution.py:28
  13.0 5.1 %collective-permute-start.6 = (bf16[144,256]{1,0:T(8,128)(2,1)S(1)}, bf16[144,256]{1,0:T(8,128)(2,1)S(1)}, u32[]{:S(2)}, u32[]{:S(2)}) collective-permute-start(bf16[144,256]{1,0:T(8,128)(2,1)S(1)} %collective-permute-done.1.refs_2_), channel_id=1, source_target_pairs={{0,4},{4,0},{8,12},{12,8},{16,20},{20,16},{24,28},{28,24},{1,5},{5... | collective-permute-start | bytes 221192 | tf_op jit(solution)/shard_map/ppermute | solution.py:28
  14.6 4.4 %collective-permute-start.5 = (bf16[144,256]{1,0:T(8,128)(2,1)S(1)}, bf16[144,256]{1,0:T(8,128)(2,1)S(1)}, u32[]{:S(2)}, u32[]{:S(2)}) collective-permute-start(bf16[144,256]{1,0:T(8,128)(2,1)S(1)} %collective-permute-done.refs_1_), channel_id=1, source_target_pairs={{0,4},{4,0},{8,12},{12,8},{16,20},{20,16},{24,28},{28,24},{1,5},{5... | collective-permute-start | bytes 221192 | tf_op jit(solution)/shard_map/ppermute | solution.py:28
  17.1 2.0 %collective-permute-start.3 = (bf16[4,144,256]{2,1,0:T(8,128)(2,1)S(1)}, bf16[4,144,256]{2,1,0:T(8,128)(2,1)S(1)}, u32[]{:S(2)}, u32[]{:S(2)}) collective-permute-start(bf16[4,144,256]{2,1,0:T(8,128)(2,1)S(1)} %stack.14.mine_a), channel_id=1, source_target_pairs={{0,1},{1,0},{2,3},{3,2},{4,5},{5,4},{6,7},{7,6},{8,9},{9,8},{10,11... | collective-permute-start | bytes 884744 | tf_op jit(solution)/shard_map/ppermute | solution.py:28
  18.9 1.6 %collective-permute-start.8 = (bf16[4,144,256]{2,1,0:T(8,128)(2,1)S(1)}, bf16[4,144,256]{2,1,0:T(8,128)(2,1)S(1)}, u32[]{:S(2)}, u32[]{:S(2)}) collective-permute-start(bf16[4,144,256]{2,1,0:T(8,128)(2,1)S(1)} %stack.15.mine_b), channel_id=1, source_target_pairs={{0,1},{1,0},{2,3},{3,2},{4,5},{5,4},{6,7},{7,6},{8,9},{9,8},{10,11... | collective-permute-start | bytes 884744 | tf_op jit(solution)/shard_map/ppermute | solution.py:28
  26.1 1.2 %collective-permute-start.9 = (f32[2,2048]{1,0:T(2,128)S(1)}, f32[2,2048]{1,0:T(2,128)S(1)}, u32[]{:S(2)}, u32[]{:S(2)}) collective-permute-start(f32[2,2048]{1,0:T(2,128)S(1)} %get-tuple-element.36.left), channel_id=1, source_target_pairs={{0,1},{1,0},{2,3},{3,2},{4,5},{5,4},{6,7},{7,6},{8,9},{9,8},{10,11... | collective-permute-start | bytes 49160 | tf_op jit(solution)/shard_map/ppermute | solution.py:28
  27.4 5.4 %collective-permute-start.12 = (f32[2,2048]{1,0:T(2,128)S(1)}, f32[2,2048]{1,0:T(2,128)S(1)}, u32[]{:S(2)}, u32[]{:S(2)}) collective-permute-start(f32[2,2048]{1,0:T(2,128)S(1)} %add.28.after.refs_0_), channel_id=1, source_target_pairs={{0,6},{1,7},{2,4},{3,5},{4,2},{5,3},{6,0},{7,1},{8,14},{9,15},{10,... | collective-permute-start | bytes 49160 | tf_op jit(solution)/shard_map/ppermute | solution.py:325
  29.4 3.7 %collective-permute-start.11 = (f32[2,2048]{1,0:T(2,128)S(1)}, f32[2,2048]{1,0:T(2,128)S(1)}, u32[]{:S(2)}, u32[]{:S(2)}) collective-permute-start(f32[2,2048]{1,0:T(2,128)S(1)} %add.28.after.refs_0_), channel_id=1, source_target_pairs={{0,4},{1,5},{2,6},{3,7},{4,0},{5,1},{6,2},{7,3},{8,12},{9,13},{10,... | collective-permute-start | bytes 49160 | tf_op jit(solution)/shard_map/ppermute | solution.py:325
  30.3 3.7 %collective-permute-start.10 = (f32[2,2048]{1,0:T(2,128)S(1)}, f32[2,2048]{1,0:T(2,128)S(1)}, u32[]{:S(2)}, u32[]{:S(2)}) collective-permute-start(f32[2,2048]{1,0:T(2,128)S(1)} %add.28.after.refs_0_), channel_id=1, source_target_pairs={{0,2},{1,3},{2,0},{3,1},{4,6},{5,7},{6,4},{7,5},{8,10},{9,11},{10,... | collective-permute-start | bytes 49160 | tf_op jit(solution)/shard_map/ppermute | solution.py:325
  36.7 1.2 %collective-permute-start.13 = (f32[1,2048]{1,0:T(1,128)S(1)}, f32[1,2048]{1,0:T(1,128)S(1)}, u32[]{:S(2)}, u32[]{:S(2)}) collective-permute-start(f32[1,2048]{1,0:T(1,128)S(1)} %get-tuple-element.41.left), channel_id=1, source_target_pairs={{0,1},{1,0},{2,3},{3,2},{4,5},{5,4},{6,7},{7,6},{8,9},{9,8},{10,11... | collective-permute-start | bytes 24584 | tf_op jit(solution)/shard_map/ppermute | solution.py:28
  37.9 5.5 %collective-permute-start.16 = (f32[1,2048]{1,0:T(1,128)S(1)}, f32[1,2048]{1,0:T(1,128)S(1)}, u32[]{:S(2)}, u32[]{:S(2)}) collective-permute-start(f32[1,2048]{1,0:T(1,128)S(1)} %add.29.after.refs_1_), channel_id=1, source_target_pairs={{0,6},{1,7},{2,4},{3,5},{4,2},{5,3},{6,0},{7,1},{8,14},{9,15},{10,... | collective-permute-start | bytes 24584 | tf_op jit(solution)/shard_map/ppermute | solution.py:325
  38.9 4.5 %collective-permute-start.15 = (f32[1,2048]{1,0:T(1,128)S(1)}, f32[1,2048]{1,0:T(1,128)S(1)}, u32[]{:S(2)}, u32[]{:S(2)}) collective-permute-start(f32[1,2048]{1,0:T(1,128)S(1)} %add.29.after.refs_1_), channel_id=1, source_target_pairs={{0,4},{1,5},{2,6},{3,7},{4,0},{5,1},{6,2},{7,3},{8,12},{9,13},{10,... | collective-permute-start | bytes 24584 | tf_op jit(solution)/shard_map/ppermute | solution.py:325
  39.9 3.7 %collective-permute-start.14 = (f32[1,2048]{1,0:T(1,128)S(1)}, f32[1,2048]{1,0:T(1,128)S(1)}, u32[]{:S(2)}, u32[]{:S(2)}) collective-permute-start(f32[1,2048]{1,0:T(1,128)S(1)} %add.29.after.refs_1_), channel_id=1, source_target_pairs={{0,2},{1,3},{2,0},{3,1},{4,6},{5,7},{6,4},{7,5},{8,10},{9,11},{10,... | collective-permute-start | bytes 24584 | tf_op jit(solution)/shard_map/ppermute | solution.py:325
  46.1 1.2 %collective-permute-start.17 = (f32[1,2048]{1,0:T(1,128)S(1)}, f32[1,2048]{1,0:T(1,128)S(1)}, u32[]{:S(2)}, u32[]{:S(2)}) collective-permute-start(f32[1,2048]{1,0:T(1,128)S(1)} %get-tuple-element.45.left), channel_id=1, source_target_pairs={{0,1},{1,0},{2,3},{3,2},{4,5},{5,4},{6,7},{7,6},{8,9},{9,8},{10,11... | collective-permute-start | bytes 24584 | tf_op jit(solution)/shard_map/ppermute | solution.py:28
  47.4 5.8 %collective-permute-start.20 = (f32[1,2048]{1,0:T(1,128)S(1)}, f32[1,2048]{1,0:T(1,128)S(1)}, u32[]{:S(2)}, u32[]{:S(2)}) collective-permute-start(f32[1,2048]{1,0:T(1,128)S(1)} %add.30.after.refs_1_), channel_id=1, source_target_pairs={{0,6},{1,7},{2,4},{3,5},{4,2},{5,3},{6,0},{7,1},{8,14},{9,15},{10,... | collective-permute-start | bytes 24584 | tf_op jit(solution)/shard_map/ppermute | solution.py:325
  49.3 3.8 %collective-permute-start.19 = (f32[1,2048]{1,0:T(1,128)S(1)}, f32[1,2048]{1,0:T(1,128)S(1)}, u32[]{:S(2)}, u32[]{:S(2)}) collective-permute-start(f32[1,2048]{1,0:T(1,128)S(1)} %add.30.after.refs_1_), channel_id=1, source_target_pairs={{0,4},{1,5},{2,6},{3,7},{4,0},{5,1},{6,2},{7,3},{8,12},{9,13},{10,... | collective-permute-start | bytes 24584 | tf_op jit(solution)/shard_map/ppermute | solution.py:325
  50.3 3.7 %collective-permute-start.18 = (f32[1,2048]{1,0:T(1,128)S(1)}, f32[1,2048]{1,0:T(1,128)S(1)}, u32[]{:S(2)}, u32[]{:S(2)}) collective-permute-start(f32[1,2048]{1,0:T(1,128)S(1)} %add.30.after.refs_1_), channel_id=1, source_target_pairs={{0,2},{1,3},{2,0},{3,1},{4,6},{5,7},{6,4},{7,5},{8,10},{9,11},{10,... | collective-permute-start | bytes 24584 | tf_op jit(solution)/shard_map/ppermute | solution.py:325
  56.5 1.2 %collective-permute-start.21 = (f32[1,2048]{1,0:T(1,128)S(1)}, f32[1,2048]{1,0:T(1,128)S(1)}, u32[]{:S(2)}, u32[]{:S(2)}) collective-permute-start(f32[1,2048]{1,0:T(1,128)S(1)} %get-tuple-element.51.left), channel_id=1, source_target_pairs={{0,1},{1,0},{2,3},{3,2},{4,5},{5,4},{6,7},{7,6},{8,9},{9,8},{10,11... | collective-permute-start | bytes 24584 | tf_op jit(solution)/shard_map/ppermute | solution.py:28
  57.8 4.9 %collective-permute-start.24 = (f32[1,2048]{1,0:T(1,128)S(1)}, f32[1,2048]{1,0:T(1,128)S(1)}, u32[]{:S(2)}, u32[]{:S(2)}) collective-permute-start(f32[1,2048]{1,0:T(1,128)S(1)} %add.31.after.refs_0_), channel_id=1, source_target_pairs={{0,6},{1,7},{2,4},{3,5},{4,2},{5,3},{6,0},{7,1},{8,14},{9,15},{10,... | collective-permute-start | bytes 24584 | tf_op jit(solution)/shard_map/ppermute | solution.py:325
  58.9 3.7 %collective-permute-start.23 = (f32[1,2048]{1,0:T(1,128)S(1)}, f32[1,2048]{1,0:T(1,128)S(1)}, u32[]{:S(2)}, u32[]{:S(2)}) collective-permute-start(f32[1,2048]{1,0:T(1,128)S(1)} %add.31.after.refs_0_), channel_id=1, source_target_pairs={{0,4},{1,5},{2,6},{3,7},{4,0},{5,1},{6,2},{7,3},{8,12},{9,13},{10,... | collective-permute-start | bytes 24584 | tf_op jit(solution)/shard_map/ppermute | solution.py:325
  59.9 3.7 %collective-permute-start.22 = (f32[1,2048]{1,0:T(1,128)S(1)}, f32[1,2048]{1,0:T(1,128)S(1)}, u32[]{:S(2)}, u32[]{:S(2)}) collective-permute-start(f32[1,2048]{1,0:T(1,128)S(1)} %add.31.after.refs_0_), channel_id=1, source_target_pairs={{0,2},{1,3},{2,0},{3,1},{4,6},{5,7},{6,4},{7,5},{8,10},{9,11},{10,... | collective-permute-start | bytes 24584 | tf_op jit(solution)/shard_map/ppermute | solution.py:325
  66.7 1.4 %collective-permute-start.25 = (f32[4,64,128]{2,1,0:T(8,128)S(1)}, f32[4,64,128]{2,1,0:T(8,128)S(1)}, u32[]{:S(2)}, u32[]{:S(2)}) collective-permute-start(f32[4,64,128]{2,1,0:T(8,128)S(1)} %get-tuple-element.54), channel_id=1, source_target_pairs={{0,1},{1,0},{2,3},{3,2},{4,5},{5,4},{6,7},{7,6},{8,9},{9,8},{10,11... | collective-permute-start | bytes 393224 | tf_op jit(solution)/shard_map/ppermute | solution.py:28
  68.1 5.3 %collective-permute-start.26 = (f32[64,128]{1,0:T(8,128)S(1)}, f32[64,128]{1,0:T(8,128)S(1)}, u32[]{:S(2)}, u32[]{:S(2)}) collective-permute-start(f32[64,128]{1,0:T(8,128)S(1)} %get-tuple-element.62), channel_id=1, source_target_pairs={{0,2},{1,3},{2,0},{3,1},{4,6},{5,7},{6,4},{7,5},{8,10},{9,11},{10,... | collective-permute-start | bytes 98312 | tf_op jit(solution)/shard_map/ppermute | solution.py:325
  69.5 4.8 %collective-permute-start.28 = (f32[64,128]{1,0:T(8,128)S(1)}, f32[64,128]{1,0:T(8,128)S(1)}, u32[]{:S(2)}, u32[]{:S(2)}) collective-permute-start(f32[64,128]{1,0:T(8,128)S(1)} %get-tuple-element.63), channel_id=1, source_target_pairs={{0,6},{1,7},{2,4},{3,5},{4,2},{5,3},{6,0},{7,1},{8,14},{9,15},{10,... | collective-permute-start | bytes 98312 | tf_op jit(solution)/shard_map/ppermute | solution.py:325
  70.7 4.0 %collective-permute-start.27 = (f32[64,128]{1,0:T(8,128)S(1)}, f32[64,128]{1,0:T(8,128)S(1)}, u32[]{:S(2)}, u32[]{:S(2)}) collective-permute-start(f32[64,128]{1,0:T(8,128)S(1)} %get-tuple-element.64), channel_id=1, source_target_pairs={{0,4},{1,5},{2,6},{3,7},{4,0},{5,1},{6,2},{7,3},{8,12},{9,13},{10,... | collective-permute-start | bytes 98312 | tf_op jit(solution)/shard_map/ppermute | solution.py:325

commit v8 on v7

--- a/solution.py
+++ b/solution.py
@@ -94,26 +94,25 @@
     refs[-1][...] = left[...] + right[...]
 
 
-def plan_kernel(logit_scale, view_scale, ids, protos, mine_a, theirs_a, mine_b, theirs_b, plan_out, cols_out, sums_out, emb_ext, view_t, row_mass, row_weight):
-    pairs, high, rows = mine_a.shape
-    blocks = 2 * pairs
+def plan_kernel(logit_scale, view_scale, second, ids, protos, mine, theirs, *refs):
+    if second:
+        _, cols_in, sums_in, *refs = refs
+    plan_out, cols_out, sums_out, emb_ext, view_t, row_mass, row_weight = refs
+    blocks, high, rows = mine.shape
     count = protos.shape[0]
     width = view_t.shape[0]
     scale = logit_scale * LOG2E
+    left = blocks * rows if second else 0
     emb_ext[high:, :] = jnp.zeros((emb_ext.shape[0] - high, blocks * rows), BF16)
 
-    def fill(embs, views):
+    def fill(emb, view):
         for block in range(blocks):
             cols = slice(block * rows, (block + 1) * rows)
-            emb_ext[0:high, cols] = embs[block % 2][block // 2]
-            view_t[:, cols] = views[block % 2][block // 2, 0:width, :]
-
-    for core in range(2):
-        for odd in range(2):
-            a, b = ((mine_a, theirs_a), (mine_b, theirs_b)) if core == 0 else ((theirs_a, mine_a), (theirs_b, mine_b))
-            low, upper = (a, b) if odd == 0 else (b, a)
-            is_this = jnp.logical_and(ids[1] & 1 == core, ids[0] & 1 == odd)
-            pl.when(is_this)(functools.partial(fill, (low[0], upper[0]), (low[1], upper[1])))
+            emb_ext[0:high, cols] = emb[block]
+            view_t[:, cols] = view[block, 0:width, :]
+
+    pl.when(ids[1] & 1 == 0)(lambda: fill(mine, theirs))
+    pl.when(ids[1] & 1 != 0)(lambda: fill(theirs, mine))
     row_mass[...] = jnp.zeros_like(row_mass)
     row_weight[...] = jnp.zeros_like(row_weight)
 
@@ -126,32 +125,41 @@
 
     def step(index, carry):
         here = pl.ds(pl.multiple_of(index * CHUNK, CHUNK), CHUNK)
-        mass = weight = jnp.zeros((CHUNK, 128), F32)
+        mass = cols_in[0, here, :] if second else jnp.zeros((CHUNK, 128), F32)
+        weight = cols_in[1, here, :] if second else mass
         for block in range(blocks):
             cols = slice(block * rows, (block + 1) * rows)
             plan = jnp.exp2(scale * mm(protos[here, :], emb_ext[:, cols]))
-            plan_out[here, cols] = plan
+            plan_out[here, left + block * rows:left + (block + 1) * rows] = plan
             across, down = folded(plan)
             mass = mass + across
             row_mass[:, cols] += down
             across, down = folded(plan * mm(protos[here, 0:width], view_t[:, cols]))
             weight = weight + across
             row_weight[:, cols] += down
-        inverse = 1.0 / lane_sums(mass)
-        cols_out[0, here, :] = inverse
-        cols_out[1, here, :] = -view_scale * lane_sums(weight) * inverse
+        if second:
+            mass = 1.0 / lane_sums(mass)
+            weight = -view_scale * lane_sums(weight) * mass
+        cols_out[0, here, :] = mass
+        cols_out[1, here, :] = weight
         return carry
 
     lax.fori_loop(0, count // CHUNK, step, 0, unroll=True)
-    sums_out[0:1, :] = jnp.sum(row_mass[...], axis=0, keepdims=True)
-    sums_out[1:2, :] = -view_scale * jnp.sum(row_weight[...], axis=0, keepdims=True)
+    if second:
+        sums_out[:, 0:left] = sums_in[...]
+    sums_out[0:1, left:] = jnp.sum(row_mass[...], axis=0, keepdims=True)
+    sums_out[1:2, left:] = -view_scale * jnp.sum(row_weight[...], axis=0, keepdims=True)
 
 
 def added(parts):
-    total = parts[0][...]
-    for other in parts[1:]:
-        total = total + other[...]
-    return total
+    plain, turned = parts[:len(parts) // 2], parts[len(parts) // 2:]
+    total, other = plain[0][...], turned[0][...]
+    for part in plain[1:]:
+        total = total + part[...]
+    for part in turned[1:]:
+        other = other + part[...]
+    half = other.shape[1] // 2
+    return total + jnp.concatenate((other[:, half:], other[:, :half]), 1)
 
 
 def by_rows(block, cols, here, spread):
@@ -204,27 +212,30 @@
         total[...] += product
         return dual
 
-    last = lax.fori_loop(1, steps, step, duals(0), unroll=2)
+    last = lax.fori_loop(1, steps, step, duals(0), unroll=True)
     total[...] += by_cols(plan.at[chunk(steps - 1), :], last)
     part_out[...] = jnp.sum(total[...], axis=0, keepdims=True)
 
 
-def embed_before_kernel(logit_scale, protos, emb_ext, after, entry_out, token):
+def embed_before_kernel(logit_scale, protos, emb_a, emb_b, after, entry_out, token):
     del after
     scale = logit_scale * LOG2E
     token[...] = jnp.zeros_like(token)
+    rows = entry_out.shape[1] // 2
 
     def step(index, carry):
         here = chunk(index)
-        entry_out[here, :] = logit_scale * jnp.exp2(scale * mm(protos[here, :], emb_ext[:, 0:entry_out.shape[1]]))
+        for half, emb in enumerate((emb_a, emb_b)):
+            entry = jnp.exp2(scale * mm(protos[here, :], emb[:, 0:rows]))
+            entry_out[here, half * rows:(half + 1) * rows] = logit_scale * entry
         return carry
 
     lax.fori_loop(0, protos.shape[0] // STEP, step, 0)
 
 
-def cotangent_kernel(view_scale, block, ids, protos, view_t, after, cot_out, token):
+def cotangent_kernel(view_scale, block, ids, protos, view_a, view_b, after, cot_out, token):
     del after
-    width = view_t.shape[0]
+    width = view_a.shape[0]
     tall, wide = cot_out.shape
     token[...] = jnp.zeros_like(token)
     first = pl.multiple_of(block(ids) * tall, tall)
@@ -232,7 +243,9 @@
     def step(index, carry):
         here = chunk(index)
         from_row = pl.ds(pl.multiple_of(first + index * STEP, STEP), STEP)
-        cot_out[here, :] = -view_scale * mm(protos[from_row, 0:width], view_t[:, 0:wide])
+        for half, view in enumerate((view_a, view_b)):
+            cot = mm(protos[from_row, 0:width], view[:, 0:wide // 2])
+            cot_out[here, half * wide // 2:(half + 1) * wide // 2] = -view_scale * cot
         return carry
 
     lax.fori_loop(0, tall // STEP, step, 0)
@@ -244,7 +257,8 @@
     rows = entries.shape[1]
     rows_out[...] = (sums[1:2, :] - added(parts)) / sums[0:1, :]
     spread[...] = jnp.broadcast_to(rows_out[...], spread.shape)
-    own_dual = rows_out[:, 0:rows]
+    split = rows_out.shape[1] // 2
+    own_dual = jnp.concatenate((rows_out[:, 0:rows // 2], rows_out[:, split:split + rows // 2]), 1)
 
     def duals(index, carry):
         here = chunk(index)
@@ -261,12 +275,12 @@
     tall = keep.shape[1]
     for place in range(shares):
         above, beside = divmod(place, shares // 2)
-        to = ((ids[0] & 1) ^ above) * shares + (ids[1] ^ (2 * beside))
+        to = above * shares + (ids[1] ^ (2 * beside))
         keep[place] = whole[pl.ds(pl.multiple_of(to * tall, tall), tall), :]
         give[place] = whole[pl.ds(pl.multiple_of((to ^ 1) * tall, tall), tall), :]
 
 
-def proto_before_kernel(logit_scale, view_scale, ids, protos, emb_ext, view_t, after, entry_out, second_out, token):
+def proto_before_kernel(logit_scale, view_scale, ids, protos, emb_a, emb_b, view_a, view_b, after, entry_out, second_out, token):
     del after
     own, rows = entry_out.shape
     width = second_out.shape[1]
@@ -274,11 +288,12 @@
     token[...] = jnp.zeros_like(token)
     here = pl.ds(pl.multiple_of((ids[0] >> 1) * own, own), own)
     total = jnp.zeros((own, width), F32)
-    for start in range(0, rows, 2 * width):
-        cols = slice(start, start + 2 * width)
-        exact = jnp.exp2(scale * mm(protos[here, :], emb_ext[:, cols]))
-        entry_out[:, cols] = logit_scale * exact
-        total = total + mm((-view_scale * exact).astype(BF16), view_t[:, cols], NT)
+    for left, emb, view in ((0, emb_a, view_a), (rows // 2, emb_b, view_b)):
+        for start in range(0, rows // 2, 2 * width):
+            cols = slice(start, start + 2 * width)
+            exact = jnp.exp2(scale * mm(protos[here, :], emb[:, cols]))
+            entry_out[:, left + start:left + start + 2 * width] = logit_scale * exact
+            total = total + mm((-view_scale * exact).astype(BF16), view[:, cols], NT)
     second_out[...] = total
 
 
@@ -288,10 +303,10 @@
     column = widened(col_dual[here, :], 2 * width)
     total = so_far[...]
     some = entries.shape[1] // 2
-    for start in range(half * some, (half + 1) * some, 2 * width):
-        cols = slice(start, start + 2 * width)
+    for start in range(0, some, 2 * width):
+        cols = slice(half * some + start, half * some + start + 2 * width)
         grad = entries[:, cols] * (cots[:, cols] - row_dual[:, cols] - column)
-        total = total + mm(grad.astype(BF16), emb_ext[0:width, cols], NT)
+        total = total + mm(grad.astype(BF16), emb_ext[0:width, start:start + 2 * width], NT)
     outs[0][...] = total
     for token in outs[1:]:
         token[...] = jnp.zeros_like(token)
@@ -363,20 +378,32 @@
     pairs = blocks // 2
     stack = call(functools.partial(stack_kernel, pairs), shape(pairs, width + EXT, rows, dtype=BF16), "stack", limit=2)
     direct = [send] + [swap(send, "row", step) for step in range(2, blocks, 2)]
-    mine_a = stack(*direct)
+    mine_a = stack(*direct, token)
     theirs_a = swap(mine_a, "proto", 1)
-    mine_b = stack(*[swap(value, "row", 1) for value in direct], token)
+    mine_b = stack(*[swap(value, "row", 1) for value in direct])
     theirs_b = swap(mine_b, "proto", 1)
 
     kept = pltpu.VMEM((count, all_rows), F32)
-    plan, cols, sums, emb_ext, view_t = call(
-        form(plan_kernel),
-        (kept, shape(2, count, 128), shape(2, all_rows), shape(2 * width, all_rows, dtype=BF16), shape(width, all_rows, dtype=BF16)),
-        "plan",
+    some = all_rows // 2
+    turned = (shape(2 * width, some, dtype=BF16), shape(width, some, dtype=BF16))
+    work = [(F32, 8, some), (F32, 8, some)]
+    plan, cols, sums, emb_a, view_a = call(
+        functools.partial(plan_kernel, *scales, False),
+        (kept, shape(2, count, 128), shape(2, some)) + turned,
+        "plan_ours",
         scalars=1,
-        scratch=[(F32, 8, all_rows), (F32, 8, all_rows)],
+        scratch=work,
         limit=12,
-    )(ids, protos, mine_a, theirs_a, mine_b, theirs_b)
+    )(ids, protos, mine_a, theirs_a)
+    plan, cols, sums, emb_b, view_b = call(
+        functools.partial(plan_kernel, *scales, True),
+        (kept, shape(2, count, 128), shape(2, all_rows)) + turned,
+        "plan_theirs",
+        scalars=1,
+        scratch=work,
+        aliases={4: 0},
+        limit=12,
+    )(ids, protos, mine_b, theirs_b, plan, cols, sums)
 
     work = [(F32, 8, all_rows), (F32, 8, all_rows)]
     token = shape(8, 128)
@@ -386,7 +413,7 @@
         (shape(count, 2 * rows), token),
         "embed_before",
         limit=6,
-    )(protos, emb_ext, parts[0])
+    )(protos, emb_a, emb_b, parts[0])
     plan, sums, part = call(
         functools.partial(sweep_kernel, True, shares),
         (kept, shape(2, all_rows), shape(1, all_rows)),
@@ -401,7 +428,7 @@
     for sweep in range(ITERS - 2):
         parts = exchange(part)
         if sweep == ITERS - 3:
-            cots, done = cotangent((count, 2 * rows), lambda ids: 0)(ids, protos, view_t, parts[0])
+            cots, done = cotangent((count, 2 * rows), lambda ids: 0)(ids, protos, view_a, view_b, parts[0])
         if sweep == 0:
             own_entries, second, done = call(
                 form(proto_before_kernel),
@@ -409,7 +436,7 @@
                 "proto_before",
                 scalars=1,
                 limit=6,
-            )(ids, protos, emb_ext, view_t, parts[0])
+            )(ids, protos, emb_a, emb_b, view_a, view_b, parts[0])
         plan, part = call(
             functools.partial(sweep_kernel, False, shares),
             (kept, shape(1, all_rows)),
@@ -419,7 +446,7 @@
             limit=4,
         )(plan, cols, sums, *parts, done)
     parts = exchange(part)
-    own_cots, done = cotangent((own, all_rows), lambda ids: ids[0] >> 1)(ids, protos, view_t, parts[0])
+    own_cots, done = cotangent((own, all_rows), lambda ids: ids[0] >> 1)(ids, protos, view_a, view_b, parts[0])
     pieces = shape(shares, rows // shares, width)
     col_dual, row_dual, keep, give = call(
         functools.partial(embed_kernel, shares),
@@ -430,12 +457,12 @@
         limit=8,
     )(ids, plan, cols, sums, protos_t, entries, cots, *parts, done)
     half = lambda number, outs: call(functools.partial(proto_kernel, number), outs, "proto_grad", scalars=1, limit=6)
-    second, done = half(0, (shape(own, width), token))(ids, emb_ext, own_entries, own_cots, second, col_dual, row_dual)
+    second, done = half(0, (shape(own, width), token))(ids, emb_a, own_entries, own_cots, second, col_dual, row_dual)
     near = call(add_kernel, pieces, "add", limit=2)(keep, swap(give, "proto", 1), done)
     embed_grad = near[0]
     for place, pair in list(enumerate(others()))[1:]:
         embed_grad = embed_grad + swap_both(near[place], *pair)
-    proto_grad = half(1, (shape(own, width),))(ids, emb_ext, own_entries, own_cots, second, col_dual, row_dual)[0]
+    proto_grad = half(1, (shape(own, width),))(ids, emb_b, own_entries, own_cots, second, col_dual, row_dual)[0]
     return embed_grad, proto_grad
 
 

time: 75.5 us -> 75 us (level)
  waiting for transfers between devices: 14.5 us -> 12.7 us
  Pallas kernels: 29.8 us -> 30.8 us
    ppermute x14, waiting for transfers between devices: 10.2 us -> 8.39 us  [swap(): return lax.ppermute(value, axis, [(i, i ^ step) for i in range(size)])]
    pallas_call x20 -> x21, Pallas kernels: 29.8 us -> 30.8 us  [run(): pl.pallas_call(kernel, out_shape=out_shape, in_specs=[small] * scalars +...]
  transfers between devices with their start and end apart: 29 -> 29, of which waited for: 17 -> 16; matrix products, arithmetic and copies ran while one was open for 0% -> 0% of each run, Pallas kernels for 16% -> 21%
where the time goes in v8:
time: 75 us; the launch traced here: 74.9 us
  Pallas kernels  30.8 us (41%)
  starting transfers between devices  29.8 us (40%)
  waiting for transfers between devices  12.7 us (17%)
  between operations  0.9 us (1%)
    pallas_call x21, Pallas kernels, run(): pl.pallas_call(kernel, out_shape=out_shape, in_specs=[small] * scalars +...  30.8 us
    ppermute x15, starting transfers between devices, swap_both(): return lax.ppermute(value, ('row', 'proto'), pairs)  17.5 us
    ppermute x14, starting transfers between devices, swap(): return lax.ppermute(value, axis, [(i, i ^ step) for i in range(size)])  12.3 us
    ppermute x14, waiting for transfers between devices, swap(): return lax.ppermute(value, axis, [(i, i ^ step) for i in range(size)])  8.39 us
    ppermute x15, waiting for transfers between devices, swap_both(): return lax.ppermute(value, ('row', 'proto'), pairs)  4.27 us
  transfers between devices with their start and end apart: 29, of which 16 were waited for; matrix products, arithmetic and copies ran while one was open for 0% of the time, Pallas kernels for 21%

profile of v8, /device:TPU:0, one launch (start us, length us, event | category | flops | bytes accessed | tf_op | source)
XLA Modules:
  0.0 74.9 jit_solution(16986940190889564928)
XLA Ops:
  0.6 0.1 pad_add_fusion.ids
  0.7 1.0 %prepare.1.refs_0_ = bf16[144,256]{1,0:T(8,128)(2,1)S(1)} custom-call(s32[2]{0:T(128)S(1)} %pad_add_fusion.ids, bf16[256,128]{1,0:T(8,128)(2,1)} %embeddings.1, bf16[256,128]{1,0:T(8,128)(2,1)} %second_view.1, f32[1,256]{1,0:T(1,128)} %bitcast.19), custom_call_target="tpu_custom_call" | custom-call | tf_op jit(solution)/shard_map/prepare/pallas_call | solution.py:319
  1.7 5.1 %collective-permute-start.5 = (bf16[144,256]{1,0:T(8,128)(2,1)S(1)}, bf16[144,256]{1,0:T(8,128)(2,1)S(1)}, u32[]{:S(2)}, u32[]{:S(2)}) collective-permute-start(bf16[144,256]{1,0:T(8,128)(2,1)S(1)} %prepare.1.refs_0_), channel_id=1, source_target_pairs={{0,24},{4,28},{8,16},{12,20},{16,8},{20,12},{24,0},{28,4},{1,25},{... | collective-permute-start | bytes 221192 | tf_op jit(solution)/shard_map/ppermute | solution.py:28
  6.8 0.0 collective-permute-start.3
  6.8 0.6 collective-permute-start.1
  7.5 1.7 %collective-permute-start = (bf16[144,256]{1,0:T(8,128)(2,1)S(1)}, bf16[144,256]{1,0:T(8,128)(2,1)S(1)}, u32[]{:S(2)}, u32[]{:S(2)}) collective-permute-start(bf16[144,256]{1,0:T(8,128)(2,1)S(1)} %prepare.1.refs_0_), channel_id=1, source_target_pairs={{0,4},{4,0},{8,12},{12,8},{16,20},{20,16},{24,28},{28,24},{1,5},{5... | collective-permute-start | bytes 221192 | tf_op jit(solution)/shard_map/ppermute | solution.py:28
  9.1 0.4 collective-permute-done.5.refs_3_
  9.6 1.9 %collective-permute-start.6 = (bf16[144,256]{1,0:T(8,128)(2,1)S(1)}, bf16[144,256]{1,0:T(8,128)(2,1)S(1)}, u32[]{:S(2)}, u32[]{:S(2)}) collective-permute-start(bf16[144,256]{1,0:T(8,128)(2,1)S(1)} %collective-permute-done.5.refs_3_), channel_id=1, source_target_pairs={{0,4},{4,0},{8,12},{12,8},{16,20},{20,16},{24,28},{28,24},{1,5},{5... | collective-permute-start | bytes 221192 | tf_op jit(solution)/shard_map/ppermute | solution.py:28
  11.5 1.6 %collective-permute-done.3.refs_2_ = bf16[144,256]{1,0:T(8,128)(2,1)S(1)} collective-permute-done((bf16[144,256]{1,0:T(8,128)(2,1)S(1)}, bf16[144,256]{1,0:T(8,128)(2,1)S(1)}, u32[]{:S(2)}, u32[]{:S(2)}) %collective-permute-start.3) | collective-permute-done | bytes 73760 | tf_op jit(solution)/shard_map/ppermute | solution.py:28
  13.0 1.5 %collective-permute-start.4 = (bf16[144,256]{1,0:T(8,128)(2,1)S(1)}, bf16[144,256]{1,0:T(8,128)(2,1)S(1)}, u32[]{:S(2)}, u32[]{:S(2)}) collective-permute-start(bf16[144,256]{1,0:T(8,128)(2,1)S(1)} %collective-permute-done.3.refs_2_), channel_id=1, source_target_pairs={{0,4},{4,0},{8,12},{12,8},{16,20},{20,16},{24,28},{28,24},{1,5},{5... | collective-permute-start | bytes 221192 | tf_op jit(solution)/shard_map/ppermute | solution.py:28
  14.6 0.5 collective-permute-start.2
  15.1 2.0 %turn.1 = (bf16[2048,256]{1,0:T(8,128)(2,1)S(1)}, bf16[128,2048]{1,0:T(8,128)(2,1)S(1)}, f32[8,128]{1,0:T(8,128)S(1)}) custom-call(s32[2]{0:T(128)S(1)} %pad_add_fusion.ids, bf16[4096,128]{1,0:T(8,128)(2,1)} %protos.1, f32[1,4096]{1,0:T(1,128)} %bitcast.18), custom_call_target="tpu_custom_call" | custom-call | tf_op jit(solution)/shard_map/turn/pallas_call | solution.py:319
  17.1 0.1 collective-permute-start.8
  17.1 0.0 collective-permute-done.refs_0_
  17.2 0.0 collective-permute-done.6.refs_3_
  17.2 0.9 %collective-permute-done.4.refs_2_ = bf16[144,256]{1,0:T(8,128)(2,1)S(1)} collective-permute-done((bf16[144,256]{1,0:T(8,128)(2,1)S(1)}, bf16[144,256]{1,0:T(8,128)(2,1)S(1)}, u32[]{:S(2)}, u32[]{:S(2)}) %collective-permute-start.4) | collective-permute-done | bytes 73760 | tf_op jit(solution)/shard_map/ppermute | solution.py:28
  18.1 0.8 %collective-permute-done.2.refs_1_ = bf16[144,256]{1,0:T(8,128)(2,1)S(1)} collective-permute-done((bf16[144,256]{1,0:T(8,128)(2,1)S(1)}, bf16[144,256]{1,0:T(8,128)(2,1)S(1)}, u32[]{:S(2)}, u32[]{:S(2)}) %collective-permute-start.2) | collective-permute-done | bytes 73760 | tf_op jit(solution)/shard_map/ppermute | solution.py:28
  18.9 0.1 collective-permute-start.7
  19.0 3.0 %plan_ours.1 = (f32[2048,2048]{1,0:T(8,128)S(1)}, f32[2,2048,128]{2,1,0:T(8,128)S(1)}, f32[2,1024]{1,0:T(2,128)S(1)}, bf16[256,1024]{1,0:T(8,128)(2,1)S(1)}, bf16[128,1024]{1,0:T(8,128)(2,1)S(1)}) custom-call(s32[2]{0:T(128)S(1)} %pad_add_fusion.ids, bf16[2048,256]{1,0:T(8,128)(2,1)S(1)} %get-tuple-element.37.protos, bf16[4,144,256]{2,1,0:T(8,128)(2,1)S(1)} %stack.15.mine, ...), custom_call_target="tpu_custom_call" | custom-call | tf_op jit(solution)/shard_map/plan_ours/pallas_call | solution.py:319
  22.1 3.5 %plan_theirs.1 = (f32[2048,2048]{1,0:T(8,128)S(1)}, f32[2,2048,128]{2,1,0:T(8,128)S(1)}, f32[2,2048]{1,0:T(2,128)S(1)}, bf16[256,1024]{1,0:T(8,128)(2,1)S(1)}, bf16[128,1024]{1,0:T(8,128)(2,1)S(1)}) custom-call(s32[2]{0:T(128)S(1)} %pad_add_fusion.ids, bf16[2048,256]{1,0:T(8,128)(2,1)S(1)} %get-tuple-element.37.protos, ...), custom_call_target="tpu_custom_call", output_to_operand_aliasing={{0}: (4, {})} | custom-call | tf_op jit(solution)/shard_map/plan_theirs/pallas_call | solution.py:319
  25.6 0.6 collective-permute-start.9
  26.2 0.8 %collective-permute-done.9.right = f32[2,2048]{1,0:T(2,128)S(1)} collective-permute-done((f32[2,2048]{1,0:T(2,128)S(1)}, f32[2,2048]{1,0:T(2,128)S(1)}, u32[]{:S(2)}, u32[]{:S(2)}) %collective-permute-start.9) | collective-permute-done | bytes 16416 | tf_op jit(solution)/shard_map/ppermute | solution.py:28
  27.0 2.0 %collective-permute-start.12 = (f32[2,2048]{1,0:T(2,128)S(1)}, f32[2,2048]{1,0:T(2,128)S(1)}, u32[]{:S(2)}, u32[]{:S(2)}) collective-permute-start(f32[2,2048]{1,0:T(2,128)S(1)} %add.28.after.refs_0_), channel_id=1, source_target_pairs={{0,6},{1,7},{2,4},{3,5},{4,2},{5,3},{6,0},{7,1},{8,14},{9,15},{10,... | collective-permute-start | bytes 49160 | tf_op jit(solution)/shard_map/ppermute | solution.py:340
  29.0 1.0 %collective-permute-start.11 = (f32[2,2048]{1,0:T(2,128)S(1)}, f32[2,2048]{1,0:T(2,128)S(1)}, u32[]{:S(2)}, u32[]{:S(2)}) collective-permute-start(f32[2,2048]{1,0:T(2,128)S(1)} %add.28.after.refs_0_), channel_id=1, source_target_pairs={{0,4},{1,5},{2,6},{3,7},{4,0},{5,1},{6,2},{7,3},{8,12},{9,13},{10,... | collective-permute-start | bytes 49160 | tf_op jit(solution)/shard_map/ppermute | solution.py:340
  29.9 0.5 collective-permute-start.10
  30.5 2.0 %embed_before.1 = (f32[2048,512]{1,0:T(8,128)S(1)}, f32[8,128]{1,0:T(8,128)S(1)}) custom-call(bf16[2048,256]{1,0:T(8,128)(2,1)S(1)} %get-tuple-element.37.protos, bf16[256,1024]{1,0:T(8,128)(2,1)S(1)} %get-tuple-element.45.emb_a.emb_ext, bf16[256,1024]{1,0:T(8,128)(2,1)S(1)} %get-tuple-element.46.emb_b.emb_ext, f32[2,2048]{1,0:T(2,128)S(1)} %add.28.after.refs_0_), custom_call_target="tpu_custom_call" | custom-call | tf_op jit(solution)/shard_map/embed_before/pallas_call | solution.py:319
  32.5 0.0 collective-permute-done.12.refs_3_
  32.5 0.2 collective-permute-done.11.refs_2_
  32.7 1.0 %collective-permute-done.10.refs_1_ = f32[2,2048]{1,0:T(2,128)S(1)} collective-permute-done((f32[2,2048]{1,0:T(2,128)S(1)}, f32[2,2048]{1,0:T(2,128)S(1)}, u32[]{:S(2)}, u32[]{:S(2)}) %collective-permute-start.10) | collective-permute-done | bytes 16416 | tf_op jit(solution)/shard_map/ppermute | solution.py:340
  33.7 2.5 %sweep.3 = (f32[2048,2048]{1,0:T(8,128)S(1)}, f32[2,2048]{1,0:T(2,128)S(1)}, f32[1,2048]{1,0:T(1,128)S(1)}) custom-call(f32[2048,2048]{1,0:T(8,128)S(1)} %get-tuple-element.42.plan, f32[2,2048,128]{2,1,0:T(8,128)S(1)} %get-tuple-element.43.cols, f32[2,2048]{1,0:T(2,128)S(1)} %add.28.after.refs_0_, ...), custom_call_target="tpu_custom_call", output_to_operand_aliasing={{0}: (0, {})} | custom-call | tf_op jit(solution)/shard_map/sweep/pallas_call | solution.py:319
  36.2 0.1 collective-permute-start.13
  36.3 1.2 %collective-permute-done.13.right = f32[1,2048]{1,0:T(1,128)S(1)} collective-permute-done((f32[1,2048]{1,0:T(1,128)S(1)}, f32[1,2048]{1,0:T(1,128)S(1)}, u32[]{:S(2)}, u32[]{:S(2)}) %collective-permute-start.13) | collective-permute-done | bytes 8224 | tf_op jit(solution)/shard_map/ppermute | solution.py:28
  37.5 1.0 %collective-permute-start.16 = (f32[1,2048]{1,0:T(1,128)S(1)}, f32[1,2048]{1,0:T(1,128)S(1)}, u32[]{:S(2)}, u32[]{:S(2)}) collective-permute-start(f32[1,2048]{1,0:T(1,128)S(1)} %add.29.after.refs_1_), channel_id=1, source_target_pairs={{0,6},{1,7},{2,4},{3,5},{4,2},{5,3},{6,0},{7,1},{8,14},{9,15},{10,... | collective-permute-start | bytes 24584 | tf_op jit(solution)/shard_map/ppermute | solution.py:340
  38.5 1.0 %collective-permute-start.15 = (f32[1,2048]{1,0:T(1,128)S(1)}, f32[1,2048]{1,0:T(1,128)S(1)}, u32[]{:S(2)}, u32[]{:S(2)}) collective-permute-start(f32[1,2048]{1,0:T(1,128)S(1)} %add.29.after.refs_1_), channel_id=1, source_target_pairs={{0,4},{1,5},{2,6},{3,7},{4,0},{5,1},{6,2},{7,3},{8,12},{9,13},{10,... | collective-permute-start | bytes 24584 | tf_op jit(solution)/shard_map/ppermute | solution.py:340
  39.5 1.5 %collective-permute-start.14 = (f32[1,2048]{1,0:T(1,128)S(1)}, f32[1,2048]{1,0:T(1,128)S(1)}, u32[]{:S(2)}, u32[]{:S(2)}) collective-permute-start(f32[1,2048]{1,0:T(1,128)S(1)} %add.29.after.refs_1_), channel_id=1, source_target_pairs={{0,2},{1,3},{2,0},{3,1},{4,6},{5,7},{6,4},{7,5},{8,10},{9,11},{10,... | collective-permute-start | bytes 24584 | tf_op jit(solution)/shard_map/ppermute | solution.py:340
  41.0 2.0 %proto_before.1 = (f32[512,2048]{1,0:T(8,128)S(1)}, f32[512,128]{1,0:T(8,128)S(1)}, f32[8,128]{1,0:T(8,128)S(1)}) custom-call(s32[2]{0:T(128)S(1)} %pad_add_fusion.ids, bf16[2048,256]{1,0:T(8,128)(2,1)S(1)} %get-tuple-element.37.protos, bf16[256,1024]{1,0:T(8,128)(2,1)S(1)} %get-tuple-element.45.emb_a.emb_ext, ...), custom_call_target="tpu_custom_call" | custom-call | tf_op jit(solution)/shard_map/proto_before/pallas_call | solution.py:319
  43.0 0.1 collective-permute-done.14.refs_2_
  43.1 2.5 %sweep.4 = (f32[2048,2048]{1,0:T(8,128)S(1)}, f32[1,2048]{1,0:T(1,128)S(1)}) custom-call(f32[2048,2048]{1,0:T(8,128)S(1)} %get-tuple-element.48.plan, f32[2,2048,128]{2,1,0:T(8,128)S(1)} %get-tuple-element.43.cols, f32[2,2048]{1,0:T(2,128)S(1)} %get-tuple-element.49.refs_0_.sums, f32[1,2048]{1,0:T(1,128)S(1)} %add.29.after.refs_1_, ...), custom_call_target="tpu_custom_call", output_to_operand_aliasing={{0}: (0, {})} | custom-call | tf_op jit(solution)/shard_map/sweep/pallas_call | solution.py:319
  45.7 0.1 collective-permute-start.17
  45.7 1.2 %collective-permute-done.17.right = f32[1,2048]{1,0:T(1,128)S(1)} collective-permute-done((f32[1,2048]{1,0:T(1,128)S(1)}, f32[1,2048]{1,0:T(1,128)S(1)}, u32[]{:S(2)}, u32[]{:S(2)}) %collective-permute-start.17) | collective-permute-done | bytes 8224 | tf_op jit(solution)/shard_map/ppermute | solution.py:28
  46.9 2.0 %collective-permute-start.20 = (f32[1,2048]{1,0:T(1,128)S(1)}, f32[1,2048]{1,0:T(1,128)S(1)}, u32[]{:S(2)}, u32[]{:S(2)}) collective-permute-start(f32[1,2048]{1,0:T(1,128)S(1)} %add.30.after.refs_1_), channel_id=1, source_target_pairs={{0,6},{1,7},{2,4},{3,5},{4,2},{5,3},{6,0},{7,1},{8,14},{9,15},{10,... | collective-permute-start | bytes 24584 | tf_op jit(solution)/shard_map/ppermute | solution.py:340
  48.9 1.0 %collective-permute-start.19 = (f32[1,2048]{1,0:T(1,128)S(1)}, f32[1,2048]{1,0:T(1,128)S(1)}, u32[]{:S(2)}, u32[]{:S(2)}) collective-permute-start(f32[1,2048]{1,0:T(1,128)S(1)} %add.30.after.refs_1_), channel_id=1, source_target_pairs={{0,4},{1,5},{2,6},{3,7},{4,0},{5,1},{6,2},{7,3},{8,12},{9,13},{10,... | collective-permute-start | bytes 24584 | tf_op jit(solution)/shard_map/ppermute | solution.py:340
  49.9 0.5 collective-permute-start.18
  50.4 2.3 %cotangent.2 = (f32[2048,512]{1,0:T(8,128)S(1)}, f32[8,128]{1,0:T(8,128)S(1)}) custom-call(s32[2]{0:T(128)S(1)} %pad_add_fusion.ids, bf16[2048,256]{1,0:T(8,128)(2,1)S(1)} %get-tuple-element.37.protos, bf16[128,1024]{1,0:T(8,128)(2,1)S(1)} %get-tuple-element.51.view_a, bf16[128,1024]{1,0:T(8,128)(2,1)S(1)} %get-tuple-element.52.view_b, ...), custom_call_target="tpu_custom_call" | custom-call | tf_op jit(solution)/shard_map/cotangent/pallas_call | solution.py:319
  52.7 0.8 %collective-permute-done.18.refs_2_ = f32[1,2048]{1,0:T(1,128)S(1)} collective-permute-done((f32[1,2048]{1,0:T(1,128)S(1)}, f32[1,2048]{1,0:T(1,128)S(1)}, u32[]{:S(2)}, u32[]{:S(2)}) %collective-permute-start.18) | collective-permute-done | bytes 8224 | tf_op jit(solution)/shard_map/ppermute | solution.py:340
  53.5 2.5 %sweep.5 = (f32[2048,2048]{1,0:T(8,128)S(1)}, f32[1,2048]{1,0:T(1,128)S(1)}) custom-call(f32[2048,2048]{1,0:T(8,128)S(1)} %get-tuple-element.54.plan, f32[2,2048,128]{2,1,0:T(8,128)S(1)} %get-tuple-element.43.cols, f32[2,2048]{1,0:T(2,128)S(1)} %get-tuple-element.49.refs_0_.sums, f32[1,2048]{1,0:T(1,128)S(1)} %add.30.after.refs_1_, ...), custom_call_target="tpu_custom_call", output_to_operand_aliasing={{0}: (0, {})} | custom-call | tf_op jit(solution)/shard_map/sweep/pallas_call | solution.py:319
  56.0 0.1 collective-permute-start.21
  56.1 1.2 %collective-permute-done.21.right = f32[1,2048]{1,0:T(1,128)S(1)} collective-permute-done((f32[1,2048]{1,0:T(1,128)S(1)}, f32[1,2048]{1,0:T(1,128)S(1)}, u32[]{:S(2)}, u32[]{:S(2)}) %collective-permute-start.21) | collective-permute-done | bytes 8224 | tf_op jit(solution)/shard_map/ppermute | solution.py:28
  57.3 1.2 %collective-permute-start.24 = (f32[1,2048]{1,0:T(1,128)S(1)}, f32[1,2048]{1,0:T(1,128)S(1)}, u32[]{:S(2)}, u32[]{:S(2)}) collective-permute-start(f32[1,2048]{1,0:T(1,128)S(1)} %add.31.after.refs_0_), channel_id=1, source_target_pairs={{0,6},{1,7},{2,4},{3,5},{4,2},{5,3},{6,0},{7,1},{8,14},{9,15},{10,... | collective-permute-start | bytes 24584 | tf_op jit(solution)/shard_map/ppermute | solution.py:340
  58.5 1.0 %collective-permute-start.23 = (f32[1,2048]{1,0:T(1,128)S(1)}, f32[1,2048]{1,0:T(1,128)S(1)}, u32[]{:S(2)}, u32[]{:S(2)}) collective-permute-start(f32[1,2048]{1,0:T(1,128)S(1)} %add.31.after.refs_0_), channel_id=1, source_target_pairs={{0,4},{1,5},{2,6},{3,7},{4,0},{5,1},{6,2},{7,3},{8,12},{9,13},{10,... | collective-permute-start | bytes 24584 | tf_op jit(solution)/shard_map/ppermute | solution.py:340
  59.4 1.3 %collective-permute-start.22 = (f32[1,2048]{1,0:T(1,128)S(1)}, f32[1,2048]{1,0:T(1,128)S(1)}, u32[]{:S(2)}, u32[]{:S(2)}) collective-permute-start(f32[1,2048]{1,0:T(1,128)S(1)} %add.31.after.refs_0_), channel_id=1, source_target_pairs={{0,2},{1,3},{2,0},{3,1},{4,6},{5,7},{6,4},{7,5},{8,10},{9,11},{10,... | collective-permute-start | bytes 24584 | tf_op jit(solution)/shard_map/ppermute | solution.py:340
  60.8 1.4 %cotangent.3 = (f32[512,2048]{1,0:T(8,128)S(1)}, f32[8,128]{1,0:T(8,128)S(1)}) custom-call(s32[2]{0:T(128)S(1)} %pad_add_fusion.ids, bf16[2048,256]{1,0:T(8,128)(2,1)S(1)} %get-tuple-element.37.protos, bf16[128,1024]{1,0:T(8,128)(2,1)S(1)} %get-tuple-element.51.view_a, bf16[128,1024]{1,0:T(8,128)(2,1)S(1)} %get-tuple-element.52.view_b, ...), custom_call_target="tpu_custom_call" | custom-call | tf_op jit(solution)/shard_map/cotangent/pallas_call | solution.py:319
  62.2 0.9 %collective-permute-done.22.refs_1_ = f32[1,2048]{1,0:T(1,128)S(1)} collective-permute-done((f32[1,2048]{1,0:T(1,128)S(1)}, f32[1,2048]{1,0:T(1,128)S(1)}, u32[]{:S(2)}, u32[]{:S(2)}) %collective-permute-start.22) | collective-permute-done | bytes 8224 | tf_op jit(solution)/shard_map/ppermute | solution.py:340
  63.1 3.1 %embed_grad.1 = (f32[2048,128]{1,0:T(8,128)S(1)}, f32[1,2048]{1,0:T(1,128)S(1)}, f32[4,64,128]{2,1,0:T(8,128)S(1)}, f32[4,64,128]{2,1,0:T(8,128)S(1)}) custom-call(s32[2]{0:T(128)S(1)} %pad_add_fusion.ids, f32[2048,2048]{1,0:T(8,128)S(1)} %get-tuple-element.57.plan, f32[2,2048,128]{2,1,0:T(8,128)S(1)} %get-tuple-element.43.cols, ...), custom_call_target="tpu_custom_call" | custom-call | tf_op jit(solution)/shard_map/embed_grad/pallas_call | solution.py:319
  66.2 0.1 collective-permute-start.25
  66.3 1.0 %proto_grad.2 = (f32[512,128]{1,0:T(8,128)S(1)}, f32[8,128]{1,0:T(8,128)S(1)}) custom-call(s32[2]{0:T(128)S(1)} %pad_add_fusion.ids, bf16[256,1024]{1,0:T(8,128)(2,1)S(1)} %get-tuple-element.45.emb_a.emb_ext, f32[512,2048]{1,0:T(8,128)S(1)} %get-tuple-element.65.entries, f32[512,2048]{1,0:T(8,128)S(1)} %get-tuple-element.66.cots, ...), custom_call_target="tpu_custom_call" | custom-call | tf_op jit(solution)/shard_map/proto_grad/pallas_call | solution.py:319
  67.4 0.3 collective-permute-done.25.right
  67.7 1.4 %collective-permute-start.26 = (f32[64,128]{1,0:T(8,128)S(1)}, f32[64,128]{1,0:T(8,128)S(1)}, u32[]{:S(2)}, u32[]{:S(2)}) collective-permute-start(f32[64,128]{1,0:T(8,128)S(1)} %get-tuple-element.72), channel_id=1, source_target_pairs={{0,2},{1,3},{2,0},{3,1},{4,6},{5,7},{6,4},{7,5},{8,10},{9,11},{10,... | collective-permute-start | bytes 98312 | tf_op jit(solution)/shard_map/ppermute | solution.py:340
  69.1 1.2 %collective-permute-start.28 = (f32[64,128]{1,0:T(8,128)S(1)}, f32[64,128]{1,0:T(8,128)S(1)}, u32[]{:S(2)}, u32[]{:S(2)}) collective-permute-start(f32[64,128]{1,0:T(8,128)S(1)} %get-tuple-element.73), channel_id=1, source_target_pairs={{0,6},{1,7},{2,4},{3,5},{4,2},{5,3},{6,0},{7,1},{8,14},{9,15},{10,... | collective-permute-start | bytes 98312 | tf_op jit(solution)/shard_map/ppermute | solution.py:340
  70.3 1.0 %collective-permute-start.27 = (f32[64,128]{1,0:T(8,128)S(1)}, f32[64,128]{1,0:T(8,128)S(1)}, u32[]{:S(2)}, u32[]{:S(2)}) collective-permute-start(f32[64,128]{1,0:T(8,128)S(1)} %get-tuple-element.74), channel_id=1, source_target_pairs={{0,4},{1,5},{2,6},{3,7},{4,0},{5,1},{6,2},{7,3},{8,12},{9,13},{10,... | collective-permute-start | bytes 98312 | tf_op jit(solution)/shard_map/ppermute | solution.py:340
  71.2 1.7 %proto_grad.3 = f32[512,128]{1,0:T(8,128)} custom-call(s32[2]{0:T(128)S(1)} %pad_add_fusion.ids, bf16[256,1024]{1,0:T(8,128)(2,1)S(1)} %get-tuple-element.46.emb_b.emb_ext, f32[512,2048]{1,0:T(8,128)S(1)} %get-tuple-element.65.entries, f32[512,2048]{1,0:T(8,128)S(1)} %get-tuple-element.66.cots, f32[512,128]{1,0:T(8,128)S(1)} %get-tuple-element.71.so_far, ...), custom_call_target="tpu_custom_call" | custom-call | tf_op jit(solution)/shard_map/proto_grad/pallas_call | solution.py:319
  73.0 0.9 %collective-permute-done.28 = f32[64,128]{1,0:T(8,128)S(1)} collective-permute-done((f32[64,128]{1,0:T(8,128)S(1)}, f32[64,128]{1,0:T(8,128)S(1)}, u32[]{:S(2)}, u32[]{:S(2)}) %collective-permute-start.28) | collective-permute-done | bytes 32800 | tf_op jit(solution)/shard_map/ppermute | solution.py:340
  73.9 0.4 collective-permute-done.27
  74.2 0.6 fusion.2
  (18 shorter events, 0.1 us)
Async XLA Ops:
  1.7 7.9 %collective-permute-start.5 = (bf16[144,256]{1,0:T(8,128)(2,1)S(1)}, bf16[144,256]{1,0:T(8,128)(2,1)S(1)}, u32[]{:S(2)}, u32[]{:S(2)}) collective-permute-start(bf16[144,256]{1,0:T(8,128)(2,1)S(1)} %prepare.1.refs_0_), channel_id=1, source_target_pairs={{0,24},{4,28},{8,16},{12,20},{16,8},{20,12},{24,0},{28,4},{1,25},{... | collective-permute-start | bytes 221192 | tf_op jit(solution)/shard_map/ppermute | solution.py:28
  6.8 6.2 %collective-permute-start.3 = (bf16[144,256]{1,0:T(8,128)(2,1)S(1)}, bf16[144,256]{1,0:T(8,128)(2,1)S(1)}, u32[]{:S(2)}, u32[]{:S(2)}) collective-permute-start(bf16[144,256]{1,0:T(8,128)(2,1)S(1)} %prepare.1.refs_0_), channel_id=1, source_target_pairs={{0,16},{4,20},{8,24},{12,28},{16,0},{20,4},{24,8},{28,12},{1,17},{... | collective-permute-start | bytes 221192 | tf_op jit(solution)/shard_map/ppermute | solution.py:28
  6.8 7.7 %collective-permute-start.1 = (bf16[144,256]{1,0:T(8,128)(2,1)S(1)}, bf16[144,256]{1,0:T(8,128)(2,1)S(1)}, u32[]{:S(2)}, u32[]{:S(2)}) collective-permute-start(bf16[144,256]{1,0:T(8,128)(2,1)S(1)} %prepare.1.refs_0_), channel_id=1, source_target_pairs={{0,8},{4,12},{8,0},{12,4},{16,24},{20,28},{24,16},{28,20},{1,9},{5... | collective-permute-start | bytes 221192 | tf_op jit(solution)/shard_map/ppermute | solution.py:28
  7.5 9.7 %collective-permute-start = (bf16[144,256]{1,0:T(8,128)(2,1)S(1)}, bf16[144,256]{1,0:T(8,128)(2,1)S(1)}, u32[]{:S(2)}, u32[]{:S(2)}) collective-permute-start(bf16[144,256]{1,0:T(8,128)(2,1)S(1)} %prepare.1.refs_0_), channel_id=1, source_target_pairs={{0,4},{4,0},{8,12},{12,8},{16,20},{20,16},{24,28},{28,24},{1,5},{5... | collective-permute-start | bytes 221192 | tf_op jit(solution)/shard_map/ppermute | solution.py:28
  9.6 7.6 %collective-permute-start.6 = (bf16[144,256]{1,0:T(8,128)(2,1)S(1)}, bf16[144,256]{1,0:T(8,128)(2,1)S(1)}, u32[]{:S(2)}, u32[]{:S(2)}) collective-permute-start(bf16[144,256]{1,0:T(8,128)(2,1)S(1)} %collective-permute-done.5.refs_3_), channel_id=1, source_target_pairs={{0,4},{4,0},{8,12},{12,8},{16,20},{20,16},{24,28},{28,24},{1,5},{5... | collective-permute-start | bytes 221192 | tf_op jit(solution)/shard_map/ppermute | solution.py:28
  13.0 5.1 %collective-permute-start.4 = (bf16[144,256]{1,0:T(8,128)(2,1)S(1)}, bf16[144,256]{1,0:T(8,128)(2,1)S(1)}, u32[]{:S(2)}, u32[]{:S(2)}) collective-permute-start(bf16[144,256]{1,0:T(8,128)(2,1)S(1)} %collective-permute-done.3.refs_2_), channel_id=1, source_target_pairs={{0,4},{4,0},{8,12},{12,8},{16,20},{20,16},{24,28},{28,24},{1,5},{5... | collective-permute-start | bytes 221192 | tf_op jit(solution)/shard_map/ppermute | solution.py:28
  14.6 4.4 %collective-permute-start.2 = (bf16[144,256]{1,0:T(8,128)(2,1)S(1)}, bf16[144,256]{1,0:T(8,128)(2,1)S(1)}, u32[]{:S(2)}, u32[]{:S(2)}) collective-permute-start(bf16[144,256]{1,0:T(8,128)(2,1)S(1)} %collective-permute-done.1.refs_1_), channel_id=1, source_target_pairs={{0,4},{4,0},{8,12},{12,8},{16,20},{20,16},{24,28},{28,24},{1,5},{5... | collective-permute-start | bytes 221192 | tf_op jit(solution)/shard_map/ppermute | solution.py:28
  17.1 2.0 %collective-permute-start.8 = (bf16[4,144,256]{2,1,0:T(8,128)(2,1)S(1)}, bf16[4,144,256]{2,1,0:T(8,128)(2,1)S(1)}, u32[]{:S(2)}, u32[]{:S(2)}) collective-permute-start(bf16[4,144,256]{2,1,0:T(8,128)(2,1)S(1)} %stack.15.mine), channel_id=1, source_target_pairs={{0,1},{1,0},{2,3},{3,2},{4,5},{5,4},{6,7},{7,6},{8,9},{9,8},{10,11... | collective-permute-start | bytes 884744 | tf_op jit(solution)/shard_map/ppermute | solution.py:28
  18.9 3.1 %collective-permute-start.7 = (bf16[4,144,256]{2,1,0:T(8,128)(2,1)S(1)}, bf16[4,144,256]{2,1,0:T(8,128)(2,1)S(1)}, u32[]{:S(2)}, u32[]{:S(2)}) collective-permute-start(bf16[4,144,256]{2,1,0:T(8,128)(2,1)S(1)} %stack.14.mine), channel_id=1, source_target_pairs={{0,1},{1,0},{2,3},{3,2},{4,5},{5,4},{6,7},{7,6},{8,9},{9,8},{10,11... | collective-permute-start | bytes 884744 | tf_op jit(solution)/shard_map/ppermute | solution.py:28
  25.6 1.4 %collective-permute-start.9 = (f32[2,2048]{1,0:T(2,128)S(1)}, f32[2,2048]{1,0:T(2,128)S(1)}, u32[]{:S(2)}, u32[]{:S(2)}) collective-permute-start(f32[2,2048]{1,0:T(2,128)S(1)} %get-tuple-element.44.left), channel_id=1, source_target_pairs={{0,1},{1,0},{2,3},{3,2},{4,5},{5,4},{6,7},{7,6},{8,9},{9,8},{10,11... | collective-permute-start | bytes 49160 | tf_op jit(solution)/shard_map/ppermute | solution.py:28
  27.0 5.5 %collective-permute-start.12 = (f32[2,2048]{1,0:T(2,128)S(1)}, f32[2,2048]{1,0:T(2,128)S(1)}, u32[]{:S(2)}, u32[]{:S(2)}) collective-permute-start(f32[2,2048]{1,0:T(2,128)S(1)} %add.28.after.refs_0_), channel_id=1, source_target_pairs={{0,6},{1,7},{2,4},{3,5},{4,2},{5,3},{6,0},{7,1},{8,14},{9,15},{10,... | collective-permute-start | bytes 49160 | tf_op jit(solution)/shard_map/ppermute | solution.py:340
  29.0 3.7 %collective-permute-start.11 = (f32[2,2048]{1,0:T(2,128)S(1)}, f32[2,2048]{1,0:T(2,128)S(1)}, u32[]{:S(2)}, u32[]{:S(2)}) collective-permute-start(f32[2,2048]{1,0:T(2,128)S(1)} %add.28.after.refs_0_), channel_id=1, source_target_pairs={{0,4},{1,5},{2,6},{3,7},{4,0},{5,1},{6,2},{7,3},{8,12},{9,13},{10,... | collective-permute-start | bytes 49160 | tf_op jit(solution)/shard_map/ppermute | solution.py:340
  29.9 3.7 %collective-permute-start.10 = (f32[2,2048]{1,0:T(2,128)S(1)}, f32[2,2048]{1,0:T(2,128)S(1)}, u32[]{:S(2)}, u32[]{:S(2)}) collective-permute-start(f32[2,2048]{1,0:T(2,128)S(1)} %add.28.after.refs_0_), channel_id=1, source_target_pairs={{0,2},{1,3},{2,0},{3,1},{4,6},{5,7},{6,4},{7,5},{8,10},{9,11},{10,... | collective-permute-start | bytes 49160 | tf_op jit(solution)/shard_map/ppermute | solution.py:340
  36.2 1.2 %collective-permute-start.13 = (f32[1,2048]{1,0:T(1,128)S(1)}, f32[1,2048]{1,0:T(1,128)S(1)}, u32[]{:S(2)}, u32[]{:S(2)}) collective-permute-start(f32[1,2048]{1,0:T(1,128)S(1)} %get-tuple-element.50.left), channel_id=1, source_target_pairs={{0,1},{1,0},{2,3},{3,2},{4,5},{5,4},{6,7},{7,6},{8,9},{9,8},{10,11... | collective-permute-start | bytes 24584 | tf_op jit(solution)/shard_map/ppermute | solution.py:28
  37.5 5.5 %collective-permute-start.16 = (f32[1,2048]{1,0:T(1,128)S(1)}, f32[1,2048]{1,0:T(1,128)S(1)}, u32[]{:S(2)}, u32[]{:S(2)}) collective-permute-start(f32[1,2048]{1,0:T(1,128)S(1)} %add.29.after.refs_1_), channel_id=1, source_target_pairs={{0,6},{1,7},{2,4},{3,5},{4,2},{5,3},{6,0},{7,1},{8,14},{9,15},{10,... | collective-permute-start | bytes 24584 | tf_op jit(solution)/shard_map/ppermute | solution.py:340
  38.5 4.5 %collective-permute-start.15 = (f32[1,2048]{1,0:T(1,128)S(1)}, f32[1,2048]{1,0:T(1,128)S(1)}, u32[]{:S(2)}, u32[]{:S(2)}) collective-permute-start(f32[1,2048]{1,0:T(1,128)S(1)} %add.29.after.refs_1_), channel_id=1, source_target_pairs={{0,4},{1,5},{2,6},{3,7},{4,0},{5,1},{6,2},{7,3},{8,12},{9,13},{10,... | collective-permute-start | bytes 24584 | tf_op jit(solution)/shard_map/ppermute | solution.py:340
  39.5 3.7 %collective-permute-start.14 = (f32[1,2048]{1,0:T(1,128)S(1)}, f32[1,2048]{1,0:T(1,128)S(1)}, u32[]{:S(2)}, u32[]{:S(2)}) collective-permute-start(f32[1,2048]{1,0:T(1,128)S(1)} %add.29.after.refs_1_), channel_id=1, source_target_pairs={{0,2},{1,3},{2,0},{3,1},{4,6},{5,7},{6,4},{7,5},{8,10},{9,11},{10,... | collective-permute-start | bytes 24584 | tf_op jit(solution)/shard_map/ppermute | solution.py:340
  45.7 1.2 %collective-permute-start.17 = (f32[1,2048]{1,0:T(1,128)S(1)}, f32[1,2048]{1,0:T(1,128)S(1)}, u32[]{:S(2)}, u32[]{:S(2)}) collective-permute-start(f32[1,2048]{1,0:T(1,128)S(1)} %get-tuple-element.55.left), channel_id=1, source_target_pairs={{0,1},{1,0},{2,3},{3,2},{4,5},{5,4},{6,7},{7,6},{8,9},{9,8},{10,11... | collective-permute-start | bytes 24584 | tf_op jit(solution)/shard_map/ppermute | solution.py:28
  46.9 5.8 %collective-permute-start.20 = (f32[1,2048]{1,0:T(1,128)S(1)}, f32[1,2048]{1,0:T(1,128)S(1)}, u32[]{:S(2)}, u32[]{:S(2)}) collective-permute-start(f32[1,2048]{1,0:T(1,128)S(1)} %add.30.after.refs_1_), channel_id=1, source_target_pairs={{0,6},{1,7},{2,4},{3,5},{4,2},{5,3},{6,0},{7,1},{8,14},{9,15},{10,... | collective-permute-start | bytes 24584 | tf_op jit(solution)/shard_map/ppermute | solution.py:340
  48.9 3.8 %collective-permute-start.19 = (f32[1,2048]{1,0:T(1,128)S(1)}, f32[1,2048]{1,0:T(1,128)S(1)}, u32[]{:S(2)}, u32[]{:S(2)}) collective-permute-start(f32[1,2048]{1,0:T(1,128)S(1)} %add.30.after.refs_1_), channel_id=1, source_target_pairs={{0,4},{1,5},{2,6},{3,7},{4,0},{5,1},{6,2},{7,3},{8,12},{9,13},{10,... | collective-permute-start | bytes 24584 | tf_op jit(solution)/shard_map/ppermute | solution.py:340
  49.9 3.7 %collective-permute-start.18 = (f32[1,2048]{1,0:T(1,128)S(1)}, f32[1,2048]{1,0:T(1,128)S(1)}, u32[]{:S(2)}, u32[]{:S(2)}) collective-permute-start(f32[1,2048]{1,0:T(1,128)S(1)} %add.30.after.refs_1_), channel_id=1, source_target_pairs={{0,2},{1,3},{2,0},{3,1},{4,6},{5,7},{6,4},{7,5},{8,10},{9,11},{10,... | collective-permute-start | bytes 24584 | tf_op jit(solution)/shard_map/ppermute | solution.py:340
  56.0 1.2 %collective-permute-start.21 = (f32[1,2048]{1,0:T(1,128)S(1)}, f32[1,2048]{1,0:T(1,128)S(1)}, u32[]{:S(2)}, u32[]{:S(2)}) collective-permute-start(f32[1,2048]{1,0:T(1,128)S(1)} %get-tuple-element.61.left), channel_id=1, source_target_pairs={{0,1},{1,0},{2,3},{3,2},{4,5},{5,4},{6,7},{7,6},{8,9},{9,8},{10,11... | collective-permute-start | bytes 24584 | tf_op jit(solution)/shard_map/ppermute | solution.py:28
  57.3 4.9 %collective-permute-start.24 = (f32[1,2048]{1,0:T(1,128)S(1)}, f32[1,2048]{1,0:T(1,128)S(1)}, u32[]{:S(2)}, u32[]{:S(2)}) collective-permute-start(f32[1,2048]{1,0:T(1,128)S(1)} %add.31.after.refs_0_), channel_id=1, source_target_pairs={{0,6},{1,7},{2,4},{3,5},{4,2},{5,3},{6,0},{7,1},{8,14},{9,15},{10,... | collective-permute-start | bytes 24584 | tf_op jit(solution)/shard_map/ppermute | solution.py:340
  58.5 3.7 %collective-permute-start.23 = (f32[1,2048]{1,0:T(1,128)S(1)}, f32[1,2048]{1,0:T(1,128)S(1)}, u32[]{:S(2)}, u32[]{:S(2)}) collective-permute-start(f32[1,2048]{1,0:T(1,128)S(1)} %add.31.after.refs_0_), channel_id=1, source_target_pairs={{0,4},{1,5},{2,6},{3,7},{4,0},{5,1},{6,2},{7,3},{8,12},{9,13},{10,... | collective-permute-start | bytes 24584 | tf_op jit(solution)/shard_map/ppermute | solution.py:340
  59.4 3.7 %collective-permute-start.22 = (f32[1,2048]{1,0:T(1,128)S(1)}, f32[1,2048]{1,0:T(1,128)S(1)}, u32[]{:S(2)}, u32[]{:S(2)}) collective-permute-start(f32[1,2048]{1,0:T(1,128)S(1)} %add.31.after.refs_0_), channel_id=1, source_target_pairs={{0,2},{1,3},{2,0},{3,1},{4,6},{5,7},{6,4},{7,5},{8,10},{9,11},{10,... | collective-permute-start | bytes 24584 | tf_op jit(solution)/shard_map/ppermute | solution.py:340
  66.2 1.4 %collective-permute-start.25 = (f32[4,64,128]{2,1,0:T(8,128)S(1)}, f32[4,64,128]{2,1,0:T(8,128)S(1)}, u32[]{:S(2)}, u32[]{:S(2)}) collective-permute-start(f32[4,64,128]{2,1,0:T(8,128)S(1)} %get-tuple-element.64), channel_id=1, source_target_pairs={{0,1},{1,0},{2,3},{3,2},{4,5},{5,4},{6,7},{7,6},{8,9},{9,8},{10,11... | collective-permute-start | bytes 393224 | tf_op jit(solution)/shard_map/ppermute | solution.py:28
  67.7 5.3 %collective-permute-start.26 = (f32[64,128]{1,0:T(8,128)S(1)}, f32[64,128]{1,0:T(8,128)S(1)}, u32[]{:S(2)}, u32[]{:S(2)}) collective-permute-start(f32[64,128]{1,0:T(8,128)S(1)} %get-tuple-element.72), channel_id=1, source_target_pairs={{0,2},{1,3},{2,0},{3,1},{4,6},{5,7},{6,4},{7,5},{8,10},{9,11},{10,... | collective-permute-start | bytes 98312 | tf_op jit(solution)/shard_map/ppermute | solution.py:340
  69.1 4.8 %collective-permute-start.28 = (f32[64,128]{1,0:T(8,128)S(1)}, f32[64,128]{1,0:T(8,128)S(1)}, u32[]{:S(2)}, u32[]{:S(2)}) collective-permute-start(f32[64,128]{1,0:T(8,128)S(1)} %get-tuple-element.73), channel_id=1, source_target_pairs={{0,6},{1,7},{2,4},{3,5},{4,2},{5,3},{6,0},{7,1},{8,14},{9,15},{10,... | collective-permute-start | bytes 98312 | tf_op jit(solution)/shard_map/ppermute | solution.py:340
  70.3 4.0 %collective-permute-start.27 = (f32[64,128]{1,0:T(8,128)S(1)}, f32[64,128]{1,0:T(8,128)S(1)}, u32[]{:S(2)}, u32[]{:S(2)}) collective-permute-start(f32[64,128]{1,0:T(8,128)S(1)} %get-tuple-element.74), channel_id=1, source_target_pairs={{0,4},{1,5},{2,6},{3,7},{4,0},{5,1},{6,2},{7,3},{8,12},{9,13},{10,... | collective-permute-start | bytes 98312 | tf_op jit(solution)/shard_map/ppermute | solution.py:340

commit v9 on v8

--- a/solution.py
+++ b/solution.py
@@ -152,7 +152,7 @@
 
 
 def added(parts):
-    plain, turned = parts[:len(parts) // 2], parts[len(parts) // 2:]
+    turned, plain = parts[:len(parts) // 2], parts[len(parts) // 2:]
     total, other = plain[0][...], turned[0][...]
     for part in plain[1:]:
         total = total + part[...]
@@ -265,7 +265,7 @@
         duals_out[here, :] = by_rows(plan.at[here, :], cols, here, spread)
         return carry
 
-    lax.fori_loop(0, plan.shape[0] // STEP, duals, 0, unroll=2)
+    lax.fori_loop(0, plan.shape[0] // STEP, duals, 0, unroll=4)
     total = jnp.zeros((width, rows), F32)
     for start in range(0, plan.shape[0], CHUNK):
         here = slice(start, start + CHUNK)
@@ -347,7 +347,7 @@
 
 def exchange(part):
     near = call(add_kernel, jax.ShapeDtypeStruct(part.shape, F32), "add", limit=2)(part, swap(part, "proto", 1))
-    return [near if pair == (0, 0) else swap_both(near, *pair) for pair in others()]
+    return near, [near if pair == (0, 0) else swap_both(near, *pair) for pair in reversed(others())]
 
 
 def kept_plan(embeddings, second_view, prototypes, row_scale, col_scale):
@@ -407,13 +407,13 @@
 
     work = [(F32, 8, all_rows), (F32, 8, all_rows)]
     token = shape(8, 128)
-    parts = exchange(sums)
+    near, parts = exchange(sums)
     entries, done = call(
         functools.partial(embed_before_kernel, scales[0]),
         (shape(count, 2 * rows), token),
         "embed_before",
         limit=6,
-    )(protos, emb_a, emb_b, parts[0])
+    )(protos, emb_a, emb_b, near)
     plan, sums, part = call(
         functools.partial(sweep_kernel, True, shares),
         (kept, shape(2, all_rows), shape(1, all_rows)),
@@ -426,9 +426,9 @@
         functools.partial(cotangent_kernel, scales[1], block), (shape(*dims), token), "cotangent", scalars=1, limit=4
     )
     for sweep in range(ITERS - 2):
-        parts = exchange(part)
+        near, parts = exchange(part)
         if sweep == ITERS - 3:
-            cots, done = cotangent((count, 2 * rows), lambda ids: 0)(ids, protos, view_a, view_b, parts[0])
+            cots, done = cotangent((count, 2 * rows), lambda ids: 0)(ids, protos, view_a, view_b, near)
         if sweep == 0:
             own_entries, second, done = call(
                 form(proto_before_kernel),
@@ -436,7 +436,7 @@
                 "proto_before",
                 scalars=1,
                 limit=6,
-            )(ids, protos, emb_a, emb_b, view_a, view_b, parts[0])
+            )(ids, protos, emb_a, emb_b, view_a, view_b, near)
         plan, part = call(
             functools.partial(sweep_kernel, False, shares),
             (kept, shape(1, all_rows)),
@@ -445,8 +445,8 @@
             aliases={0: 0},
             limit=4,
         )(plan, cols, sums, *parts, done)
-    parts = exchange(part)
-    own_cots, done = cotangent((own, all_rows), lambda ids: ids[0] >> 1)(ids, protos, view_a, view_b, parts[0])
+    near, parts = exchange(part)
+    own_cots, done = cotangent((own, all_rows), lambda ids: ids[0] >> 1)(ids, protos, view_a, view_b, near)
     pieces = shape(shares, rows // shares, width)
     col_dual, row_dual, keep, give = call(
         functools.partial(embed_kernel, shares),
@@ -460,7 +460,7 @@
     second, done = half(0, (shape(own, width), token))(ids, emb_a, own_entries, own_cots, second, col_dual, row_dual)
     near = call(add_kernel, pieces, "add", limit=2)(keep, swap(give, "proto", 1), done)
     embed_grad = near[0]
-    for place, pair in list(enumerate(others()))[1:]:
+    for place, pair in reversed(list(enumerate(others()))[1:]):
         embed_grad = embed_grad + swap_both(near[place], *pair)
     proto_grad = half(1, (shape(own, width),))(ids, emb_b, own_entries, own_cots, second, col_dual, row_dual)[0]
     return embed_grad, proto_grad

time: 75 us -> 76.4 us (1.019)
  waiting for transfers between devices: 12.7 us -> 14.2 us
    ppermute x15, waiting for transfers between devices: 4.27 us -> 5.83 us  [swap_both(): return lax.ppermute(value, ('row', 'proto'), pairs)]
  transfers between devices with their start and end apart: 29 -> 29, of which waited for: 16 -> 15; matrix products, arithmetic and copies ran while one was open for 0% -> 0% of each run, Pallas kernels for 21% -> 20%
where the time goes in v9:
time: 76.4 us; the launch traced here: 76.3 us
  Pallas kernels  30.6 us (40%)
  starting transfers between devices  29.8 us (39%)
  waiting for transfers between devices  14.2 us (19%)
  between operations  0.91 us (1%)
    pallas_call x21, Pallas kernels, run(): pl.pallas_call(kernel, out_shape=out_shape, in_specs=[small] * scalars +...  30.6 us
    ppermute x15, starting transfers between devices, swap_both(): return lax.ppermute(value, ('row', 'proto'), pairs)  17.5 us
    ppermute x14, starting transfers between devices, swap(): return lax.ppermute(value, axis, [(i, i ^ step) for i in range(size)])  12.3 us
    ppermute x14, waiting for transfers between devices, swap(): return lax.ppermute(value, axis, [(i, i ^ step) for i in range(size)])  8.39 us
    ppermute x15, waiting for transfers between devices, swap_both(): return lax.ppermute(value, ('row', 'proto'), pairs)  5.83 us
  transfers between devices with their start and end apart: 29, of which 15 were waited for; matrix products, arithmetic and copies ran while one was open for 0% of the time, Pallas kernels for 20%

profile of v9, /device:TPU:0, one launch (start us, length us, event | category | flops | bytes accessed | tf_op | source)
XLA Modules:
  0.0 76.3 jit_solution(11933373207839863172)
XLA Ops:
  0.6 0.1 pad_add_fusion.ids
  0.7 1.0 %prepare.1.refs_0_ = bf16[144,256]{1,0:T(8,128)(2,1)S(1)} custom-call(s32[2]{0:T(128)S(1)} %pad_add_fusion.ids, bf16[256,128]{1,0:T(8,128)(2,1)} %embeddings.1, bf16[256,128]{1,0:T(8,128)(2,1)} %second_view.1, f32[1,256]{1,0:T(1,128)} %bitcast.19), custom_call_target="tpu_custom_call" | custom-call | tf_op jit(solution)/shard_map/prepare/pallas_call | solution.py:319
  1.7 5.1 %collective-permute-start.5 = (bf16[144,256]{1,0:T(8,128)(2,1)S(1)}, bf16[144,256]{1,0:T(8,128)(2,1)S(1)}, u32[]{:S(2)}, u32[]{:S(2)}) collective-permute-start(bf16[144,256]{1,0:T(8,128)(2,1)S(1)} %prepare.1.refs_0_), channel_id=1, source_target_pairs={{0,24},{4,28},{8,16},{12,20},{16,8},{20,12},{24,0},{28,4},{1,25},{... | collective-permute-start | bytes 221192 | tf_op jit(solution)/shard_map/ppermute | solution.py:28
  6.8 0.6 collective-permute-start.1
  7.5 1.7 %collective-permute-start = (bf16[144,256]{1,0:T(8,128)(2,1)S(1)}, bf16[144,256]{1,0:T(8,128)(2,1)S(1)}, u32[]{:S(2)}, u32[]{:S(2)}) collective-permute-start(bf16[144,256]{1,0:T(8,128)(2,1)S(1)} %prepare.1.refs_0_), channel_id=1, source_target_pairs={{0,4},{4,0},{8,12},{12,8},{16,20},{20,16},{24,28},{28,24},{1,5},{5... | collective-permute-start | bytes 221192 | tf_op jit(solution)/shard_map/ppermute | solution.py:28
  9.1 0.4 collective-permute-done.5.refs_3_
  9.6 1.9 %collective-permute-start.6 = (bf16[144,256]{1,0:T(8,128)(2,1)S(1)}, bf16[144,256]{1,0:T(8,128)(2,1)S(1)}, u32[]{:S(2)}, u32[]{:S(2)}) collective-permute-start(bf16[144,256]{1,0:T(8,128)(2,1)S(1)} %collective-permute-done.5.refs_3_), channel_id=1, source_target_pairs={{0,4},{4,0},{8,12},{12,8},{16,20},{20,16},{24,28},{28,24},{1,5},{5... | collective-permute-start | bytes 221192 | tf_op jit(solution)/shard_map/ppermute | solution.py:28
  11.5 1.6 %collective-permute-done.3.refs_2_ = bf16[144,256]{1,0:T(8,128)(2,1)S(1)} collective-permute-done((bf16[144,256]{1,0:T(8,128)(2,1)S(1)}, bf16[144,256]{1,0:T(8,128)(2,1)S(1)}, u32[]{:S(2)}, u32[]{:S(2)}) %collective-permute-start.3) | collective-permute-done | bytes 73760 | tf_op jit(solution)/shard_map/ppermute | solution.py:28
  13.0 1.5 %collective-permute-start.4 = (bf16[144,256]{1,0:T(8,128)(2,1)S(1)}, bf16[144,256]{1,0:T(8,128)(2,1)S(1)}, u32[]{:S(2)}, u32[]{:S(2)}) collective-permute-start(bf16[144,256]{1,0:T(8,128)(2,1)S(1)} %collective-permute-done.3.refs_2_), channel_id=1, source_target_pairs={{0,4},{4,0},{8,12},{12,8},{16,20},{20,16},{24,28},{28,24},{1,5},{5... | collective-permute-start | bytes 221192 | tf_op jit(solution)/shard_map/ppermute | solution.py:28
  14.6 0.5 collective-permute-start.2
  15.1 2.0 %turn.1 = (bf16[2048,256]{1,0:T(8,128)(2,1)S(1)}, bf16[128,2048]{1,0:T(8,128)(2,1)S(1)}, f32[8,128]{1,0:T(8,128)S(1)}) custom-call(s32[2]{0:T(128)S(1)} %pad_add_fusion.ids, bf16[4096,128]{1,0:T(8,128)(2,1)} %protos.1, f32[1,4096]{1,0:T(1,128)} %bitcast.18), custom_call_target="tpu_custom_call" | custom-call | tf_op jit(solution)/shard_map/turn/pallas_call | solution.py:319
  17.1 0.1 collective-permute-start.8
  17.1 0.0 collective-permute-done.refs_0_
  17.2 0.0 collective-permute-done.6.refs_3_
  17.2 0.9 %collective-permute-done.4.refs_2_ = bf16[144,256]{1,0:T(8,128)(2,1)S(1)} collective-permute-done((bf16[144,256]{1,0:T(8,128)(2,1)S(1)}, bf16[144,256]{1,0:T(8,128)(2,1)S(1)}, u32[]{:S(2)}, u32[]{:S(2)}) %collective-permute-start.4) | collective-permute-done | bytes 73760 | tf_op jit(solution)/shard_map/ppermute | solution.py:28
  18.1 0.8 %collective-permute-done.2.refs_1_ = bf16[144,256]{1,0:T(8,128)(2,1)S(1)} collective-permute-done((bf16[144,256]{1,0:T(8,128)(2,1)S(1)}, bf16[144,256]{1,0:T(8,128)(2,1)S(1)}, u32[]{:S(2)}, u32[]{:S(2)}) %collective-permute-start.2) | collective-permute-done | bytes 73760 | tf_op jit(solution)/shard_map/ppermute | solution.py:28
  18.9 0.1 collective-permute-start.7
  19.0 3.0 %plan_ours.1 = (f32[2048,2048]{1,0:T(8,128)S(1)}, f32[2,2048,128]{2,1,0:T(8,128)S(1)}, f32[2,1024]{1,0:T(2,128)S(1)}, bf16[256,1024]{1,0:T(8,128)(2,1)S(1)}, bf16[128,1024]{1,0:T(8,128)(2,1)S(1)}) custom-call(s32[2]{0:T(128)S(1)} %pad_add_fusion.ids, bf16[2048,256]{1,0:T(8,128)(2,1)S(1)} %get-tuple-element.37.protos, bf16[4,144,256]{2,1,0:T(8,128)(2,1)S(1)} %stack.15.mine, ...), custom_call_target="tpu_custom_call" | custom-call | tf_op jit(solution)/shard_map/plan_ours/pallas_call | solution.py:319
  22.1 3.5 %plan_theirs.1 = (f32[2048,2048]{1,0:T(8,128)S(1)}, f32[2,2048,128]{2,1,0:T(8,128)S(1)}, f32[2,2048]{1,0:T(2,128)S(1)}, bf16[256,1024]{1,0:T(8,128)(2,1)S(1)}, bf16[128,1024]{1,0:T(8,128)(2,1)S(1)}) custom-call(s32[2]{0:T(128)S(1)} %pad_add_fusion.ids, bf16[2048,256]{1,0:T(8,128)(2,1)S(1)} %get-tuple-element.37.protos, ...), custom_call_target="tpu_custom_call", output_to_operand_aliasing={{0}: (4, {})} | custom-call | tf_op jit(solution)/shard_map/plan_theirs/pallas_call | solution.py:319
  25.6 0.6 collective-permute-start.9
  26.2 0.8 %collective-permute-done.9.right = f32[2,2048]{1,0:T(2,128)S(1)} collective-permute-done((f32[2,2048]{1,0:T(2,128)S(1)}, f32[2,2048]{1,0:T(2,128)S(1)}, u32[]{:S(2)}, u32[]{:S(2)}) %collective-permute-start.9) | collective-permute-done | bytes 16416 | tf_op jit(solution)/shard_map/ppermute | solution.py:28
  27.0 1.5 %collective-permute-start.12 = (f32[2,2048]{1,0:T(2,128)S(1)}, f32[2,2048]{1,0:T(2,128)S(1)}, u32[]{:S(2)}, u32[]{:S(2)}) collective-permute-start(f32[2,2048]{1,0:T(2,128)S(1)} %add.28.after.refs_3_), channel_id=1, source_target_pairs={{0,2},{1,3},{2,0},{3,1},{4,6},{5,7},{6,4},{7,5},{8,10},{9,11},{10,... | collective-permute-start | bytes 49160 | tf_op jit(solution)/shard_map/ppermute | solution.py:340
  28.5 1.1 %collective-permute-start.11 = (f32[2,2048]{1,0:T(2,128)S(1)}, f32[2,2048]{1,0:T(2,128)S(1)}, u32[]{:S(2)}, u32[]{:S(2)}) collective-permute-start(f32[2,2048]{1,0:T(2,128)S(1)} %add.28.after.refs_3_), channel_id=1, source_target_pairs={{0,4},{1,5},{2,6},{3,7},{4,0},{5,1},{6,2},{7,3},{8,12},{9,13},{10,... | collective-permute-start | bytes 49160 | tf_op jit(solution)/shard_map/ppermute | solution.py:340
  29.5 0.9 %collective-permute-start.10 = (f32[2,2048]{1,0:T(2,128)S(1)}, f32[2,2048]{1,0:T(2,128)S(1)}, u32[]{:S(2)}, u32[]{:S(2)}) collective-permute-start(f32[2,2048]{1,0:T(2,128)S(1)} %add.28.after.refs_3_), channel_id=1, source_target_pairs={{0,6},{1,7},{2,4},{3,5},{4,2},{5,3},{6,0},{7,1},{8,14},{9,15},{10,... | collective-permute-start | bytes 49160 | tf_op jit(solution)/shard_map/ppermute | solution.py:340
  30.5 2.0 %embed_before.1 = (f32[2048,512]{1,0:T(8,128)S(1)}, f32[8,128]{1,0:T(8,128)S(1)}) custom-call(bf16[2048,256]{1,0:T(8,128)(2,1)S(1)} %get-tuple-element.37.protos, bf16[256,1024]{1,0:T(8,128)(2,1)S(1)} %get-tuple-element.45.emb_a.emb_ext, bf16[256,1024]{1,0:T(8,128)(2,1)S(1)} %get-tuple-element.46.emb_b.emb_ext, f32[2,2048]{1,0:T(2,128)S(1)} %add.28.after.refs_3_), custom_call_target="tpu_custom_call" | custom-call | tf_op jit(solution)/shard_map/embed_before/pallas_call | solution.py:319
  32.5 0.0 collective-permute-done.12.refs_2_
  32.5 0.0 collective-permute-done.11.refs_1_
  32.5 1.7 %collective-permute-done.10.refs_0_ = f32[2,2048]{1,0:T(2,128)S(1)} collective-permute-done((f32[2,2048]{1,0:T(2,128)S(1)}, f32[2,2048]{1,0:T(2,128)S(1)}, u32[]{:S(2)}, u32[]{:S(2)}) %collective-permute-start.10) | collective-permute-done | bytes 16416 | tf_op jit(solution)/shard_map/ppermute | solution.py:340
  34.2 2.5 %sweep.3 = (f32[2048,2048]{1,0:T(8,128)S(1)}, f32[2,2048]{1,0:T(2,128)S(1)}, f32[1,2048]{1,0:T(1,128)S(1)}) custom-call(f32[2048,2048]{1,0:T(8,128)S(1)} %get-tuple-element.42.plan, f32[2,2048,128]{2,1,0:T(8,128)S(1)} %get-tuple-element.43.cols, f32[2,2048]{1,0:T(2,128)S(1)} %collective-permute-done.10.refs_0_, ...), custom_call_target="tpu_custom_call", output_to_operand_aliasing={{0}: (0, {})} | custom-call | tf_op jit(solution)/shard_map/sweep/pallas_call | solution.py:319
  36.7 0.1 collective-permute-start.13
  36.8 1.2 %collective-permute-done.13.right = f32[1,2048]{1,0:T(1,128)S(1)} collective-permute-done((f32[1,2048]{1,0:T(1,128)S(1)}, f32[1,2048]{1,0:T(1,128)S(1)}, u32[]{:S(2)}, u32[]{:S(2)}) %collective-permute-start.13) | collective-permute-done | bytes 8224 | tf_op jit(solution)/shard_map/ppermute | solution.py:28
  38.0 0.5 collective-permute-start.16
  38.5 1.0 %collective-permute-start.15 = (f32[1,2048]{1,0:T(1,128)S(1)}, f32[1,2048]{1,0:T(1,128)S(1)}, u32[]{:S(2)}, u32[]{:S(2)}) collective-permute-start(f32[1,2048]{1,0:T(1,128)S(1)} %add.29.after.refs_4_), channel_id=1, source_target_pairs={{0,4},{1,5},{2,6},{3,7},{4,0},{5,1},{6,2},{7,3},{8,12},{9,13},{10,... | collective-permute-start | bytes 24584 | tf_op jit(solution)/shard_map/ppermute | solution.py:340
  39.5 2.0 %collective-permute-start.14 = (f32[1,2048]{1,0:T(1,128)S(1)}, f32[1,2048]{1,0:T(1,128)S(1)}, u32[]{:S(2)}, u32[]{:S(2)}) collective-permute-start(f32[1,2048]{1,0:T(1,128)S(1)} %add.29.after.refs_4_), channel_id=1, source_target_pairs={{0,6},{1,7},{2,4},{3,5},{4,2},{5,3},{6,0},{7,1},{8,14},{9,15},{10,... | collective-permute-start | bytes 24584 | tf_op jit(solution)/shard_map/ppermute | solution.py:340
  41.4 2.0 %proto_before.1 = (f32[512,2048]{1,0:T(8,128)S(1)}, f32[512,128]{1,0:T(8,128)S(1)}, f32[8,128]{1,0:T(8,128)S(1)}) custom-call(s32[2]{0:T(128)S(1)} %pad_add_fusion.ids, bf16[2048,256]{1,0:T(8,128)(2,1)S(1)} %get-tuple-element.37.protos, bf16[256,1024]{1,0:T(8,128)(2,1)S(1)} %get-tuple-element.45.emb_a.emb_ext, ...), custom_call_target="tpu_custom_call" | custom-call | tf_op jit(solution)/shard_map/proto_before/pallas_call | solution.py:319
  43.5 0.0 collective-permute-done.15.refs_2_
  43.5 0.5 collective-permute-done.14.refs_1_
  44.0 2.5 %sweep.4 = (f32[2048,2048]{1,0:T(8,128)S(1)}, f32[1,2048]{1,0:T(1,128)S(1)}) custom-call(f32[2048,2048]{1,0:T(8,128)S(1)} %get-tuple-element.48.plan, f32[2,2048,128]{2,1,0:T(8,128)S(1)} %get-tuple-element.43.cols, f32[2,2048]{1,0:T(2,128)S(1)} %get-tuple-element.49.refs_0_.sums, ...), custom_call_target="tpu_custom_call", output_to_operand_aliasing={{0}: (0, {})} | custom-call | tf_op jit(solution)/shard_map/sweep/pallas_call | solution.py:319
  46.6 0.1 collective-permute-start.17
  46.6 1.2 %collective-permute-done.17.right = f32[1,2048]{1,0:T(1,128)S(1)} collective-permute-done((f32[1,2048]{1,0:T(1,128)S(1)}, f32[1,2048]{1,0:T(1,128)S(1)}, u32[]{:S(2)}, u32[]{:S(2)}) %collective-permute-start.17) | collective-permute-done | bytes 8224 | tf_op jit(solution)/shard_map/ppermute | solution.py:28
  47.8 1.5 %collective-permute-start.20 = (f32[1,2048]{1,0:T(1,128)S(1)}, f32[1,2048]{1,0:T(1,128)S(1)}, u32[]{:S(2)}, u32[]{:S(2)}) collective-permute-start(f32[1,2048]{1,0:T(1,128)S(1)} %add.30.after.refs_4_), channel_id=1, source_target_pairs={{0,2},{1,3},{2,0},{3,1},{4,6},{5,7},{6,4},{7,5},{8,10},{9,11},{10,... | collective-permute-start | bytes 24584 | tf_op jit(solution)/shard_map/ppermute | solution.py:340
  49.3 1.1 %collective-permute-start.19 = (f32[1,2048]{1,0:T(1,128)S(1)}, f32[1,2048]{1,0:T(1,128)S(1)}, u32[]{:S(2)}, u32[]{:S(2)}) collective-permute-start(f32[1,2048]{1,0:T(1,128)S(1)} %add.30.after.refs_4_), channel_id=1, source_target_pairs={{0,4},{1,5},{2,6},{3,7},{4,0},{5,1},{6,2},{7,3},{8,12},{9,13},{10,... | collective-permute-start | bytes 24584 | tf_op jit(solution)/shard_map/ppermute | solution.py:340
  50.3 0.9 %collective-permute-start.18 = (f32[1,2048]{1,0:T(1,128)S(1)}, f32[1,2048]{1,0:T(1,128)S(1)}, u32[]{:S(2)}, u32[]{:S(2)}) collective-permute-start(f32[1,2048]{1,0:T(1,128)S(1)} %add.30.after.refs_4_), channel_id=1, source_target_pairs={{0,6},{1,7},{2,4},{3,5},{4,2},{5,3},{6,0},{7,1},{8,14},{9,15},{10,... | collective-permute-start | bytes 24584 | tf_op jit(solution)/shard_map/ppermute | solution.py:340
  51.3 2.3 %cotangent.2 = (f32[2048,512]{1,0:T(8,128)S(1)}, f32[8,128]{1,0:T(8,128)S(1)}) custom-call(s32[2]{0:T(128)S(1)} %pad_add_fusion.ids, bf16[2048,256]{1,0:T(8,128)(2,1)S(1)} %get-tuple-element.37.protos, bf16[128,1024]{1,0:T(8,128)(2,1)S(1)} %get-tuple-element.51.view_a, bf16[128,1024]{1,0:T(8,128)(2,1)S(1)} %get-tuple-element.52.view_b, ...), custom_call_target="tpu_custom_call" | custom-call | tf_op jit(solution)/shard_map/cotangent/pallas_call | solution.py:319
  53.6 1.3 %collective-permute-done.18.refs_1_ = f32[1,2048]{1,0:T(1,128)S(1)} collective-permute-done((f32[1,2048]{1,0:T(1,128)S(1)}, f32[1,2048]{1,0:T(1,128)S(1)}, u32[]{:S(2)}, u32[]{:S(2)}) %collective-permute-start.18) | collective-permute-done | bytes 8224 | tf_op jit(solution)/shard_map/ppermute | solution.py:340
  54.9 2.5 %sweep.5 = (f32[2048,2048]{1,0:T(8,128)S(1)}, f32[1,2048]{1,0:T(1,128)S(1)}) custom-call(f32[2048,2048]{1,0:T(8,128)S(1)} %get-tuple-element.54.plan, f32[2,2048,128]{2,1,0:T(8,128)S(1)} %get-tuple-element.43.cols, f32[2,2048]{1,0:T(2,128)S(1)} %get-tuple-element.49.refs_0_.sums, ...), custom_call_target="tpu_custom_call", output_to_operand_aliasing={{0}: (0, {})} | custom-call | tf_op jit(solution)/shard_map/sweep/pallas_call | solution.py:319
  57.4 0.1 collective-permute-start.21
  57.5 1.2 %collective-permute-done.21.right = f32[1,2048]{1,0:T(1,128)S(1)} collective-permute-done((f32[1,2048]{1,0:T(1,128)S(1)}, f32[1,2048]{1,0:T(1,128)S(1)}, u32[]{:S(2)}, u32[]{:S(2)}) %collective-permute-start.21) | collective-permute-done | bytes 8224 | tf_op jit(solution)/shard_map/ppermute | solution.py:28
  58.7 0.5 collective-permute-start.24
  59.2 1.0 %collective-permute-start.23 = (f32[1,2048]{1,0:T(1,128)S(1)}, f32[1,2048]{1,0:T(1,128)S(1)}, u32[]{:S(2)}, u32[]{:S(2)}) collective-permute-start(f32[1,2048]{1,0:T(1,128)S(1)} %add.31.after.refs_3_), channel_id=1, source_target_pairs={{0,4},{1,5},{2,6},{3,7},{4,0},{5,1},{6,2},{7,3},{8,12},{9,13},{10,... | collective-permute-start | bytes 24584 | tf_op jit(solution)/shard_map/ppermute | solution.py:340
  60.2 2.0 %collective-permute-start.22 = (f32[1,2048]{1,0:T(1,128)S(1)}, f32[1,2048]{1,0:T(1,128)S(1)}, u32[]{:S(2)}, u32[]{:S(2)}) collective-permute-start(f32[1,2048]{1,0:T(1,128)S(1)} %add.31.after.refs_3_), channel_id=1, source_target_pairs={{0,6},{1,7},{2,4},{3,5},{4,2},{5,3},{6,0},{7,1},{8,14},{9,15},{10,... | collective-permute-start | bytes 24584 | tf_op jit(solution)/shard_map/ppermute | solution.py:340
  62.2 1.4 %cotangent.3 = (f32[512,2048]{1,0:T(8,128)S(1)}, f32[8,128]{1,0:T(8,128)S(1)}) custom-call(s32[2]{0:T(128)S(1)} %pad_add_fusion.ids, bf16[2048,256]{1,0:T(8,128)(2,1)S(1)} %get-tuple-element.37.protos, bf16[128,1024]{1,0:T(8,128)(2,1)S(1)} %get-tuple-element.51.view_a, bf16[128,1024]{1,0:T(8,128)(2,1)S(1)} %get-tuple-element.52.view_b, ...), custom_call_target="tpu_custom_call" | custom-call | tf_op jit(solution)/shard_map/cotangent/pallas_call | solution.py:319
  63.6 1.2 %collective-permute-done.22.refs_0_ = f32[1,2048]{1,0:T(1,128)S(1)} collective-permute-done((f32[1,2048]{1,0:T(1,128)S(1)}, f32[1,2048]{1,0:T(1,128)S(1)}, u32[]{:S(2)}, u32[]{:S(2)}) %collective-permute-start.22) | collective-permute-done | bytes 8224 | tf_op jit(solution)/shard_map/ppermute | solution.py:340
  64.7 3.0 %embed_grad.1 = (f32[2048,128]{1,0:T(8,128)S(1)}, f32[1,2048]{1,0:T(1,128)S(1)}, f32[4,64,128]{2,1,0:T(8,128)S(1)}, f32[4,64,128]{2,1,0:T(8,128)S(1)}) custom-call(s32[2]{0:T(128)S(1)} %pad_add_fusion.ids, f32[2048,2048]{1,0:T(8,128)S(1)} %get-tuple-element.57.plan, f32[2,2048,128]{2,1,0:T(8,128)S(1)} %get-tuple-element.43.cols, ...), custom_call_target="tpu_custom_call" | custom-call | tf_op jit(solution)/shard_map/embed_grad/pallas_call | solution.py:319
  67.7 0.1 collective-permute-start.25
  67.8 1.0 %proto_grad.2 = (f32[512,128]{1,0:T(8,128)S(1)}, f32[8,128]{1,0:T(8,128)S(1)}) custom-call(s32[2]{0:T(128)S(1)} %pad_add_fusion.ids, bf16[256,1024]{1,0:T(8,128)(2,1)S(1)} %get-tuple-element.45.emb_a.emb_ext, f32[512,2048]{1,0:T(8,128)S(1)} %get-tuple-element.65.entries, f32[512,2048]{1,0:T(8,128)S(1)} %get-tuple-element.66.cots, ...), custom_call_target="tpu_custom_call" | custom-call | tf_op jit(solution)/shard_map/proto_grad/pallas_call | solution.py:319
  68.8 0.3 collective-permute-done.25.right
  69.1 2.0 %collective-permute-start.26 = (f32[64,128]{1,0:T(8,128)S(1)}, f32[64,128]{1,0:T(8,128)S(1)}, u32[]{:S(2)}, u32[]{:S(2)}) collective-permute-start(f32[64,128]{1,0:T(8,128)S(1)} %get-tuple-element.72), channel_id=1, source_target_pairs={{0,6},{1,7},{2,4},{3,5},{4,2},{5,3},{6,0},{7,1},{8,14},{9,15},{10,... | collective-permute-start | bytes 98312 | tf_op jit(solution)/shard_map/ppermute | solution.py:340
  71.2 0.5 collective-permute-start.28
  71.7 1.0 %collective-permute-start.27 = (f32[64,128]{1,0:T(8,128)S(1)}, f32[64,128]{1,0:T(8,128)S(1)}, u32[]{:S(2)}, u32[]{:S(2)}) collective-permute-start(f32[64,128]{1,0:T(8,128)S(1)} %get-tuple-element.74), channel_id=1, source_target_pairs={{0,4},{1,5},{2,6},{3,7},{4,0},{5,1},{6,2},{7,3},{8,12},{9,13},{10,... | collective-permute-start | bytes 98312 | tf_op jit(solution)/shard_map/ppermute | solution.py:340
  72.7 1.7 %proto_grad.3 = f32[512,128]{1,0:T(8,128)} custom-call(s32[2]{0:T(128)S(1)} %pad_add_fusion.ids, bf16[256,1024]{1,0:T(8,128)(2,1)S(1)} %get-tuple-element.46.emb_b.emb_ext, f32[512,2048]{1,0:T(8,128)S(1)} %get-tuple-element.65.entries, f32[512,2048]{1,0:T(8,128)S(1)} %get-tuple-element.66.cots, f32[512,128]{1,0:T(8,128)S(1)} %get-tuple-element.71.so_far, ...), custom_call_target="tpu_custom_call" | custom-call | tf_op jit(solution)/shard_map/proto_grad/pallas_call | solution.py:319
  74.4 0.6 collective-permute-done.28
  75.1 0.5 collective-permute-done.27
  75.6 0.6 fusion.2
  (18 shorter events, 0.1 us)
Async XLA Ops:
  1.7 7.9 %collective-permute-start.5 = (bf16[144,256]{1,0:T(8,128)(2,1)S(1)}, bf16[144,256]{1,0:T(8,128)(2,1)S(1)}, u32[]{:S(2)}, u32[]{:S(2)}) collective-permute-start(bf16[144,256]{1,0:T(8,128)(2,1)S(1)} %prepare.1.refs_0_), channel_id=1, source_target_pairs={{0,24},{4,28},{8,16},{12,20},{16,8},{20,12},{24,0},{28,4},{1,25},{... | collective-permute-start | bytes 221192 | tf_op jit(solution)/shard_map/ppermute | solution.py:28
  6.8 6.2 %collective-permute-start.3 = (bf16[144,256]{1,0:T(8,128)(2,1)S(1)}, bf16[144,256]{1,0:T(8,128)(2,1)S(1)}, u32[]{:S(2)}, u32[]{:S(2)}) collective-permute-start(bf16[144,256]{1,0:T(8,128)(2,1)S(1)} %prepare.1.refs_0_), channel_id=1, source_target_pairs={{0,16},{4,20},{8,24},{12,28},{16,0},{20,4},{24,8},{28,12},{1,17},{... | collective-permute-start | bytes 221192 | tf_op jit(solution)/shard_map/ppermute | solution.py:28
  6.8 7.7 %collective-permute-start.1 = (bf16[144,256]{1,0:T(8,128)(2,1)S(1)}, bf16[144,256]{1,0:T(8,128)(2,1)S(1)}, u32[]{:S(2)}, u32[]{:S(2)}) collective-permute-start(bf16[144,256]{1,0:T(8,128)(2,1)S(1)} %prepare.1.refs_0_), channel_id=1, source_target_pairs={{0,8},{4,12},{8,0},{12,4},{16,24},{20,28},{24,16},{28,20},{1,9},{5... | collective-permute-start | bytes 221192 | tf_op jit(solution)/shard_map/ppermute | solution.py:28
  7.5 9.7 %collective-permute-start = (bf16[144,256]{1,0:T(8,128)(2,1)S(1)}, bf16[144,256]{1,0:T(8,128)(2,1)S(1)}, u32[]{:S(2)}, u32[]{:S(2)}) collective-permute-start(bf16[144,256]{1,0:T(8,128)(2,1)S(1)} %prepare.1.refs_0_), channel_id=1, source_target_pairs={{0,4},{4,0},{8,12},{12,8},{16,20},{20,16},{24,28},{28,24},{1,5},{5... | collective-permute-start | bytes 221192 | tf_op jit(solution)/shard_map/ppermute | solution.py:28
  9.6 7.6 %collective-permute-start.6 = (bf16[144,256]{1,0:T(8,128)(2,1)S(1)}, bf16[144,256]{1,0:T(8,128)(2,1)S(1)}, u32[]{:S(2)}, u32[]{:S(2)}) collective-permute-start(bf16[144,256]{1,0:T(8,128)(2,1)S(1)} %collective-permute-done.5.refs_3_), channel_id=1, source_target_pairs={{0,4},{4,0},{8,12},{12,8},{16,20},{20,16},{24,28},{28,24},{1,5},{5... | collective-permute-start | bytes 221192 | tf_op jit(solution)/shard_map/ppermute | solution.py:28
  13.0 5.1 %collective-permute-start.4 = (bf16[144,256]{1,0:T(8,128)(2,1)S(1)}, bf16[144,256]{1,0:T(8,128)(2,1)S(1)}, u32[]{:S(2)}, u32[]{:S(2)}) collective-permute-start(bf16[144,256]{1,0:T(8,128)(2,1)S(1)} %collective-permute-done.3.refs_2_), channel_id=1, source_target_pairs={{0,4},{4,0},{8,12},{12,8},{16,20},{20,16},{24,28},{28,24},{1,5},{5... | collective-permute-start | bytes 221192 | tf_op jit(solution)/shard_map/ppermute | solution.py:28
  14.6 4.4 %collective-permute-start.2 = (bf16[144,256]{1,0:T(8,128)(2,1)S(1)}, bf16[144,256]{1,0:T(8,128)(2,1)S(1)}, u32[]{:S(2)}, u32[]{:S(2)}) collective-permute-start(bf16[144,256]{1,0:T(8,128)(2,1)S(1)} %collective-permute-done.1.refs_1_), channel_id=1, source_target_pairs={{0,4},{4,0},{8,12},{12,8},{16,20},{20,16},{24,28},{28,24},{1,5},{5... | collective-permute-start | bytes 221192 | tf_op jit(solution)/shard_map/ppermute | solution.py:28
  17.1 2.0 %collective-permute-start.8 = (bf16[4,144,256]{2,1,0:T(8,128)(2,1)S(1)}, bf16[4,144,256]{2,1,0:T(8,128)(2,1)S(1)}, u32[]{:S(2)}, u32[]{:S(2)}) collective-permute-start(bf16[4,144,256]{2,1,0:T(8,128)(2,1)S(1)} %stack.15.mine), channel_id=1, source_target_pairs={{0,1},{1,0},{2,3},{3,2},{4,5},{5,4},{6,7},{7,6},{8,9},{9,8},{10,11... | collective-permute-start | bytes 884744 | tf_op jit(solution)/shard_map/ppermute | solution.py:28
  18.9 3.1 %collective-permute-start.7 = (bf16[4,144,256]{2,1,0:T(8,128)(2,1)S(1)}, bf16[4,144,256]{2,1,0:T(8,128)(2,1)S(1)}, u32[]{:S(2)}, u32[]{:S(2)}) collective-permute-start(bf16[4,144,256]{2,1,0:T(8,128)(2,1)S(1)} %stack.14.mine), channel_id=1, source_target_pairs={{0,1},{1,0},{2,3},{3,2},{4,5},{5,4},{6,7},{7,6},{8,9},{9,8},{10,11... | collective-permute-start | bytes 884744 | tf_op jit(solution)/shard_map/ppermute | solution.py:28
  25.6 1.4 %collective-permute-start.9 = (f32[2,2048]{1,0:T(2,128)S(1)}, f32[2,2048]{1,0:T(2,128)S(1)}, u32[]{:S(2)}, u32[]{:S(2)}) collective-permute-start(f32[2,2048]{1,0:T(2,128)S(1)} %get-tuple-element.44.left), channel_id=1, source_target_pairs={{0,1},{1,0},{2,3},{3,2},{4,5},{5,4},{6,7},{7,6},{8,9},{9,8},{10,11... | collective-permute-start | bytes 49160 | tf_op jit(solution)/shard_map/ppermute | solution.py:28
  27.0 5.5 %collective-permute-start.12 = (f32[2,2048]{1,0:T(2,128)S(1)}, f32[2,2048]{1,0:T(2,128)S(1)}, u32[]{:S(2)}, u32[]{:S(2)}) collective-permute-start(f32[2,2048]{1,0:T(2,128)S(1)} %add.28.after.refs_3_), channel_id=1, source_target_pairs={{0,2},{1,3},{2,0},{3,1},{4,6},{5,7},{6,4},{7,5},{8,10},{9,11},{10,... | collective-permute-start | bytes 49160 | tf_op jit(solution)/shard_map/ppermute | solution.py:340
  28.5 4.0 %collective-permute-start.11 = (f32[2,2048]{1,0:T(2,128)S(1)}, f32[2,2048]{1,0:T(2,128)S(1)}, u32[]{:S(2)}, u32[]{:S(2)}) collective-permute-start(f32[2,2048]{1,0:T(2,128)S(1)} %add.28.after.refs_3_), channel_id=1, source_target_pairs={{0,4},{1,5},{2,6},{3,7},{4,0},{5,1},{6,2},{7,3},{8,12},{9,13},{10,... | collective-permute-start | bytes 49160 | tf_op jit(solution)/shard_map/ppermute | solution.py:340
  29.5 4.6 %collective-permute-start.10 = (f32[2,2048]{1,0:T(2,128)S(1)}, f32[2,2048]{1,0:T(2,128)S(1)}, u32[]{:S(2)}, u32[]{:S(2)}) collective-permute-start(f32[2,2048]{1,0:T(2,128)S(1)} %add.28.after.refs_3_), channel_id=1, source_target_pairs={{0,6},{1,7},{2,4},{3,5},{4,2},{5,3},{6,0},{7,1},{8,14},{9,15},{10,... | collective-permute-start | bytes 49160 | tf_op jit(solution)/shard_map/ppermute | solution.py:340
  36.7 1.2 %collective-permute-start.13 = (f32[1,2048]{1,0:T(1,128)S(1)}, f32[1,2048]{1,0:T(1,128)S(1)}, u32[]{:S(2)}, u32[]{:S(2)}) collective-permute-start(f32[1,2048]{1,0:T(1,128)S(1)} %get-tuple-element.50.left), channel_id=1, source_target_pairs={{0,1},{1,0},{2,3},{3,2},{4,5},{5,4},{6,7},{7,6},{8,9},{9,8},{10,11... | collective-permute-start | bytes 24584 | tf_op jit(solution)/shard_map/ppermute | solution.py:28
  38.0 5.5 %collective-permute-start.16 = (f32[1,2048]{1,0:T(1,128)S(1)}, f32[1,2048]{1,0:T(1,128)S(1)}, u32[]{:S(2)}, u32[]{:S(2)}) collective-permute-start(f32[1,2048]{1,0:T(1,128)S(1)} %add.29.after.refs_4_), channel_id=1, source_target_pairs={{0,2},{1,3},{2,0},{3,1},{4,6},{5,7},{6,4},{7,5},{8,10},{9,11},{10,... | collective-permute-start | bytes 24584 | tf_op jit(solution)/shard_map/ppermute | solution.py:340
  38.5 5.0 %collective-permute-start.15 = (f32[1,2048]{1,0:T(1,128)S(1)}, f32[1,2048]{1,0:T(1,128)S(1)}, u32[]{:S(2)}, u32[]{:S(2)}) collective-permute-start(f32[1,2048]{1,0:T(1,128)S(1)} %add.29.after.refs_4_), channel_id=1, source_target_pairs={{0,4},{1,5},{2,6},{3,7},{4,0},{5,1},{6,2},{7,3},{8,12},{9,13},{10,... | collective-permute-start | bytes 24584 | tf_op jit(solution)/shard_map/ppermute | solution.py:340
  39.5 4.5 %collective-permute-start.14 = (f32[1,2048]{1,0:T(1,128)S(1)}, f32[1,2048]{1,0:T(1,128)S(1)}, u32[]{:S(2)}, u32[]{:S(2)}) collective-permute-start(f32[1,2048]{1,0:T(1,128)S(1)} %add.29.after.refs_4_), channel_id=1, source_target_pairs={{0,6},{1,7},{2,4},{3,5},{4,2},{5,3},{6,0},{7,1},{8,14},{9,15},{10,... | collective-permute-start | bytes 24584 | tf_op jit(solution)/shard_map/ppermute | solution.py:340
  46.6 1.2 %collective-permute-start.17 = (f32[1,2048]{1,0:T(1,128)S(1)}, f32[1,2048]{1,0:T(1,128)S(1)}, u32[]{:S(2)}, u32[]{:S(2)}) collective-permute-start(f32[1,2048]{1,0:T(1,128)S(1)} %get-tuple-element.55.left), channel_id=1, source_target_pairs={{0,1},{1,0},{2,3},{3,2},{4,5},{5,4},{6,7},{7,6},{8,9},{9,8},{10,11... | collective-permute-start | bytes 24584 | tf_op jit(solution)/shard_map/ppermute | solution.py:28
  47.8 5.8 %collective-permute-start.20 = (f32[1,2048]{1,0:T(1,128)S(1)}, f32[1,2048]{1,0:T(1,128)S(1)}, u32[]{:S(2)}, u32[]{:S(2)}) collective-permute-start(f32[1,2048]{1,0:T(1,128)S(1)} %add.30.after.refs_4_), channel_id=1, source_target_pairs={{0,2},{1,3},{2,0},{3,1},{4,6},{5,7},{6,4},{7,5},{8,10},{9,11},{10,... | collective-permute-start | bytes 24584 | tf_op jit(solution)/shard_map/ppermute | solution.py:340
  49.3 4.3 %collective-permute-start.19 = (f32[1,2048]{1,0:T(1,128)S(1)}, f32[1,2048]{1,0:T(1,128)S(1)}, u32[]{:S(2)}, u32[]{:S(2)}) collective-permute-start(f32[1,2048]{1,0:T(1,128)S(1)} %add.30.after.refs_4_), channel_id=1, source_target_pairs={{0,4},{1,5},{2,6},{3,7},{4,0},{5,1},{6,2},{7,3},{8,12},{9,13},{10,... | collective-permute-start | bytes 24584 | tf_op jit(solution)/shard_map/ppermute | solution.py:340
  50.3 4.5 %collective-permute-start.18 = (f32[1,2048]{1,0:T(1,128)S(1)}, f32[1,2048]{1,0:T(1,128)S(1)}, u32[]{:S(2)}, u32[]{:S(2)}) collective-permute-start(f32[1,2048]{1,0:T(1,128)S(1)} %add.30.after.refs_4_), channel_id=1, source_target_pairs={{0,6},{1,7},{2,4},{3,5},{4,2},{5,3},{6,0},{7,1},{8,14},{9,15},{10,... | collective-permute-start | bytes 24584 | tf_op jit(solution)/shard_map/ppermute | solution.py:340
  57.4 1.2 %collective-permute-start.21 = (f32[1,2048]{1,0:T(1,128)S(1)}, f32[1,2048]{1,0:T(1,128)S(1)}, u32[]{:S(2)}, u32[]{:S(2)}) collective-permute-start(f32[1,2048]{1,0:T(1,128)S(1)} %get-tuple-element.61.left), channel_id=1, source_target_pairs={{0,1},{1,0},{2,3},{3,2},{4,5},{5,4},{6,7},{7,6},{8,9},{9,8},{10,11... | collective-permute-start | bytes 24584 | tf_op jit(solution)/shard_map/ppermute | solution.py:28
  58.7 4.9 %collective-permute-start.24 = (f32[1,2048]{1,0:T(1,128)S(1)}, f32[1,2048]{1,0:T(1,128)S(1)}, u32[]{:S(2)}, u32[]{:S(2)}) collective-permute-start(f32[1,2048]{1,0:T(1,128)S(1)} %add.31.after.refs_3_), channel_id=1, source_target_pairs={{0,2},{1,3},{2,0},{3,1},{4,6},{5,7},{6,4},{7,5},{8,10},{9,11},{10,... | collective-permute-start | bytes 24584 | tf_op jit(solution)/shard_map/ppermute | solution.py:340
  59.2 4.4 %collective-permute-start.23 = (f32[1,2048]{1,0:T(1,128)S(1)}, f32[1,2048]{1,0:T(1,128)S(1)}, u32[]{:S(2)}, u32[]{:S(2)}) collective-permute-start(f32[1,2048]{1,0:T(1,128)S(1)} %add.31.after.refs_3_), channel_id=1, source_target_pairs={{0,4},{1,5},{2,6},{3,7},{4,0},{5,1},{6,2},{7,3},{8,12},{9,13},{10,... | collective-permute-start | bytes 24584 | tf_op jit(solution)/shard_map/ppermute | solution.py:340
  60.2 4.5 %collective-permute-start.22 = (f32[1,2048]{1,0:T(1,128)S(1)}, f32[1,2048]{1,0:T(1,128)S(1)}, u32[]{:S(2)}, u32[]{:S(2)}) collective-permute-start(f32[1,2048]{1,0:T(1,128)S(1)} %add.31.after.refs_3_), channel_id=1, source_target_pairs={{0,6},{1,7},{2,4},{3,5},{4,2},{5,3},{6,0},{7,1},{8,14},{9,15},{10,... | collective-permute-start | bytes 24584 | tf_op jit(solution)/shard_map/ppermute | solution.py:340
  67.7 1.4 %collective-permute-start.25 = (f32[4,64,128]{2,1,0:T(8,128)S(1)}, f32[4,64,128]{2,1,0:T(8,128)S(1)}, u32[]{:S(2)}, u32[]{:S(2)}) collective-permute-start(f32[4,64,128]{2,1,0:T(8,128)S(1)} %get-tuple-element.64), channel_id=1, source_target_pairs={{0,1},{1,0},{2,3},{3,2},{4,5},{5,4},{6,7},{7,6},{8,9},{9,8},{10,11... | collective-permute-start | bytes 393224 | tf_op jit(solution)/shard_map/ppermute | solution.py:28
  69.1 5.3 %collective-permute-start.26 = (f32[64,128]{1,0:T(8,128)S(1)}, f32[64,128]{1,0:T(8,128)S(1)}, u32[]{:S(2)}, u32[]{:S(2)}) collective-permute-start(f32[64,128]{1,0:T(8,128)S(1)} %get-tuple-element.72), channel_id=1, source_target_pairs={{0,6},{1,7},{2,4},{3,5},{4,2},{5,3},{6,0},{7,1},{8,14},{9,15},{10,... | collective-permute-start | bytes 98312 | tf_op jit(solution)/shard_map/ppermute | solution.py:340
  71.2 3.9 %collective-permute-start.28 = (f32[64,128]{1,0:T(8,128)S(1)}, f32[64,128]{1,0:T(8,128)S(1)}, u32[]{:S(2)}, u32[]{:S(2)}) collective-permute-start(f32[64,128]{1,0:T(8,128)S(1)} %get-tuple-element.73), channel_id=1, source_target_pairs={{0,2},{1,3},{2,0},{3,1},{4,6},{5,7},{6,4},{7,5},{8,10},{9,11},{10,... | collective-permute-start | bytes 98312 | tf_op jit(solution)/shard_map/ppermute | solution.py:340
  71.7 3.9 %collective-permute-start.27 = (f32[64,128]{1,0:T(8,128)S(1)}, f32[64,128]{1,0:T(8,128)S(1)}, u32[]{:S(2)}, u32[]{:S(2)}) collective-permute-start(f32[64,128]{1,0:T(8,128)S(1)} %get-tuple-element.74), channel_id=1, source_target_pairs={{0,4},{1,5},{2,6},{3,7},{4,0},{5,1},{6,2},{7,3},{8,12},{9,13},{10,... | collective-permute-start | bytes 98312 | tf_op jit(solution)/shard_map/ppermute | solution.py:340

commit v10 on v8

--- a/solution.py
+++ b/solution.py
@@ -127,10 +127,10 @@
         here = pl.ds(pl.multiple_of(index * CHUNK, CHUNK), CHUNK)
         mass = cols_in[0, here, :] if second else jnp.zeros((CHUNK, 128), F32)
         weight = cols_in[1, here, :] if second else mass
-        for block in range(blocks):
-            cols = slice(block * rows, (block + 1) * rows)
+        for start in range(0, blocks * rows, 2 * rows):
+            cols = slice(start, start + 2 * rows)
             plan = jnp.exp2(scale * mm(protos[here, :], emb_ext[:, cols]))
-            plan_out[here, left + block * rows:left + (block + 1) * rows] = plan
+            plan_out[here, left + start:left + start + 2 * rows] = plan
             across, down = folded(plan)
             mass = mass + across
             row_mass[:, cols] += down
@@ -265,7 +265,7 @@
         duals_out[here, :] = by_rows(plan.at[here, :], cols, here, spread)
         return carry
 
-    lax.fori_loop(0, plan.shape[0] // STEP, duals, 0, unroll=2)
+    lax.fori_loop(0, plan.shape[0] // STEP, duals, 0, unroll=4)
     total = jnp.zeros((width, rows), F32)
     for start in range(0, plan.shape[0], CHUNK):
         here = slice(start, start + CHUNK)

time: 75 us -> 75 us (level)
  no operation moved by 1% of the time
where the time goes in v10:
time: 75 us; the launch traced here: 74.8 us
  Pallas kernels  30.7 us (41%)
  starting transfers between devices  29.8 us (40%)
  waiting for transfers between devices  12.7 us (17%)
  between operations  0.9 us (1%)
    pallas_call x21, Pallas kernels, run(): pl.pallas_call(kernel, out_shape=out_shape, in_specs=[small] * scalars +...  30.7 us
    ppermute x15, starting transfers between devices, swap_both(): return lax.ppermute(value, ('row', 'proto'), pairs)  17.5 us
    ppermute x14, starting transfers between devices, swap(): return lax.ppermute(value, axis, [(i, i ^ step) for i in range(size)])  12.3 us
    ppermute x14, waiting for transfers between devices, swap(): return lax.ppermute(value, axis, [(i, i ^ step) for i in range(size)])  8.39 us
    ppermute x15, waiting for transfers between devices, swap_both(): return lax.ppermute(value, ('row', 'proto'), pairs)  4.28 us
  transfers between devices with their start and end apart: 29, of which 16 were waited for; matrix products, arithmetic and copies ran while one was open for 0% of the time, Pallas kernels for 21%

profile of v10, /device:TPU:0, one launch (start us, length us, event | category | flops | bytes accessed | tf_op | source)
XLA Modules:
  0.0 74.8 jit_solution(13223962605656107480)
XLA Ops:
  0.6 0.1 pad_add_fusion.ids
  0.7 1.0 %prepare.1.refs_0_ = bf16[144,256]{1,0:T(8,128)(2,1)S(1)} custom-call(s32[2]{0:T(128)S(1)} %pad_add_fusion.ids, bf16[256,128]{1,0:T(8,128)(2,1)} %embeddings.1, bf16[256,128]{1,0:T(8,128)(2,1)} %second_view.1, f32[1,256]{1,0:T(1,128)} %bitcast.19), custom_call_target="tpu_custom_call" | custom-call | tf_op jit(solution)/shard_map/prepare/pallas_call | solution.py:319
  1.7 5.1 %collective-permute-start.5 = (bf16[144,256]{1,0:T(8,128)(2,1)S(1)}, bf16[144,256]{1,0:T(8,128)(2,1)S(1)}, u32[]{:S(2)}, u32[]{:S(2)}) collective-permute-start(bf16[144,256]{1,0:T(8,128)(2,1)S(1)} %prepare.1.refs_0_), channel_id=1, source_target_pairs={{0,24},{4,28},{8,16},{12,20},{16,8},{20,12},{24,0},{28,4},{1,25},{... | collective-permute-start | bytes 221192 | tf_op jit(solution)/shard_map/ppermute | solution.py:28
  6.8 0.0 collective-permute-start.3
  6.8 0.6 collective-permute-start.1
  7.5 1.7 %collective-permute-start = (bf16[144,256]{1,0:T(8,128)(2,1)S(1)}, bf16[144,256]{1,0:T(8,128)(2,1)S(1)}, u32[]{:S(2)}, u32[]{:S(2)}) collective-permute-start(bf16[144,256]{1,0:T(8,128)(2,1)S(1)} %prepare.1.refs_0_), channel_id=1, source_target_pairs={{0,4},{4,0},{8,12},{12,8},{16,20},{20,16},{24,28},{28,24},{1,5},{5... | collective-permute-start | bytes 221192 | tf_op jit(solution)/shard_map/ppermute | solution.py:28
  9.1 0.4 collective-permute-done.5.refs_3_
  9.6 1.9 %collective-permute-start.6 = (bf16[144,256]{1,0:T(8,128)(2,1)S(1)}, bf16[144,256]{1,0:T(8,128)(2,1)S(1)}, u32[]{:S(2)}, u32[]{:S(2)}) collective-permute-start(bf16[144,256]{1,0:T(8,128)(2,1)S(1)} %collective-permute-done.5.refs_3_), channel_id=1, source_target_pairs={{0,4},{4,0},{8,12},{12,8},{16,20},{20,16},{24,28},{28,24},{1,5},{5... | collective-permute-start | bytes 221192 | tf_op jit(solution)/shard_map/ppermute | solution.py:28
  11.5 1.6 %collective-permute-done.3.refs_2_ = bf16[144,256]{1,0:T(8,128)(2,1)S(1)} collective-permute-done((bf16[144,256]{1,0:T(8,128)(2,1)S(1)}, bf16[144,256]{1,0:T(8,128)(2,1)S(1)}, u32[]{:S(2)}, u32[]{:S(2)}) %collective-permute-start.3) | collective-permute-done | bytes 73760 | tf_op jit(solution)/shard_map/ppermute | solution.py:28
  13.0 1.5 %collective-permute-start.4 = (bf16[144,256]{1,0:T(8,128)(2,1)S(1)}, bf16[144,256]{1,0:T(8,128)(2,1)S(1)}, u32[]{:S(2)}, u32[]{:S(2)}) collective-permute-start(bf16[144,256]{1,0:T(8,128)(2,1)S(1)} %collective-permute-done.3.refs_2_), channel_id=1, source_target_pairs={{0,4},{4,0},{8,12},{12,8},{16,20},{20,16},{24,28},{28,24},{1,5},{5... | collective-permute-start | bytes 221192 | tf_op jit(solution)/shard_map/ppermute | solution.py:28
  14.6 0.5 collective-permute-start.2
  15.1 2.0 %turn.1 = (bf16[2048,256]{1,0:T(8,128)(2,1)S(1)}, bf16[128,2048]{1,0:T(8,128)(2,1)S(1)}, f32[8,128]{1,0:T(8,128)S(1)}) custom-call(s32[2]{0:T(128)S(1)} %pad_add_fusion.ids, bf16[4096,128]{1,0:T(8,128)(2,1)} %protos.1, f32[1,4096]{1,0:T(1,128)} %bitcast.18), custom_call_target="tpu_custom_call" | custom-call | tf_op jit(solution)/shard_map/turn/pallas_call | solution.py:319
  17.1 0.1 collective-permute-start.8
  17.1 0.0 collective-permute-done.refs_0_
  17.2 0.0 collective-permute-done.6.refs_3_
  17.2 0.9 %collective-permute-done.4.refs_2_ = bf16[144,256]{1,0:T(8,128)(2,1)S(1)} collective-permute-done((bf16[144,256]{1,0:T(8,128)(2,1)S(1)}, bf16[144,256]{1,0:T(8,128)(2,1)S(1)}, u32[]{:S(2)}, u32[]{:S(2)}) %collective-permute-start.4) | collective-permute-done | bytes 73760 | tf_op jit(solution)/shard_map/ppermute | solution.py:28
  18.1 0.8 %collective-permute-done.2.refs_1_ = bf16[144,256]{1,0:T(8,128)(2,1)S(1)} collective-permute-done((bf16[144,256]{1,0:T(8,128)(2,1)S(1)}, bf16[144,256]{1,0:T(8,128)(2,1)S(1)}, u32[]{:S(2)}, u32[]{:S(2)}) %collective-permute-start.2) | collective-permute-done | bytes 73760 | tf_op jit(solution)/shard_map/ppermute | solution.py:28
  18.9 0.1 collective-permute-start.7
  19.0 3.2 %plan_ours.1 = (f32[2048,2048]{1,0:T(8,128)S(1)}, f32[2,2048,128]{2,1,0:T(8,128)S(1)}, f32[2,1024]{1,0:T(2,128)S(1)}, bf16[256,1024]{1,0:T(8,128)(2,1)S(1)}, bf16[128,1024]{1,0:T(8,128)(2,1)S(1)}) custom-call(s32[2]{0:T(128)S(1)} %pad_add_fusion.ids, bf16[2048,256]{1,0:T(8,128)(2,1)S(1)} %get-tuple-element.37.protos, bf16[4,144,256]{2,1,0:T(8,128)(2,1)S(1)} %stack.15.mine, ...), custom_call_target="tpu_custom_call" | custom-call | tf_op jit(solution)/shard_map/plan_ours/pallas_call | solution.py:319
  22.2 0.0 collective-permute-done.7.theirs
  22.2 3.4 %plan_theirs.1 = (f32[2048,2048]{1,0:T(8,128)S(1)}, f32[2,2048,128]{2,1,0:T(8,128)S(1)}, f32[2,2048]{1,0:T(2,128)S(1)}, bf16[256,1024]{1,0:T(8,128)(2,1)S(1)}, bf16[128,1024]{1,0:T(8,128)(2,1)S(1)}) custom-call(s32[2]{0:T(128)S(1)} %pad_add_fusion.ids, bf16[2048,256]{1,0:T(8,128)(2,1)S(1)} %get-tuple-element.37.protos, ...), custom_call_target="tpu_custom_call", output_to_operand_aliasing={{0}: (4, {})} | custom-call | tf_op jit(solution)/shard_map/plan_theirs/pallas_call | solution.py:319
  25.7 0.6 collective-permute-start.9
  26.3 0.8 %collective-permute-done.9.right = f32[2,2048]{1,0:T(2,128)S(1)} collective-permute-done((f32[2,2048]{1,0:T(2,128)S(1)}, f32[2,2048]{1,0:T(2,128)S(1)}, u32[]{:S(2)}, u32[]{:S(2)}) %collective-permute-start.9) | collective-permute-done | bytes 16416 | tf_op jit(solution)/shard_map/ppermute | solution.py:28
  27.1 2.0 %collective-permute-start.12 = (f32[2,2048]{1,0:T(2,128)S(1)}, f32[2,2048]{1,0:T(2,128)S(1)}, u32[]{:S(2)}, u32[]{:S(2)}) collective-permute-start(f32[2,2048]{1,0:T(2,128)S(1)} %add.28.after.refs_0_), channel_id=1, source_target_pairs={{0,6},{1,7},{2,4},{3,5},{4,2},{5,3},{6,0},{7,1},{8,14},{9,15},{10,... | collective-permute-start | bytes 49160 | tf_op jit(solution)/shard_map/ppermute | solution.py:340
  29.1 1.0 %collective-permute-start.11 = (f32[2,2048]{1,0:T(2,128)S(1)}, f32[2,2048]{1,0:T(2,128)S(1)}, u32[]{:S(2)}, u32[]{:S(2)}) collective-permute-start(f32[2,2048]{1,0:T(2,128)S(1)} %add.28.after.refs_0_), channel_id=1, source_target_pairs={{0,4},{1,5},{2,6},{3,7},{4,0},{5,1},{6,2},{7,3},{8,12},{9,13},{10,... | collective-permute-start | bytes 49160 | tf_op jit(solution)/shard_map/ppermute | solution.py:340
  30.1 0.5 collective-permute-start.10
  30.6 2.0 %embed_before.1 = (f32[2048,512]{1,0:T(8,128)S(1)}, f32[8,128]{1,0:T(8,128)S(1)}) custom-call(bf16[2048,256]{1,0:T(8,128)(2,1)S(1)} %get-tuple-element.37.protos, bf16[256,1024]{1,0:T(8,128)(2,1)S(1)} %get-tuple-element.45.emb_a.emb_ext, bf16[256,1024]{1,0:T(8,128)(2,1)S(1)} %get-tuple-element.46.emb_b.emb_ext, f32[2,2048]{1,0:T(2,128)S(1)} %add.28.after.refs_0_), custom_call_target="tpu_custom_call" | custom-call | tf_op jit(solution)/shard_map/embed_before/pallas_call | solution.py:319
  32.6 0.2 collective-permute-done.11.refs_2_
  32.8 1.0 %collective-permute-done.10.refs_1_ = f32[2,2048]{1,0:T(2,128)S(1)} collective-permute-done((f32[2,2048]{1,0:T(2,128)S(1)}, f32[2,2048]{1,0:T(2,128)S(1)}, u32[]{:S(2)}, u32[]{:S(2)}) %collective-permute-start.10) | collective-permute-done | bytes 16416 | tf_op jit(solution)/shard_map/ppermute | solution.py:340
  33.8 2.5 %sweep.3 = (f32[2048,2048]{1,0:T(8,128)S(1)}, f32[2,2048]{1,0:T(2,128)S(1)}, f32[1,2048]{1,0:T(1,128)S(1)}) custom-call(f32[2048,2048]{1,0:T(8,128)S(1)} %get-tuple-element.42.plan, f32[2,2048,128]{2,1,0:T(8,128)S(1)} %get-tuple-element.43.cols, f32[2,2048]{1,0:T(2,128)S(1)} %add.28.after.refs_0_, ...), custom_call_target="tpu_custom_call", output_to_operand_aliasing={{0}: (0, {})} | custom-call | tf_op jit(solution)/shard_map/sweep/pallas_call | solution.py:319
  36.3 0.1 collective-permute-start.13
  36.4 1.2 %collective-permute-done.13.right = f32[1,2048]{1,0:T(1,128)S(1)} collective-permute-done((f32[1,2048]{1,0:T(1,128)S(1)}, f32[1,2048]{1,0:T(1,128)S(1)}, u32[]{:S(2)}, u32[]{:S(2)}) %collective-permute-start.13) | collective-permute-done | bytes 8224 | tf_op jit(solution)/shard_map/ppermute | solution.py:28
  37.6 1.0 %collective-permute-start.16 = (f32[1,2048]{1,0:T(1,128)S(1)}, f32[1,2048]{1,0:T(1,128)S(1)}, u32[]{:S(2)}, u32[]{:S(2)}) collective-permute-start(f32[1,2048]{1,0:T(1,128)S(1)} %add.29.after.refs_1_), channel_id=1, source_target_pairs={{0,6},{1,7},{2,4},{3,5},{4,2},{5,3},{6,0},{7,1},{8,14},{9,15},{10,... | collective-permute-start | bytes 24584 | tf_op jit(solution)/shard_map/ppermute | solution.py:340
  38.6 1.0 %collective-permute-start.15 = (f32[1,2048]{1,0:T(1,128)S(1)}, f32[1,2048]{1,0:T(1,128)S(1)}, u32[]{:S(2)}, u32[]{:S(2)}) collective-permute-start(f32[1,2048]{1,0:T(1,128)S(1)} %add.29.after.refs_1_), channel_id=1, source_target_pairs={{0,4},{1,5},{2,6},{3,7},{4,0},{5,1},{6,2},{7,3},{8,12},{9,13},{10,... | collective-permute-start | bytes 24584 | tf_op jit(solution)/shard_map/ppermute | solution.py:340
  39.6 1.5 %collective-permute-start.14 = (f32[1,2048]{1,0:T(1,128)S(1)}, f32[1,2048]{1,0:T(1,128)S(1)}, u32[]{:S(2)}, u32[]{:S(2)}) collective-permute-start(f32[1,2048]{1,0:T(1,128)S(1)} %add.29.after.refs_1_), channel_id=1, source_target_pairs={{0,2},{1,3},{2,0},{3,1},{4,6},{5,7},{6,4},{7,5},{8,10},{9,11},{10,... | collective-permute-start | bytes 24584 | tf_op jit(solution)/shard_map/ppermute | solution.py:340
  41.1 2.0 %proto_before.1 = (f32[512,2048]{1,0:T(8,128)S(1)}, f32[512,128]{1,0:T(8,128)S(1)}, f32[8,128]{1,0:T(8,128)S(1)}) custom-call(s32[2]{0:T(128)S(1)} %pad_add_fusion.ids, bf16[2048,256]{1,0:T(8,128)(2,1)S(1)} %get-tuple-element.37.protos, bf16[256,1024]{1,0:T(8,128)(2,1)S(1)} %get-tuple-element.45.emb_a.emb_ext, ...), custom_call_target="tpu_custom_call" | custom-call | tf_op jit(solution)/shard_map/proto_before/pallas_call | solution.py:319
  43.1 0.1 collective-permute-done.14.refs_2_
  43.2 2.5 %sweep.4 = (f32[2048,2048]{1,0:T(8,128)S(1)}, f32[1,2048]{1,0:T(1,128)S(1)}) custom-call(f32[2048,2048]{1,0:T(8,128)S(1)} %get-tuple-element.48.plan, f32[2,2048,128]{2,1,0:T(8,128)S(1)} %get-tuple-element.43.cols, f32[2,2048]{1,0:T(2,128)S(1)} %get-tuple-element.49.refs_0_.sums, f32[1,2048]{1,0:T(1,128)S(1)} %add.29.after.refs_1_, ...), custom_call_target="tpu_custom_call", output_to_operand_aliasing={{0}: (0, {})} | custom-call | tf_op jit(solution)/shard_map/sweep/pallas_call | solution.py:319
  45.8 0.1 collective-permute-start.17
  45.8 1.2 %collective-permute-done.17.right = f32[1,2048]{1,0:T(1,128)S(1)} collective-permute-done((f32[1,2048]{1,0:T(1,128)S(1)}, f32[1,2048]{1,0:T(1,128)S(1)}, u32[]{:S(2)}, u32[]{:S(2)}) %collective-permute-start.17) | collective-permute-done | bytes 8224 | tf_op jit(solution)/shard_map/ppermute | solution.py:28
  47.0 2.0 %collective-permute-start.20 = (f32[1,2048]{1,0:T(1,128)S(1)}, f32[1,2048]{1,0:T(1,128)S(1)}, u32[]{:S(2)}, u32[]{:S(2)}) collective-permute-start(f32[1,2048]{1,0:T(1,128)S(1)} %add.30.after.refs_1_), channel_id=1, source_target_pairs={{0,6},{1,7},{2,4},{3,5},{4,2},{5,3},{6,0},{7,1},{8,14},{9,15},{10,... | collective-permute-start | bytes 24584 | tf_op jit(solution)/shard_map/ppermute | solution.py:340
  49.0 1.0 %collective-permute-start.19 = (f32[1,2048]{1,0:T(1,128)S(1)}, f32[1,2048]{1,0:T(1,128)S(1)}, u32[]{:S(2)}, u32[]{:S(2)}) collective-permute-start(f32[1,2048]{1,0:T(1,128)S(1)} %add.30.after.refs_1_), channel_id=1, source_target_pairs={{0,4},{1,5},{2,6},{3,7},{4,0},{5,1},{6,2},{7,3},{8,12},{9,13},{10,... | collective-permute-start | bytes 24584 | tf_op jit(solution)/shard_map/ppermute | solution.py:340
  50.0 0.5 collective-permute-start.18
  50.5 2.3 %cotangent.2 = (f32[2048,512]{1,0:T(8,128)S(1)}, f32[8,128]{1,0:T(8,128)S(1)}) custom-call(s32[2]{0:T(128)S(1)} %pad_add_fusion.ids, bf16[2048,256]{1,0:T(8,128)(2,1)S(1)} %get-tuple-element.37.protos, bf16[128,1024]{1,0:T(8,128)(2,1)S(1)} %get-tuple-element.51.view_a, bf16[128,1024]{1,0:T(8,128)(2,1)S(1)} %get-tuple-element.52.view_b, ...), custom_call_target="tpu_custom_call" | custom-call | tf_op jit(solution)/shard_map/cotangent/pallas_call | solution.py:319
  52.8 0.8 %collective-permute-done.18.refs_2_ = f32[1,2048]{1,0:T(1,128)S(1)} collective-permute-done((f32[1,2048]{1,0:T(1,128)S(1)}, f32[1,2048]{1,0:T(1,128)S(1)}, u32[]{:S(2)}, u32[]{:S(2)}) %collective-permute-start.18) | collective-permute-done | bytes 8224 | tf_op jit(solution)/shard_map/ppermute | solution.py:340
  53.6 2.5 %sweep.5 = (f32[2048,2048]{1,0:T(8,128)S(1)}, f32[1,2048]{1,0:T(1,128)S(1)}) custom-call(f32[2048,2048]{1,0:T(8,128)S(1)} %get-tuple-element.54.plan, f32[2,2048,128]{2,1,0:T(8,128)S(1)} %get-tuple-element.43.cols, f32[2,2048]{1,0:T(2,128)S(1)} %get-tuple-element.49.refs_0_.sums, f32[1,2048]{1,0:T(1,128)S(1)} %add.30.after.refs_1_, ...), custom_call_target="tpu_custom_call", output_to_operand_aliasing={{0}: (0, {})} | custom-call | tf_op jit(solution)/shard_map/sweep/pallas_call | solution.py:319
  56.2 0.1 collective-permute-start.21
  56.2 1.2 %collective-permute-done.21.right = f32[1,2048]{1,0:T(1,128)S(1)} collective-permute-done((f32[1,2048]{1,0:T(1,128)S(1)}, f32[1,2048]{1,0:T(1,128)S(1)}, u32[]{:S(2)}, u32[]{:S(2)}) %collective-permute-start.21) | collective-permute-done | bytes 8224 | tf_op jit(solution)/shard_map/ppermute | solution.py:28
  57.4 1.2 %collective-permute-start.24 = (f32[1,2048]{1,0:T(1,128)S(1)}, f32[1,2048]{1,0:T(1,128)S(1)}, u32[]{:S(2)}, u32[]{:S(2)}) collective-permute-start(f32[1,2048]{1,0:T(1,128)S(1)} %add.31.after.refs_0_), channel_id=1, source_target_pairs={{0,6},{1,7},{2,4},{3,5},{4,2},{5,3},{6,0},{7,1},{8,14},{9,15},{10,... | collective-permute-start | bytes 24584 | tf_op jit(solution)/shard_map/ppermute | solution.py:340
  58.6 1.0 %collective-permute-start.23 = (f32[1,2048]{1,0:T(1,128)S(1)}, f32[1,2048]{1,0:T(1,128)S(1)}, u32[]{:S(2)}, u32[]{:S(2)}) collective-permute-start(f32[1,2048]{1,0:T(1,128)S(1)} %add.31.after.refs_0_), channel_id=1, source_target_pairs={{0,4},{1,5},{2,6},{3,7},{4,0},{5,1},{6,2},{7,3},{8,12},{9,13},{10,... | collective-permute-start | bytes 24584 | tf_op jit(solution)/shard_map/ppermute | solution.py:340
  59.6 1.3 %collective-permute-start.22 = (f32[1,2048]{1,0:T(1,128)S(1)}, f32[1,2048]{1,0:T(1,128)S(1)}, u32[]{:S(2)}, u32[]{:S(2)}) collective-permute-start(f32[1,2048]{1,0:T(1,128)S(1)} %add.31.after.refs_0_), channel_id=1, source_target_pairs={{0,2},{1,3},{2,0},{3,1},{4,6},{5,7},{6,4},{7,5},{8,10},{9,11},{10,... | collective-permute-start | bytes 24584 | tf_op jit(solution)/shard_map/ppermute | solution.py:340
  60.9 1.4 %cotangent.3 = (f32[512,2048]{1,0:T(8,128)S(1)}, f32[8,128]{1,0:T(8,128)S(1)}) custom-call(s32[2]{0:T(128)S(1)} %pad_add_fusion.ids, bf16[2048,256]{1,0:T(8,128)(2,1)S(1)} %get-tuple-element.37.protos, bf16[128,1024]{1,0:T(8,128)(2,1)S(1)} %get-tuple-element.51.view_a, bf16[128,1024]{1,0:T(8,128)(2,1)S(1)} %get-tuple-element.52.view_b, ...), custom_call_target="tpu_custom_call" | custom-call | tf_op jit(solution)/shard_map/cotangent/pallas_call | solution.py:319
  62.3 0.9 %collective-permute-done.22.refs_1_ = f32[1,2048]{1,0:T(1,128)S(1)} collective-permute-done((f32[1,2048]{1,0:T(1,128)S(1)}, f32[1,2048]{1,0:T(1,128)S(1)}, u32[]{:S(2)}, u32[]{:S(2)}) %collective-permute-start.22) | collective-permute-done | bytes 8224 | tf_op jit(solution)/shard_map/ppermute | solution.py:340
  63.2 3.0 %embed_grad.1 = (f32[2048,128]{1,0:T(8,128)S(1)}, f32[1,2048]{1,0:T(1,128)S(1)}, f32[4,64,128]{2,1,0:T(8,128)S(1)}, f32[4,64,128]{2,1,0:T(8,128)S(1)}) custom-call(s32[2]{0:T(128)S(1)} %pad_add_fusion.ids, f32[2048,2048]{1,0:T(8,128)S(1)} %get-tuple-element.57.plan, f32[2,2048,128]{2,1,0:T(8,128)S(1)} %get-tuple-element.43.cols, ...), custom_call_target="tpu_custom_call" | custom-call | tf_op jit(solution)/shard_map/embed_grad/pallas_call | solution.py:319
  66.2 0.1 collective-permute-start.25
  66.3 1.0 %proto_grad.2 = (f32[512,128]{1,0:T(8,128)S(1)}, f32[8,128]{1,0:T(8,128)S(1)}) custom-call(s32[2]{0:T(128)S(1)} %pad_add_fusion.ids, bf16[256,1024]{1,0:T(8,128)(2,1)S(1)} %get-tuple-element.45.emb_a.emb_ext, f32[512,2048]{1,0:T(8,128)S(1)} %get-tuple-element.65.entries, f32[512,2048]{1,0:T(8,128)S(1)} %get-tuple-element.66.cots, ...), custom_call_target="tpu_custom_call" | custom-call | tf_op jit(solution)/shard_map/proto_grad/pallas_call | solution.py:319
  67.3 0.3 collective-permute-done.25.right
  67.6 1.4 %collective-permute-start.26 = (f32[64,128]{1,0:T(8,128)S(1)}, f32[64,128]{1,0:T(8,128)S(1)}, u32[]{:S(2)}, u32[]{:S(2)}) collective-permute-start(f32[64,128]{1,0:T(8,128)S(1)} %get-tuple-element.72), channel_id=1, source_target_pairs={{0,2},{1,3},{2,0},{3,1},{4,6},{5,7},{6,4},{7,5},{8,10},{9,11},{10,... | collective-permute-start | bytes 98312 | tf_op jit(solution)/shard_map/ppermute | solution.py:340
  69.0 1.2 %collective-permute-start.28 = (f32[64,128]{1,0:T(8,128)S(1)}, f32[64,128]{1,0:T(8,128)S(1)}, u32[]{:S(2)}, u32[]{:S(2)}) collective-permute-start(f32[64,128]{1,0:T(8,128)S(1)} %get-tuple-element.73), channel_id=1, source_target_pairs={{0,6},{1,7},{2,4},{3,5},{4,2},{5,3},{6,0},{7,1},{8,14},{9,15},{10,... | collective-permute-start | bytes 98312 | tf_op jit(solution)/shard_map/ppermute | solution.py:340
  70.2 1.0 %collective-permute-start.27 = (f32[64,128]{1,0:T(8,128)S(1)}, f32[64,128]{1,0:T(8,128)S(1)}, u32[]{:S(2)}, u32[]{:S(2)}) collective-permute-start(f32[64,128]{1,0:T(8,128)S(1)} %get-tuple-element.74), channel_id=1, source_target_pairs={{0,4},{1,5},{2,6},{3,7},{4,0},{5,1},{6,2},{7,3},{8,12},{9,13},{10,... | collective-permute-start | bytes 98312 | tf_op jit(solution)/shard_map/ppermute | solution.py:340
  71.2 1.7 %proto_grad.3 = f32[512,128]{1,0:T(8,128)} custom-call(s32[2]{0:T(128)S(1)} %pad_add_fusion.ids, bf16[256,1024]{1,0:T(8,128)(2,1)S(1)} %get-tuple-element.46.emb_b.emb_ext, f32[512,2048]{1,0:T(8,128)S(1)} %get-tuple-element.65.entries, f32[512,2048]{1,0:T(8,128)S(1)} %get-tuple-element.66.cots, f32[512,128]{1,0:T(8,128)S(1)} %get-tuple-element.71.so_far, ...), custom_call_target="tpu_custom_call" | custom-call | tf_op jit(solution)/shard_map/proto_grad/pallas_call | solution.py:319
  72.9 0.9 %collective-permute-done.28 = f32[64,128]{1,0:T(8,128)S(1)} collective-permute-done((f32[64,128]{1,0:T(8,128)S(1)}, f32[64,128]{1,0:T(8,128)S(1)}, u32[]{:S(2)}, u32[]{:S(2)}) %collective-permute-start.28) | collective-permute-done | bytes 32800 | tf_op jit(solution)/shard_map/ppermute | solution.py:340
  73.8 0.3 collective-permute-done.27
  74.2 0.6 fusion.2
  (18 shorter events, 0.1 us)
Async XLA Ops:
  1.7 7.9 %collective-permute-start.5 = (bf16[144,256]{1,0:T(8,128)(2,1)S(1)}, bf16[144,256]{1,0:T(8,128)(2,1)S(1)}, u32[]{:S(2)}, u32[]{:S(2)}) collective-permute-start(bf16[144,256]{1,0:T(8,128)(2,1)S(1)} %prepare.1.refs_0_), channel_id=1, source_target_pairs={{0,24},{4,28},{8,16},{12,20},{16,8},{20,12},{24,0},{28,4},{1,25},{... | collective-permute-start | bytes 221192 | tf_op jit(solution)/shard_map/ppermute | solution.py:28
  6.8 6.2 %collective-permute-start.3 = (bf16[144,256]{1,0:T(8,128)(2,1)S(1)}, bf16[144,256]{1,0:T(8,128)(2,1)S(1)}, u32[]{:S(2)}, u32[]{:S(2)}) collective-permute-start(bf16[144,256]{1,0:T(8,128)(2,1)S(1)} %prepare.1.refs_0_), channel_id=1, source_target_pairs={{0,16},{4,20},{8,24},{12,28},{16,0},{20,4},{24,8},{28,12},{1,17},{... | collective-permute-start | bytes 221192 | tf_op jit(solution)/shard_map/ppermute | solution.py:28
  6.8 7.7 %collective-permute-start.1 = (bf16[144,256]{1,0:T(8,128)(2,1)S(1)}, bf16[144,256]{1,0:T(8,128)(2,1)S(1)}, u32[]{:S(2)}, u32[]{:S(2)}) collective-permute-start(bf16[144,256]{1,0:T(8,128)(2,1)S(1)} %prepare.1.refs_0_), channel_id=1, source_target_pairs={{0,8},{4,12},{8,0},{12,4},{16,24},{20,28},{24,16},{28,20},{1,9},{5... | collective-permute-start | bytes 221192 | tf_op jit(solution)/shard_map/ppermute | solution.py:28
  7.5 9.7 %collective-permute-start = (bf16[144,256]{1,0:T(8,128)(2,1)S(1)}, bf16[144,256]{1,0:T(8,128)(2,1)S(1)}, u32[]{:S(2)}, u32[]{:S(2)}) collective-permute-start(bf16[144,256]{1,0:T(8,128)(2,1)S(1)} %prepare.1.refs_0_), channel_id=1, source_target_pairs={{0,4},{4,0},{8,12},{12,8},{16,20},{20,16},{24,28},{28,24},{1,5},{5... | collective-permute-start | bytes 221192 | tf_op jit(solution)/shard_map/ppermute | solution.py:28
  9.6 7.6 %collective-permute-start.6 = (bf16[144,256]{1,0:T(8,128)(2,1)S(1)}, bf16[144,256]{1,0:T(8,128)(2,1)S(1)}, u32[]{:S(2)}, u32[]{:S(2)}) collective-permute-start(bf16[144,256]{1,0:T(8,128)(2,1)S(1)} %collective-permute-done.5.refs_3_), channel_id=1, source_target_pairs={{0,4},{4,0},{8,12},{12,8},{16,20},{20,16},{24,28},{28,24},{1,5},{5... | collective-permute-start | bytes 221192 | tf_op jit(solution)/shard_map/ppermute | solution.py:28
  13.0 5.1 %collective-permute-start.4 = (bf16[144,256]{1,0:T(8,128)(2,1)S(1)}, bf16[144,256]{1,0:T(8,128)(2,1)S(1)}, u32[]{:S(2)}, u32[]{:S(2)}) collective-permute-start(bf16[144,256]{1,0:T(8,128)(2,1)S(1)} %collective-permute-done.3.refs_2_), channel_id=1, source_target_pairs={{0,4},{4,0},{8,12},{12,8},{16,20},{20,16},{24,28},{28,24},{1,5},{5... | collective-permute-start | bytes 221192 | tf_op jit(solution)/shard_map/ppermute | solution.py:28
  14.6 4.4 %collective-permute-start.2 = (bf16[144,256]{1,0:T(8,128)(2,1)S(1)}, bf16[144,256]{1,0:T(8,128)(2,1)S(1)}, u32[]{:S(2)}, u32[]{:S(2)}) collective-permute-start(bf16[144,256]{1,0:T(8,128)(2,1)S(1)} %collective-permute-done.1.refs_1_), channel_id=1, source_target_pairs={{0,4},{4,0},{8,12},{12,8},{16,20},{20,16},{24,28},{28,24},{1,5},{5... | collective-permute-start | bytes 221192 | tf_op jit(solution)/shard_map/ppermute | solution.py:28
  17.1 2.0 %collective-permute-start.8 = (bf16[4,144,256]{2,1,0:T(8,128)(2,1)S(1)}, bf16[4,144,256]{2,1,0:T(8,128)(2,1)S(1)}, u32[]{:S(2)}, u32[]{:S(2)}) collective-permute-start(bf16[4,144,256]{2,1,0:T(8,128)(2,1)S(1)} %stack.15.mine), channel_id=1, source_target_pairs={{0,1},{1,0},{2,3},{3,2},{4,5},{5,4},{6,7},{7,6},{8,9},{9,8},{10,11... | collective-permute-start | bytes 884744 | tf_op jit(solution)/shard_map/ppermute | solution.py:28
  18.9 3.3 %collective-permute-start.7 = (bf16[4,144,256]{2,1,0:T(8,128)(2,1)S(1)}, bf16[4,144,256]{2,1,0:T(8,128)(2,1)S(1)}, u32[]{:S(2)}, u32[]{:S(2)}) collective-permute-start(bf16[4,144,256]{2,1,0:T(8,128)(2,1)S(1)} %stack.14.mine), channel_id=1, source_target_pairs={{0,1},{1,0},{2,3},{3,2},{4,5},{5,4},{6,7},{7,6},{8,9},{9,8},{10,11... | collective-permute-start | bytes 884744 | tf_op jit(solution)/shard_map/ppermute | solution.py:28
  25.7 1.4 %collective-permute-start.9 = (f32[2,2048]{1,0:T(2,128)S(1)}, f32[2,2048]{1,0:T(2,128)S(1)}, u32[]{:S(2)}, u32[]{:S(2)}) collective-permute-start(f32[2,2048]{1,0:T(2,128)S(1)} %get-tuple-element.44.left), channel_id=1, source_target_pairs={{0,1},{1,0},{2,3},{3,2},{4,5},{5,4},{6,7},{7,6},{8,9},{9,8},{10,11... | collective-permute-start | bytes 49160 | tf_op jit(solution)/shard_map/ppermute | solution.py:28
  27.1 5.5 %collective-permute-start.12 = (f32[2,2048]{1,0:T(2,128)S(1)}, f32[2,2048]{1,0:T(2,128)S(1)}, u32[]{:S(2)}, u32[]{:S(2)}) collective-permute-start(f32[2,2048]{1,0:T(2,128)S(1)} %add.28.after.refs_0_), channel_id=1, source_target_pairs={{0,6},{1,7},{2,4},{3,5},{4,2},{5,3},{6,0},{7,1},{8,14},{9,15},{10,... | collective-permute-start | bytes 49160 | tf_op jit(solution)/shard_map/ppermute | solution.py:340
  29.1 3.7 %collective-permute-start.11 = (f32[2,2048]{1,0:T(2,128)S(1)}, f32[2,2048]{1,0:T(2,128)S(1)}, u32[]{:S(2)}, u32[]{:S(2)}) collective-permute-start(f32[2,2048]{1,0:T(2,128)S(1)} %add.28.after.refs_0_), channel_id=1, source_target_pairs={{0,4},{1,5},{2,6},{3,7},{4,0},{5,1},{6,2},{7,3},{8,12},{9,13},{10,... | collective-permute-start | bytes 49160 | tf_op jit(solution)/shard_map/ppermute | solution.py:340
  30.1 3.7 %collective-permute-start.10 = (f32[2,2048]{1,0:T(2,128)S(1)}, f32[2,2048]{1,0:T(2,128)S(1)}, u32[]{:S(2)}, u32[]{:S(2)}) collective-permute-start(f32[2,2048]{1,0:T(2,128)S(1)} %add.28.after.refs_0_), channel_id=1, source_target_pairs={{0,2},{1,3},{2,0},{3,1},{4,6},{5,7},{6,4},{7,5},{8,10},{9,11},{10,... | collective-permute-start | bytes 49160 | tf_op jit(solution)/shard_map/ppermute | solution.py:340
  36.3 1.2 %collective-permute-start.13 = (f32[1,2048]{1,0:T(1,128)S(1)}, f32[1,2048]{1,0:T(1,128)S(1)}, u32[]{:S(2)}, u32[]{:S(2)}) collective-permute-start(f32[1,2048]{1,0:T(1,128)S(1)} %get-tuple-element.50.left), channel_id=1, source_target_pairs={{0,1},{1,0},{2,3},{3,2},{4,5},{5,4},{6,7},{7,6},{8,9},{9,8},{10,11... | collective-permute-start | bytes 24584 | tf_op jit(solution)/shard_map/ppermute | solution.py:28
  37.6 5.5 %collective-permute-start.16 = (f32[1,2048]{1,0:T(1,128)S(1)}, f32[1,2048]{1,0:T(1,128)S(1)}, u32[]{:S(2)}, u32[]{:S(2)}) collective-permute-start(f32[1,2048]{1,0:T(1,128)S(1)} %add.29.after.refs_1_), channel_id=1, source_target_pairs={{0,6},{1,7},{2,4},{3,5},{4,2},{5,3},{6,0},{7,1},{8,14},{9,15},{10,... | collective-permute-start | bytes 24584 | tf_op jit(solution)/shard_map/ppermute | solution.py:340
  38.6 4.5 %collective-permute-start.15 = (f32[1,2048]{1,0:T(1,128)S(1)}, f32[1,2048]{1,0:T(1,128)S(1)}, u32[]{:S(2)}, u32[]{:S(2)}) collective-permute-start(f32[1,2048]{1,0:T(1,128)S(1)} %add.29.after.refs_1_), channel_id=1, source_target_pairs={{0,4},{1,5},{2,6},{3,7},{4,0},{5,1},{6,2},{7,3},{8,12},{9,13},{10,... | collective-permute-start | bytes 24584 | tf_op jit(solution)/shard_map/ppermute | solution.py:340
  39.6 3.7 %collective-permute-start.14 = (f32[1,2048]{1,0:T(1,128)S(1)}, f32[1,2048]{1,0:T(1,128)S(1)}, u32[]{:S(2)}, u32[]{:S(2)}) collective-permute-start(f32[1,2048]{1,0:T(1,128)S(1)} %add.29.after.refs_1_), channel_id=1, source_target_pairs={{0,2},{1,3},{2,0},{3,1},{4,6},{5,7},{6,4},{7,5},{8,10},{9,11},{10,... | collective-permute-start | bytes 24584 | tf_op jit(solution)/shard_map/ppermute | solution.py:340
  45.8 1.2 %collective-permute-start.17 = (f32[1,2048]{1,0:T(1,128)S(1)}, f32[1,2048]{1,0:T(1,128)S(1)}, u32[]{:S(2)}, u32[]{:S(2)}) collective-permute-start(f32[1,2048]{1,0:T(1,128)S(1)} %get-tuple-element.55.left), channel_id=1, source_target_pairs={{0,1},{1,0},{2,3},{3,2},{4,5},{5,4},{6,7},{7,6},{8,9},{9,8},{10,11... | collective-permute-start | bytes 24584 | tf_op jit(solution)/shard_map/ppermute | solution.py:28
  47.0 5.8 %collective-permute-start.20 = (f32[1,2048]{1,0:T(1,128)S(1)}, f32[1,2048]{1,0:T(1,128)S(1)}, u32[]{:S(2)}, u32[]{:S(2)}) collective-permute-start(f32[1,2048]{1,0:T(1,128)S(1)} %add.30.after.refs_1_), channel_id=1, source_target_pairs={{0,6},{1,7},{2,4},{3,5},{4,2},{5,3},{6,0},{7,1},{8,14},{9,15},{10,... | collective-permute-start | bytes 24584 | tf_op jit(solution)/shard_map/ppermute | solution.py:340
  49.0 3.8 %collective-permute-start.19 = (f32[1,2048]{1,0:T(1,128)S(1)}, f32[1,2048]{1,0:T(1,128)S(1)}, u32[]{:S(2)}, u32[]{:S(2)}) collective-permute-start(f32[1,2048]{1,0:T(1,128)S(1)} %add.30.after.refs_1_), channel_id=1, source_target_pairs={{0,4},{1,5},{2,6},{3,7},{4,0},{5,1},{6,2},{7,3},{8,12},{9,13},{10,... | collective-permute-start | bytes 24584 | tf_op jit(solution)/shard_map/ppermute | solution.py:340
  50.0 3.7 %collective-permute-start.18 = (f32[1,2048]{1,0:T(1,128)S(1)}, f32[1,2048]{1,0:T(1,128)S(1)}, u32[]{:S(2)}, u32[]{:S(2)}) collective-permute-start(f32[1,2048]{1,0:T(1,128)S(1)} %add.30.after.refs_1_), channel_id=1, source_target_pairs={{0,2},{1,3},{2,0},{3,1},{4,6},{5,7},{6,4},{7,5},{8,10},{9,11},{10,... | collective-permute-start | bytes 24584 | tf_op jit(solution)/shard_map/ppermute | solution.py:340
  56.2 1.2 %collective-permute-start.21 = (f32[1,2048]{1,0:T(1,128)S(1)}, f32[1,2048]{1,0:T(1,128)S(1)}, u32[]{:S(2)}, u32[]{:S(2)}) collective-permute-start(f32[1,2048]{1,0:T(1,128)S(1)} %get-tuple-element.61.left), channel_id=1, source_target_pairs={{0,1},{1,0},{2,3},{3,2},{4,5},{5,4},{6,7},{7,6},{8,9},{9,8},{10,11... | collective-permute-start | bytes 24584 | tf_op jit(solution)/shard_map/ppermute | solution.py:28
  57.4 4.9 %collective-permute-start.24 = (f32[1,2048]{1,0:T(1,128)S(1)}, f32[1,2048]{1,0:T(1,128)S(1)}, u32[]{:S(2)}, u32[]{:S(2)}) collective-permute-start(f32[1,2048]{1,0:T(1,128)S(1)} %add.31.after.refs_0_), channel_id=1, source_target_pairs={{0,6},{1,7},{2,4},{3,5},{4,2},{5,3},{6,0},{7,1},{8,14},{9,15},{10,... | collective-permute-start | bytes 24584 | tf_op jit(solution)/shard_map/ppermute | solution.py:340
  58.6 3.7 %collective-permute-start.23 = (f32[1,2048]{1,0:T(1,128)S(1)}, f32[1,2048]{1,0:T(1,128)S(1)}, u32[]{:S(2)}, u32[]{:S(2)}) collective-permute-start(f32[1,2048]{1,0:T(1,128)S(1)} %add.31.after.refs_0_), channel_id=1, source_target_pairs={{0,4},{1,5},{2,6},{3,7},{4,0},{5,1},{6,2},{7,3},{8,12},{9,13},{10,... | collective-permute-start | bytes 24584 | tf_op jit(solution)/shard_map/ppermute | solution.py:340
  59.6 3.7 %collective-permute-start.22 = (f32[1,2048]{1,0:T(1,128)S(1)}, f32[1,2048]{1,0:T(1,128)S(1)}, u32[]{:S(2)}, u32[]{:S(2)}) collective-permute-start(f32[1,2048]{1,0:T(1,128)S(1)} %add.31.after.refs_0_), channel_id=1, source_target_pairs={{0,2},{1,3},{2,0},{3,1},{4,6},{5,7},{6,4},{7,5},{8,10},{9,11},{10,... | collective-permute-start | bytes 24584 | tf_op jit(solution)/shard_map/ppermute | solution.py:340
  66.2 1.4 %collective-permute-start.25 = (f32[4,64,128]{2,1,0:T(8,128)S(1)}, f32[4,64,128]{2,1,0:T(8,128)S(1)}, u32[]{:S(2)}, u32[]{:S(2)}) collective-permute-start(f32[4,64,128]{2,1,0:T(8,128)S(1)} %get-tuple-element.64), channel_id=1, source_target_pairs={{0,1},{1,0},{2,3},{3,2},{4,5},{5,4},{6,7},{7,6},{8,9},{9,8},{10,11... | collective-permute-start | bytes 393224 | tf_op jit(solution)/shard_map/ppermute | solution.py:28
  67.6 5.3 %collective-permute-start.26 = (f32[64,128]{1,0:T(8,128)S(1)}, f32[64,128]{1,0:T(8,128)S(1)}, u32[]{:S(2)}, u32[]{:S(2)}) collective-permute-start(f32[64,128]{1,0:T(8,128)S(1)} %get-tuple-element.72), channel_id=1, source_target_pairs={{0,2},{1,3},{2,0},{3,1},{4,6},{5,7},{6,4},{7,5},{8,10},{9,11},{10,... | collective-permute-start | bytes 98312 | tf_op jit(solution)/shard_map/ppermute | solution.py:340
  69.0 4.8 %collective-permute-start.28 = (f32[64,128]{1,0:T(8,128)S(1)}, f32[64,128]{1,0:T(8,128)S(1)}, u32[]{:S(2)}, u32[]{:S(2)}) collective-permute-start(f32[64,128]{1,0:T(8,128)S(1)} %get-tuple-element.73), channel_id=1, source_target_pairs={{0,6},{1,7},{2,4},{3,5},{4,2},{5,3},{6,0},{7,1},{8,14},{9,15},{10,... | collective-permute-start | bytes 98312 | tf_op jit(solution)/shard_map/ppermute | solution.py:340
  70.2 4.0 %collective-permute-start.27 = (f32[64,128]{1,0:T(8,128)S(1)}, f32[64,128]{1,0:T(8,128)S(1)}, u32[]{:S(2)}, u32[]{:S(2)}) collective-permute-start(f32[64,128]{1,0:T(8,128)S(1)} %get-tuple-element.74), channel_id=1, source_target_pairs={{0,4},{1,5},{2,6},{3,7},{4,0},{5,1},{6,2},{7,3},{8,12},{9,13},{10,... | collective-permute-start | bytes 98312 | tf_op jit(solution)/shard_map/ppermute | solution.py:340

commit v11 on v8

--- a/solution.py
+++ b/solution.py
@@ -82,7 +82,7 @@
         protos_t[:, here] = jnp.transpose(block.astype(F32)).astype(BF16)
         return carry
 
-    lax.fori_loop(0, count // CHUNK, step, 0)
+    lax.fori_loop(0, count // CHUNK, step, 0, unroll=True)
 
 
 def stack_kernel(count, *refs):
@@ -230,7 +230,7 @@
             entry_out[here, half * rows:(half + 1) * rows] = logit_scale * entry
         return carry
 
-    lax.fori_loop(0, protos.shape[0] // STEP, step, 0)
+    lax.fori_loop(0, protos.shape[0] // STEP, step, 0, unroll=2)
 
 
 def cotangent_kernel(view_scale, block, ids, protos, view_a, view_b, after, cot_out, token):
@@ -248,7 +248,7 @@
             cot_out[here, half * wide // 2:(half + 1) * wide // 2] = -view_scale * cot
         return carry
 
-    lax.fori_loop(0, tall // STEP, step, 0)
+    lax.fori_loop(0, tall // STEP, step, 0, unroll=2)
 
 
 def embed_kernel(shares, ids, plan, cols, sums, protos_t, entries, cots, *refs):
@@ -265,7 +265,7 @@
         duals_out[here, :] = by_rows(plan.at[here, :], cols, here, spread)
         return carry
 
-    lax.fori_loop(0, plan.shape[0] // STEP, duals, 0, unroll=2)
+    lax.fori_loop(0, plan.shape[0] // STEP, duals, 0, unroll=4)
     total = jnp.zeros((width, rows), F32)
     for start in range(0, plan.shape[0], CHUNK):
         here = slice(start, start + CHUNK)

time: 75 us -> 74.9 us (level)
  Pallas kernels: 30.8 us -> 28.8 us
  waiting for transfers between devices: 12.7 us -> 14.5 us
    pallas_call x21, Pallas kernels: 30.8 us -> 28.8 us  [run(): pl.pallas_call(kernel, out_shape=out_shape, in_specs=[small] * scalars +...]
    ppermute x15, waiting for transfers between devices: 4.27 us -> 5.76 us  [swap_both(): return lax.ppermute(value, ('row', 'proto'), pairs)]
  transfers between devices with their start and end apart: 29 -> 29, of which waited for: 16 -> 17; matrix products, arithmetic and copies ran while one was open for 0% -> 0% of each run, Pallas kernels for 21% -> 18%
where the time goes in v11:
time: 74.9 us; the launch traced here: 74.7 us
  starting transfers between devices  29.8 us (40%)
  Pallas kernels  28.8 us (38%)
  waiting for transfers between devices  14.5 us (19%)
  between operations  0.89 us (1%)
    pallas_call x21, Pallas kernels, run(): pl.pallas_call(kernel, out_shape=out_shape, in_specs=[small] * scalars +...  28.8 us
    ppermute x15, starting transfers between devices, swap_both(): return lax.ppermute(value, ('row', 'proto'), pairs)  17.5 us
    ppermute x14, starting transfers between devices, swap(): return lax.ppermute(value, axis, [(i, i ^ step) for i in range(size)])  12.3 us
    ppermute x14, waiting for transfers between devices, swap(): return lax.ppermute(value, axis, [(i, i ^ step) for i in range(size)])  8.71 us
    ppermute x15, waiting for transfers between devices, swap_both(): return lax.ppermute(value, ('row', 'proto'), pairs)  5.76 us
  transfers between devices with their start and end apart: 29, of which 17 were waited for; matrix products, arithmetic and copies ran while one was open for 0% of the time, Pallas kernels for 18%

profile of v11, /device:TPU:0, one launch (start us, length us, event | category | flops | bytes accessed | tf_op | source)
XLA Modules:
  0.0 74.7 jit_solution(1969009471254787318)
XLA Ops:
  0.6 0.1 pad_add_fusion.ids
  0.7 1.0 %prepare.1.refs_0_ = bf16[144,256]{1,0:T(8,128)(2,1)S(1)} custom-call(s32[2]{0:T(128)S(1)} %pad_add_fusion.ids, bf16[256,128]{1,0:T(8,128)(2,1)} %embeddings.1, bf16[256,128]{1,0:T(8,128)(2,1)} %second_view.1, f32[1,256]{1,0:T(1,128)} %bitcast.19), custom_call_target="tpu_custom_call" | custom-call | tf_op jit(solution)/shard_map/prepare/pallas_call | solution.py:319
  1.7 5.1 %collective-permute-start.5 = (bf16[144,256]{1,0:T(8,128)(2,1)S(1)}, bf16[144,256]{1,0:T(8,128)(2,1)S(1)}, u32[]{:S(2)}, u32[]{:S(2)}) collective-permute-start(bf16[144,256]{1,0:T(8,128)(2,1)S(1)} %prepare.1.refs_0_), channel_id=1, source_target_pairs={{0,24},{4,28},{8,16},{12,20},{16,8},{20,12},{24,0},{28,4},{1,25},{... | collective-permute-start | bytes 221192 | tf_op jit(solution)/shard_map/ppermute | solution.py:28
  6.8 0.6 collective-permute-start.1
  7.5 1.7 %collective-permute-start = (bf16[144,256]{1,0:T(8,128)(2,1)S(1)}, bf16[144,256]{1,0:T(8,128)(2,1)S(1)}, u32[]{:S(2)}, u32[]{:S(2)}) collective-permute-start(bf16[144,256]{1,0:T(8,128)(2,1)S(1)} %prepare.1.refs_0_), channel_id=1, source_target_pairs={{0,4},{4,0},{8,12},{12,8},{16,20},{20,16},{24,28},{28,24},{1,5},{5... | collective-permute-start | bytes 221192 | tf_op jit(solution)/shard_map/ppermute | solution.py:28
  9.1 0.4 collective-permute-done.5.refs_3_
  9.6 1.9 %collective-permute-start.6 = (bf16[144,256]{1,0:T(8,128)(2,1)S(1)}, bf16[144,256]{1,0:T(8,128)(2,1)S(1)}, u32[]{:S(2)}, u32[]{:S(2)}) collective-permute-start(bf16[144,256]{1,0:T(8,128)(2,1)S(1)} %collective-permute-done.5.refs_3_), channel_id=1, source_target_pairs={{0,4},{4,0},{8,12},{12,8},{16,20},{20,16},{24,28},{28,24},{1,5},{5... | collective-permute-start | bytes 221192 | tf_op jit(solution)/shard_map/ppermute | solution.py:28
  11.5 1.6 %collective-permute-done.3.refs_2_ = bf16[144,256]{1,0:T(8,128)(2,1)S(1)} collective-permute-done((bf16[144,256]{1,0:T(8,128)(2,1)S(1)}, bf16[144,256]{1,0:T(8,128)(2,1)S(1)}, u32[]{:S(2)}, u32[]{:S(2)}) %collective-permute-start.3) | collective-permute-done | bytes 73760 | tf_op jit(solution)/shard_map/ppermute | solution.py:28
  13.0 1.5 %collective-permute-start.4 = (bf16[144,256]{1,0:T(8,128)(2,1)S(1)}, bf16[144,256]{1,0:T(8,128)(2,1)S(1)}, u32[]{:S(2)}, u32[]{:S(2)}) collective-permute-start(bf16[144,256]{1,0:T(8,128)(2,1)S(1)} %collective-permute-done.3.refs_2_), channel_id=1, source_target_pairs={{0,4},{4,0},{8,12},{12,8},{16,20},{20,16},{24,28},{28,24},{1,5},{5... | collective-permute-start | bytes 221192 | tf_op jit(solution)/shard_map/ppermute | solution.py:28
  14.6 0.5 collective-permute-start.2
  15.1 1.6 %turn.1 = (bf16[2048,256]{1,0:T(8,128)(2,1)S(1)}, bf16[128,2048]{1,0:T(8,128)(2,1)S(1)}, f32[8,128]{1,0:T(8,128)S(1)}) custom-call(s32[2]{0:T(128)S(1)} %pad_add_fusion.ids, bf16[4096,128]{1,0:T(8,128)(2,1)} %protos.1, f32[1,4096]{1,0:T(1,128)} %bitcast.18), custom_call_target="tpu_custom_call" | custom-call | tf_op jit(solution)/shard_map/turn/pallas_call | solution.py:319
  16.8 0.1 collective-permute-start.8
  16.8 0.0 collective-permute-done.refs_0_
  16.9 1.3 %collective-permute-done.4.refs_2_ = bf16[144,256]{1,0:T(8,128)(2,1)S(1)} collective-permute-done((bf16[144,256]{1,0:T(8,128)(2,1)S(1)}, bf16[144,256]{1,0:T(8,128)(2,1)S(1)}, u32[]{:S(2)}, u32[]{:S(2)}) %collective-permute-start.4) | collective-permute-done | bytes 73760 | tf_op jit(solution)/shard_map/ppermute | solution.py:28
  18.1 0.8 %collective-permute-done.2.refs_1_ = bf16[144,256]{1,0:T(8,128)(2,1)S(1)} collective-permute-done((bf16[144,256]{1,0:T(8,128)(2,1)S(1)}, bf16[144,256]{1,0:T(8,128)(2,1)S(1)}, u32[]{:S(2)}, u32[]{:S(2)}) %collective-permute-start.2) | collective-permute-done | bytes 73760 | tf_op jit(solution)/shard_map/ppermute | solution.py:28
  18.9 0.1 collective-permute-start.7
  19.0 3.0 %plan_ours.1 = (f32[2048,2048]{1,0:T(8,128)S(1)}, f32[2,2048,128]{2,1,0:T(8,128)S(1)}, f32[2,1024]{1,0:T(2,128)S(1)}, bf16[256,1024]{1,0:T(8,128)(2,1)S(1)}, bf16[128,1024]{1,0:T(8,128)(2,1)S(1)}) custom-call(s32[2]{0:T(128)S(1)} %pad_add_fusion.ids, bf16[2048,256]{1,0:T(8,128)(2,1)S(1)} %get-tuple-element.37.protos, bf16[4,144,256]{2,1,0:T(8,128)(2,1)S(1)} %stack.15.mine, ...), custom_call_target="tpu_custom_call" | custom-call | tf_op jit(solution)/shard_map/plan_ours/pallas_call | solution.py:319
  22.1 3.5 %plan_theirs.1 = (f32[2048,2048]{1,0:T(8,128)S(1)}, f32[2,2048,128]{2,1,0:T(8,128)S(1)}, f32[2,2048]{1,0:T(2,128)S(1)}, bf16[256,1024]{1,0:T(8,128)(2,1)S(1)}, bf16[128,1024]{1,0:T(8,128)(2,1)S(1)}) custom-call(s32[2]{0:T(128)S(1)} %pad_add_fusion.ids, bf16[2048,256]{1,0:T(8,128)(2,1)S(1)} %get-tuple-element.37.protos, ...), custom_call_target="tpu_custom_call", output_to_operand_aliasing={{0}: (4, {})} | custom-call | tf_op jit(solution)/shard_map/plan_theirs/pallas_call | solution.py:319
  25.6 0.6 collective-permute-start.9
  26.2 0.8 %collective-permute-done.9.right = f32[2,2048]{1,0:T(2,128)S(1)} collective-permute-done((f32[2,2048]{1,0:T(2,128)S(1)}, f32[2,2048]{1,0:T(2,128)S(1)}, u32[]{:S(2)}, u32[]{:S(2)}) %collective-permute-start.9) | collective-permute-done | bytes 16416 | tf_op jit(solution)/shard_map/ppermute | solution.py:28
  27.0 2.0 %collective-permute-start.12 = (f32[2,2048]{1,0:T(2,128)S(1)}, f32[2,2048]{1,0:T(2,128)S(1)}, u32[]{:S(2)}, u32[]{:S(2)}) collective-permute-start(f32[2,2048]{1,0:T(2,128)S(1)} %add.28.after.refs_0_), channel_id=1, source_target_pairs={{0,6},{1,7},{2,4},{3,5},{4,2},{5,3},{6,0},{7,1},{8,14},{9,15},{10,... | collective-permute-start | bytes 49160 | tf_op jit(solution)/shard_map/ppermute | solution.py:340
  29.0 1.0 %collective-permute-start.11 = (f32[2,2048]{1,0:T(2,128)S(1)}, f32[2,2048]{1,0:T(2,128)S(1)}, u32[]{:S(2)}, u32[]{:S(2)}) collective-permute-start(f32[2,2048]{1,0:T(2,128)S(1)} %add.28.after.refs_0_), channel_id=1, source_target_pairs={{0,4},{1,5},{2,6},{3,7},{4,0},{5,1},{6,2},{7,3},{8,12},{9,13},{10,... | collective-permute-start | bytes 49160 | tf_op jit(solution)/shard_map/ppermute | solution.py:340
  29.9 0.5 collective-permute-start.10
  30.5 1.3 %embed_before.1 = (f32[2048,512]{1,0:T(8,128)S(1)}, f32[8,128]{1,0:T(8,128)S(1)}) custom-call(bf16[2048,256]{1,0:T(8,128)(2,1)S(1)} %get-tuple-element.37.protos, bf16[256,1024]{1,0:T(8,128)(2,1)S(1)} %get-tuple-element.45.emb_a.emb_ext, bf16[256,1024]{1,0:T(8,128)(2,1)S(1)} %get-tuple-element.46.emb_b.emb_ext, f32[2,2048]{1,0:T(2,128)S(1)} %add.28.after.refs_0_), custom_call_target="tpu_custom_call" | custom-call | tf_op jit(solution)/shard_map/embed_before/pallas_call | solution.py:319
  31.8 0.9 %collective-permute-done.11.refs_2_ = f32[2,2048]{1,0:T(2,128)S(1)} collective-permute-done((f32[2,2048]{1,0:T(2,128)S(1)}, f32[2,2048]{1,0:T(2,128)S(1)}, u32[]{:S(2)}, u32[]{:S(2)}) %collective-permute-start.11) | collective-permute-done | bytes 16416 | tf_op jit(solution)/shard_map/ppermute | solution.py:340
  32.7 1.0 %collective-permute-done.10.refs_1_ = f32[2,2048]{1,0:T(2,128)S(1)} collective-permute-done((f32[2,2048]{1,0:T(2,128)S(1)}, f32[2,2048]{1,0:T(2,128)S(1)}, u32[]{:S(2)}, u32[]{:S(2)}) %collective-permute-start.10) | collective-permute-done | bytes 16416 | tf_op jit(solution)/shard_map/ppermute | solution.py:340
  33.7 2.5 %sweep.3 = (f32[2048,2048]{1,0:T(8,128)S(1)}, f32[2,2048]{1,0:T(2,128)S(1)}, f32[1,2048]{1,0:T(1,128)S(1)}) custom-call(f32[2048,2048]{1,0:T(8,128)S(1)} %get-tuple-element.42.plan, f32[2,2048,128]{2,1,0:T(8,128)S(1)} %get-tuple-element.43.cols, f32[2,2048]{1,0:T(2,128)S(1)} %add.28.after.refs_0_, ...), custom_call_target="tpu_custom_call", output_to_operand_aliasing={{0}: (0, {})} | custom-call | tf_op jit(solution)/shard_map/sweep/pallas_call | solution.py:319
  36.2 0.1 collective-permute-start.13
  36.3 1.2 %collective-permute-done.13.right = f32[1,2048]{1,0:T(1,128)S(1)} collective-permute-done((f32[1,2048]{1,0:T(1,128)S(1)}, f32[1,2048]{1,0:T(1,128)S(1)}, u32[]{:S(2)}, u32[]{:S(2)}) %collective-permute-start.13) | collective-permute-done | bytes 8224 | tf_op jit(solution)/shard_map/ppermute | solution.py:28
  37.5 1.0 %collective-permute-start.16 = (f32[1,2048]{1,0:T(1,128)S(1)}, f32[1,2048]{1,0:T(1,128)S(1)}, u32[]{:S(2)}, u32[]{:S(2)}) collective-permute-start(f32[1,2048]{1,0:T(1,128)S(1)} %add.29.after.refs_1_), channel_id=1, source_target_pairs={{0,6},{1,7},{2,4},{3,5},{4,2},{5,3},{6,0},{7,1},{8,14},{9,15},{10,... | collective-permute-start | bytes 24584 | tf_op jit(solution)/shard_map/ppermute | solution.py:340
  38.5 1.0 %collective-permute-start.15 = (f32[1,2048]{1,0:T(1,128)S(1)}, f32[1,2048]{1,0:T(1,128)S(1)}, u32[]{:S(2)}, u32[]{:S(2)}) collective-permute-start(f32[1,2048]{1,0:T(1,128)S(1)} %add.29.after.refs_1_), channel_id=1, source_target_pairs={{0,4},{1,5},{2,6},{3,7},{4,0},{5,1},{6,2},{7,3},{8,12},{9,13},{10,... | collective-permute-start | bytes 24584 | tf_op jit(solution)/shard_map/ppermute | solution.py:340
  39.5 1.5 %collective-permute-start.14 = (f32[1,2048]{1,0:T(1,128)S(1)}, f32[1,2048]{1,0:T(1,128)S(1)}, u32[]{:S(2)}, u32[]{:S(2)}) collective-permute-start(f32[1,2048]{1,0:T(1,128)S(1)} %add.29.after.refs_1_), channel_id=1, source_target_pairs={{0,2},{1,3},{2,0},{3,1},{4,6},{5,7},{6,4},{7,5},{8,10},{9,11},{10,... | collective-permute-start | bytes 24584 | tf_op jit(solution)/shard_map/ppermute | solution.py:340
  41.0 2.0 %proto_before.1 = (f32[512,2048]{1,0:T(8,128)S(1)}, f32[512,128]{1,0:T(8,128)S(1)}, f32[8,128]{1,0:T(8,128)S(1)}) custom-call(s32[2]{0:T(128)S(1)} %pad_add_fusion.ids, bf16[2048,256]{1,0:T(8,128)(2,1)S(1)} %get-tuple-element.37.protos, bf16[256,1024]{1,0:T(8,128)(2,1)S(1)} %get-tuple-element.45.emb_a.emb_ext, ...), custom_call_target="tpu_custom_call" | custom-call | tf_op jit(solution)/shard_map/proto_before/pallas_call | solution.py:319
  43.0 0.0 collective-permute-done.16.refs_4_
  43.0 0.1 collective-permute-done.14.refs_2_
  43.1 2.5 %sweep.4 = (f32[2048,2048]{1,0:T(8,128)S(1)}, f32[1,2048]{1,0:T(1,128)S(1)}) custom-call(f32[2048,2048]{1,0:T(8,128)S(1)} %get-tuple-element.48.plan, f32[2,2048,128]{2,1,0:T(8,128)S(1)} %get-tuple-element.43.cols, f32[2,2048]{1,0:T(2,128)S(1)} %get-tuple-element.49.refs_0_.sums, f32[1,2048]{1,0:T(1,128)S(1)} %add.29.after.refs_1_, ...), custom_call_target="tpu_custom_call", output_to_operand_aliasing={{0}: (0, {})} | custom-call | tf_op jit(solution)/shard_map/sweep/pallas_call | solution.py:319
  45.7 0.1 collective-permute-start.17
  45.7 1.2 %collective-permute-done.17.right = f32[1,2048]{1,0:T(1,128)S(1)} collective-permute-done((f32[1,2048]{1,0:T(1,128)S(1)}, f32[1,2048]{1,0:T(1,128)S(1)}, u32[]{:S(2)}, u32[]{:S(2)}) %collective-permute-start.17) | collective-permute-done | bytes 8224 | tf_op jit(solution)/shard_map/ppermute | solution.py:28
  46.9 2.0 %collective-permute-start.20 = (f32[1,2048]{1,0:T(1,128)S(1)}, f32[1,2048]{1,0:T(1,128)S(1)}, u32[]{:S(2)}, u32[]{:S(2)}) collective-permute-start(f32[1,2048]{1,0:T(1,128)S(1)} %add.30.after.refs_1_), channel_id=1, source_target_pairs={{0,6},{1,7},{2,4},{3,5},{4,2},{5,3},{6,0},{7,1},{8,14},{9,15},{10,... | collective-permute-start | bytes 24584 | tf_op jit(solution)/shard_map/ppermute | solution.py:340
  48.9 1.0 %collective-permute-start.19 = (f32[1,2048]{1,0:T(1,128)S(1)}, f32[1,2048]{1,0:T(1,128)S(1)}, u32[]{:S(2)}, u32[]{:S(2)}) collective-permute-start(f32[1,2048]{1,0:T(1,128)S(1)} %add.30.after.refs_1_), channel_id=1, source_target_pairs={{0,4},{1,5},{2,6},{3,7},{4,0},{5,1},{6,2},{7,3},{8,12},{9,13},{10,... | collective-permute-start | bytes 24584 | tf_op jit(solution)/shard_map/ppermute | solution.py:340
  49.9 0.5 collective-permute-start.18
  50.4 1.7 %cotangent.2 = (f32[2048,512]{1,0:T(8,128)S(1)}, f32[8,128]{1,0:T(8,128)S(1)}) custom-call(s32[2]{0:T(128)S(1)} %pad_add_fusion.ids, bf16[2048,256]{1,0:T(8,128)(2,1)S(1)} %get-tuple-element.37.protos, bf16[128,1024]{1,0:T(8,128)(2,1)S(1)} %get-tuple-element.51.view_a, bf16[128,1024]{1,0:T(8,128)(2,1)S(1)} %get-tuple-element.52.view_b, ...), custom_call_target="tpu_custom_call" | custom-call | tf_op jit(solution)/shard_map/cotangent/pallas_call | solution.py:319
  52.1 0.0 collective-permute-done.20.refs_4_
  52.1 0.4 collective-permute-done.19.refs_3_
  52.5 1.0 %collective-permute-done.18.refs_2_ = f32[1,2048]{1,0:T(1,128)S(1)} collective-permute-done((f32[1,2048]{1,0:T(1,128)S(1)}, f32[1,2048]{1,0:T(1,128)S(1)}, u32[]{:S(2)}, u32[]{:S(2)}) %collective-permute-start.18) | collective-permute-done | bytes 8224 | tf_op jit(solution)/shard_map/ppermute | solution.py:340
  53.5 2.5 %sweep.5 = (f32[2048,2048]{1,0:T(8,128)S(1)}, f32[1,2048]{1,0:T(1,128)S(1)}) custom-call(f32[2048,2048]{1,0:T(8,128)S(1)} %get-tuple-element.54.plan, f32[2,2048,128]{2,1,0:T(8,128)S(1)} %get-tuple-element.43.cols, f32[2,2048]{1,0:T(2,128)S(1)} %get-tuple-element.49.refs_0_.sums, f32[1,2048]{1,0:T(1,128)S(1)} %add.30.after.refs_1_, ...), custom_call_target="tpu_custom_call", output_to_operand_aliasing={{0}: (0, {})} | custom-call | tf_op jit(solution)/shard_map/sweep/pallas_call | solution.py:319
  56.0 0.1 collective-permute-start.21
  56.1 1.2 %collective-permute-done.21.right = f32[1,2048]{1,0:T(1,128)S(1)} collective-permute-done((f32[1,2048]{1,0:T(1,128)S(1)}, f32[1,2048]{1,0:T(1,128)S(1)}, u32[]{:S(2)}, u32[]{:S(2)}) %collective-permute-start.21) | collective-permute-done | bytes 8224 | tf_op jit(solution)/shard_map/ppermute | solution.py:28
  57.3 1.0 %collective-permute-start.24 = (f32[1,2048]{1,0:T(1,128)S(1)}, f32[1,2048]{1,0:T(1,128)S(1)}, u32[]{:S(2)}, u32[]{:S(2)}) collective-permute-start(f32[1,2048]{1,0:T(1,128)S(1)} %add.31.after.refs_0_), channel_id=1, source_target_pairs={{0,6},{1,7},{2,4},{3,5},{4,2},{5,3},{6,0},{7,1},{8,14},{9,15},{10,... | collective-permute-start | bytes 24584 | tf_op jit(solution)/shard_map/ppermute | solution.py:340
  58.3 1.0 %collective-permute-start.23 = (f32[1,2048]{1,0:T(1,128)S(1)}, f32[1,2048]{1,0:T(1,128)S(1)}, u32[]{:S(2)}, u32[]{:S(2)}) collective-permute-start(f32[1,2048]{1,0:T(1,128)S(1)} %add.31.after.refs_0_), channel_id=1, source_target_pairs={{0,4},{1,5},{2,6},{3,7},{4,0},{5,1},{6,2},{7,3},{8,12},{9,13},{10,... | collective-permute-start | bytes 24584 | tf_op jit(solution)/shard_map/ppermute | solution.py:340
  59.3 1.5 %collective-permute-start.22 = (f32[1,2048]{1,0:T(1,128)S(1)}, f32[1,2048]{1,0:T(1,128)S(1)}, u32[]{:S(2)}, u32[]{:S(2)}) collective-permute-start(f32[1,2048]{1,0:T(1,128)S(1)} %add.31.after.refs_0_), channel_id=1, source_target_pairs={{0,2},{1,3},{2,0},{3,1},{4,6},{5,7},{6,4},{7,5},{8,10},{9,11},{10,... | collective-permute-start | bytes 24584 | tf_op jit(solution)/shard_map/ppermute | solution.py:340
  60.8 1.2 %cotangent.3 = (f32[512,2048]{1,0:T(8,128)S(1)}, f32[8,128]{1,0:T(8,128)S(1)}) custom-call(s32[2]{0:T(128)S(1)} %pad_add_fusion.ids, bf16[2048,256]{1,0:T(8,128)(2,1)S(1)} %get-tuple-element.37.protos, bf16[128,1024]{1,0:T(8,128)(2,1)S(1)} %get-tuple-element.51.view_a, bf16[128,1024]{1,0:T(8,128)(2,1)S(1)} %get-tuple-element.52.view_b, ...), custom_call_target="tpu_custom_call" | custom-call | tf_op jit(solution)/shard_map/cotangent/pallas_call | solution.py:319
  62.0 0.9 %collective-permute-done.22.refs_1_ = f32[1,2048]{1,0:T(1,128)S(1)} collective-permute-done((f32[1,2048]{1,0:T(1,128)S(1)}, f32[1,2048]{1,0:T(1,128)S(1)}, u32[]{:S(2)}, u32[]{:S(2)}) %collective-permute-start.22) | collective-permute-done | bytes 8224 | tf_op jit(solution)/shard_map/ppermute | solution.py:340
  62.9 3.0 %embed_grad.1 = (f32[2048,128]{1,0:T(8,128)S(1)}, f32[1,2048]{1,0:T(1,128)S(1)}, f32[4,64,128]{2,1,0:T(8,128)S(1)}, f32[4,64,128]{2,1,0:T(8,128)S(1)}) custom-call(s32[2]{0:T(128)S(1)} %pad_add_fusion.ids, f32[2048,2048]{1,0:T(8,128)S(1)} %get-tuple-element.57.plan, f32[2,2048,128]{2,1,0:T(8,128)S(1)} %get-tuple-element.43.cols, ...), custom_call_target="tpu_custom_call" | custom-call | tf_op jit(solution)/shard_map/embed_grad/pallas_call | solution.py:319
  65.9 0.1 collective-permute-start.25
  66.0 1.0 %proto_grad.2 = (f32[512,128]{1,0:T(8,128)S(1)}, f32[8,128]{1,0:T(8,128)S(1)}) custom-call(s32[2]{0:T(128)S(1)} %pad_add_fusion.ids, bf16[256,1024]{1,0:T(8,128)(2,1)S(1)} %get-tuple-element.45.emb_a.emb_ext, f32[512,2048]{1,0:T(8,128)S(1)} %get-tuple-element.65.entries, f32[512,2048]{1,0:T(8,128)S(1)} %get-tuple-element.66.cots, ...), custom_call_target="tpu_custom_call" | custom-call | tf_op jit(solution)/shard_map/proto_grad/pallas_call | solution.py:319
  67.0 0.3 collective-permute-done.25.right
  67.3 1.6 %collective-permute-start.26 = (f32[64,128]{1,0:T(8,128)S(1)}, f32[64,128]{1,0:T(8,128)S(1)}, u32[]{:S(2)}, u32[]{:S(2)}) collective-permute-start(f32[64,128]{1,0:T(8,128)S(1)} %get-tuple-element.72), channel_id=1, source_target_pairs={{0,2},{1,3},{2,0},{3,1},{4,6},{5,7},{6,4},{7,5},{8,10},{9,11},{10,... | collective-permute-start | bytes 98312 | tf_op jit(solution)/shard_map/ppermute | solution.py:340
  68.9 1.0 %collective-permute-start.28 = (f32[64,128]{1,0:T(8,128)S(1)}, f32[64,128]{1,0:T(8,128)S(1)}, u32[]{:S(2)}, u32[]{:S(2)}) collective-permute-start(f32[64,128]{1,0:T(8,128)S(1)} %get-tuple-element.73), channel_id=1, source_target_pairs={{0,6},{1,7},{2,4},{3,5},{4,2},{5,3},{6,0},{7,1},{8,14},{9,15},{10,... | collective-permute-start | bytes 98312 | tf_op jit(solution)/shard_map/ppermute | solution.py:340
  69.9 1.0 %collective-permute-start.27 = (f32[64,128]{1,0:T(8,128)S(1)}, f32[64,128]{1,0:T(8,128)S(1)}, u32[]{:S(2)}, u32[]{:S(2)}) collective-permute-start(f32[64,128]{1,0:T(8,128)S(1)} %get-tuple-element.74), channel_id=1, source_target_pairs={{0,4},{1,5},{2,6},{3,7},{4,0},{5,1},{6,2},{7,3},{8,12},{9,13},{10,... | collective-permute-start | bytes 98312 | tf_op jit(solution)/shard_map/ppermute | solution.py:340
  70.9 1.7 %proto_grad.3 = f32[512,128]{1,0:T(8,128)} custom-call(s32[2]{0:T(128)S(1)} %pad_add_fusion.ids, bf16[256,1024]{1,0:T(8,128)(2,1)S(1)} %get-tuple-element.46.emb_b.emb_ext, f32[512,2048]{1,0:T(8,128)S(1)} %get-tuple-element.65.entries, f32[512,2048]{1,0:T(8,128)S(1)} %get-tuple-element.66.cots, f32[512,128]{1,0:T(8,128)S(1)} %get-tuple-element.71.so_far, ...), custom_call_target="tpu_custom_call" | custom-call | tf_op jit(solution)/shard_map/proto_grad/pallas_call | solution.py:319
  72.6 1.1 %collective-permute-done.28 = f32[64,128]{1,0:T(8,128)S(1)} collective-permute-done((f32[64,128]{1,0:T(8,128)S(1)}, f32[64,128]{1,0:T(8,128)S(1)}, u32[]{:S(2)}, u32[]{:S(2)}) %collective-permute-start.28) | collective-permute-done | bytes 32800 | tf_op jit(solution)/shard_map/ppermute | solution.py:340
  73.7 0.3 collective-permute-done.27
  74.1 0.6 fusion.2
  (18 shorter events, 0.1 us)
Async XLA Ops:
  1.7 7.9 %collective-permute-start.5 = (bf16[144,256]{1,0:T(8,128)(2,1)S(1)}, bf16[144,256]{1,0:T(8,128)(2,1)S(1)}, u32[]{:S(2)}, u32[]{:S(2)}) collective-permute-start(bf16[144,256]{1,0:T(8,128)(2,1)S(1)} %prepare.1.refs_0_), channel_id=1, source_target_pairs={{0,24},{4,28},{8,16},{12,20},{16,8},{20,12},{24,0},{28,4},{1,25},{... | collective-permute-start | bytes 221192 | tf_op jit(solution)/shard_map/ppermute | solution.py:28
  6.8 6.2 %collective-permute-start.3 = (bf16[144,256]{1,0:T(8,128)(2,1)S(1)}, bf16[144,256]{1,0:T(8,128)(2,1)S(1)}, u32[]{:S(2)}, u32[]{:S(2)}) collective-permute-start(bf16[144,256]{1,0:T(8,128)(2,1)S(1)} %prepare.1.refs_0_), channel_id=1, source_target_pairs={{0,16},{4,20},{8,24},{12,28},{16,0},{20,4},{24,8},{28,12},{1,17},{... | collective-permute-start | bytes 221192 | tf_op jit(solution)/shard_map/ppermute | solution.py:28
  6.8 7.7 %collective-permute-start.1 = (bf16[144,256]{1,0:T(8,128)(2,1)S(1)}, bf16[144,256]{1,0:T(8,128)(2,1)S(1)}, u32[]{:S(2)}, u32[]{:S(2)}) collective-permute-start(bf16[144,256]{1,0:T(8,128)(2,1)S(1)} %prepare.1.refs_0_), channel_id=1, source_target_pairs={{0,8},{4,12},{8,0},{12,4},{16,24},{20,28},{24,16},{28,20},{1,9},{5... | collective-permute-start | bytes 221192 | tf_op jit(solution)/shard_map/ppermute | solution.py:28
  7.5 9.4 %collective-permute-start = (bf16[144,256]{1,0:T(8,128)(2,1)S(1)}, bf16[144,256]{1,0:T(8,128)(2,1)S(1)}, u32[]{:S(2)}, u32[]{:S(2)}) collective-permute-start(bf16[144,256]{1,0:T(8,128)(2,1)S(1)} %prepare.1.refs_0_), channel_id=1, source_target_pairs={{0,4},{4,0},{8,12},{12,8},{16,20},{20,16},{24,28},{28,24},{1,5},{5... | collective-permute-start | bytes 221192 | tf_op jit(solution)/shard_map/ppermute | solution.py:28
  9.6 7.3 %collective-permute-start.6 = (bf16[144,256]{1,0:T(8,128)(2,1)S(1)}, bf16[144,256]{1,0:T(8,128)(2,1)S(1)}, u32[]{:S(2)}, u32[]{:S(2)}) collective-permute-start(bf16[144,256]{1,0:T(8,128)(2,1)S(1)} %collective-permute-done.5.refs_3_), channel_id=1, source_target_pairs={{0,4},{4,0},{8,12},{12,8},{16,20},{20,16},{24,28},{28,24},{1,5},{5... | collective-permute-start | bytes 221192 | tf_op jit(solution)/shard_map/ppermute | solution.py:28
  13.0 5.1 %collective-permute-start.4 = (bf16[144,256]{1,0:T(8,128)(2,1)S(1)}, bf16[144,256]{1,0:T(8,128)(2,1)S(1)}, u32[]{:S(2)}, u32[]{:S(2)}) collective-permute-start(bf16[144,256]{1,0:T(8,128)(2,1)S(1)} %collective-permute-done.3.refs_2_), channel_id=1, source_target_pairs={{0,4},{4,0},{8,12},{12,8},{16,20},{20,16},{24,28},{28,24},{1,5},{5... | collective-permute-start | bytes 221192 | tf_op jit(solution)/shard_map/ppermute | solution.py:28
  14.6 4.4 %collective-permute-start.2 = (bf16[144,256]{1,0:T(8,128)(2,1)S(1)}, bf16[144,256]{1,0:T(8,128)(2,1)S(1)}, u32[]{:S(2)}, u32[]{:S(2)}) collective-permute-start(bf16[144,256]{1,0:T(8,128)(2,1)S(1)} %collective-permute-done.1.refs_1_), channel_id=1, source_target_pairs={{0,4},{4,0},{8,12},{12,8},{16,20},{20,16},{24,28},{28,24},{1,5},{5... | collective-permute-start | bytes 221192 | tf_op jit(solution)/shard_map/ppermute | solution.py:28
  16.8 2.3 %collective-permute-start.8 = (bf16[4,144,256]{2,1,0:T(8,128)(2,1)S(1)}, bf16[4,144,256]{2,1,0:T(8,128)(2,1)S(1)}, u32[]{:S(2)}, u32[]{:S(2)}) collective-permute-start(bf16[4,144,256]{2,1,0:T(8,128)(2,1)S(1)} %stack.15.mine), channel_id=1, source_target_pairs={{0,1},{1,0},{2,3},{3,2},{4,5},{5,4},{6,7},{7,6},{8,9},{9,8},{10,11... | collective-permute-start | bytes 884744 | tf_op jit(solution)/shard_map/ppermute | solution.py:28
  18.9 3.1 %collective-permute-start.7 = (bf16[4,144,256]{2,1,0:T(8,128)(2,1)S(1)}, bf16[4,144,256]{2,1,0:T(8,128)(2,1)S(1)}, u32[]{:S(2)}, u32[]{:S(2)}) collective-permute-start(bf16[4,144,256]{2,1,0:T(8,128)(2,1)S(1)} %stack.14.mine), channel_id=1, source_target_pairs={{0,1},{1,0},{2,3},{3,2},{4,5},{5,4},{6,7},{7,6},{8,9},{9,8},{10,11... | collective-permute-start | bytes 884744 | tf_op jit(solution)/shard_map/ppermute | solution.py:28
  25.6 1.4 %collective-permute-start.9 = (f32[2,2048]{1,0:T(2,128)S(1)}, f32[2,2048]{1,0:T(2,128)S(1)}, u32[]{:S(2)}, u32[]{:S(2)}) collective-permute-start(f32[2,2048]{1,0:T(2,128)S(1)} %get-tuple-element.44.left), channel_id=1, source_target_pairs={{0,1},{1,0},{2,3},{3,2},{4,5},{5,4},{6,7},{7,6},{8,9},{9,8},{10,11... | collective-permute-start | bytes 49160 | tf_op jit(solution)/shard_map/ppermute | solution.py:28
  27.0 4.8 %collective-permute-start.12 = (f32[2,2048]{1,0:T(2,128)S(1)}, f32[2,2048]{1,0:T(2,128)S(1)}, u32[]{:S(2)}, u32[]{:S(2)}) collective-permute-start(f32[2,2048]{1,0:T(2,128)S(1)} %add.28.after.refs_0_), channel_id=1, source_target_pairs={{0,6},{1,7},{2,4},{3,5},{4,2},{5,3},{6,0},{7,1},{8,14},{9,15},{10,... | collective-permute-start | bytes 49160 | tf_op jit(solution)/shard_map/ppermute | solution.py:340
  29.0 3.7 %collective-permute-start.11 = (f32[2,2048]{1,0:T(2,128)S(1)}, f32[2,2048]{1,0:T(2,128)S(1)}, u32[]{:S(2)}, u32[]{:S(2)}) collective-permute-start(f32[2,2048]{1,0:T(2,128)S(1)} %add.28.after.refs_0_), channel_id=1, source_target_pairs={{0,4},{1,5},{2,6},{3,7},{4,0},{5,1},{6,2},{7,3},{8,12},{9,13},{10,... | collective-permute-start | bytes 49160 | tf_op jit(solution)/shard_map/ppermute | solution.py:340
  29.9 3.7 %collective-permute-start.10 = (f32[2,2048]{1,0:T(2,128)S(1)}, f32[2,2048]{1,0:T(2,128)S(1)}, u32[]{:S(2)}, u32[]{:S(2)}) collective-permute-start(f32[2,2048]{1,0:T(2,128)S(1)} %add.28.after.refs_0_), channel_id=1, source_target_pairs={{0,2},{1,3},{2,0},{3,1},{4,6},{5,7},{6,4},{7,5},{8,10},{9,11},{10,... | collective-permute-start | bytes 49160 | tf_op jit(solution)/shard_map/ppermute | solution.py:340
  36.2 1.2 %collective-permute-start.13 = (f32[1,2048]{1,0:T(1,128)S(1)}, f32[1,2048]{1,0:T(1,128)S(1)}, u32[]{:S(2)}, u32[]{:S(2)}) collective-permute-start(f32[1,2048]{1,0:T(1,128)S(1)} %get-tuple-element.50.left), channel_id=1, source_target_pairs={{0,1},{1,0},{2,3},{3,2},{4,5},{5,4},{6,7},{7,6},{8,9},{9,8},{10,11... | collective-permute-start | bytes 24584 | tf_op jit(solution)/shard_map/ppermute | solution.py:28
  37.5 5.5 %collective-permute-start.16 = (f32[1,2048]{1,0:T(1,128)S(1)}, f32[1,2048]{1,0:T(1,128)S(1)}, u32[]{:S(2)}, u32[]{:S(2)}) collective-permute-start(f32[1,2048]{1,0:T(1,128)S(1)} %add.29.after.refs_1_), channel_id=1, source_target_pairs={{0,6},{1,7},{2,4},{3,5},{4,2},{5,3},{6,0},{7,1},{8,14},{9,15},{10,... | collective-permute-start | bytes 24584 | tf_op jit(solution)/shard_map/ppermute | solution.py:340
  38.5 4.5 %collective-permute-start.15 = (f32[1,2048]{1,0:T(1,128)S(1)}, f32[1,2048]{1,0:T(1,128)S(1)}, u32[]{:S(2)}, u32[]{:S(2)}) collective-permute-start(f32[1,2048]{1,0:T(1,128)S(1)} %add.29.after.refs_1_), channel_id=1, source_target_pairs={{0,4},{1,5},{2,6},{3,7},{4,0},{5,1},{6,2},{7,3},{8,12},{9,13},{10,... | collective-permute-start | bytes 24584 | tf_op jit(solution)/shard_map/ppermute | solution.py:340
  39.5 3.7 %collective-permute-start.14 = (f32[1,2048]{1,0:T(1,128)S(1)}, f32[1,2048]{1,0:T(1,128)S(1)}, u32[]{:S(2)}, u32[]{:S(2)}) collective-permute-start(f32[1,2048]{1,0:T(1,128)S(1)} %add.29.after.refs_1_), channel_id=1, source_target_pairs={{0,2},{1,3},{2,0},{3,1},{4,6},{5,7},{6,4},{7,5},{8,10},{9,11},{10,... | collective-permute-start | bytes 24584 | tf_op jit(solution)/shard_map/ppermute | solution.py:340
  45.7 1.2 %collective-permute-start.17 = (f32[1,2048]{1,0:T(1,128)S(1)}, f32[1,2048]{1,0:T(1,128)S(1)}, u32[]{:S(2)}, u32[]{:S(2)}) collective-permute-start(f32[1,2048]{1,0:T(1,128)S(1)} %get-tuple-element.55.left), channel_id=1, source_target_pairs={{0,1},{1,0},{2,3},{3,2},{4,5},{5,4},{6,7},{7,6},{8,9},{9,8},{10,11... | collective-permute-start | bytes 24584 | tf_op jit(solution)/shard_map/ppermute | solution.py:28
  46.9 5.2 %collective-permute-start.20 = (f32[1,2048]{1,0:T(1,128)S(1)}, f32[1,2048]{1,0:T(1,128)S(1)}, u32[]{:S(2)}, u32[]{:S(2)}) collective-permute-start(f32[1,2048]{1,0:T(1,128)S(1)} %add.30.after.refs_1_), channel_id=1, source_target_pairs={{0,6},{1,7},{2,4},{3,5},{4,2},{5,3},{6,0},{7,1},{8,14},{9,15},{10,... | collective-permute-start | bytes 24584 | tf_op jit(solution)/shard_map/ppermute | solution.py:340
  48.9 3.7 %collective-permute-start.19 = (f32[1,2048]{1,0:T(1,128)S(1)}, f32[1,2048]{1,0:T(1,128)S(1)}, u32[]{:S(2)}, u32[]{:S(2)}) collective-permute-start(f32[1,2048]{1,0:T(1,128)S(1)} %add.30.after.refs_1_), channel_id=1, source_target_pairs={{0,4},{1,5},{2,6},{3,7},{4,0},{5,1},{6,2},{7,3},{8,12},{9,13},{10,... | collective-permute-start | bytes 24584 | tf_op jit(solution)/shard_map/ppermute | solution.py:340
  49.9 3.7 %collective-permute-start.18 = (f32[1,2048]{1,0:T(1,128)S(1)}, f32[1,2048]{1,0:T(1,128)S(1)}, u32[]{:S(2)}, u32[]{:S(2)}) collective-permute-start(f32[1,2048]{1,0:T(1,128)S(1)} %add.30.after.refs_1_), channel_id=1, source_target_pairs={{0,2},{1,3},{2,0},{3,1},{4,6},{5,7},{6,4},{7,5},{8,10},{9,11},{10,... | collective-permute-start | bytes 24584 | tf_op jit(solution)/shard_map/ppermute | solution.py:340
  56.0 1.2 %collective-permute-start.21 = (f32[1,2048]{1,0:T(1,128)S(1)}, f32[1,2048]{1,0:T(1,128)S(1)}, u32[]{:S(2)}, u32[]{:S(2)}) collective-permute-start(f32[1,2048]{1,0:T(1,128)S(1)} %get-tuple-element.61.left), channel_id=1, source_target_pairs={{0,1},{1,0},{2,3},{3,2},{4,5},{5,4},{6,7},{7,6},{8,9},{9,8},{10,11... | collective-permute-start | bytes 24584 | tf_op jit(solution)/shard_map/ppermute | solution.py:28
  57.3 4.7 %collective-permute-start.24 = (f32[1,2048]{1,0:T(1,128)S(1)}, f32[1,2048]{1,0:T(1,128)S(1)}, u32[]{:S(2)}, u32[]{:S(2)}) collective-permute-start(f32[1,2048]{1,0:T(1,128)S(1)} %add.31.after.refs_0_), channel_id=1, source_target_pairs={{0,6},{1,7},{2,4},{3,5},{4,2},{5,3},{6,0},{7,1},{8,14},{9,15},{10,... | collective-permute-start | bytes 24584 | tf_op jit(solution)/shard_map/ppermute | solution.py:340
  58.3 3.7 %collective-permute-start.23 = (f32[1,2048]{1,0:T(1,128)S(1)}, f32[1,2048]{1,0:T(1,128)S(1)}, u32[]{:S(2)}, u32[]{:S(2)}) collective-permute-start(f32[1,2048]{1,0:T(1,128)S(1)} %add.31.after.refs_0_), channel_id=1, source_target_pairs={{0,4},{1,5},{2,6},{3,7},{4,0},{5,1},{6,2},{7,3},{8,12},{9,13},{10,... | collective-permute-start | bytes 24584 | tf_op jit(solution)/shard_map/ppermute | solution.py:340
  59.3 3.7 %collective-permute-start.22 = (f32[1,2048]{1,0:T(1,128)S(1)}, f32[1,2048]{1,0:T(1,128)S(1)}, u32[]{:S(2)}, u32[]{:S(2)}) collective-permute-start(f32[1,2048]{1,0:T(1,128)S(1)} %add.31.after.refs_0_), channel_id=1, source_target_pairs={{0,2},{1,3},{2,0},{3,1},{4,6},{5,7},{6,4},{7,5},{8,10},{9,11},{10,... | collective-permute-start | bytes 24584 | tf_op jit(solution)/shard_map/ppermute | solution.py:340
  65.9 1.4 %collective-permute-start.25 = (f32[4,64,128]{2,1,0:T(8,128)S(1)}, f32[4,64,128]{2,1,0:T(8,128)S(1)}, u32[]{:S(2)}, u32[]{:S(2)}) collective-permute-start(f32[4,64,128]{2,1,0:T(8,128)S(1)} %get-tuple-element.64), channel_id=1, source_target_pairs={{0,1},{1,0},{2,3},{3,2},{4,5},{5,4},{6,7},{7,6},{8,9},{9,8},{10,11... | collective-permute-start | bytes 393224 | tf_op jit(solution)/shard_map/ppermute | solution.py:28
  67.3 5.3 %collective-permute-start.26 = (f32[64,128]{1,0:T(8,128)S(1)}, f32[64,128]{1,0:T(8,128)S(1)}, u32[]{:S(2)}, u32[]{:S(2)}) collective-permute-start(f32[64,128]{1,0:T(8,128)S(1)} %get-tuple-element.72), channel_id=1, source_target_pairs={{0,2},{1,3},{2,0},{3,1},{4,6},{5,7},{6,4},{7,5},{8,10},{9,11},{10,... | collective-permute-start | bytes 98312 | tf_op jit(solution)/shard_map/ppermute | solution.py:340
  68.9 4.8 %collective-permute-start.28 = (f32[64,128]{1,0:T(8,128)S(1)}, f32[64,128]{1,0:T(8,128)S(1)}, u32[]{:S(2)}, u32[]{:S(2)}) collective-permute-start(f32[64,128]{1,0:T(8,128)S(1)} %get-tuple-element.73), channel_id=1, source_target_pairs={{0,6},{1,7},{2,4},{3,5},{4,2},{5,3},{6,0},{7,1},{8,14},{9,15},{10,... | collective-permute-start | bytes 98312 | tf_op jit(solution)/shard_map/ppermute | solution.py:340
  69.9 4.1 %collective-permute-start.27 = (f32[64,128]{1,0:T(8,128)S(1)}, f32[64,128]{1,0:T(8,128)S(1)}, u32[]{:S(2)}, u32[]{:S(2)}) collective-permute-start(f32[64,128]{1,0:T(8,128)S(1)} %get-tuple-element.74), channel_id=1, source_target_pairs={{0,4},{1,5},{2,6},{3,7},{4,0},{5,1},{6,2},{7,3},{8,12},{9,13},{10,... | collective-permute-start | bytes 98312 | tf_op jit(solution)/shard_map/ppermute | solution.py:340
